TPU v7x, 32 devices: a whole 2x2x4 slice. The times are simulated.
32 devices in a mesh: member: 2 (over y), tile: 4 (over z), sub: 2 (over x), comp: 2 (over core).
Axes of the slice: x: 2, y: 2, z: 4, core: 2. Of those that a mesh axis runs over, the one named last changes fastest.
Arguments:
- atm_state: float32 [3, 16, 128, 512], P(None, None, ('member', 'tile'), ('sub', 'comp')), parts along dimension 2, may hold values from -6 to 6
- air_temp: float32 [128, 512], P(('member', 'tile'), ('sub', 'comp')), parts along dimension 0, may hold values from -6 to 6
- depth: float32 [128, 512], P(('member', 'tile'), ('sub', 'comp')), parts along dimension 0, may hold values from 0.5 to 1.5
- wave_speed: float32 [16], replicated, may hold values from 0.1 to 0.6
- ocean_state: float32 [2, 8, 128, 512], P(None, None, ('member', 'tile'), ('sub', 'comp')), parts along dimension 2, may hold values from -6 to 6
- wet_mask: int32 [128, 512], P(('member', 'tile'), ('sub', 'comp')), parts along dimension 0, may hold values 0 or 1
- diffusivity: float32 [128, 512], P(('member', 'tile'), ('sub', 'comp')), parts along dimension 0, may hold values from 0.05 to 0.2
- xg_atm_cell: int32 [8, 4, 2048], P(('member', 'tile'), ('sub', 'comp')), parts along dimension 0, may hold values from 0 to 2047
- xg_dest: int32 [8, 4, 2048, 1], P(('member', 'tile'), ('sub', 'comp')), parts along dimension 0, may hold values from 0 to 3; in each aligned block of 2048 rows (0 to 2047, 2048 to 4095, ..., all dimensions but the last counted through in order) at most 512 rows name the same one
- xg_ocean_cell: int32 [8, 4, 2048], P(('member', 'tile'), ('sub', 'comp')), parts along dimension 0, may hold values from 0 to 2047
- xg_weight: float32 [8, 4, 2048], P(('member', 'tile'), ('sub', 'comp')), parts along dimension 0, may hold values from 0.2 to 1
Outputs:
- atm_out: float32 [3, 16, 128, 512], P(None, None, ('member', 'tile'), ('sub', 'comp')), parts along dimension 2
- ocean_out: float32 [2, 8, 128, 512], P(None, None, ('member', 'tile'), ('sub', 'comp')), parts along dimension 2
There are 2 independent parts, one for each index of `member`. A program takes and returns all parts, laid end to end along the dimension named above; an argument that names none is the same for every part. Nothing has to cross between parts.
Inputs may be any that keep to these rules, and one draw needn't show every extreme that they name: `xg_dest`: of the 2048 exchange-grid cells of one device at most 512 name any one row block, and some device names one row block exactly 512 times in every draw.
All inputs are finite; a program needn't handle non-finite values. No bound on the sum of `wet_mask` on one device may be relied on, other than what follows from the above.
Results may differ from a plain program's by a relative error of at most 0.00002.
Values sent between devices are 32-bit elements; how exact they have to be, the bound alone decides.
No kernel may reach another device: no remote copies, remote signals or barrier semaphores. Data moves between devices by JAX's collectives and lax.ppermute only.
A program may use at most 64 MiB of HBM per device.

v0:
```python
import jax
import jax.numpy as jnp
from jax import lax
from jax.sharding import PartitionSpec as P

ACOUSTIC = 2
OCEAN_STEPS = 2


atm_gain = 0.5
sea_gain = 0.5


def padded_2(block, sides, width):
    for axis, dim in sides:
        count = lax.axis_size(axis)
        forward = [(i, i + 1) for i in range(count - 1)]
        forward.append((count - 1, 0))
        backward = [(target, source) for source, target in forward]
        low = lax.ppermute(
            lax.slice_in_dim(block, block.shape[dim] - width, None, axis=dim), axis, forward
        )
        high = lax.ppermute(lax.slice_in_dim(block, 0, width, axis=dim), axis, backward)
        block = jnp.concatenate([low, block, high], axis=dim)
    return block


def trim(field, cycle):
    return field[..., cycle : field.shape[-2] - cycle, cycle : field.shape[-1] - cycle]


def east_west(padded):
    return (padded[..., 1:-1, 2:] - padded[..., 1:-1, :-2]) * 0.5


def north_south(padded):
    return (padded[..., 2:, 1:-1] - padded[..., :-2, 1:-1]) * 0.5


def diffuse_padded(padded, padded_wet, kappa):
    center = trim(padded, 1)
    total = padded_wet[1:-1, 2:] * (padded[..., 1:-1, 2:] - center)
    total = total + padded_wet[1:-1, :-2] * (padded[..., 1:-1, :-2] - center)
    total = total + padded_wet[2:, 1:-1] * (padded[..., 2:, 1:-1] - center)
    total = total + padded_wet[:-2, 1:-1] * (padded[..., :-2, 1:-1] - center)
    return center + kappa * (trim(padded_wet, 1) * total)


def on_device(
    atm_state,
    air_temp,
    depth,
    wave_speed,
    ocean_state,
    wet_mask,
    diffusivity,
    xg_atm_cell,
    xg_dest,
    xg_ocean_cell,
    xg_weight,
):
    levels = atm_state.shape[1]
    tile_count = lax.axis_size("tile")
    atm_cells = xg_atm_cell[0, 0]
    sea_cells = xg_ocean_cell[0, 0]
    weights = xg_weight[0, 0]
    target = xg_dest[0, 0, :, 0]
    xcount = atm_cells.shape[0]
    capacity = 4 * xcount // max(tile_count, 16)
    ordering = jnp.argsort(target, stable=True)
    sorted_target = target[ordering]
    counts = jnp.sum(
        (target[:, None] == jnp.arange(tile_count, dtype=jnp.int32)[None, :]).astype(jnp.int32), 0
    )
    offsets = jnp.cumsum(counts) - counts
    ranking = jnp.arange(xcount, dtype=jnp.int32) - offsets[sorted_target]
    position = jnp.zeros((xcount,), jnp.int32).at[ordering].set(sorted_target * capacity + ranking)
    slots = tile_count * capacity
    surface_sea = ocean_state[0, 0].reshape(-1)
    air_flat = air_temp.reshape(-1)
    air_slot = air_flat[atm_cells]
    index_buffer = (
        jnp.zeros((slots,), jnp.int32).at[position].set(sea_cells).reshape(tile_count, capacity)
    )
    received = lax.all_to_all(index_buffer, "tile", split_axis=0, concat_axis=0, tiled=True)
    surface_values = surface_sea[received]
    returned = lax.all_to_all(surface_values, "tile", split_axis=0, concat_axis=0, tiled=True)
    surface_slot = returned.reshape(-1)[position]
    heat_flux = weights * (air_slot - surface_slot)
    flux_buffer = (
        jnp.zeros((slots,), jnp.float32).at[position].set(heat_flux).reshape(tile_count, capacity)
    )
    got_flux = lax.all_to_all(flux_buffer, "tile", split_axis=0, concat_axis=0, tiled=True)
    atm_flux = (
        jnp.zeros(air_flat.shape, jnp.float32).at[atm_cells].add(heat_flux).reshape(air_temp.shape)
    )
    sea_flux = (
        jnp.zeros(surface_sea.shape, jnp.float32)
        .at[received.reshape(-1)]
        .add(got_flux.reshape(-1))
        .reshape(ocean_state.shape[2:])
    )
    wetness = wet_mask.astype(jnp.float32)
    column_speed = wave_speed[:, None, None] * depth[None]
    winds_east, winds_north, height = (atm_state[0], atm_state[1], atm_state[2])
    for substep in range(ACOUSTIC):
        padded = padded_2(
            jnp.stack([winds_east, winds_north]), (("tile", 2), (("sub", "comp"), 3)), 1
        )
        height = height - column_speed * (east_west(padded[0]) + north_south(padded[1]))
        padded_height = padded_2(height, (("tile", 1), (("sub", "comp"), 2)), 1)
        winds_east = winds_east - east_west(padded_height)
        winds_north = winds_north - north_south(padded_height)
    padded_wet = padded_2(wetness, (("tile", 0), (("sub", "comp"), 1)), 1)
    tracers = ocean_state
    for substep in range(OCEAN_STEPS):
        padded_tracers = padded_2(tracers, (("tile", 2), (("sub", "comp"), 3)), 1)
        tracers = diffuse_padded(padded_tracers, padded_wet, diffusivity)
    height = height.at[levels - 1].add(-atm_gain * atm_flux)
    tracers = tracers.at[0, 0].add(sea_gain * sea_flux)
    return (jnp.stack([winds_east, winds_north, height]), tracers)


def solution(mesh):
    return jax.shard_map(
        on_device,
        mesh=mesh,
        in_specs=(
            P(None, None, ("member", "tile"), ("sub", "comp")),
            P(("member", "tile"), ("sub", "comp")),
            P(("member", "tile"), ("sub", "comp")),
            P(),
            P(None, None, ("member", "tile"), ("sub", "comp")),
            P(("member", "tile"), ("sub", "comp")),
            P(("member", "tile"), ("sub", "comp")),
            P(("member", "tile"), ("sub", "comp"), None),
            P(("member", "tile"), ("sub", "comp"), None, None),
            P(("member", "tile"), ("sub", "comp"), None),
            P(("member", "tile"), ("sub", "comp"), None),
        ),
        out_specs=(
            P(None, None, ("member", "tile"), ("sub", "comp")),
            P(None, None, ("member", "tile"), ("sub", "comp")),
        ),
        check_vma=False,
    )
```

profile of v0, /device:TPU:0, one launch (start us, length us, event | category | flops | bytes accessed | tf_op | source)
XLA Modules:
  0.0 199.5 jit_solution(5005152355330076453)
XLA Ops:
  0.7 1.0 fusion.64
  1.7 5.1 %collective-permute-start.1 = (f32[2,16,1,128]{3,2,1,0:T(1,128)S(1)}, f32[2,16,1,128]{3,2,1,0:T(1,128)S(1)}, u32[]{:S(2)}, u32[]{:S(2)}) collective-permute-start(f32[2,16,1,128]{3,2,1,0:T(1,128)S(1)} %get-tuple-element.39), channel_id=1, source_target_pairs={{4,0},{8,4},{12,8},{0,12},{5,1},{9,5},{13,9},{1,13},{6,2},{10,6},{... | collective-permute-start | bytes 49160 | tf_op jit(solution)/shard_map/ppermute | solution.py:23
  6.9 5.0 %sort.17 = (s32[2048]{0:T(1024)}, s32[2048]{0:T(1024)S(1)}) sort(s32[2048]{0:T(1024)S(1)} %bitcast.64, s32[2048]{0:T(1024)S(1)} %iota.11), dimensions={0}, to_apply=%region_0.0 | sort | flops 22528 | bytes 32768 | tf_op jit(solution)/shard_map/jit(argsort)/sort | solution.py:70
  12.0 11.8 %gather_fusion.1 = s32[2048]{0:T(1024)S(1)} fusion(s32[2048]{0:T(1024)S(1)} %bitcast.65, s32[2048]{0:T(1024)S(1)} %get-tuple-element.70), kind=kCustom, calls=%fused_computation.1 | custom fusion | bytes 24576 | tf_op jit(solution)/shard_map/gather | solution.py:71
  23.9 0.6 fusion.75
  24.6 2.5 %compare_select_fusion.4 = s32[2048,1]{0,1:T(1,128)S(1)} fusion(s32[2048,1]{0,1:T(1,128)S(1)} %bitcast.72, s32[]{:T(128)} %bitcast.21, s32[]{:T(128)} %bitcast.22, s32[]{:T(128)} %bitcast.24, s32[]{:T(128)} %bitcast.23), kind=kLoop, calls=%fused_computation.114 | loop fusion | flops 18432 | bytes 16400 | tf_op jit(solution)/shard_map/gather | solution.py:76
  27.1 8.0 %scatter_custom_fusion = s32[2048]{0:T(1024)S(1)} fusion(s32[2048]{0:T(1024)S(1)} %get-tuple-element.71, s32[2048]{0:T(1024)S(1)} %subtract_add_fusion, s32[]{:T(128)} %constant.73.clone.1), kind=kCustom, calls=%fused_computation.144 | custom fusion | bytes 8196 | tf_op jit(solution)/shard_map/scatter | solution.py:77
  35.2 8.8 %scatter_custom_fusion.1 = s32[2048]{0:T(1024)} fusion(s32[2048]{0:T(1024)S(1)} %get-tuple-element.69, s32[2048]{0:T(1024)} %bitcast.81, s32[]{:T(128)} %constant.73.clone.1), kind=kCustom, calls=%fused_computation.142 | custom fusion | bytes 8704 | tf_op jit(solution)/shard_map/scatter | solution.py:83
  44.0 5.1 %all-to-all-start = ((s32[4,1,512]{2,1,0:T(1,128)}), s32[4,1,512]{2,1,0:T(1,128)S(1)}, u32[]{:S(2)}, u32[]{:S(2)}) async-start(s32[4,1,512]{2,1,0:T(1,128)} %bitcast.27), calls=%async_computation | async-start | bytes 16384 | tf_op jit(solution)/shard_map/all_to_all | solution.py:85
  49.1 2.1 %collective-permute-start.19 = (f32[2,8,1,128]{3,2,1,0:T(1,128)S(1)}, f32[2,8,1,128]{3,2,1,0:T(1,128)S(1)}, u32[]{:S(2)}, u32[]{:S(2)}) collective-permute-start(f32[2,8,1,128]{3,2,1,0:T(1,128)S(1)} %get-tuple-element.55), channel_id=1, source_target_pairs={{0,4},{4,8},{8,12},{12,0},{1,5},{5,9},{9,13},{13,1},{2,6},{6,10},{... | collective-permute-start | bytes 24584 | tf_op jit(solution)/shard_map/ppermute | solution.py:20
  51.2 2.4 %collective-permute-start.17 = (f32[1,128]{1,0:T(1,128)S(1)}, f32[1,128]{1,0:T(1,128)S(1)}, u32[]{:S(2)}, u32[]{:S(2)}) collective-permute-start(f32[1,128]{1,0:T(1,128)S(1)} %get-tuple-element.66), channel_id=1, source_target_pairs={{4,0},{8,4},{12,8},{0,12},{5,1},{9,5},{13,9},{1,13},{6,2},{10,6},{... | collective-permute-start | bytes 1544 | tf_op jit(solution)/shard_map/ppermute | solution.py:23
  53.6 0.7 copy-done.8
  54.4 11.8 %gather_fusion = f32[2048]{0:T(1024)S(1)} fusion(f32[2048]{0:T(1024)S(1)} %bitcast.62, s32[2048]{0:T(1024)S(1)} %broadcast_clamp_fusion.3), kind=kCustom, calls=%fused_computation | custom fusion | bytes 24576 | tf_op jit(solution)/shard_map/gather | solution.py:81
  66.2 3.2 %collective-permute-start.20 = (f32[2,8,1,128]{3,2,1,0:T(1,128)S(1)}, f32[2,8,1,128]{3,2,1,0:T(1,128)S(1)}, u32[]{:S(2)}, u32[]{:S(2)}) collective-permute-start(f32[2,8,1,128]{3,2,1,0:T(1,128)S(1)} %get-tuple-element.54), channel_id=1, source_target_pairs={{4,0},{8,4},{12,8},{0,12},{5,1},{9,5},{13,9},{1,13},{6,2},{10,6},{... | collective-permute-start | bytes 24584 | tf_op jit(solution)/shard_map/ppermute | solution.py:23
  69.4 0.5 collective-permute-start.22
  69.9 0.8 collective-permute-done.20
  71.3 1.3 collective-permute-start.21
  72.8 3.2 %collective-permute-done.23 = f32[2,8,18,1]{3,2,1,0:T(8,128)S(1)} collective-permute-done((f32[2,8,18,1]{3,2,1,0:T(8,128)S(1)}, f32[2,8,18,1]{3,2,1,0:T(8,128)S(1)}, u32[]{:S(2)}, u32[]{:S(2)}) %collective-permute-start.23) | collective-permute-done | bytes 1184 | tf_op jit(solution)/shard_map/ppermute | solution.py:20
  76.0 1.1 collective-permute-done.21
  77.4 4.1 %collective-permute-start.25 = (f32[2,8,1,128]{3,2,1,0:T(1,128)S(1)}, f32[2,8,1,128]{3,2,1,0:T(1,128)S(1)}, u32[]{:S(2)}, u32[]{:S(2)}) collective-permute-start(f32[2,8,1,128]{3,2,1,0:T(1,128)S(1)} %get-tuple-element.52), channel_id=1, source_target_pairs={{4,0},{8,4},{12,8},{0,12},{5,1},{9,5},{13,9},{1,13},{6,2},{10,6},{... | collective-permute-start | bytes 24584 | tf_op jit(solution)/shard_map/ppermute | solution.py:23
  81.6 20.6 %gather_fusion.2 = f32[2048]{0:T(1024)} fusion(f32[2048]{0:T(1024)S(1)} %slice_bitcast_fusion.4, s32[2048]{0:T(1024)S(1)} %broadcast_clamp_fusion.1), kind=kCustom, calls=%fused_computation.2 | custom fusion | bytes 24576 | tf_op jit(solution)/shard_map/gather | solution.py:86
  102.2 3.2 %all-to-all-start.1 = ((f32[4,1,512]{2,1,0:T(1,128)}), f32[4,1,512]{2,1,0:T(1,128)S(1)}, u32[]{:S(2)}, u32[]{:S(2)}) async-start(f32[4,1,512]{2,1,0:T(1,128)} %bitcast.30), calls=%async_computation.1 | async-start | bytes 16384 | tf_op jit(solution)/shard_map/all_to_all | solution.py:87
  105.7 1.7 collective-permute-start.3
  107.4 9.5 %collective-permute-done.3 = f32[2,16,18,1]{3,2,1,0:T(8,128)S(1)} collective-permute-done((f32[2,16,18,1]{3,2,1,0:T(8,128)S(1)}, f32[2,16,18,1]{3,2,1,0:T(8,128)S(1)}, u32[]{:S(2)}, u32[]{:S(2)}) %collective-permute-start.3) | collective-permute-done | bytes 2336 | tf_op jit(solution)/shard_map/ppermute | solution.py:23
  116.9 1.0 collective-permute-done.2
  117.9 0.5 pad_maximum_fusion
  118.5 0.6 copy-done.6
  119.3 3.5 %collective-permute-start.5 = (f32[16,1,128]{2,1,0:T(1,128)S(1)}, f32[16,1,128]{2,1,0:T(1,128)S(1)}, u32[]{:S(2)}, u32[]{:S(2)}) collective-permute-start(f32[16,1,128]{2,1,0:T(1,128)S(1)} %get-tuple-element.58), channel_id=1, source_target_pairs={{4,0},{8,4},{12,8},{0,12},{5,1},{9,5},{13,9},{1,13},{6,2},{10,6},{... | collective-permute-start | bytes 24584 | tf_op jit(solution)/shard_map/ppermute | solution.py:23
  122.9 1.3 collective-permute-done.5
  124.2 4.1 %collective-permute-done.4 = f32[16,1,128]{2,1,0:T(1,128)S(1)} collective-permute-done((f32[16,1,128]{2,1,0:T(1,128)S(1)}, f32[16,1,128]{2,1,0:T(1,128)S(1)}, u32[]{:S(2)}, u32[]{:S(2)}) %collective-permute-start.4) | collective-permute-done | bytes 8224 | tf_op jit(solution)/shard_map/ppermute | solution.py:20
  128.5 1.7 collective-permute-start.6
  130.4 1.7 collective-permute-start.26
  132.2 11.8 %gather_fusion.3 = f32[2048]{0:T(1024)S(1)} fusion(f32[2048]{0:T(1024)S(1)} %bitcast.66, s32[2048]{0:T(1024)S(1)} %get-tuple-element.68), kind=kCustom, calls=%fused_computation.3 | custom fusion | bytes 24576 | tf_op jit(solution)/shard_map/gather | solution.py:88
  144.3 2.0 %collective-permute-start.8 = (f32[2,16,1,128]{3,2,1,0:T(1,128)S(1)}, f32[2,16,1,128]{3,2,1,0:T(1,128)S(1)}, u32[]{:S(2)}, u32[]{:S(2)}) collective-permute-start(f32[2,16,1,128]{3,2,1,0:T(1,128)S(1)} %get-tuple-element.40), channel_id=1, source_target_pairs={{0,4},{4,8},{8,12},{12,0},{1,5},{5,9},{9,13},{13,1},{2,6},{6,10},{... | collective-permute-start | bytes 49160 | tf_op jit(solution)/shard_map/ppermute | solution.py:20
  146.3 8.6 %scatter_custom_fusion.3 = f32[2048]{0:T(1024)} fusion(s32[2048]{0:T(1024)S(1)} %get-tuple-element.69, f32[2048]{0:T(1024)S(1)} %subtract_multiply_fusion, f32[]{:T(128)} %constant.72.clone.1), kind=kCustom, calls=%fused_computation.148 | custom fusion | bytes 8196 | tf_op jit(solution)/shard_map/scatter | solution.py:91
  154.9 3.2 %all-to-all-start.2 = ((f32[4,1,512]{2,1,0:T(1,128)}), f32[4,1,512]{2,1,0:T(1,128)S(1)}, u32[]{:S(2)}, u32[]{:S(2)}) async-start(f32[4,1,512]{2,1,0:T(1,128)} %bitcast.36), calls=%async_computation.2 | async-start | bytes 16384 | tf_op jit(solution)/shard_map/all_to_all | solution.py:93
  158.5 0.5 collective-permute-start.10
  159.3 11.5 %scatter_custom_fusion.2 = f32[2048]{0:T(1024)S(1)} fusion(s32[2048]{0:T(1024)S(1)} %bitcast.75, f32[2048]{0:T(1024)S(1)} %subtract_multiply_fusion, f32[]{:T(128)} %constant.72.clone.1), kind=kCustom, calls=%fused_computation.150 | custom fusion | flops 2048 | bytes 8196 | tf_op jit(solution)/shard_map/scatter-add | solution.py:95
  170.8 11.3 %scatter_custom_fusion.4 = f32[2048]{0:T(1024)S(1)} fusion(s32[2048]{0:T(1024)S(1)} %bitcast.77, f32[2048]{0:T(1024)S(1)} %bitcast.78, f32[]{:T(128)} %constant.72.clone.1), kind=kCustom, calls=%fused_computation.146 | custom fusion | flops 2048 | bytes 8196 | tf_op jit(solution)/shard_map/scatter-add | solution.py:100
  182.1 0.5 pad_maximum_fusion.1
  182.9 3.9 %collective-permute-start.13 = (f32[16,1,128]{2,1,0:T(1,128)S(1)}, f32[16,1,128]{2,1,0:T(1,128)S(1)}, u32[]{:S(2)}, u32[]{:S(2)}) collective-permute-start(f32[16,1,128]{2,1,0:T(1,128)S(1)} %get-tuple-element.56), channel_id=1, source_target_pairs={{4,0},{8,4},{12,8},{0,12},{5,1},{9,5},{13,9},{1,13},{6,2},{10,6},{... | collective-permute-start | bytes 24584 | tf_op jit(solution)/shard_map/ppermute | solution.py:23
  186.8 0.6 copy-done.4
  187.4 0.7 collective-permute-done.13
  188.1 4.1 %collective-permute-done.12 = f32[16,1,128]{2,1,0:T(1,128)S(1)} collective-permute-done((f32[16,1,128]{2,1,0:T(1,128)S(1)}, f32[16,1,128]{2,1,0:T(1,128)S(1)}, u32[]{:S(2)}, u32[]{:S(2)}) %collective-permute-start.12) | collective-permute-done | bytes 8224 | tf_op jit(solution)/shard_map/ppermute | solution.py:20
  192.4 1.7 collective-permute-start.14
  194.1 3.7 %collective-permute-done.15 = f32[16,18,1]{2,1,0:T(8,128)S(1)} collective-permute-done((f32[16,18,1]{2,1,0:T(8,128)S(1)}, f32[16,18,1]{2,1,0:T(8,128)S(1)}, u32[]{:S(2)}, u32[]{:S(2)}) %collective-permute-start.15) | collective-permute-done | bytes 1184 | tf_op jit(solution)/shard_map/ppermute | solution.py:20
  197.8 0.7 collective-permute-done.14
  198.8 0.8 pad_maximum_fusion.4
  (100 shorter events, 4.1 us)
Async XLA Ops:
  0.6 53.7 %copy-start = (f32[16,128]{1,0:T(8,128)S(1)}, f32[16,128]{1,0:T(8,128)}, u32[]{:S(2)}) copy-start(f32[16,128]{1,0:T(8,128)} %param.16) | copy-start | bytes 24580
  0.6 6.1 %copy-start.1 = (s32[1,1,2048,1]{2,3,1,0:T(1,128)S(1)}, s32[1,1,2048,1]{2,3,1,0:T(1,128)}, u32[]{:S(2)}) copy-start(s32[1,1,2048,1]{2,3,1,0:T(1,128)} %param.23) | copy-start | bytes 24580
  1.7 103.8 %collective-permute-start.1 = (f32[2,16,1,128]{3,2,1,0:T(1,128)S(1)}, f32[2,16,1,128]{3,2,1,0:T(1,128)S(1)}, u32[]{:S(2)}, u32[]{:S(2)}) collective-permute-start(f32[2,16,1,128]{3,2,1,0:T(1,128)S(1)} %get-tuple-element.39), channel_id=1, source_target_pairs={{4,0},{8,4},{12,8},{0,12},{5,1},{9,5},{13,9},{1,13},{6,2},{10,6},{... | collective-permute-start | bytes 49160 | tf_op jit(solution)/shard_map/ppermute | solution.py:23
  6.8 98.7 %collective-permute-start = (f32[2,16,1,128]{3,2,1,0:T(1,128)S(1)}, f32[2,16,1,128]{3,2,1,0:T(1,128)S(1)}, u32[]{:S(2)}, u32[]{:S(2)}) collective-permute-start(f32[2,16,1,128]{3,2,1,0:T(1,128)S(1)} %get-tuple-element.38), channel_id=1, source_target_pairs={{0,4},{4,8},{8,12},{12,0},{1,5},{5,9},{9,13},{13,1},{2,6},{6,10},{... | collective-permute-start | bytes 49160 | tf_op jit(solution)/shard_map/ppermute | solution.py:20
  12.0 42.4 %copy-start.2 = (f32[3,16,16,128]{3,2,1,0:T(8,128)S(1)}, f32[3,16,16,128]{3,2,1,0:T(8,128)}, u32[]{:S(2)}) copy-start(f32[3,16,16,128]{3,2,1,0:T(8,128)} %param.15) | copy-start | bytes 1179652
  23.7 25.3 %copy-start.3 = (f32[2,8,16,128]{3,2,1,0:T(8,128)S(1)}, f32[2,8,16,128]{3,2,1,0:T(8,128)}, u32[]{:S(2)}) copy-start(f32[2,8,16,128]{3,2,1,0:T(8,128)} %param.19) | copy-start | bytes 393220
  44.0 37.6 %all-to-all-start = ((s32[4,1,512]{2,1,0:T(1,128)}), s32[4,1,512]{2,1,0:T(1,128)S(1)}, u32[]{:S(2)}, u32[]{:S(2)}) async-start(s32[4,1,512]{2,1,0:T(1,128)} %bitcast.27), calls=%async_computation | async-start | bytes 16384 | tf_op jit(solution)/shard_map/all_to_all | solution.py:85
  49.0 2.1 %copy-start.7 = (s32[16,128]{1,0:T(8,128)S(1)}, s32[16,128]{1,0:T(8,128)}, u32[]{:S(2)}) copy-start(s32[16,128]{1,0:T(8,128)} %param.20) | copy-start | bytes 24580
  49.1 20.4 %collective-permute-start.19 = (f32[2,8,1,128]{3,2,1,0:T(1,128)S(1)}, f32[2,8,1,128]{3,2,1,0:T(1,128)S(1)}, u32[]{:S(2)}, u32[]{:S(2)}) collective-permute-start(f32[2,8,1,128]{3,2,1,0:T(1,128)S(1)} %get-tuple-element.55), channel_id=1, source_target_pairs={{0,4},{4,8},{8,12},{12,0},{1,5},{5,9},{9,13},{13,1},{2,6},{6,10},{... | collective-permute-start | bytes 24584 | tf_op jit(solution)/shard_map/ppermute | solution.py:20
  51.2 15.0 %collective-permute-start.17 = (f32[1,128]{1,0:T(1,128)S(1)}, f32[1,128]{1,0:T(1,128)S(1)}, u32[]{:S(2)}, u32[]{:S(2)}) collective-permute-start(f32[1,128]{1,0:T(1,128)S(1)} %get-tuple-element.66), channel_id=1, source_target_pairs={{4,0},{8,4},{12,8},{0,12},{5,1},{9,5},{13,9},{1,13},{6,2},{10,6},{... | collective-permute-start | bytes 1544 | tf_op jit(solution)/shard_map/ppermute | solution.py:23
  53.6 0.7 copy-start.8
  53.6 15.8 %collective-permute-start.16 = (f32[1,128]{1,0:T(1,128)S(1)}, f32[1,128]{1,0:T(1,128)S(1)}, u32[]{:S(2)}, u32[]{:S(2)}) collective-permute-start(f32[1,128]{1,0:T(1,128)S(1)} %get-tuple-element.67), channel_id=1, source_target_pairs={{0,4},{4,8},{8,12},{12,0},{1,5},{5,9},{9,13},{13,1},{2,6},{6,10},{... | collective-permute-start | bytes 1544 | tf_op jit(solution)/shard_map/ppermute | solution.py:20
  66.2 4.6 %collective-permute-start.20 = (f32[2,8,1,128]{3,2,1,0:T(1,128)S(1)}, f32[2,8,1,128]{3,2,1,0:T(1,128)S(1)}, u32[]{:S(2)}, u32[]{:S(2)}) collective-permute-start(f32[2,8,1,128]{3,2,1,0:T(1,128)S(1)} %get-tuple-element.54), channel_id=1, source_target_pairs={{4,0},{8,4},{12,8},{0,12},{5,1},{9,5},{13,9},{1,13},{6,2},{10,6},{... | collective-permute-start | bytes 24584 | tf_op jit(solution)/shard_map/ppermute | solution.py:23
  69.4 1.9 collective-permute-start.18
  69.4 3.3 %collective-permute-start.22 = (f32[18,1]{1,0:T(8,128)S(1)}, f32[18,1]{1,0:T(8,128)S(1)}, u32[]{:S(2)}, u32[]{:S(2)}) collective-permute-start(f32[18,1]{1,0:T(8,128)S(1)} %get-tuple-element.61), channel_id=1, source_target_pairs={{0,1},{1,2},{2,3},{3,0},{4,5},{5,6},{6,7},{7,4},{8,9},{9,10},{10,1... | collective-permute-start | bytes 224 | tf_op jit(solution)/shard_map/ppermute | solution.py:20
  70.9 5.1 %collective-permute-start.23 = (f32[2,8,18,1]{3,2,1,0:T(8,128)S(1)}, f32[2,8,18,1]{3,2,1,0:T(8,128)S(1)}, u32[]{:S(2)}, u32[]{:S(2)}) collective-permute-start(f32[2,8,18,1]{3,2,1,0:T(8,128)S(1)} %get-tuple-element.45), channel_id=1, source_target_pairs={{0,1},{1,2},{2,3},{3,0},{4,5},{5,6},{6,7},{7,4},{8,9},{9,10},{10,1... | collective-permute-start | bytes 3464 | tf_op jit(solution)/shard_map/ppermute | solution.py:20
  71.3 5.8 %collective-permute-start.21 = (f32[2,8,18,1]{3,2,1,0:T(8,128)S(1)}, f32[2,8,18,1]{3,2,1,0:T(8,128)S(1)}, u32[]{:S(2)}, u32[]{:S(2)}) collective-permute-start(f32[2,8,18,1]{3,2,1,0:T(8,128)S(1)} %get-tuple-element.44), channel_id=1, source_target_pairs={{1,0},{2,1},{3,2},{0,3},{5,4},{6,5},{7,6},{4,7},{9,8},{10,9},{11,1... | collective-permute-start | bytes 3464 | tf_op jit(solution)/shard_map/ppermute | solution.py:23
  72.7 4.4 %copy-start.5 = (f32[16,128]{1,0:T(8,128)S(1)}, f32[16,128]{1,0:T(8,128)}, u32[]{:S(2)}) copy-start(f32[16,128]{1,0:T(8,128)} %param.21) | copy-start | bytes 24580
  77.4 45.5 %collective-permute-start.24 = (f32[2,8,1,128]{3,2,1,0:T(1,128)S(1)}, f32[2,8,1,128]{3,2,1,0:T(1,128)S(1)}, u32[]{:S(2)}, u32[]{:S(2)}) collective-permute-start(f32[2,8,1,128]{3,2,1,0:T(1,128)S(1)} %get-tuple-element.53), channel_id=1, source_target_pairs={{0,4},{4,8},{8,12},{12,0},{1,5},{5,9},{9,13},{13,1},{2,6},{6,10},{... | collective-permute-start | bytes 24584 | tf_op jit(solution)/shard_map/ppermute | solution.py:20
  77.4 45.4 %collective-permute-start.25 = (f32[2,8,1,128]{3,2,1,0:T(1,128)S(1)}, f32[2,8,1,128]{3,2,1,0:T(1,128)S(1)}, u32[]{:S(2)}, u32[]{:S(2)}) collective-permute-start(f32[2,8,1,128]{3,2,1,0:T(1,128)S(1)} %get-tuple-element.52), channel_id=1, source_target_pairs={{4,0},{8,4},{12,8},{0,12},{5,1},{9,5},{13,9},{1,13},{6,2},{10,6},{... | collective-permute-start | bytes 24584 | tf_op jit(solution)/shard_map/ppermute | solution.py:23
  102.2 30.0 %all-to-all-start.1 = ((f32[4,1,512]{2,1,0:T(1,128)}), f32[4,1,512]{2,1,0:T(1,128)S(1)}, u32[]{:S(2)}, u32[]{:S(2)}) async-start(f32[4,1,512]{2,1,0:T(1,128)} %bitcast.30), calls=%async_computation.1 | async-start | bytes 16384 | tf_op jit(solution)/shard_map/all_to_all | solution.py:87
  105.7 11.2 %collective-permute-start.3 = (f32[2,16,18,1]{3,2,1,0:T(8,128)S(1)}, f32[2,16,18,1]{3,2,1,0:T(8,128)S(1)}, u32[]{:S(2)}, u32[]{:S(2)}) collective-permute-start(f32[2,16,18,1]{3,2,1,0:T(8,128)S(1)} %get-tuple-element.37), channel_id=1, source_target_pairs={{1,0},{2,1},{3,2},{0,3},{5,4},{6,5},{7,6},{4,7},{9,8},{10,9},{11,1... | collective-permute-start | bytes 6920 | tf_op jit(solution)/shard_map/ppermute | solution.py:23
  107.4 10.5 %collective-permute-start.2 = (f32[2,16,18,1]{3,2,1,0:T(8,128)S(1)}, f32[2,16,18,1]{3,2,1,0:T(8,128)S(1)}, u32[]{:S(2)}, u32[]{:S(2)}) collective-permute-start(f32[2,16,18,1]{3,2,1,0:T(8,128)S(1)} %get-tuple-element.36), channel_id=1, source_target_pairs={{0,1},{1,2},{2,3},{3,0},{4,5},{5,6},{6,7},{7,4},{8,9},{9,10},{10,1... | collective-permute-start | bytes 6920 | tf_op jit(solution)/shard_map/ppermute | solution.py:20
  118.4 0.7 copy-start.6
  118.4 0.7 copy-start.10
  119.3 4.9 %collective-permute-start.5 = (f32[16,1,128]{2,1,0:T(1,128)S(1)}, f32[16,1,128]{2,1,0:T(1,128)S(1)}, u32[]{:S(2)}, u32[]{:S(2)}) collective-permute-start(f32[16,1,128]{2,1,0:T(1,128)S(1)} %get-tuple-element.58), channel_id=1, source_target_pairs={{4,0},{8,4},{12,8},{0,12},{5,1},{9,5},{13,9},{1,13},{6,2},{10,6},{... | collective-permute-start | bytes 24584 | tf_op jit(solution)/shard_map/ppermute | solution.py:23
  122.9 5.4 %collective-permute-start.4 = (f32[16,1,128]{2,1,0:T(1,128)S(1)}, f32[16,1,128]{2,1,0:T(1,128)S(1)}, u32[]{:S(2)}, u32[]{:S(2)}) collective-permute-start(f32[16,1,128]{2,1,0:T(1,128)S(1)} %get-tuple-element.59), channel_id=1, source_target_pairs={{0,4},{4,8},{8,12},{12,0},{1,5},{5,9},{9,13},{13,1},{2,6},{6,10},{... | collective-permute-start | bytes 24584 | tf_op jit(solution)/shard_map/ppermute | solution.py:20
  128.5 15.5 %collective-permute-start.7 = (f32[16,18,1]{2,1,0:T(8,128)S(1)}, f32[16,18,1]{2,1,0:T(8,128)S(1)}, u32[]{:S(2)}, u32[]{:S(2)}) collective-permute-start(f32[16,18,1]{2,1,0:T(8,128)S(1)} %get-tuple-element.49), channel_id=1, source_target_pairs={{0,1},{1,2},{2,3},{3,0},{4,5},{5,6},{6,7},{7,4},{8,9},{9,10},{10,1... | collective-permute-start | bytes 3464 | tf_op jit(solution)/shard_map/ppermute | solution.py:20
  128.5 15.4 %collective-permute-start.6 = (f32[16,18,1]{2,1,0:T(8,128)S(1)}, f32[16,18,1]{2,1,0:T(8,128)S(1)}, u32[]{:S(2)}, u32[]{:S(2)}) collective-permute-start(f32[16,18,1]{2,1,0:T(8,128)S(1)} %get-tuple-element.48), channel_id=1, source_target_pairs={{1,0},{2,1},{3,2},{0,3},{5,4},{6,5},{7,6},{4,7},{9,8},{10,9},{11,1... | collective-permute-start | bytes 3464 | tf_op jit(solution)/shard_map/ppermute | solution.py:23
  130.4 28.7 %collective-permute-start.27 = (f32[2,8,18,1]{3,2,1,0:T(8,128)S(1)}, f32[2,8,18,1]{3,2,1,0:T(8,128)S(1)}, u32[]{:S(2)}, u32[]{:S(2)}) collective-permute-start(f32[2,8,18,1]{3,2,1,0:T(8,128)S(1)} %get-tuple-element.43), channel_id=1, source_target_pairs={{0,1},{1,2},{2,3},{3,0},{4,5},{5,6},{6,7},{7,4},{8,9},{9,10},{10,1... | collective-permute-start | bytes 3464 | tf_op jit(solution)/shard_map/ppermute | solution.py:20
  130.4 28.6 %collective-permute-start.26 = (f32[2,8,18,1]{3,2,1,0:T(8,128)S(1)}, f32[2,8,18,1]{3,2,1,0:T(8,128)S(1)}, u32[]{:S(2)}, u32[]{:S(2)}) collective-permute-start(f32[2,8,18,1]{3,2,1,0:T(8,128)S(1)} %get-tuple-element.42), channel_id=1, source_target_pairs={{1,0},{2,1},{3,2},{0,3},{5,4},{6,5},{7,6},{4,7},{9,8},{10,9},{11,1... | collective-permute-start | bytes 3464 | tf_op jit(solution)/shard_map/ppermute | solution.py:23
  144.2 2.1 %copy-start.9 = (f32[1,1,2048]{2,1,0:T(1,128)S(1)}, f32[1,1,2048]{2,1,0:T(1,128)}, u32[]{:S(2)}) copy-start(f32[1,1,2048]{2,1,0:T(1,128)} %param.25) | copy-start | bytes 24580
  144.2 14.0 %collective-permute-start.9 = (f32[2,16,1,128]{3,2,1,0:T(1,128)S(1)}, f32[2,16,1,128]{3,2,1,0:T(1,128)S(1)}, u32[]{:S(2)}, u32[]{:S(2)}) collective-permute-start(f32[2,16,1,128]{3,2,1,0:T(1,128)S(1)} %get-tuple-element.41), channel_id=1, source_target_pairs={{4,0},{8,4},{12,8},{0,12},{5,1},{9,5},{13,9},{1,13},{6,2},{10,6},{... | collective-permute-start | bytes 49160 | tf_op jit(solution)/shard_map/ppermute | solution.py:23
  144.3 13.9 %collective-permute-start.8 = (f32[2,16,1,128]{3,2,1,0:T(1,128)S(1)}, f32[2,16,1,128]{3,2,1,0:T(1,128)S(1)}, u32[]{:S(2)}, u32[]{:S(2)}) collective-permute-start(f32[2,16,1,128]{3,2,1,0:T(1,128)S(1)} %get-tuple-element.40), channel_id=1, source_target_pairs={{0,4},{4,8},{8,12},{12,0},{1,5},{5,9},{9,13},{13,1},{2,6},{6,10},{... | collective-permute-start | bytes 49160 | tf_op jit(solution)/shard_map/ppermute | solution.py:20
  154.9 15.8 %all-to-all-start.2 = ((f32[4,1,512]{2,1,0:T(1,128)}), f32[4,1,512]{2,1,0:T(1,128)S(1)}, u32[]{:S(2)}, u32[]{:S(2)}) async-start(f32[4,1,512]{2,1,0:T(1,128)} %bitcast.36), calls=%async_computation.2 | async-start | bytes 16384 | tf_op jit(solution)/shard_map/all_to_all | solution.py:93
  158.5 23.6 %collective-permute-start.11 = (f32[2,16,18,1]{3,2,1,0:T(8,128)S(1)}, f32[2,16,18,1]{3,2,1,0:T(8,128)S(1)}, u32[]{:S(2)}, u32[]{:S(2)}) collective-permute-start(f32[2,16,18,1]{3,2,1,0:T(8,128)S(1)} %get-tuple-element.35), channel_id=1, source_target_pairs={{1,0},{2,1},{3,2},{0,3},{5,4},{6,5},{7,6},{4,7},{9,8},{10,9},{11,1... | collective-permute-start | bytes 6920 | tf_op jit(solution)/shard_map/ppermute | solution.py:23
  158.5 23.5 %collective-permute-start.10 = (f32[2,16,18,1]{3,2,1,0:T(8,128)S(1)}, f32[2,16,18,1]{3,2,1,0:T(8,128)S(1)}, u32[]{:S(2)}, u32[]{:S(2)}) collective-permute-start(f32[2,16,18,1]{3,2,1,0:T(8,128)S(1)} %get-tuple-element.34), channel_id=1, source_target_pairs={{0,1},{1,2},{2,3},{3,0},{4,5},{5,6},{6,7},{7,4},{8,9},{9,10},{10,1... | collective-permute-start | bytes 6920 | tf_op jit(solution)/shard_map/ppermute | solution.py:20
  182.9 5.2 %collective-permute-start.13 = (f32[16,1,128]{2,1,0:T(1,128)S(1)}, f32[16,1,128]{2,1,0:T(1,128)S(1)}, u32[]{:S(2)}, u32[]{:S(2)}) collective-permute-start(f32[16,1,128]{2,1,0:T(1,128)S(1)} %get-tuple-element.56), channel_id=1, source_target_pairs={{4,0},{8,4},{12,8},{0,12},{5,1},{9,5},{13,9},{1,13},{6,2},{10,6},{... | collective-permute-start | bytes 24584 | tf_op jit(solution)/shard_map/ppermute | solution.py:23
  186.7 5.4 %collective-permute-start.12 = (f32[16,1,128]{2,1,0:T(1,128)S(1)}, f32[16,1,128]{2,1,0:T(1,128)S(1)}, u32[]{:S(2)}, u32[]{:S(2)}) collective-permute-start(f32[16,1,128]{2,1,0:T(1,128)S(1)} %get-tuple-element.57), channel_id=1, source_target_pairs={{0,4},{4,8},{8,12},{12,0},{1,5},{5,9},{9,13},{13,1},{2,6},{6,10},{... | collective-permute-start | bytes 24584 | tf_op jit(solution)/shard_map/ppermute | solution.py:20
  186.7 0.7 copy-start.4
  192.3 5.5 %collective-permute-start.15 = (f32[16,18,1]{2,1,0:T(8,128)S(1)}, f32[16,18,1]{2,1,0:T(8,128)S(1)}, u32[]{:S(2)}, u32[]{:S(2)}) collective-permute-start(f32[16,18,1]{2,1,0:T(8,128)S(1)} %get-tuple-element.47), channel_id=1, source_target_pairs={{0,1},{1,2},{2,3},{3,0},{4,5},{5,6},{6,7},{7,4},{8,9},{9,10},{10,1... | collective-permute-start | bytes 3464 | tf_op jit(solution)/shard_map/ppermute | solution.py:20
  192.4 6.1 %collective-permute-start.14 = (f32[16,18,1]{2,1,0:T(8,128)S(1)}, f32[16,18,1]{2,1,0:T(8,128)S(1)}, u32[]{:S(2)}, u32[]{:S(2)}) collective-permute-start(f32[16,18,1]{2,1,0:T(8,128)S(1)} %get-tuple-element.46), channel_id=1, source_target_pairs={{1,0},{2,1},{3,2},{0,3},{5,4},{6,5},{7,6},{4,7},{9,8},{10,9},{11,1... | collective-permute-start | bytes 3464 | tf_op jit(solution)/shard_map/ppermute | solution.py:23
where the time goes:
time: 201 us; the launch traced here: 200 us
  local copies, waits for them, and re-layouts  86 us (43%)
  starting transfers between devices  48 us (24%)
  other arithmetic  34.2 us (17%)
  waiting for transfers between devices  30.2 us (15%)
    ppermute x14, starting transfers between devices, padded_2(): lax.ppermute(lax.slice_in_dim(block, 0, width, axis=dim), axis, backward)  30.6 us
    gather x1, local copies, waits for them, and re-layouts, on_device(): surface_values = surface_sea[received]  20.6 us
    ppermute x14, waiting for transfers between devices, padded_2(): lax.ppermute(lax.slice_in_dim(block, block.shape[dim] - width, None, axis...  16.1 us
    ppermute x14, waiting for transfers between devices, padded_2(): lax.ppermute(lax.slice_in_dim(block, 0, width, axis=dim), axis, backward)  14.1 us
    gather x1, local copies, waits for them, and re-layouts, on_device(): air_slot = air_flat[atm_cells]  11.8 us
    gather x1, local copies, waits for them, and re-layouts, on_device(): surface_slot = returned.reshape(-1)[position]  11.8 us
    gather x1, local copies, waits for them, and re-layouts, on_device(): sorted_target = target[ordering]  11.8 us
    scatter-add x1, other arithmetic, on_device(): jnp.zeros(air_flat.shape, jnp.float32).at[atm_cells].add(heat_flux)  11.5 us
  transfers between devices with their start and end apart: 31, of which 12 were waited for; matrix products, arithmetic and copies ran while one was open for 58% of the time, Pallas kernels for 0%

commit v1 on v0

v1 whole, which is shorter than its diff:
```python
import functools

import jax
import jax.numpy as jnp
from jax import lax
from jax.experimental import pallas as pl
from jax.experimental.pallas import tpu as pltpu
from jax.sharding import PartitionSpec as P

ACOUSTIC = 2
OCEAN_STEPS = 2
AH = 2 * ACOUSTIC
OH = OCEAN_STEPS

ATM_GAIN = 0.5
SEA_GAIN = 0.5

F32 = jnp.float32
BF16 = jnp.bfloat16


def lane_slots(levels, tracers):
    slots = [AH * i for i in range(3 * levels)]
    base = AH * 3 * levels
    slots += [base + OH * i for i in range(tracers)]
    base += OH * tracers
    slots += [base + AH * i for i in range(3)]
    total = base + 3 * AH
    return slots, -(-total // 128) * 128


def row_slots(levels, tracers):
    per = 3 * AH - 2
    base = per * levels
    misc = base + OH * tracers
    return per, base, misc, misc + AH + 2 * OH


def pack_kernel(atm, ocean, depth, wet, kappa, up, down, left, right, lu, ld, ru, rd):
    levels = atm.shape[1]
    rows, cols = atm.shape[2:]
    tracers = ocean.shape[0] * ocean.shape[1]
    each = ocean.shape[1]
    per, obase, mbase, _ = row_slots(levels, tracers)
    slots, _ = lane_slots(levels, tracers)
    wetness = wet[...].astype(F32)

    for level in range(levels):
        base = per * level
        for at, which, width in ((0, 1, AH), (AH, 0, AH - 1), (2 * AH - 1, 2, AH - 1)):
            up[base + at : base + at + width, :] = atm[which, level, 0:width, :]
            down[base + at : base + at + width, :] = atm[which, level, rows - width : rows, :]
    for i in range(tracers):
        at = obase + OH * i
        up[at : at + OH, :] = ocean[i // each, i % each, 0:OH, :]
        down[at : at + OH, :] = ocean[i // each, i % each, rows - OH : rows, :]
    for at, value, width in (
        (mbase, depth[...], AH),
        (mbase + AH, wetness, OH),
        (mbase + AH + OH, kappa[...], OH),
    ):
        up[at : at + width, :] = value[0:width]
        down[at : at + width, :] = value[rows - width : rows]

    lane = lax.broadcasted_iota(jnp.int32, (rows, cols), 1)
    fields = [(atm, (k, l), AH) for k in range(3) for l in range(levels)]
    fields += [(ocean, (i // each, i % each), OH) for i in range(tracers)]
    fields += [(depth, None, AH), (None, None, AH), (kappa, None, AH)]
    packed = {}
    for (ref, at, width), slot in zip(fields, slots):
        value = wetness if ref is None else (ref[...] if at is None else ref[at[0], at[1]])
        tile, offset = slot // cols, slot % cols
        mask = (lane >= offset) & (lane < offset + width)
        first = pltpu.roll(value, offset, 1) if offset else value
        turn = (offset + width) % cols
        last = pltpu.roll(value, turn, 1) if turn else value
        if tile in packed:
            a, b = packed[tile]
            packed[tile] = (jnp.where(mask, first, a), jnp.where(mask, last, b))
        else:
            packed[tile] = (first, last)
    for tile, (a, b) in packed.items():
        where = slice(tile * cols, (tile + 1) * cols)
        left[:, where] = a
        right[:, where] = b
        lu[:, where] = a[0:AH]
        ld[:, where] = a[rows - AH : rows]
        ru[:, where] = b[0:AH]
        rd[:, where] = b[rows - AH : rows]


def split3(value):
    hi = value.astype(BF16)
    rest = value - hi.astype(F32)
    mid = rest.astype(BF16)
    low = (rest - mid.astype(F32)).astype(BF16)
    return hi, mid, low


def one_hot(index, size):
    shape = (size, index.shape[-1])
    return lax.broadcasted_iota(jnp.int32, shape, 0) == index


def gather_rows(table, hot_rows, hot_cols):
    r = table.shape[0]
    parts = jnp.concatenate(split3(table), axis=0)
    g = jnp.dot(parts, hot_cols, preferred_element_type=F32)
    g = g[0:r] + g[r : 2 * r] + g[2 * r : 3 * r]
    return jnp.sum(jnp.where(hot_rows, g, 0.0), axis=0, keepdims=True)


def scatter_rows(values, hot_rows, hot_cols):
    r = hot_rows.shape[0]
    parts = []
    for value in values:
        for part in split3(value):
            parts.append(jnp.where(hot_rows, part.astype(F32), 0.0).astype(BF16))
    s = lax.dot_general(
        jnp.concatenate(parts, axis=0),
        hot_cols,
        (((1,), (1,)), ((), ())),
        preferred_element_type=F32,
    )
    out = []
    for i in range(len(values)):
        base = 3 * r * i
        out.append(s[base : base + r] + s[base + r : base + 2 * r] + s[base + 2 * r : base + 3 * r])
    return out


def send_kernel(air, sst, atm_cell, dest, sea_cell, weight, message, wair_out):
    rows, cols = air.shape
    tiles = message.shape[0]
    cell = atm_cell[...]
    hot_atm = jnp.where(one_hot(cell % cols, cols), 1.0, 0.0).astype(BF16)
    airx = gather_rows(air[...], one_hot(cell // cols, rows), hot_atm)
    w = weight[...]
    wair = w * airx
    wair_out[...] = wair
    cell = sea_cell[...]
    hot_sea = jnp.where(one_hot(cell % cols, cols), 1.0, 0.0).astype(BF16)
    row = dest[...] * rows + cell // cols
    surface = sst[...].reshape(rows, cols)
    for tile in range(tiles):
        s1, s2 = scatter_rows([wair, w], one_hot(row - tile * rows, rows), hot_sea)
        message[tile, 0:rows, :] = s1
        message[tile, rows : 2 * rows, :] = s2
        message[tile, 2 * rows : 3 * rows, :] = surface


def flux_kernel(got, sst, atm_cell, dest, sea_cell, weight, wair, atm_in, ocean_in, atm_out, ocean_out):
    rows, cols = atm_in.shape[-2:]
    tiles = got.shape[0]
    surface = sst[...].reshape(rows, cols)
    s1, s2 = got[0, 0:rows, :], got[0, rows : 2 * rows, :]
    for tile in range(1, tiles):
        s1 = s1 + got[tile, 0:rows, :]
        s2 = s2 + got[tile, rows : 2 * rows, :]
    sea_flux = s1 - surface * s2
    ocean_out[...] = ocean_in[...] + (SEA_GAIN * sea_flux).reshape(ocean_in.shape)

    cell = sea_cell[...]
    hot_sea = jnp.where(one_hot(cell % cols, cols), 1.0, 0.0).astype(BF16)
    row = dest[...] * rows + cell // cols
    sstx = jnp.zeros(cell.shape, F32)
    for tile in range(tiles):
        table = got[tile, 2 * rows : 3 * rows, :]
        sstx = sstx + gather_rows(table, one_hot(row - tile * rows, rows), hot_sea)
    flux = wair[...] - weight[...] * sstx
    cell = atm_cell[...]
    hot_atm = jnp.where(one_hot(cell % cols, cols), 1.0, 0.0).astype(BF16)
    (atm_flux,) = scatter_rows([flux], one_hot(cell // cols, rows), hot_atm)
    atm_out[...] = atm_in[...] - (ATM_GAIN * atm_flux).reshape(atm_in.shape)


def step_kernel(
    speed,
    atm,
    ocean,
    depth,
    wet,
    kappa,
    from_up,
    from_down,
    from_left,
    from_right,
    from_ul,
    from_dl,
    from_ur,
    from_dr,
    atm_out,
    ocean_out,
    ext,
):
    levels = atm.shape[1]
    rows, cols = atm.shape[2:]
    tracers = ocean.shape[0] * ocean.shape[1]
    each = ocean.shape[1]
    per, obase, mbase, _ = row_slots(levels, tracers)
    slots, _ = lane_slots(levels, tracers)
    full = rows + 2 * AH
    lane = lax.broadcasted_iota(jnp.int32, (1, cols), 1)
    low_half = lane < cols // 2

    def strips(slot, width, left_ref, right_ref):
        where = slice(slot // cols * cols, slot // cols * cols + cols)
        offset = slot % cols
        a = right_ref[:, where]
        b = left_ref[:, where]
        if offset:
            a = pltpu.roll(a, cols - offset, 1)
        turn = (cols - width - offset) % cols
        if turn:
            b = pltpu.roll(b, turn, 1)
        return jnp.where(low_half, a, b)

    def extended(buffer, value, row_at, row_width, slot, width):
        view = ext.at[buffer]
        view[0:rows, 0:cols] = value
        view[rows : rows + row_width, 0:cols] = from_down[row_at : row_at + row_width, :]
        view[full - row_width : full, 0:cols] = from_up[row_at : row_at + row_width, :]
        view[0:rows, cols : 2 * cols] = strips(slot, width, from_left, from_right)
        view[rows : rows + AH, cols : 2 * cols] = strips(slot, width, from_dl, from_dr)
        view[full - AH : full, cols : 2 * cols] = strips(slot, width, from_ul, from_ur)
        return view[...]

    def east(f):
        return pltpu.roll(f, 2 * cols - 1, 1)

    def west(f):
        return pltpu.roll(f, 1, 1)

    def south(f):
        return pltpu.roll(f, full - 1, 0)

    def north(f):
        return pltpu.roll(f, 1, 0)

    base = 3 * levels + tracers
    depth_ext = extended(0, depth[...], mbase, AH, slots[base], AH)
    for level in range(levels):
        at = per * level
        u = extended(1, atm[0, level], at + AH, AH - 1, slots[level], AH)
        v = extended(2, atm[1, level], at, AH, slots[levels + level], AH)
        h = extended(3, atm[2, level], at + 2 * AH - 1, AH - 1, slots[2 * levels + level], AH)
        column_speed = speed[level] * depth_ext
        for _ in range(ACOUSTIC):
            h = h - column_speed * ((east(u) - west(u)) * 0.5 + (south(v) - north(v)) * 0.5)
            u = u - (east(h) - west(h)) * 0.5
            v = v - (south(h) - north(h)) * 0.5
        atm_out[0, level] = u[0:rows, 0:cols]
        atm_out[1, level] = v[0:rows, 0:cols]
        atm_out[2, level] = h[0:rows, 0:cols]

    w = extended(4, wet[...].astype(F32), mbase + AH, OH, slots[base + 1], AH)
    k = extended(5, kappa[...], mbase + AH + OH, OH, slots[base + 2], AH)
    we, ww, ws, wn = east(w), west(w), south(w), north(w)
    for i in range(tracers):
        f = extended(6, ocean[i // each, i % each], obase + OH * i, OH, slots[3 * levels + i], OH)
        for _ in range(OCEAN_STEPS):
            total = we * (east(f) - f)
            total = total + ww * (west(f) - f)
            total = total + ws * (south(f) - f)
            total = total + wn * (north(f) - f)
            f = f + k * (w * total)
        ocean_out[i // each, i % each] = f[0:rows, 0:cols]


def on_device(
    tile_count,
    atm_state,
    air_temp,
    depth,
    wave_speed,
    ocean_state,
    wet_mask,
    diffusivity,
    xg_atm_cell,
    xg_dest,
    xg_ocean_cell,
    xg_weight,
):
    levels = atm_state.shape[1]
    rows, cols = atm_state.shape[2:]
    tracers = ocean_state.shape[0] * ocean_state.shape[1]
    cells = xg_weight.shape[-1]
    _, lanes = lane_slots(levels, tracers)
    _, _, _, message_rows = row_slots(levels, tracers)
    vmem = pl.BlockSpec(memory_space=pltpu.VMEM)
    limit = 32 * 1024 * 1024

    def shape(*dims):
        return jax.ShapeDtypeStruct(dims, F32)

    up, down, left, right, lu, ld, ru, rd = pl.pallas_call(
        pack_kernel,
        out_shape=[shape(message_rows, cols)] * 2 + [shape(rows, lanes)] * 2 + [shape(AH, lanes)] * 4,
        in_specs=[vmem] * 5,
        out_specs=[vmem] * 8,
        compiler_params=pltpu.CompilerParams(vmem_limit_bytes=limit),
        name="pack",
    )(atm_state, ocean_state, depth, wet_mask, diffusivity)

    column_axes = ("sub", "comp")
    column_count = lax.axis_size("sub") * lax.axis_size("comp")
    axes = ("tile",) + column_axes

    def send(value, dt, dc):
        pairs = []
        for t in range(tile_count):
            for c in range(column_count):
                target = (t + dt) % tile_count * column_count + (c + dc) % column_count
                pairs.append((t * column_count + c, target))
        return lax.ppermute(value, axes, pairs)

    from_down = send(up, -1, 0)
    from_up = send(down, 1, 0)
    from_right = send(left, 0, -1)
    from_left = send(right, 0, 1)
    from_dr = send(lu, -1, -1)
    from_ur = send(ld, 1, -1)
    from_dl = send(ru, -1, 1)
    from_ul = send(rd, 1, 1)

    atm_cell = xg_atm_cell.reshape(1, cells)
    dest = xg_dest.reshape(1, cells)
    sea_cell = xg_ocean_cell.reshape(1, cells)
    weight = xg_weight.reshape(1, cells)
    surface = pl.BlockSpec((1, 1, rows, cols), lambda i: (0, 0, 0, 0))
    last = pl.BlockSpec((1, 1, rows, cols), lambda i: (2, levels - 1, 0, 0))

    message, wair = pl.pallas_call(
        send_kernel,
        grid=(1,),
        out_shape=[shape(tile_count, 3 * rows, cols), shape(1, cells)],
        in_specs=[vmem, surface] + [vmem] * 4,
        out_specs=[vmem] * 2,
        compiler_params=pltpu.CompilerParams(vmem_limit_bytes=limit),
        name="exchange_send",
    )(air_temp, ocean_state, atm_cell, dest, sea_cell, weight)
    got = lax.all_to_all(message, "tile", split_axis=0, concat_axis=0, tiled=True)

    atm_new, ocean_new = pl.pallas_call(
        step_kernel,
        out_shape=[shape(*atm_state.shape), shape(*ocean_state.shape)],
        in_specs=[pl.BlockSpec(memory_space=pltpu.SMEM)] + [vmem] * 13,
        out_specs=[vmem] * 2,
        scratch_shapes=[pltpu.VMEM((7, rows + 2 * AH, 2 * cols), F32)],
        compiler_params=pltpu.CompilerParams(vmem_limit_bytes=limit),
        name="steps",
    )(
        wave_speed,
        atm_state,
        ocean_state,
        depth,
        wet_mask,
        diffusivity,
        from_up,
        from_down,
        from_left,
        from_right,
        from_ul,
        from_dl,
        from_ur,
        from_dr,
    )

    return pl.pallas_call(
        flux_kernel,
        grid=(1,),
        out_shape=[shape(*atm_state.shape), shape(*ocean_state.shape)],
        in_specs=[vmem, surface] + [vmem] * 5 + [last, surface],
        out_specs=[last, surface],
        input_output_aliases={7: 0, 8: 1},
        compiler_params=pltpu.CompilerParams(vmem_limit_bytes=limit),
        name="exchange_receive",
    )(got, ocean_state, atm_cell, dest, sea_cell, weight, wair, atm_new, ocean_new)


def solution(mesh):
    grid = P(("member", "tile"), ("sub", "comp"))
    state = P(None, None, ("member", "tile"), ("sub", "comp"))
    cells = P(("member", "tile"), ("sub", "comp"), None)
    return jax.shard_map(
        functools.partial(on_device, mesh.shape["tile"]),
        mesh=mesh,
        in_specs=(
            state,
            grid,
            grid,
            P(),
            state,
            grid,
            grid,
            cells,
            P(("member", "tile"), ("sub", "comp"), None, None),
            cells,
            cells,
        ),
        out_specs=(state, state),
        check_vma=False,
    )
```

time: 201 us -> 47.1 us (0.23)
  local copies, waits for them, and re-layouts: 86 us -> 5.42 us
  starting transfers between devices: 48 us -> 13 us
  other arithmetic: 34.2 us -> 0 us
  waiting for transfers between devices: 30.2 us -> 15.1 us
  Pallas kernels: 0 us -> 12.2 us
    gather x5 -> x0, local copies, waits for them, and re-layouts: 56.5 us -> none  [the longest x1 20.6 us: on_device(): surface_values = surface_sea[received]]
    ppermute x28 -> x8, starting transfers between devices: 36.4 us -> 6.51 us  [send(): return lax.ppermute(value, axes, pairs)]
    scatter x3 -> x0, local copies, waits for them, and re-layouts: 25.4 us -> none  [the longest x1 8.78 us: on_device(): jnp.zeros((slots,), jnp.int32).at[position].set(sea_cells)]
    scatter-add x4 -> x0, other arithmetic: 22.8 us -> none  [the longest x1 11.5 us: on_device(): jnp.zeros(air_flat.shape, jnp.float32).at[atm_cells].add(heat_flux)]
    ppermute x28 -> x8, waiting for transfers between devices: 30.2 us -> 15.1 us  [send(): return lax.ppermute(value, axes, pairs)]
    pallas_call x0 -> x4, Pallas kernels: none -> 12.2 us  [the longest x1 8.16 us: on_device(): pl.pallas_call(step_kernel, out_shape=[shape(*atm_state.shape), shape(*oc...]
    all_to_all x3 -> x1, starting transfers between devices: 11.6 us -> 6.46 us  [on_device(): lax.all_to_all(message, 'tile', split_axis=0, concat_axis=0, tiled=True)]
    sort x1 -> x0, other arithmetic: 5.04 us -> none  [on_device(): ordering = jnp.argsort(target, stable=True)]
  transfers between devices with their start and end apart: 31 -> 9, of which waited for: 12 -> 4; matrix products, arithmetic and copies ran while one was open for 58% -> 0% of each run, Pallas kernels for 0% -> 18%
where the time goes in v1:
time: 47.1 us; the launch traced here: 46.4 us
  waiting for transfers between devices  15.1 us (32%)
  starting transfers between devices  13 us (28%)
  Pallas kernels  12.2 us (26%)
  local copies, waits for them, and re-layouts  5.42 us (12%)
  between operations  0.75 us (2%)
    ppermute x8, waiting for transfers between devices, send(): return lax.ppermute(value, axes, pairs)  15.1 us
    pallas_call x1, Pallas kernels, on_device(): pl.pallas_call(step_kernel, out_shape=[shape(*atm_state.shape), shape(*oc...  8.16 us
    ppermute x8, starting transfers between devices, send(): return lax.ppermute(value, axes, pairs)  6.51 us
    all_to_all x1, starting transfers between devices, on_device(): lax.all_to_all(message, 'tile', split_axis=0, concat_axis=0, tiled=True)  6.46 us
    unnamed x32, local copies, waits for them, and re-layouts  5.42 us
    pallas_call x1, Pallas kernels, on_device(): pl.pallas_call(flux_kernel, grid=(1,), out_shape=[shape(*atm_state.shape)...  2.06 us
    pallas_call x1, Pallas kernels, on_device(): pl.pallas_call(send_kernel, grid=(1,), out_shape=[shape(tile_count, 3 * r...  1.57 us
  transfers between devices with their start and end apart: 9, of which 4 were waited for; matrix products, arithmetic and copies ran while one was open for 0% of the time, Pallas kernels for 18%

profile of v1, /device:TPU:0, one launch (start us, length us, event | category | flops | bytes accessed | tf_op | source)
XLA Modules:
  0.0 46.4 jit_solution(10128834199380933666)
XLA Ops:
  0.6 0.0 copy-start
  0.6 0.9 %copy-done = f32[2,8,16,128]{3,2,1,0:T(8,128)S(1)} copy-done((f32[2,8,16,128]{3,2,1,0:T(8,128)S(1)}, f32[2,8,16,128]{3,2,1,0:T(8,128)}, u32[]{:S(2)}) %copy-start) | copy-done | bytes 131096
  1.5 0.0 copy-start.6
  1.5 0.7 %copy-done.6 = s32[1,1,2048]{2,1,0:T(1,128)S(1)} copy-done((s32[1,1,2048]{2,1,0:T(1,128)S(1)}, s32[1,1,2048]{2,1,0:T(1,128)}, u32[]{:S(2)}) %copy-start.6) | copy-done | bytes 8216
  2.2 0.0 copy-start.8
  2.2 0.7 %copy-done.8 = s32[1,1,2048,1]{2,3,1,0:T(1,128)S(1)} copy-done((s32[1,1,2048,1]{2,3,1,0:T(1,128)S(1)}, s32[1,1,2048,1]{2,3,1,0:T(1,128)}, u32[]{:S(2)}) %copy-start.8) | copy-done | bytes 8216
  2.9 0.0 copy-start.10
  2.9 0.7 %copy-done.10 = s32[1,1,2048]{2,1,0:T(1,128)S(1)} copy-done((s32[1,1,2048]{2,1,0:T(1,128)S(1)}, s32[1,1,2048]{2,1,0:T(1,128)}, u32[]{:S(2)}) %copy-start.10) | copy-done | bytes 8216
  3.6 0.0 copy-start.12
  3.6 0.7 %copy-done.12 = f32[1,1,2048]{2,1,0:T(1,128)S(1)} copy-done((f32[1,1,2048]{2,1,0:T(1,128)S(1)}, f32[1,1,2048]{2,1,0:T(1,128)}, u32[]{:S(2)}) %copy-start.12) | copy-done | bytes 8216
  4.3 0.7 %copy-done.14 = f32[16,128]{1,0:T(8,128)S(1)} copy-done((f32[16,128]{1,0:T(8,128)S(1)}, f32[16,128]{1,0:T(8,128)}, u32[]{:S(2)}) %copy-start.14) | copy-done | bytes 8216
  5.0 1.6 %exchange_send.1 = (f32[4,48,128]{2,1,0:T(8,128)}, f32[1,2048]{1,0:T(1,128)S(1)}) custom-call(f32[16,128]{1,0:T(8,128)S(1)} %copy-done.14, f32[2,8,16,128]{3,2,1,0:T(8,128)S(1)} %copy-done, s32[1,2048]{1,0:T(1,128)S(1)} %bitcast.4, s32[1,2048]{1,0:T(1,128)S(1)} %bitcast.6, s32[1,2048]{1,0:T(1,128)S(1)} %bitcast.8, f32[1,2048]{1,0:T(1,128)S(1)} %bitcast.10), custom_call_target="tpu_custom_call" | custom-call | tf_op jit(solution)/shard_map/exchange_send/pallas_call | solution.py:333
  6.6 6.5 %all-to-all-start = ((f32[4,48,128]{2,1,0:T(8,128)}), f32[4,48,128]{2,1,0:T(8,128)S(1)}, u32[]{:S(2)}, u32[]{:S(2)}) async-start(f32[4,48,128]{2,1,0:T(8,128)} %get-tuple-element.14), calls=%async_computation | async-start | bytes 196608 | tf_op jit(solution)/shard_map/all_to_all | solution.py:342
  13.1 0.0 copy-done.1
  13.1 0.0 copy-done.3
  13.1 0.0 copy-done.4
  13.1 0.0 copy-done.5
  13.1 0.0 copy-start.2
  13.1 1.0 %copy-done.2 = f32[3,16,16,128]{3,2,1,0:T(8,128)S(1)} copy-done((f32[3,16,16,128]{3,2,1,0:T(8,128)S(1)}, f32[3,16,16,128]{3,2,1,0:T(8,128)}, u32[]{:S(2)}) %copy-start.2) | copy-done | bytes 393240
  14.1 0.4 pack.1
  14.5 2.1 %collective-permute-start = (f32[200,128]{1,0:T(8,128)S(1)}, f32[200,128]{1,0:T(8,128)S(1)}, u32[]{:S(2)}, u32[]{:S(2)}) collective-permute-start(f32[200,128]{1,0:T(8,128)S(1)} %get-tuple-element.16), channel_id=1, source_target_pairs={{0,4},{1,5},{2,6},{3,7},{4,8},{5,9},{6,10},{7,11},{8,12},{9,13},{1... | collective-permute-start | bytes 307208 | tf_op jit(solution)/shard_map/ppermute | solution.py:315
  16.5 1.9 %collective-permute-start.1 = (f32[200,128]{1,0:T(8,128)S(1)}, f32[200,128]{1,0:T(8,128)S(1)}, u32[]{:S(2)}, u32[]{:S(2)}) collective-permute-start(f32[200,128]{1,0:T(8,128)S(1)} %get-tuple-element.17), channel_id=1, source_target_pairs={{0,12},{1,13},{2,14},{3,15},{4,0},{5,1},{6,2},{7,3},{8,4},{9,5},{1... | collective-permute-start | bytes 307208 | tf_op jit(solution)/shard_map/ppermute | solution.py:315
  18.4 0.0 collective-permute-start.4
  18.4 1.2 %collective-permute-start.2 = (f32[16,256]{1,0:T(8,128)S(1)}, f32[16,256]{1,0:T(8,128)S(1)}, u32[]{:S(2)}, u32[]{:S(2)}) collective-permute-start(f32[16,256]{1,0:T(8,128)S(1)} %get-tuple-element.18), channel_id=1, source_target_pairs={{0,1},{1,2},{2,3},{3,0},{4,5},{5,6},{6,7},{7,4},{8,9},{9,10},{10,1... | collective-permute-start | bytes 49160 | tf_op jit(solution)/shard_map/ppermute | solution.py:315
  19.6 0.5 %collective-permute-start.3 = (f32[16,256]{1,0:T(8,128)S(1)}, f32[16,256]{1,0:T(8,128)S(1)}, u32[]{:S(2)}, u32[]{:S(2)}) collective-permute-start(f32[16,256]{1,0:T(8,128)S(1)} %get-tuple-element.19), channel_id=1, source_target_pairs={{0,3},{1,0},{2,1},{3,2},{4,7},{5,4},{6,5},{7,6},{8,11},{9,8},{10,9... | collective-permute-start | bytes 49160 | tf_op jit(solution)/shard_map/ppermute | solution.py:315
  20.1 4.1 %collective-permute-done.4.from_ul = f32[4,256]{1,0:T(4,128)S(1)} collective-permute-done((f32[4,256]{1,0:T(4,128)S(1)}, f32[4,256]{1,0:T(4,128)S(1)}, u32[]{:S(2)}, u32[]{:S(2)}) %collective-permute-start.4) | collective-permute-done | bytes 4128 | tf_op jit(solution)/shard_map/ppermute | solution.py:315
  24.2 0.0 collective-permute-start.5
  24.2 3.9 %collective-permute-done.5.from_dl = f32[4,256]{1,0:T(4,128)S(1)} collective-permute-done((f32[4,256]{1,0:T(4,128)S(1)}, f32[4,256]{1,0:T(4,128)S(1)}, u32[]{:S(2)}, u32[]{:S(2)}) %collective-permute-start.5) | collective-permute-done | bytes 4128 | tf_op jit(solution)/shard_map/ppermute | solution.py:315
  28.2 0.0 collective-permute-start.6
  28.2 4.8 %collective-permute-done.6.from_ur = f32[4,256]{1,0:T(4,128)S(1)} collective-permute-done((f32[4,256]{1,0:T(4,128)S(1)}, f32[4,256]{1,0:T(4,128)S(1)}, u32[]{:S(2)}, u32[]{:S(2)}) %collective-permute-start.6) | collective-permute-done | bytes 4128 | tf_op jit(solution)/shard_map/ppermute | solution.py:315
  33.0 0.8 %collective-permute-start.7 = (f32[4,256]{1,0:T(4,128)S(1)}, f32[4,256]{1,0:T(4,128)S(1)}, u32[]{:S(2)}, u32[]{:S(2)}) collective-permute-start(f32[4,256]{1,0:T(4,128)S(1)} %get-tuple-element.23), channel_id=1, source_target_pairs={{0,15},{1,12},{2,13},{3,14},{4,3},{5,0},{6,1},{7,2},{8,7},{9,4},{1... | collective-permute-start | bytes 12296 | tf_op jit(solution)/shard_map/ppermute | solution.py:315
  33.8 2.2 %collective-permute-done.7.from_dr = f32[4,256]{1,0:T(4,128)S(1)} collective-permute-done((f32[4,256]{1,0:T(4,128)S(1)}, f32[4,256]{1,0:T(4,128)S(1)}, u32[]{:S(2)}, u32[]{:S(2)}) %collective-permute-start.7) | collective-permute-done | bytes 4128 | tf_op jit(solution)/shard_map/ppermute | solution.py:315
  36.0 0.0 collective-permute-done.2.from_left
  36.0 0.0 collective-permute-done.3.from_right
  36.0 0.0 collective-permute-done.from_up
  36.0 0.0 collective-permute-done.1.from_down
  36.1 0.0 copy-done.15
  36.1 0.0 copy-start.7
  36.1 0.0 copy-start.9
  36.1 0.0 copy-start.11
  36.1 0.0 copy-start.13
  36.1 8.2 %steps.1 = (f32[3,16,16,128]{3,2,1,0:T(8,128)}, f32[2,8,16,128]{3,2,1,0:T(8,128)}) custom-call(f32[16]{0:T(128)S(1)} %copy-done.15, f32[3,16,16,128]{3,2,1,0:T(8,128)S(1)} %copy-done.2, f32[2,8,16,128]{3,2,1,0:T(8,128)S(1)} %copy-done.1, f32[16,128]{1,0:T(8,128)S(1)} %copy-done.3, s32[16,128]{1,0:T(8,128)S(1)} %copy-done.4, f32[16,128]{1,0:T(8,128)S(1)} %copy-done.5, ...), custom_call_target="tpu_custom_call" | custom-call | tf_op jit(solution)/shard_map/steps/pallas_call | solution.py:344
  44.3 0.0 all-to-all-done.got
  44.3 0.0 copy-done.7
  44.3 0.0 copy-done.9
  44.3 0.0 copy-done.11
  44.3 0.0 copy-done.13
  44.3 2.1 %exchange_receive.1 = (f32[3,16,16,128]{3,2,1,0:T(8,128)}, f32[2,8,16,128]{3,2,1,0:T(8,128)}) custom-call(f32[4,48,128]{2,1,0:T(8,128)S(1)} %all-to-all-done.got, f32[2,8,16,128]{3,2,1,0:T(8,128)S(1)} %copy-done.1, s32[1,2048]{1,0:T(1,128)S(1)} %bitcast.5, s32[1,2048]{1,0:T(1,128)S(1)} %bitcast.7, ...), custom_call_target="tpu_custom_call", output_to_operand_aliasing={{0}: (7, {}), {1}: (8, {})} | custom-call | tf_op jit(solution)/shard_map/exchange_receive/pallas_call | solution.py:369
  (6 shorter events, 0.0 us)
Async XLA Ops:
  0.6 0.9 %copy-start = (f32[2,8,16,128]{3,2,1,0:T(8,128)S(1)}, f32[2,8,16,128]{3,2,1,0:T(8,128)}, u32[]{:S(2)}) copy-start(f32[2,8,16,128]{3,2,1,0:T(8,128)} %sst.3) | copy-start | bytes 393220
  1.5 0.7 %copy-start.6 = (s32[1,1,2048]{2,1,0:T(1,128)S(1)}, s32[1,1,2048]{2,1,0:T(1,128)}, u32[]{:S(2)}) copy-start(s32[1,1,2048]{2,1,0:T(1,128)} %param.18) | copy-start | bytes 24580
  2.2 0.7 %copy-start.8 = (s32[1,1,2048,1]{2,3,1,0:T(1,128)S(1)}, s32[1,1,2048,1]{2,3,1,0:T(1,128)}, u32[]{:S(2)}) copy-start(s32[1,1,2048,1]{2,3,1,0:T(1,128)} %param.19) | copy-start | bytes 24580
  2.9 0.7 %copy-start.10 = (s32[1,1,2048]{2,1,0:T(1,128)S(1)}, s32[1,1,2048]{2,1,0:T(1,128)}, u32[]{:S(2)}) copy-start(s32[1,1,2048]{2,1,0:T(1,128)} %param.20) | copy-start | bytes 24580
  3.6 0.7 %copy-start.12 = (f32[1,1,2048]{2,1,0:T(1,128)S(1)}, f32[1,1,2048]{2,1,0:T(1,128)}, u32[]{:S(2)}) copy-start(f32[1,1,2048]{2,1,0:T(1,128)} %param.21) | copy-start | bytes 24580
  4.3 0.7 %copy-start.14 = (f32[16,128]{1,0:T(8,128)S(1)}, f32[16,128]{1,0:T(8,128)}, u32[]{:S(2)}) copy-start(f32[16,128]{1,0:T(8,128)} %air.1) | copy-start | bytes 24580
  6.6 6.5 %copy-start.1 = (f32[2,8,16,128]{3,2,1,0:T(8,128)S(1)}, f32[2,8,16,128]{3,2,1,0:T(8,128)}, u32[]{:S(2)}) copy-start(f32[2,8,16,128]{3,2,1,0:T(8,128)} %sst.3) | copy-start | bytes 393220
  6.6 6.5 %copy-start.3 = (f32[16,128]{1,0:T(8,128)S(1)}, f32[16,128]{1,0:T(8,128)}, u32[]{:S(2)}) copy-start(f32[16,128]{1,0:T(8,128)} %depth.3) | copy-start | bytes 24580
  6.6 6.5 %copy-start.4 = (s32[16,128]{1,0:T(8,128)S(1)}, s32[16,128]{1,0:T(8,128)}, u32[]{:S(2)}) copy-start(s32[16,128]{1,0:T(8,128)} %wet.3) | copy-start | bytes 24580
  6.6 6.5 %copy-start.5 = (f32[16,128]{1,0:T(8,128)S(1)}, f32[16,128]{1,0:T(8,128)}, u32[]{:S(2)}) copy-start(f32[16,128]{1,0:T(8,128)} %kappa.3) | copy-start | bytes 24580
  6.6 37.7 %all-to-all-start = ((f32[4,48,128]{2,1,0:T(8,128)}), f32[4,48,128]{2,1,0:T(8,128)S(1)}, u32[]{:S(2)}, u32[]{:S(2)}) async-start(f32[4,48,128]{2,1,0:T(8,128)} %get-tuple-element.14), calls=%async_computation | async-start | bytes 196608 | tf_op jit(solution)/shard_map/all_to_all | solution.py:342
  13.1 1.0 %copy-start.2 = (f32[3,16,16,128]{3,2,1,0:T(8,128)S(1)}, f32[3,16,16,128]{3,2,1,0:T(8,128)}, u32[]{:S(2)}) copy-start(f32[3,16,16,128]{3,2,1,0:T(8,128)} %atm.3) | copy-start | bytes 1179652
  14.5 21.6 %collective-permute-start = (f32[200,128]{1,0:T(8,128)S(1)}, f32[200,128]{1,0:T(8,128)S(1)}, u32[]{:S(2)}, u32[]{:S(2)}) collective-permute-start(f32[200,128]{1,0:T(8,128)S(1)} %get-tuple-element.16), channel_id=1, source_target_pairs={{0,4},{1,5},{2,6},{3,7},{4,8},{5,9},{6,10},{7,11},{8,12},{9,13},{1... | collective-permute-start | bytes 307208 | tf_op jit(solution)/shard_map/ppermute | solution.py:315
  16.5 19.5 %collective-permute-start.1 = (f32[200,128]{1,0:T(8,128)S(1)}, f32[200,128]{1,0:T(8,128)S(1)}, u32[]{:S(2)}, u32[]{:S(2)}) collective-permute-start(f32[200,128]{1,0:T(8,128)S(1)} %get-tuple-element.17), channel_id=1, source_target_pairs={{0,12},{1,13},{2,14},{3,15},{4,0},{5,1},{6,2},{7,3},{8,4},{9,5},{1... | collective-permute-start | bytes 307208 | tf_op jit(solution)/shard_map/ppermute | solution.py:315
  18.4 5.8 %collective-permute-start.4 = (f32[4,256]{1,0:T(4,128)S(1)}, f32[4,256]{1,0:T(4,128)S(1)}, u32[]{:S(2)}, u32[]{:S(2)}) collective-permute-start(f32[4,256]{1,0:T(4,128)S(1)} %get-tuple-element.20), channel_id=1, source_target_pairs={{0,5},{1,6},{2,7},{3,4},{4,9},{5,10},{6,11},{7,8},{8,13},{9,14},{1... | collective-permute-start | bytes 12296 | tf_op jit(solution)/shard_map/ppermute | solution.py:315
  18.4 17.6 %collective-permute-start.2 = (f32[16,256]{1,0:T(8,128)S(1)}, f32[16,256]{1,0:T(8,128)S(1)}, u32[]{:S(2)}, u32[]{:S(2)}) collective-permute-start(f32[16,256]{1,0:T(8,128)S(1)} %get-tuple-element.18), channel_id=1, source_target_pairs={{0,1},{1,2},{2,3},{3,0},{4,5},{5,6},{6,7},{7,4},{8,9},{9,10},{10,1... | collective-permute-start | bytes 49160 | tf_op jit(solution)/shard_map/ppermute | solution.py:315
  19.6 16.4 %collective-permute-start.3 = (f32[16,256]{1,0:T(8,128)S(1)}, f32[16,256]{1,0:T(8,128)S(1)}, u32[]{:S(2)}, u32[]{:S(2)}) collective-permute-start(f32[16,256]{1,0:T(8,128)S(1)} %get-tuple-element.19), channel_id=1, source_target_pairs={{0,3},{1,0},{2,1},{3,2},{4,7},{5,4},{6,5},{7,6},{8,11},{9,8},{10,9... | collective-permute-start | bytes 49160 | tf_op jit(solution)/shard_map/ppermute | solution.py:315
  24.2 3.9 %collective-permute-start.5 = (f32[4,256]{1,0:T(4,128)S(1)}, f32[4,256]{1,0:T(4,128)S(1)}, u32[]{:S(2)}, u32[]{:S(2)}) collective-permute-start(f32[4,256]{1,0:T(4,128)S(1)} %get-tuple-element.21), channel_id=1, source_target_pairs={{0,13},{1,14},{2,15},{3,12},{4,1},{5,2},{6,3},{7,0},{8,5},{9,6},{1... | collective-permute-start | bytes 12296 | tf_op jit(solution)/shard_map/ppermute | solution.py:315
  28.2 7.9 %copy-start.15 = (f32[16]{0:T(128)S(1)}, f32[16]{0:T(128)}, u32[]{:S(2)}) copy-start(f32[16]{0:T(128)} %speed.1) | copy-start | bytes 196
  28.2 4.8 %collective-permute-start.6 = (f32[4,256]{1,0:T(4,128)S(1)}, f32[4,256]{1,0:T(4,128)S(1)}, u32[]{:S(2)}, u32[]{:S(2)}) collective-permute-start(f32[4,256]{1,0:T(4,128)S(1)} %get-tuple-element.22), channel_id=1, source_target_pairs={{0,7},{1,4},{2,5},{3,6},{4,11},{5,8},{6,9},{7,10},{8,15},{9,12},{1... | collective-permute-start | bytes 12296 | tf_op jit(solution)/shard_map/ppermute | solution.py:315
  33.0 3.0 %collective-permute-start.7 = (f32[4,256]{1,0:T(4,128)S(1)}, f32[4,256]{1,0:T(4,128)S(1)}, u32[]{:S(2)}, u32[]{:S(2)}) collective-permute-start(f32[4,256]{1,0:T(4,128)S(1)} %get-tuple-element.23), channel_id=1, source_target_pairs={{0,15},{1,12},{2,13},{3,14},{4,3},{5,0},{6,1},{7,2},{8,7},{9,4},{1... | collective-permute-start | bytes 12296 | tf_op jit(solution)/shard_map/ppermute | solution.py:315
  36.1 8.2 %copy-start.7 = (s32[1,1,2048]{2,1,0:T(1,128)S(1)}, s32[1,1,2048]{2,1,0:T(1,128)}, u32[]{:S(2)}) copy-start(s32[1,1,2048]{2,1,0:T(1,128)} %param.18) | copy-start | bytes 24580
  36.1 8.2 %copy-start.9 = (s32[1,1,2048,1]{2,3,1,0:T(1,128)S(1)}, s32[1,1,2048,1]{2,3,1,0:T(1,128)}, u32[]{:S(2)}) copy-start(s32[1,1,2048,1]{2,3,1,0:T(1,128)} %param.19) | copy-start | bytes 24580
  36.1 8.2 %copy-start.11 = (s32[1,1,2048]{2,1,0:T(1,128)S(1)}, s32[1,1,2048]{2,1,0:T(1,128)}, u32[]{:S(2)}) copy-start(s32[1,1,2048]{2,1,0:T(1,128)} %param.20) | copy-start | bytes 24580
  36.1 8.2 %copy-start.13 = (f32[1,1,2048]{2,1,0:T(1,128)S(1)}, f32[1,1,2048]{2,1,0:T(1,128)}, u32[]{:S(2)}) copy-start(f32[1,1,2048]{2,1,0:T(1,128)} %param.21) | copy-start | bytes 24580

commit v2 on v1

v2 whole, which is shorter than its diff:
```python
import functools

import jax
import jax.numpy as jnp
from jax import lax
from jax.experimental import pallas as pl
from jax.experimental.pallas import tpu as pltpu
from jax.sharding import PartitionSpec as P

ACOUSTIC = 2
OCEAN_STEPS = 2
AH = 2 * ACOUSTIC
OH = OCEAN_STEPS

ATM_GAIN = 0.5
SEA_GAIN = 0.5

F32 = jnp.float32
BF16 = jnp.bfloat16


def lane_slots(levels, tracers):
    slots = [AH * i for i in range(3 * levels)]
    base = AH * 3 * levels
    slots += [base + OH * i for i in range(tracers)]
    base += OH * tracers
    slots += [base + AH * i for i in range(3)]
    total = base + 3 * AH
    return slots, -(-total // 128) * 128


def row_slots(levels, tracers):
    per = 3 * AH - 2
    base = per * levels
    misc = base + OH * tracers
    return per, base, misc, misc + AH + 2 * OH


def pack_kernel(*refs):
    sources, rest = refs[:11], refs[11:]
    atm, ocean, depth, wet, kappa = rest[:5]
    up, down, left, right, sems = rest[11:]
    copies = [
        pltpu.make_async_copy(source, target, sems.at[i])
        for i, (source, target) in enumerate(zip(sources, rest[:11]))
    ]
    for copy in copies:
        copy.start()
    levels = atm.shape[1]
    rows, cols = atm.shape[2:]
    tracers = ocean.shape[0] * ocean.shape[1]
    each = ocean.shape[1]
    per, obase, mbase, _ = row_slots(levels, tracers)
    slots, _ = lane_slots(levels, tracers)
    for copy in copies:
        copy.wait()
    wetness = wet[...].astype(F32)

    lane = lax.broadcasted_iota(jnp.int32, (rows, cols), 1)
    fields = [(atm, (k, l), AH) for k in range(3) for l in range(levels)]
    fields += [(ocean, (i // each, i % each), OH) for i in range(tracers)]
    fields += [(depth, None, AH), (None, None, AH), (kappa, None, AH)]
    packed = {}
    for (ref, at, width), slot in zip(fields, slots):
        value = wetness if ref is None else (ref[...] if at is None else ref[at[0], at[1]])
        tile, offset = slot // cols, slot % cols
        mask = (lane >= offset) & (lane < offset + width)
        first = pltpu.roll(value, offset, 1) if offset else value
        turn = (offset + width) % cols
        last = pltpu.roll(value, turn, 1) if turn else value
        if tile in packed:
            a, b = packed[tile]
            packed[tile] = (jnp.where(mask, first, a), jnp.where(mask, last, b))
        else:
            packed[tile] = (first, last)
    for tile, (a, b) in packed.items():
        where = slice(tile * cols, (tile + 1) * cols)
        left[:, where] = a
        right[:, where] = b

    for level in range(levels):
        base = per * level
        for at, which, width in ((0, 1, AH), (AH, 0, AH - 1), (2 * AH - 1, 2, AH - 1)):
            up[base + at : base + at + width, :] = atm[which, level, 0:width, :]
            down[base + at : base + at + width, :] = atm[which, level, rows - width : rows, :]
    for i in range(tracers):
        at = obase + OH * i
        up[at : at + OH, :] = ocean[i // each, i % each, 0:OH, :]
        down[at : at + OH, :] = ocean[i // each, i % each, rows - OH : rows, :]
    for at, value, width in (
        (mbase, depth[...], AH),
        (mbase + AH, wetness, OH),
        (mbase + AH + OH, kappa[...], OH),
    ):
        up[at : at + width, :] = value[0:width]
        down[at : at + width, :] = value[rows - width : rows]


def split3(value):
    hi = value.astype(BF16)
    rest = value - hi.astype(F32)
    mid = rest.astype(BF16)
    low = (rest - mid.astype(F32)).astype(BF16)
    return hi, mid, low


def one_hot(index, size):
    shape = (size, index.shape[-1])
    return lax.broadcasted_iota(jnp.int32, shape, 0) == index


def gather_rows(table, hot_rows, hot_cols):
    r = table.shape[0]
    parts = jnp.concatenate(split3(table), axis=0)
    g = jnp.dot(parts, hot_cols, preferred_element_type=F32)
    g = g[0:r] + g[r : 2 * r] + g[2 * r : 3 * r]
    return jnp.sum(jnp.where(hot_rows, g, 0.0), axis=0, keepdims=True)


def scatter_rows(values, hot_rows, hot_cols):
    r = hot_rows.shape[0]
    parts = []
    for value in values:
        for part in split3(value):
            parts.append(jnp.where(hot_rows, part.astype(F32), 0.0).astype(BF16))
    s = lax.dot_general(
        jnp.concatenate(parts, axis=0),
        hot_cols,
        (((1,), (1,)), ((), ())),
        preferred_element_type=F32,
    )
    out = []
    for i in range(len(values)):
        base = 3 * r * i
        out.append(s[base : base + r] + s[base + r : base + 2 * r] + s[base + 2 * r : base + 3 * r])
    return out


def send_kernel(air, ocean, atm_cell, dest, sea_cell, weight, from_left, from_right, message, wair_out):
    rows, cols = air.shape
    tiles = message.shape[0]
    tile_lanes = from_left.shape[1] // cols
    cell = atm_cell[...]
    hot_atm = jnp.where(one_hot(cell % cols, cols), 1.0, 0.0).astype(BF16)
    airx = gather_rows(air[...], one_hot(cell // cols, rows), hot_atm)
    w = weight[...]
    wair = w * airx
    wair_out[...] = wair
    cell = sea_cell[...]
    hot_sea = jnp.where(one_hot(cell % cols, cols), 1.0, 0.0).astype(BF16)
    row = dest[...] * rows + cell // cols
    surface = ocean[0, 0]
    for tile in range(tiles):
        s1, s2 = scatter_rows([wair, w], one_hot(row - tile * rows, rows), hot_sea)
        message[tile, 0:rows, :] = s1
        message[tile, rows : 2 * rows, :] = s2
        message[tile, 2 * rows : 3 * rows, :] = surface
        message[tile, 3 * rows :, :] = jnp.zeros((message.shape[1] - 3 * rows, cols), F32)
    me = lax.axis_index("tile")
    above, below = lax.rem(me + tiles - 1, tiles), lax.rem(me + 1, tiles)
    at = 3 * rows
    for ref in (from_left, from_right):
        for i in range(tile_lanes):
            where = slice(i * cols, (i + 1) * cols)
            message[above, at : at + AH, :] = ref[0:AH, where]
            message[below, at : at + AH, :] = ref[rows - AH : rows, where]
            at += AH


def final_kernel(
    speed,
    atm,
    ocean,
    depth,
    wet,
    kappa,
    atm_cell,
    dest,
    sea_cell,
    weight,
    wair,
    from_up,
    from_down,
    from_left,
    from_right,
    got,
    atm_out,
    ocean_out,
    us,
    vs,
    hs,
    fs,
    ms,
    atm_buf,
    ocean_buf,
    sems,
):
    levels = atm.shape[1]
    rows, cols = atm.shape[2:]
    tracers = ocean.shape[0] * ocean.shape[1]
    each = ocean.shape[1]
    per, obase, mbase, _ = row_slots(levels, tracers)
    slots, lanes = lane_slots(levels, tracers)
    full = rows + 2 * AH
    tiles = got.shape[0]
    me = lax.axis_index("tile")
    above, below = lax.rem(me + tiles - 1, tiles), lax.rem(me + 1, tiles)
    low_half = lax.broadcasted_iota(jnp.int32, (1, cols), 1) < cols // 2

    surface = ocean[0, 0]
    s1, s2 = got[0, 0:rows, :], got[0, rows : 2 * rows, :]
    for tile in range(1, tiles):
        s1 = s1 + got[tile, 0:rows, :]
        s2 = s2 + got[tile, rows : 2 * rows, :]
    sea_flux = s1 - surface * s2
    cell = sea_cell[...]
    hot_sea = jnp.where(one_hot(cell % cols, cols), 1.0, 0.0).astype(BF16)
    row = dest[...] * rows + cell // cols
    sstx = jnp.zeros(cell.shape, F32)
    for tile in range(tiles):
        table = got[tile, 2 * rows : 3 * rows, :]
        sstx = sstx + gather_rows(table, one_hot(row - tile * rows, rows), hot_sea)
    flux = wair[...] - weight[...] * sstx
    cell = atm_cell[...]
    hot_atm = jnp.where(one_hot(cell % cols, cols), 1.0, 0.0).astype(BF16)
    (atm_flux,) = scatter_rows([flux], one_hot(cell // cols, rows), hot_atm)

    def strips(slot, width, left_part, right_part):
        offset = slot % cols
        a, b = right_part(slot // cols), left_part(slot // cols)
        if offset:
            a = pltpu.roll(a, cols - offset, 1)
        turn = (cols - width - offset) % cols
        if turn:
            b = pltpu.roll(b, turn, 1)
        return jnp.where(low_half, a, b)

    def side(ref):
        return lambda i: ref[:, i * cols : (i + 1) * cols]

    def corner(tile, which):
        base = 3 * rows + which * AH * (lanes // cols)
        return lambda i: got[tile, base + AH * i : base + AH * (i + 1), :]

    def extend(view, value, row_at, row_width, slot, width):
        view[0:rows, 0:cols] = value
        view[rows : rows + row_width, 0:cols] = from_down[row_at : row_at + row_width, :]
        view[full - row_width : full, 0:cols] = from_up[row_at : row_at + row_width, :]
        view[0:rows, cols : 2 * cols] = strips(slot, width, side(from_left), side(from_right))
        view[rows : rows + AH, cols : 2 * cols] = strips(slot, width, corner(below, 0), corner(below, 1))
        view[full - AH : full, cols : 2 * cols] = strips(slot, width, corner(above, 0), corner(above, 1))

    def east(f):
        return pltpu.roll(f, 2 * cols - 1, 1)

    def west(f):
        return pltpu.roll(f, 1, 1)

    def south(f):
        return pltpu.roll(f, full - 1, 0)

    def north(f):
        return pltpu.roll(f, 1, 0)

    base = 3 * levels + tracers
    extend(ms.at[0], depth[...], mbase, AH, slots[base], AH)
    extend(ms.at[1], wet[...].astype(F32), mbase + AH, OH, slots[base + 1], AH)
    extend(ms.at[2], kappa[...], mbase + AH + OH, OH, slots[base + 2], AH)
    for i in range(tracers):
        extend(fs.at[i], ocean[i // each, i % each], obase + OH * i, OH, slots[3 * levels + i], OH)
    for level in range(levels):
        at = per * level
        extend(us.at[level], atm[0, level], at + AH, AH - 1, slots[level], AH)
        extend(vs.at[level], atm[1, level], at, AH, slots[levels + level], AH)
        extend(hs.at[level], atm[2, level], at + 2 * AH - 1, AH - 1, slots[2 * levels + level], AH)

    w = ms[1]
    k = ms[2]
    we, ww, ws, wn = east(w), west(w), south(w), north(w)
    for step in range(OCEAN_STEPS):
        for i in range(tracers):
            f = fs[i]
            total = we * (east(f) - f)
            total = total + ww * (west(f) - f)
            total = total + ws * (south(f) - f)
            total = total + wn * (north(f) - f)
            f = f + k * (w * total)
            if step < OCEAN_STEPS - 1:
                fs[i] = f
            else:
                f = f[0:rows, 0:cols]
                ocean_buf[i // each, i % each] = f + SEA_GAIN * sea_flux if i == 0 else f
    copies = [pltpu.make_async_copy(ocean_buf, ocean_out, sems.at[0])]
    copies[0].start()

    d = ms[0]
    chunk = max(1, levels // 4)
    for step in range(ACOUSTIC):
        for level in range(levels):
            u, v = us[level], vs[level]
            column_speed = speed[level] * d
            hs[level] = hs[level] - column_speed * (
                (east(u) - west(u)) * 0.5 + (south(v) - north(v)) * 0.5
            )
        for level in range(levels):
            u, v, h = us[level], vs[level], hs[level]
            u = u - (east(h) - west(h)) * 0.5
            v = v - (south(h) - north(h)) * 0.5
            if step < ACOUSTIC - 1:
                us[level], vs[level] = u, v
            else:
                h = h[0:rows, 0:cols]
                atm_buf[0, level] = u[0:rows, 0:cols]
                atm_buf[1, level] = v[0:rows, 0:cols]
                atm_buf[2, level] = h - ATM_GAIN * atm_flux if level == levels - 1 else h
                if (level + 1) % chunk == 0:
                    where = pl.ds(level + 1 - chunk, chunk)
                    copies.append(
                        pltpu.make_async_copy(
                            atm_buf.at[:, where], atm_out.at[:, where], sems.at[len(copies)]
                        )
                    )
                    copies[-1].start()
    for copy in copies:
        copy.wait()


def on_device(
    tile_count,
    atm_state,
    air_temp,
    depth,
    wave_speed,
    ocean_state,
    wet_mask,
    diffusivity,
    xg_atm_cell,
    xg_dest,
    xg_ocean_cell,
    xg_weight,
):
    levels = atm_state.shape[1]
    rows, cols = atm_state.shape[2:]
    tracers = ocean_state.shape[0] * ocean_state.shape[1]
    cells = xg_weight.shape[-1]
    _, lanes = lane_slots(levels, tracers)
    _, _, _, message_rows = row_slots(levels, tracers)
    vmem = pl.BlockSpec(memory_space=pltpu.VMEM)
    hbm = pl.BlockSpec(memory_space=pltpu.HBM)
    smem = pl.BlockSpec(memory_space=pltpu.SMEM)
    params = pltpu.CompilerParams(vmem_limit_bytes=32 * 1024 * 1024)
    full = rows + 2 * AH

    def shape(*dims):
        return jax.ShapeDtypeStruct(dims, F32)

    operands = (
        atm_state,
        ocean_state,
        depth,
        wet_mask,
        diffusivity,
        air_temp,
        xg_atm_cell.reshape(1, cells),
        xg_dest.reshape(1, cells),
        xg_ocean_cell.reshape(1, cells),
        xg_weight.reshape(1, cells),
        wave_speed,
    )
    atm, ocean, dep, wet, kappa, air, atm_cell, dest, sea_cell, weight, speed, up, down, left, right = pl.pallas_call(
        pack_kernel,
        out_shape=[jax.ShapeDtypeStruct(x.shape, x.dtype) for x in operands]
        + [shape(message_rows, cols)] * 2
        + [shape(rows, lanes)] * 2,
        in_specs=[hbm] * 11,
        out_specs=[vmem] * 10 + [smem] + [vmem] * 4,
        scratch_shapes=[pltpu.SemaphoreType.DMA((11,))],
        compiler_params=params,
        name="pack",
    )(*operands)

    column_axes = ("sub", "comp")
    column_count = lax.axis_size("sub") * lax.axis_size("comp")

    def shift(value, axes, count, by):
        return lax.ppermute(value, axes, [(i, (i + by) % count) for i in range(count)])

    from_right = shift(left, column_axes, column_count, -1)
    from_left = shift(right, column_axes, column_count, 1)
    from_down = shift(up, "tile", tile_count, -1)
    from_up = shift(down, "tile", tile_count, 1)

    corner_rows = 2 * AH * (lanes // cols)
    message, wair = pl.pallas_call(
        send_kernel,
        out_shape=[shape(tile_count, 3 * rows + corner_rows, cols), shape(1, cells)],
        in_specs=[vmem] * 8,
        out_specs=[vmem] * 2,
        compiler_params=params,
        name="exchange_send",
    )(air, ocean, atm_cell, dest, sea_cell, weight, from_left, from_right)
    got = lax.all_to_all(message, "tile", split_axis=0, concat_axis=0, tiled=True)

    return tuple(
        pl.pallas_call(
            final_kernel,
            out_shape=[shape(*atm_state.shape), shape(*ocean_state.shape)],
            in_specs=[smem] + [vmem] * 15,
            out_specs=[hbm] * 2,
            scratch_shapes=[pltpu.VMEM((levels, full, 2 * cols), F32)] * 3
            + [
                pltpu.VMEM((tracers, full, 2 * cols), F32),
                pltpu.VMEM((3, full, 2 * cols), F32),
                pltpu.VMEM(atm_state.shape, F32),
                pltpu.VMEM(ocean_state.shape, F32),
                pltpu.SemaphoreType.DMA((8,)),
            ],
            compiler_params=params,
            name="steps",
        )(
            speed,
            atm,
            ocean,
            dep,
            wet,
            kappa,
            atm_cell,
            dest,
            sea_cell,
            weight,
            wair,
            from_up,
            from_down,
            from_left,
            from_right,
            got,
        )
    )


def solution(mesh):
    grid = P(("member", "tile"), ("sub", "comp"))
    state = P(None, None, ("member", "tile"), ("sub", "comp"))
    cells = P(("member", "tile"), ("sub", "comp"), None)
    return jax.shard_map(
        functools.partial(on_device, mesh.shape["tile"]),
        mesh=mesh,
        in_specs=(
            state,
            grid,
            grid,
            P(),
            state,
            grid,
            grid,
            cells,
            P(("member", "tile"), ("sub", "comp"), None, None),
            cells,
            cells,
        ),
        out_specs=(state, state),
        check_vma=False,
    )
```

time: 47.1 us -> 37 us (0.79)
  waiting for transfers between devices: 15.1 us -> 8.58 us
  Pallas kernels: 12.2 us -> 7.05 us
  local copies, waits for them, and re-layouts: 5.42 us -> 8.12 us
  starting transfers between devices: 13 us -> 12 us
    ppermute x8 -> x4, waiting for transfers between devices: 15.1 us -> 8.58 us  [shift(): lax.ppermute(value, axes, [(i, (i + by) % count) for i in range(count)])]
    pallas_call x4 -> x3, Pallas kernels: 12.2 us -> 7.05 us  [the longest x1 3.42 us: on_device(): pl.pallas_call(final_kernel, out_shape=[shape(*atm_state.shape), shape(*o...]
    unnamed x32 -> x22, local copies, waits for them, and re-layouts: 5.42 us -> 8.12 us
    all_to_all x1, starting transfers between devices: 6.46 us -> 5.62 us  [on_device(): lax.all_to_all(message, 'tile', split_axis=0, concat_axis=0, tiled=True)]
    ppermute x8 -> x4, starting transfers between devices: 6.51 us -> 6.35 us  [shift(): lax.ppermute(value, axes, [(i, (i + by) % count) for i in range(count)])]
  transfers between devices with their start and end apart: 9 -> 5, of which waited for: 4 -> 4; matrix products, arithmetic and copies ran while one was open for 0% -> 0% of each run, Pallas kernels for 18% -> 0%
where the time goes in v2:
time: 37 us; the launch traced here: 36.4 us
  starting transfers between devices  12 us (32%)
  waiting for transfers between devices  8.58 us (23%)
  local copies, waits for them, and re-layouts  8.12 us (22%)
  Pallas kernels  7.05 us (19%)
  between operations  0.67 us (2%)
    ppermute x4, waiting for transfers between devices, shift(): lax.ppermute(value, axes, [(i, (i + by) % count) for i in range(count)])  8.58 us
    unnamed x22, local copies, waits for them, and re-layouts  8.12 us
    ppermute x4, starting transfers between devices, shift(): lax.ppermute(value, axes, [(i, (i + by) % count) for i in range(count)])  6.35 us
    all_to_all x1, starting transfers between devices, on_device(): lax.all_to_all(message, 'tile', split_axis=0, concat_axis=0, tiled=True)  5.62 us
    pallas_call x1, Pallas kernels, on_device(): pl.pallas_call(final_kernel, out_shape=[shape(*atm_state.shape), shape(*o...  3.42 us
    pallas_call x1, Pallas kernels, on_device(): pl.pallas_call(pack_kernel, out_shape=[jax.ShapeDtypeStruct(x.shape, x.dt...  2.06 us
    pallas_call x1, Pallas kernels, on_device(): pl.pallas_call(send_kernel, out_shape=[shape(tile_count, 3 * rows + corne...  1.57 us
  transfers between devices with their start and end apart: 5, of which 4 were waited for; matrix products, arithmetic and copies ran while one was open for 0% of the time, Pallas kernels for 0%

profile of v2, /device:TPU:0, one launch (start us, length us, event | category | flops | bytes accessed | tf_op | source)
XLA Modules:
  0.0 36.4 jit_solution(16270049646430196283)
XLA Ops:
  0.6 0.0 copy-start.10
  0.6 0.6 %copy-done.10 = f32[16]{0:T(128)S(1)} copy-done((f32[16]{0:T(128)S(1)}, f32[16]{0:T(128)}, u32[]{:S(2)}) %copy-start.10) | copy-done | bytes 88
  1.3 0.0 copy-start
  1.3 1.0 %copy-done = f32[3,16,16,128]{3,2,1,0:T(8,128)S(1)} copy-done((f32[3,16,16,128]{3,2,1,0:T(8,128)S(1)}, f32[3,16,16,128]{3,2,1,0:T(8,128)}, u32[]{:S(2)}) %copy-start) | copy-done | bytes 393240
  2.3 0.0 copy-start.1
  2.3 0.9 %copy-done.1 = f32[2,8,16,128]{3,2,1,0:T(8,128)S(1)} copy-done((f32[2,8,16,128]{3,2,1,0:T(8,128)S(1)}, f32[2,8,16,128]{3,2,1,0:T(8,128)}, u32[]{:S(2)}) %copy-start.1) | copy-done | bytes 131096
  3.2 0.0 copy-start.2
  3.2 0.7 %copy-done.2 = f32[16,128]{1,0:T(8,128)S(1)} copy-done((f32[16,128]{1,0:T(8,128)S(1)}, f32[16,128]{1,0:T(8,128)}, u32[]{:S(2)}) %copy-start.2) | copy-done | bytes 8216
  3.9 0.0 copy-start.3
  3.9 0.7 %copy-done.3 = s32[16,128]{1,0:T(8,128)S(1)} copy-done((s32[16,128]{1,0:T(8,128)S(1)}, s32[16,128]{1,0:T(8,128)}, u32[]{:S(2)}) %copy-start.3) | copy-done | bytes 8216
  4.6 0.0 copy-start.4
  4.6 0.7 %copy-done.4 = f32[16,128]{1,0:T(8,128)S(1)} copy-done((f32[16,128]{1,0:T(8,128)S(1)}, f32[16,128]{1,0:T(8,128)}, u32[]{:S(2)}) %copy-start.4) | copy-done | bytes 8216
  5.3 0.0 copy-start.5
  5.3 0.7 %copy-done.5 = f32[16,128]{1,0:T(8,128)S(1)} copy-done((f32[16,128]{1,0:T(8,128)S(1)}, f32[16,128]{1,0:T(8,128)}, u32[]{:S(2)}) %copy-start.5) | copy-done | bytes 8216
  6.0 0.0 copy-start.6
  6.0 0.7 %copy-done.6 = s32[1,1,2048]{2,1,0:T(1,128)S(1)} copy-done((s32[1,1,2048]{2,1,0:T(1,128)S(1)}, s32[1,1,2048]{2,1,0:T(1,128)}, u32[]{:S(2)}) %copy-start.6) | copy-done | bytes 8216
  6.7 0.0 copy-start.7
  6.7 0.7 %copy-done.7 = s32[1,1,2048,1]{2,3,1,0:T(1,128)S(1)} copy-done((s32[1,1,2048,1]{2,3,1,0:T(1,128)S(1)}, s32[1,1,2048,1]{2,3,1,0:T(1,128)}, u32[]{:S(2)}) %copy-start.7) | copy-done | bytes 8216
  7.4 0.0 copy-start.8
  7.4 0.7 %copy-done.8 = s32[1,1,2048]{2,1,0:T(1,128)S(1)} copy-done((s32[1,1,2048]{2,1,0:T(1,128)S(1)}, s32[1,1,2048]{2,1,0:T(1,128)}, u32[]{:S(2)}) %copy-start.8) | copy-done | bytes 8216
  8.1 0.0 copy-start.9
  8.1 0.7 %copy-done.9 = f32[1,1,2048]{2,1,0:T(1,128)S(1)} copy-done((f32[1,1,2048]{2,1,0:T(1,128)S(1)}, f32[1,1,2048]{2,1,0:T(1,128)}, u32[]{:S(2)}) %copy-start.9) | copy-done | bytes 8216
  8.8 2.1 %pack.1 = (f32[3,16,16,128]{3,2,1,0:T(8,128)S(1)}, f32[2,8,16,128]{3,2,1,0:T(8,128)S(1)}, f32[16,128]{1,0:T(8,128)S(1)}, s32[16,128]{1,0:T(8,128)S(1)}, f32[16,1...) custom-call(f32[3,16,16,128]{3,2,1,0:T(8,128)S(1)} %copy-done, ...), custom_call_target="tpu_custom_call" | custom-call | tf_op jit(solution)/shard_map/pack/pallas_call | solution.py:370
  10.8 0.5 %collective-permute-start = (f32[16,256]{1,0:T(8,128)S(1)}, f32[16,256]{1,0:T(8,128)S(1)}, u32[]{:S(2)}, u32[]{:S(2)}) collective-permute-start(f32[16,256]{1,0:T(8,128)S(1)} %get-tuple-element.30), channel_id=1, source_target_pairs={{0,1},{1,2},{2,3},{3,0},{4,5},{5,6},{6,7},{7,4},{8,9},{9,10},{10,1... | collective-permute-start | bytes 49160 | tf_op jit(solution)/shard_map/ppermute | solution.py:386
  11.3 2.0 %collective-permute-start.1 = (f32[16,256]{1,0:T(8,128)S(1)}, f32[16,256]{1,0:T(8,128)S(1)}, u32[]{:S(2)}, u32[]{:S(2)}) collective-permute-start(f32[16,256]{1,0:T(8,128)S(1)} %get-tuple-element.31), channel_id=1, source_target_pairs={{0,3},{1,0},{2,1},{3,2},{4,7},{5,4},{6,5},{7,6},{8,11},{9,8},{10,9... | collective-permute-start | bytes 49160 | tf_op jit(solution)/shard_map/ppermute | solution.py:386
  13.3 1.4 %collective-permute-done.from_left = f32[16,256]{1,0:T(8,128)S(1)} collective-permute-done((f32[16,256]{1,0:T(8,128)S(1)}, f32[16,256]{1,0:T(8,128)S(1)}, u32[]{:S(2)}, u32[]{:S(2)}) %collective-permute-start) | collective-permute-done | bytes 16416 | tf_op jit(solution)/shard_map/ppermute | solution.py:386
  14.7 0.1 collective-permute-done.1.from_right
  14.8 1.6 %exchange_send.1 = (f32[4,64,128]{2,1,0:T(8,128)}, f32[1,2048]{1,0:T(1,128)S(1)}) custom-call(f32[16,128]{1,0:T(8,128)S(1)} %get-tuple-element.29.air, f32[2,8,16,128]{3,2,1,0:T(8,128)S(1)} %get-tuple-element.21.ocean, s32[1,2048]{1,0:T(1,128)S(1)} %get-tuple-element.25.atm_cell, s32[1,2048]{1,0:T(1,128)S(1)} %get-tuple-element.26.dest, ...), custom_call_target="tpu_custom_call" | custom-call | tf_op jit(solution)/shard_map/exchange_send/pallas_call | solution.py:394
  16.3 5.6 %all-to-all-start = ((f32[4,64,128]{2,1,0:T(8,128)}), f32[4,64,128]{2,1,0:T(8,128)S(1)}, u32[]{:S(2)}, u32[]{:S(2)}) async-start(f32[4,64,128]{2,1,0:T(8,128)} %get-tuple-element.35), calls=%async_computation | async-start | bytes 262144 | tf_op jit(solution)/shard_map/all_to_all | solution.py:402
  22.0 2.0 %collective-permute-start.2 = (f32[200,128]{1,0:T(8,128)S(1)}, f32[200,128]{1,0:T(8,128)S(1)}, u32[]{:S(2)}, u32[]{:S(2)}) collective-permute-start(f32[200,128]{1,0:T(8,128)S(1)} %get-tuple-element.33), channel_id=1, source_target_pairs={{0,4},{4,8},{8,12},{12,0},{1,5},{5,9},{9,13},{13,1},{2,6},{6,10},{... | collective-permute-start | bytes 307208 | tf_op jit(solution)/shard_map/ppermute | solution.py:386
  24.0 1.8 %collective-permute-start.3 = (f32[200,128]{1,0:T(8,128)S(1)}, f32[200,128]{1,0:T(8,128)S(1)}, u32[]{:S(2)}, u32[]{:S(2)}) collective-permute-start(f32[200,128]{1,0:T(8,128)S(1)} %get-tuple-element.34), channel_id=1, source_target_pairs={{0,12},{4,0},{8,4},{12,8},{1,13},{5,1},{9,5},{13,9},{2,14},{6,2},{... | collective-permute-start | bytes 307208 | tf_op jit(solution)/shard_map/ppermute | solution.py:386
  25.8 5.8 %collective-permute-done.2.from_up = f32[200,128]{1,0:T(8,128)S(1)} collective-permute-done((f32[200,128]{1,0:T(8,128)S(1)}, f32[200,128]{1,0:T(8,128)S(1)}, u32[]{:S(2)}, u32[]{:S(2)}) %collective-permute-start.2) | collective-permute-done | bytes 102432 | tf_op jit(solution)/shard_map/ppermute | solution.py:386
  31.6 1.4 %collective-permute-done.3.from_down = f32[200,128]{1,0:T(8,128)S(1)} collective-permute-done((f32[200,128]{1,0:T(8,128)S(1)}, f32[200,128]{1,0:T(8,128)S(1)}, u32[]{:S(2)}, u32[]{:S(2)}) %collective-permute-start.3) | collective-permute-done | bytes 102432 | tf_op jit(solution)/shard_map/ppermute | solution.py:386
  33.0 0.0 all-to-all-done.got
  33.0 3.4 %steps.1 = (f32[3,16,16,128]{3,2,1,0:T(8,128)}, f32[2,8,16,128]{3,2,1,0:T(8,128)}) custom-call(f32[16]{0:T(128)S(1)} %get-tuple-element.19.speed, f32[3,16,16,128]{3,2,1,0:T(8,128)S(1)} %get-tuple-element.20.atm, f32[2,8,16,128]{3,2,1,0:T(8,128)S(1)} %get-tuple-element.21.ocean, f32[16,128]{1,0:T(8,128)S(1)} %get-tuple-element.22.depth, ...), custom_call_target="tpu_custom_call" | custom-call | tf_op jit(solution)/shard_map/steps/pallas_call | solution.py:405
Async XLA Ops:
  0.6 0.7 %copy-start.10 = (f32[16]{0:T(128)S(1)}, f32[16]{0:T(128)}, u32[]{:S(2)}) copy-start(f32[16]{0:T(128)} %refs_10_.1) | copy-start | bytes 196
  1.3 1.0 %copy-start = (f32[3,16,16,128]{3,2,1,0:T(8,128)S(1)}, f32[3,16,16,128]{3,2,1,0:T(8,128)}, u32[]{:S(2)}) copy-start(f32[3,16,16,128]{3,2,1,0:T(8,128)} %refs_0_.1) | copy-start | bytes 1179652
  2.3 0.9 %copy-start.1 = (f32[2,8,16,128]{3,2,1,0:T(8,128)S(1)}, f32[2,8,16,128]{3,2,1,0:T(8,128)}, u32[]{:S(2)}) copy-start(f32[2,8,16,128]{3,2,1,0:T(8,128)} %refs_1_.1) | copy-start | bytes 393220
  3.2 0.7 %copy-start.2 = (f32[16,128]{1,0:T(8,128)S(1)}, f32[16,128]{1,0:T(8,128)}, u32[]{:S(2)}) copy-start(f32[16,128]{1,0:T(8,128)} %refs_2_.1) | copy-start | bytes 24580
  3.9 0.7 %copy-start.3 = (s32[16,128]{1,0:T(8,128)S(1)}, s32[16,128]{1,0:T(8,128)}, u32[]{:S(2)}) copy-start(s32[16,128]{1,0:T(8,128)} %refs_3_.1) | copy-start | bytes 24580
  4.6 0.7 %copy-start.4 = (f32[16,128]{1,0:T(8,128)S(1)}, f32[16,128]{1,0:T(8,128)}, u32[]{:S(2)}) copy-start(f32[16,128]{1,0:T(8,128)} %refs_4_.1) | copy-start | bytes 24580
  5.3 0.7 %copy-start.5 = (f32[16,128]{1,0:T(8,128)S(1)}, f32[16,128]{1,0:T(8,128)}, u32[]{:S(2)}) copy-start(f32[16,128]{1,0:T(8,128)} %refs_5_.1) | copy-start | bytes 24580
  6.0 0.7 %copy-start.6 = (s32[1,1,2048]{2,1,0:T(1,128)S(1)}, s32[1,1,2048]{2,1,0:T(1,128)}, u32[]{:S(2)}) copy-start(s32[1,1,2048]{2,1,0:T(1,128)} %param.18) | copy-start | bytes 24580
  6.7 0.7 %copy-start.7 = (s32[1,1,2048,1]{2,3,1,0:T(1,128)S(1)}, s32[1,1,2048,1]{2,3,1,0:T(1,128)}, u32[]{:S(2)}) copy-start(s32[1,1,2048,1]{2,3,1,0:T(1,128)} %param.19) | copy-start | bytes 24580
  7.4 0.7 %copy-start.8 = (s32[1,1,2048]{2,1,0:T(1,128)S(1)}, s32[1,1,2048]{2,1,0:T(1,128)}, u32[]{:S(2)}) copy-start(s32[1,1,2048]{2,1,0:T(1,128)} %param.20) | copy-start | bytes 24580
  8.1 0.7 %copy-start.9 = (f32[1,1,2048]{2,1,0:T(1,128)S(1)}, f32[1,1,2048]{2,1,0:T(1,128)}, u32[]{:S(2)}) copy-start(f32[1,1,2048]{2,1,0:T(1,128)} %param.21) | copy-start | bytes 24580
  10.8 3.9 %collective-permute-start = (f32[16,256]{1,0:T(8,128)S(1)}, f32[16,256]{1,0:T(8,128)S(1)}, u32[]{:S(2)}, u32[]{:S(2)}) collective-permute-start(f32[16,256]{1,0:T(8,128)S(1)} %get-tuple-element.30), channel_id=1, source_target_pairs={{0,1},{1,2},{2,3},{3,0},{4,5},{5,6},{6,7},{7,4},{8,9},{9,10},{10,1... | collective-permute-start | bytes 49160 | tf_op jit(solution)/shard_map/ppermute | solution.py:386
  11.3 3.4 %collective-permute-start.1 = (f32[16,256]{1,0:T(8,128)S(1)}, f32[16,256]{1,0:T(8,128)S(1)}, u32[]{:S(2)}, u32[]{:S(2)}) collective-permute-start(f32[16,256]{1,0:T(8,128)S(1)} %get-tuple-element.31), channel_id=1, source_target_pairs={{0,3},{1,0},{2,1},{3,2},{4,7},{5,4},{6,5},{7,6},{8,11},{9,8},{10,9... | collective-permute-start | bytes 49160 | tf_op jit(solution)/shard_map/ppermute | solution.py:386
  16.3 16.6 %all-to-all-start = ((f32[4,64,128]{2,1,0:T(8,128)}), f32[4,64,128]{2,1,0:T(8,128)S(1)}, u32[]{:S(2)}, u32[]{:S(2)}) async-start(f32[4,64,128]{2,1,0:T(8,128)} %get-tuple-element.35), calls=%async_computation | async-start | bytes 262144 | tf_op jit(solution)/shard_map/all_to_all | solution.py:402
  22.0 9.6 %collective-permute-start.2 = (f32[200,128]{1,0:T(8,128)S(1)}, f32[200,128]{1,0:T(8,128)S(1)}, u32[]{:S(2)}, u32[]{:S(2)}) collective-permute-start(f32[200,128]{1,0:T(8,128)S(1)} %get-tuple-element.33), channel_id=1, source_target_pairs={{0,4},{4,8},{8,12},{12,0},{1,5},{5,9},{9,13},{13,1},{2,6},{6,10},{... | collective-permute-start | bytes 307208 | tf_op jit(solution)/shard_map/ppermute | solution.py:386
  24.0 9.0 %collective-permute-start.3 = (f32[200,128]{1,0:T(8,128)S(1)}, f32[200,128]{1,0:T(8,128)S(1)}, u32[]{:S(2)}, u32[]{:S(2)}) collective-permute-start(f32[200,128]{1,0:T(8,128)S(1)} %get-tuple-element.34), channel_id=1, source_target_pairs={{0,12},{4,0},{8,4},{12,8},{1,13},{5,1},{9,5},{13,9},{2,14},{6,2},{... | collective-permute-start | bytes 307208 | tf_op jit(solution)/shard_map/ppermute | solution.py:386

commit v3 on v2

--- a/solution.py
+++ b/solution.py
@@ -37,12 +37,11 @@
 
 
 def pack_kernel(*refs):
-    sources, rest = refs[:11], refs[11:]
-    atm, ocean, depth, wet, kappa = rest[:5]
-    up, down, left, right, sems = rest[11:]
+    sources, (up, down, left, right), held, sems = refs[:5], refs[5:9], refs[9:14], refs[14]
+    atm, ocean, depth, wet, kappa = held
     copies = [
         pltpu.make_async_copy(source, target, sems.at[i])
-        for i, (source, target) in enumerate(zip(sources, rest[:11]))
+        for i, (source, target) in enumerate(zip(sources, held))
     ]
     for copy in copies:
         copy.start()
@@ -136,7 +135,17 @@
     return out
 
 
-def send_kernel(air, ocean, atm_cell, dest, sea_cell, weight, from_left, from_right, message, wair_out):
+def send_kernel(*refs):
+    sources, (message, wair_out), held, sems = refs[:8], refs[8:10], refs[10:18], refs[18]
+    air, surface, atm_cell, dest, sea_cell, weight, from_left, from_right = held
+    copies = [
+        pltpu.make_async_copy(source.at[0, 0] if i == 1 else source, target, sems.at[i])
+        for i, (source, target) in enumerate(zip(sources, held))
+    ]
+    for copy in copies:
+        copy.start()
+    for copy in copies:
+        copy.wait()
     rows, cols = air.shape
     tiles = message.shape[0]
     tile_lanes = from_left.shape[1] // cols
@@ -149,12 +158,11 @@
     cell = sea_cell[...]
     hot_sea = jnp.where(one_hot(cell % cols, cols), 1.0, 0.0).astype(BF16)
     row = dest[...] * rows + cell // cols
-    surface = ocean[0, 0]
     for tile in range(tiles):
         s1, s2 = scatter_rows([wair, w], one_hot(row - tile * rows, rows), hot_sea)
         message[tile, 0:rows, :] = s1
         message[tile, rows : 2 * rows, :] = s2
-        message[tile, 2 * rows : 3 * rows, :] = surface
+        message[tile, 2 * rows : 3 * rows, :] = surface[...]
         message[tile, 3 * rows :, :] = jnp.zeros((message.shape[1] - 3 * rows, cols), F32)
     me = lax.axis_index("tile")
     above, below = lax.rem(me + tiles - 1, tiles), lax.rem(me + 1, tiles)
@@ -167,22 +175,62 @@
             at += AH
 
 
+def strips(cols, slot, width, left_part, right_part):
+    low_half = lax.broadcasted_iota(jnp.int32, (1, cols), 1) < cols // 2
+    offset = slot % cols
+    a, b = right_part(slot // cols), left_part(slot // cols)
+    if offset:
+        a = pltpu.roll(a, cols - offset, 1)
+    turn = (cols - width - offset) % cols
+    if turn:
+        b = pltpu.roll(b, turn, 1)
+    return jnp.where(low_half, a, b)
+
+
+def extend_kernel(atm, ocean, depth, wet, kappa, from_up, from_down, from_left, from_right, us, vs, hs, fs, ms):
+    levels = atm.shape[1]
+    rows, cols = atm.shape[2:]
+    tracers = ocean.shape[0] * ocean.shape[1]
+    each = ocean.shape[1]
+    per, obase, mbase, _ = row_slots(levels, tracers)
+    slots, _ = lane_slots(levels, tracers)
+    full = rows + 2 * AH
+
+    def side(ref):
+        return lambda i: ref[:, i * cols : (i + 1) * cols]
+
+    def extend(view, value, row_at, row_width, slot, width):
+        view[0:rows, 0:cols] = value
+        view[rows : rows + row_width, 0:cols] = from_down[row_at : row_at + row_width, :]
+        view[full - row_width : full, 0:cols] = from_up[row_at : row_at + row_width, :]
+        view[0:rows, cols : 2 * cols] = strips(cols, slot, width, side(from_left), side(from_right))
+
+    base = 3 * levels + tracers
+    extend(ms.at[0], depth[...], mbase, AH, slots[base], AH)
+    extend(ms.at[1], wet[...].astype(F32), mbase + AH, OH, slots[base + 1], AH)
+    extend(ms.at[2], kappa[...], mbase + AH + OH, OH, slots[base + 2], AH)
+    for i in range(tracers):
+        extend(fs.at[i], ocean[i // each, i % each], obase + OH * i, OH, slots[3 * levels + i], OH)
+    for level in range(levels):
+        at = per * level
+        extend(us.at[level], atm[0, level], at + AH, AH - 1, slots[level], AH)
+        extend(vs.at[level], atm[1, level], at, AH, slots[levels + level], AH)
+        extend(hs.at[level], atm[2, level], at + 2 * AH - 1, AH - 1, slots[2 * levels + level], AH)
+
+
 def final_kernel(
     speed,
-    atm,
+    us_in,
+    vs_in,
+    hs_in,
+    fs_in,
+    ms_in,
     ocean,
-    depth,
-    wet,
-    kappa,
     atm_cell,
     dest,
     sea_cell,
     weight,
     wair,
-    from_up,
-    from_down,
-    from_left,
-    from_right,
     got,
     atm_out,
     ocean_out,
@@ -190,22 +238,20 @@
     vs,
     hs,
     fs,
-    ms,
+    edge,
     atm_buf,
     ocean_buf,
     sems,
 ):
-    levels = atm.shape[1]
-    rows, cols = atm.shape[2:]
-    tracers = ocean.shape[0] * ocean.shape[1]
+    levels = us.shape[0]
+    rows, cols = ocean.shape[2:]
+    tracers = fs.shape[0]
     each = ocean.shape[1]
-    per, obase, mbase, _ = row_slots(levels, tracers)
     slots, lanes = lane_slots(levels, tracers)
     full = rows + 2 * AH
     tiles = got.shape[0]
     me = lax.axis_index("tile")
     above, below = lax.rem(me + tiles - 1, tiles), lax.rem(me + 1, tiles)
-    low_half = lax.broadcasted_iota(jnp.int32, (1, cols), 1) < cols // 2
 
     surface = ocean[0, 0]
     s1, s2 = got[0, 0:rows, :], got[0, rows : 2 * rows, :]
@@ -225,30 +271,16 @@
     hot_atm = jnp.where(one_hot(cell % cols, cols), 1.0, 0.0).astype(BF16)
     (atm_flux,) = scatter_rows([flux], one_hot(cell // cols, rows), hot_atm)
 
-    def strips(slot, width, left_part, right_part):
-        offset = slot % cols
-        a, b = right_part(slot // cols), left_part(slot // cols)
-        if offset:
-            a = pltpu.roll(a, cols - offset, 1)
-        turn = (cols - width - offset) % cols
-        if turn:
-            b = pltpu.roll(b, turn, 1)
-        return jnp.where(low_half, a, b)
-
-    def side(ref):
-        return lambda i: ref[:, i * cols : (i + 1) * cols]
-
-    def corner(tile, which):
-        base = 3 * rows + which * AH * (lanes // cols)
-        return lambda i: got[tile, base + AH * i : base + AH * (i + 1), :]
-
-    def extend(view, value, row_at, row_width, slot, width):
-        view[0:rows, 0:cols] = value
-        view[rows : rows + row_width, 0:cols] = from_down[row_at : row_at + row_width, :]
-        view[full - row_width : full, 0:cols] = from_up[row_at : row_at + row_width, :]
-        view[0:rows, cols : 2 * cols] = strips(slot, width, side(from_left), side(from_right))
-        view[rows : rows + AH, cols : 2 * cols] = strips(slot, width, corner(below, 0), corner(below, 1))
-        view[full - AH : full, cols : 2 * cols] = strips(slot, width, corner(above, 0), corner(above, 1))
+    for i in range(2 * (lanes // cols)):
+        at = 3 * rows + AH * i
+        edge[i, 0:AH, :] = got[below, at : at + AH, :]
+        edge[i, AH : 2 * AH, :] = got[above, at : at + AH, :]
+    half = lanes // cols
+
+    def load(ref, i, slot, width):
+        corner = strips(cols, slot, width, lambda t: edge[t], lambda t: edge[half + t])
+        outer = jnp.concatenate([ref[i, rows:full, 0:cols], corner], axis=1)
+        return jnp.concatenate([ref[i, 0:rows, :], outer], axis=0)
 
     def east(f):
         return pltpu.roll(f, 2 * cols - 1, 1)
@@ -263,23 +295,12 @@
         return pltpu.roll(f, 1, 0)
 
     base = 3 * levels + tracers
-    extend(ms.at[0], depth[...], mbase, AH, slots[base], AH)
-    extend(ms.at[1], wet[...].astype(F32), mbase + AH, OH, slots[base + 1], AH)
-    extend(ms.at[2], kappa[...], mbase + AH + OH, OH, slots[base + 2], AH)
-    for i in range(tracers):
-        extend(fs.at[i], ocean[i // each, i % each], obase + OH * i, OH, slots[3 * levels + i], OH)
-    for level in range(levels):
-        at = per * level
-        extend(us.at[level], atm[0, level], at + AH, AH - 1, slots[level], AH)
-        extend(vs.at[level], atm[1, level], at, AH, slots[levels + level], AH)
-        extend(hs.at[level], atm[2, level], at + 2 * AH - 1, AH - 1, slots[2 * levels + level], AH)
-
-    w = ms[1]
-    k = ms[2]
+    w = load(ms_in, 1, slots[base + 1], AH)
+    k = load(ms_in, 2, slots[base + 2], AH)
     we, ww, ws, wn = east(w), west(w), south(w), north(w)
     for step in range(OCEAN_STEPS):
         for i in range(tracers):
-            f = fs[i]
+            f = load(fs_in, i, slots[3 * levels + i], OH) if step == 0 else fs[i]
             total = we * (east(f) - f)
             total = total + ww * (west(f) - f)
             total = total + ws * (south(f) - f)
@@ -293,15 +314,19 @@
     copies = [pltpu.make_async_copy(ocean_buf, ocean_out, sems.at[0])]
     copies[0].start()
 
-    d = ms[0]
+    d = load(ms_in, 0, slots[base], AH)
     chunk = max(1, levels // 4)
     for step in range(ACOUSTIC):
         for level in range(levels):
-            u, v = us[level], vs[level]
+            if step == 0:
+                u = load(us_in, level, slots[level], AH)
+                v = load(vs_in, level, slots[levels + level], AH)
+                h = load(hs_in, level, slots[2 * levels + level], AH)
+                us[level], vs[level] = u, v
+            else:
+                u, v, h = us[level], vs[level], hs[level]
             column_speed = speed[level] * d
-            hs[level] = hs[level] - column_speed * (
-                (east(u) - west(u)) * 0.5 + (south(v) - north(v)) * 0.5
-            )
+            hs[level] = h - column_speed * ((east(u) - west(u)) * 0.5 + (south(v) - north(v)) * 0.5)
         for level in range(levels):
             u, v, h = us[level], vs[level], hs[level]
             u = u - (east(h) - west(h)) * 0.5
@@ -348,36 +373,27 @@
     vmem = pl.BlockSpec(memory_space=pltpu.VMEM)
     hbm = pl.BlockSpec(memory_space=pltpu.HBM)
     smem = pl.BlockSpec(memory_space=pltpu.SMEM)
-    params = pltpu.CompilerParams(vmem_limit_bytes=32 * 1024 * 1024)
+    params = pltpu.CompilerParams(vmem_limit_bytes=16 * 1024 * 1024)
+    whole = pltpu.CompilerParams(vmem_limit_bytes=64 * 1024 * 1024)
     full = rows + 2 * AH
 
     def shape(*dims):
         return jax.ShapeDtypeStruct(dims, F32)
 
-    operands = (
-        atm_state,
-        ocean_state,
-        depth,
-        wet_mask,
-        diffusivity,
-        air_temp,
-        xg_atm_cell.reshape(1, cells),
-        xg_dest.reshape(1, cells),
-        xg_ocean_cell.reshape(1, cells),
-        xg_weight.reshape(1, cells),
-        wave_speed,
-    )
-    atm, ocean, dep, wet, kappa, air, atm_cell, dest, sea_cell, weight, speed, up, down, left, right = pl.pallas_call(
+    fields = (atm_state, ocean_state, depth, wet_mask, diffusivity)
+    up, down, left, right = pl.pallas_call(
         pack_kernel,
-        out_shape=[jax.ShapeDtypeStruct(x.shape, x.dtype) for x in operands]
-        + [shape(message_rows, cols)] * 2
-        + [shape(rows, lanes)] * 2,
-        in_specs=[hbm] * 11,
-        out_specs=[vmem] * 10 + [smem] + [vmem] * 4,
-        scratch_shapes=[pltpu.SemaphoreType.DMA((11,))],
-        compiler_params=params,
+        out_shape=[shape(message_rows, cols)] * 2 + [shape(rows, lanes)] * 2,
+        in_specs=[hbm] * 5,
+        out_specs=[vmem] * 4,
+        scratch_shapes=[pltpu.VMEM(x.shape, x.dtype) for x in fields] + [pltpu.SemaphoreType.DMA((5,))],
+        compiler_params=whole,
         name="pack",
-    )(*operands)
+    )(*fields)
+    atm_cell = xg_atm_cell.reshape(1, cells)
+    dest = xg_dest.reshape(1, cells)
+    sea_cell = xg_ocean_cell.reshape(1, cells)
+    weight = xg_weight.reshape(1, cells)
 
     column_axes = ("sub", "comp")
     column_count = lax.axis_size("sub") * lax.axis_size("comp")
@@ -394,48 +410,46 @@
     message, wair = pl.pallas_call(
         send_kernel,
         out_shape=[shape(tile_count, 3 * rows + corner_rows, cols), shape(1, cells)],
-        in_specs=[vmem] * 8,
+        in_specs=[hbm] * 8,
         out_specs=[vmem] * 2,
+        scratch_shapes=[pltpu.VMEM((rows, cols), F32)] * 2
+        + [pltpu.VMEM((1, cells), jnp.int32)] * 3
+        + [pltpu.VMEM((1, cells), F32)]
+        + [pltpu.VMEM((rows, lanes), F32)] * 2
+        + [pltpu.SemaphoreType.DMA((8,))],
+        compiler_params=whole,
+        cost_estimate=pl.CostEstimate(flops=0, bytes_accessed=20_000_000, transcendentals=0),
+        name="exchange_send",
+    )(air_temp, ocean_state, atm_cell, dest, sea_cell, weight, from_left, from_right)
+    got = lax.all_to_all(message, "tile", split_axis=0, concat_axis=0, tiled=True)
+
+    extended = [shape(levels, full, 2 * cols)] * 3 + [shape(tracers, full, 2 * cols), shape(3, full, 2 * cols)]
+    us, vs, hs, fs, ms = pl.pallas_call(
+        extend_kernel,
+        out_shape=extended,
+        in_specs=[vmem] * 9,
+        out_specs=[vmem] * 5,
         compiler_params=params,
-        name="exchange_send",
-    )(air, ocean, atm_cell, dest, sea_cell, weight, from_left, from_right)
-    got = lax.all_to_all(message, "tile", split_axis=0, concat_axis=0, tiled=True)
-
-    return tuple(
-        pl.pallas_call(
-            final_kernel,
-            out_shape=[shape(*atm_state.shape), shape(*ocean_state.shape)],
-            in_specs=[smem] + [vmem] * 15,
-            out_specs=[hbm] * 2,
-            scratch_shapes=[pltpu.VMEM((levels, full, 2 * cols), F32)] * 3
-            + [
-                pltpu.VMEM((tracers, full, 2 * cols), F32),
-                pltpu.VMEM((3, full, 2 * cols), F32),
-                pltpu.VMEM(atm_state.shape, F32),
-                pltpu.VMEM(ocean_state.shape, F32),
-                pltpu.SemaphoreType.DMA((8,)),
-            ],
-            compiler_params=params,
-            name="steps",
-        )(
-            speed,
-            atm,
-            ocean,
-            dep,
-            wet,
-            kappa,
-            atm_cell,
-            dest,
-            sea_cell,
-            weight,
-            wair,
-            from_up,
-            from_down,
-            from_left,
-            from_right,
-            got,
-        )
-    )
+        cost_estimate=pl.CostEstimate(flops=0, bytes_accessed=8_000_000, transcendentals=0),
+        name="extend",
+    )(*fields, from_up, from_down, from_left, from_right)
+
+    results = pl.pallas_call(
+        final_kernel,
+        out_shape=[shape(*atm_state.shape), shape(*ocean_state.shape)],
+        in_specs=[smem] + [vmem] * 12,
+        out_specs=[hbm] * 2,
+        scratch_shapes=[pltpu.VMEM(x.shape, F32) for x in extended[:4]]
+        + [
+            pltpu.VMEM((2 * (lanes // cols), 2 * AH, cols), F32),
+            pltpu.VMEM(atm_state.shape, F32),
+            pltpu.VMEM(ocean_state.shape, F32),
+            pltpu.SemaphoreType.DMA((8,)),
+        ],
+        compiler_params=params,
+        name="steps",
+    )(wave_speed, us, vs, hs, fs, ms, ocean_state, atm_cell, dest, sea_cell, weight, wair, got)
+    return tuple(results)
 
 
 def solution(mesh):

time: 37 us -> 34 us (0.919)
  local copies, waits for them, and re-layouts: 8.12 us -> 1.67 us
  Pallas kernels: 7.05 us -> 10.1 us
    unnamed x22 -> x24, local copies, waits for them, and re-layouts: 8.12 us -> 1.67 us
    pallas_call x1 -> x2, Pallas kernels: 2.06 us -> 3.24 us  [the longest x1 2.04 us: on_device(): pl.pallas_call(pack_kernel, out_shape=[shape(message_rows, cols)] * 2 + [...]
    pallas_call x1, Pallas kernels: 3.42 us -> 4.36 us  [on_device(): pl.pallas_call(final_kernel, out_shape=[shape(*atm_state.shape), shape(*o...]
    pallas_call x1, Pallas kernels: 1.57 us -> 2.48 us  [on_device(): pl.pallas_call(send_kernel, out_shape=[shape(tile_count, 3 * rows + corne...]
  transfers between devices with their start and end apart: 5 -> 5, of which waited for: 4 -> 3; matrix products, arithmetic and copies ran while one was open for 0% -> 0% of each run, Pallas kernels for 0% -> 4%
where the time goes in v3:
time: 34 us; the launch traced here: 33.6 us
  starting transfers between devices  12.2 us (36%)
  Pallas kernels  10.1 us (30%)
  waiting for transfers between devices  8.86 us (26%)
  local copies, waits for them, and re-layouts  1.67 us (5%)
  between operations  0.78 us (2%)
    ppermute x4, waiting for transfers between devices, shift(): lax.ppermute(value, axes, [(i, (i + by) % count) for i in range(count)])  8.86 us
    ppermute x4, starting transfers between devices, shift(): lax.ppermute(value, axes, [(i, (i + by) % count) for i in range(count)])  6.35 us
    all_to_all x1, starting transfers between devices, on_device(): lax.all_to_all(message, 'tile', split_axis=0, concat_axis=0, tiled=True)  5.82 us
    pallas_call x1, Pallas kernels, on_device(): pl.pallas_call(final_kernel, out_shape=[shape(*atm_state.shape), shape(*o...  4.36 us
    pallas_call x1, Pallas kernels, on_device(): pl.pallas_call(send_kernel, out_shape=[shape(tile_count, 3 * rows + corne...  2.48 us
    pallas_call x1, Pallas kernels, on_device(): pl.pallas_call(pack_kernel, out_shape=[shape(message_rows, cols)] * 2 + [...  2.04 us
    unnamed x24, local copies, waits for them, and re-layouts  1.67 us
    pallas_call x1, Pallas kernels, on_device(): pl.pallas_call(extend_kernel, out_shape=extended, in_specs=[vmem] * 9, ou...  1.21 us
  transfers between devices with their start and end apart: 5, of which 3 were waited for; matrix products, arithmetic and copies ran while one was open for 0% of the time, Pallas kernels for 4%

profile of v3, /device:TPU:0, one launch (start us, length us, event | category | flops | bytes accessed | tf_op | source)
XLA Modules:
  0.0 33.6 jit_solution(13636948899906013573)
XLA Ops:
  0.6 2.0 %pack.1 = (f32[200,128]{1,0:T(8,128)}, f32[200,128]{1,0:T(8,128)}, f32[16,256]{1,0:T(8,128)}, f32[16,256]{1,0:T(8,128)}) custom-call(f32[3,16,16,128]{3,2,1,0:T(8,128)} %atm.1, f32[2,8,16,128]{3,2,1,0:T(8,128)} %ocean.3, f32[16,128]{1,0:T(8,128)} %depth.1, s32[16,128]{1,0:T(8,128)} %wet.1, f32[16,128]{1,0:T(8,128)} %kappa.1), custom_call_target="tpu_custom_call" | custom-call | tf_op jit(solution)/shard_map/pack/pallas_call | solution.py:384
  2.7 0.5 %collective-permute-start.2 = (f32[16,256]{1,0:T(8,128)}, f32[16,256]{1,0:T(8,128)}, u32[]{:S(2)}, u32[]{:S(2)}) collective-permute-start(f32[16,256]{1,0:T(8,128)} %get-tuple-element.15), channel_id=1, source_target_pairs={{0,1},{1,2},{2,3},{3,0},{4,5},{5,6},{6,7},{7,4},{8,9},{9,10},{10,1... | collective-permute-start | bytes 49160 | tf_op jit(solution)/shard_map/ppermute | solution.py:402
  3.2 2.0 %collective-permute-start.3 = (f32[16,256]{1,0:T(8,128)}, f32[16,256]{1,0:T(8,128)}, u32[]{:S(2)}, u32[]{:S(2)}) collective-permute-start(f32[16,256]{1,0:T(8,128)} %get-tuple-element.16), channel_id=1, source_target_pairs={{0,3},{1,0},{2,1},{3,2},{4,7},{5,4},{6,5},{7,6},{8,11},{9,8},{10,9... | collective-permute-start | bytes 49160 | tf_op jit(solution)/shard_map/ppermute | solution.py:402
  5.2 1.7 %collective-permute-done.2.from_left.refs_6_ = f32[16,256]{1,0:T(8,128)} collective-permute-done((f32[16,256]{1,0:T(8,128)}, f32[16,256]{1,0:T(8,128)}, u32[]{:S(2)}, u32[]{:S(2)}) %collective-permute-start.2) | collective-permute-done | bytes 16416 | tf_op jit(solution)/shard_map/ppermute | solution.py:402
  6.8 0.0 collective-permute-done.3.from_right.refs_7_
  6.8 2.5 %exchange_send.1 = (f32[4,64,128]{2,1,0:T(8,128)}, f32[1,2048]{1,0:T(1,128)}) custom-call(f32[16,128]{1,0:T(8,128)} %refs_0_.3, f32[2,8,16,128]{3,2,1,0:T(8,128)} %ocean.3, s32[1,2048]{1,0:T(1,128)} %bitcast.4, s32[1,2048]{1,0:T(1,128)} %bitcast.6, s32[1,2048]{1,0:T(1,128)} %bitcast.8, f32[1,2048]{1,0:T(1,128)} %bitcast.10, ...), custom_call_target="tpu_custom_call" | custom-call | bytes 20000000 | tf_op jit(solution)/shard_map/exchange_send/pallas_call | solution.py:410
  9.3 0.0 copy-start.11
  9.3 0.0 copy-start
  9.4 0.0 copy-start.2
  9.4 0.0 copy-start.3
  9.4 0.0 copy-start.4
  9.4 5.8 %all-to-all-start = ((f32[4,64,128]{2,1,0:T(8,128)}), f32[4,64,128]{2,1,0:T(8,128)S(1)}, u32[]{:S(2)}, u32[]{:S(2)}) async-start(f32[4,64,128]{2,1,0:T(8,128)} %get-tuple-element.23), calls=%async_computation | async-start | bytes 262144 | tf_op jit(solution)/shard_map/all_to_all | solution.py:424
  15.2 2.0 %collective-permute-start = (f32[200,128]{1,0:T(8,128)}, f32[200,128]{1,0:T(8,128)S(1)}, u32[]{:S(2)}, u32[]{:S(2)}) collective-permute-start(f32[200,128]{1,0:T(8,128)} %get-tuple-element.13), channel_id=1, source_target_pairs={{0,4},{4,8},{8,12},{12,0},{1,5},{5,9},{9,13},{13,1},{2,6},{6,10},{... | collective-permute-start | bytes 307208 | tf_op jit(solution)/shard_map/ppermute | solution.py:402
  17.2 0.0 copy-done.11
  17.2 1.8 %collective-permute-start.1 = (f32[200,128]{1,0:T(8,128)S(1)}, f32[200,128]{1,0:T(8,128)S(1)}, u32[]{:S(2)}, u32[]{:S(2)}) collective-permute-start(f32[200,128]{1,0:T(8,128)S(1)} %copy-done.11), channel_id=1, source_target_pairs={{0,12},{4,0},{8,4},{12,8},{1,13},{5,1},{9,5},{13,9},{2,14},{6,2},{... | collective-permute-start | bytes 307208 | tf_op jit(solution)/shard_map/ppermute | solution.py:402
  19.1 5.8 %collective-permute-done.from_up = f32[200,128]{1,0:T(8,128)S(1)} collective-permute-done((f32[200,128]{1,0:T(8,128)}, f32[200,128]{1,0:T(8,128)S(1)}, u32[]{:S(2)}, u32[]{:S(2)}) %collective-permute-start) | collective-permute-done | bytes 102432 | tf_op jit(solution)/shard_map/ppermute | solution.py:402
  24.9 1.4 %collective-permute-done.1.from_down = f32[200,128]{1,0:T(8,128)S(1)} collective-permute-done((f32[200,128]{1,0:T(8,128)S(1)}, f32[200,128]{1,0:T(8,128)S(1)}, u32[]{:S(2)}, u32[]{:S(2)}) %collective-permute-start.1) | collective-permute-done | bytes 102432 | tf_op jit(solution)/shard_map/ppermute | solution.py:402
  26.3 0.0 copy-done
  26.3 0.0 copy-done.2
  26.3 0.0 copy-done.3
  26.3 0.0 copy-done.4
  26.3 0.0 copy-start.1
  26.3 1.0 %copy-done.1 = f32[3,16,16,128]{3,2,1,0:T(8,128)S(1)} copy-done((f32[3,16,16,128]{3,2,1,0:T(8,128)S(1)}, f32[3,16,16,128]{3,2,1,0:T(8,128)}, u32[]{:S(2)}) %copy-start.1) | copy-done | bytes 393240
  27.3 0.0 copy-start.6
  27.3 0.0 copy-start.7
  27.3 0.0 copy-start.8
  27.3 0.0 copy-start.9
  27.3 1.2 %extend.1 = (f32[16,24,256]{2,1,0:T(8,128)S(1)}, f32[16,24,256]{2,1,0:T(8,128)S(1)}, f32[16,24,256]{2,1,0:T(8,128)S(1)}, f32[16,24,256]{2,1,0:T(8,128)S(1)}, f32[3,24,256]{2,1,0:T(8,128)S(1)}) custom-call(f32[3,16,16,128]{3,2,1,0:T(8,128)S(1)} %copy-done.1, f32[2,8,16,128]{3,2,1,0:T(8,128)S(1)} %copy-done, f32[16,128]{1,0:T(8,128)S(1)} %copy-done.2, ...), custom_call_target="tpu_custom_call" | custom-call | bytes 8000000 | tf_op jit(solution)/shard_map/extend/pallas_call | solution.py:427
  28.5 0.0 copy-start.5
  28.5 0.0 all-to-all-done.got
  28.5 0.0 copy-start.10
  28.5 0.0 copy-done.6
  28.5 0.0 copy-done.7
  28.6 0.0 copy-done.8
  28.6 0.0 copy-done.9
  28.6 0.6 %copy-done.5 = s32[1,1,2048]{2,1,0:T(1,128)S(1)} copy-done((s32[1,1,2048]{2,1,0:T(1,128)S(1)}, s32[1,1,2048]{2,1,0:T(1,128)}, u32[]{:S(2)}) %copy-start.5) | copy-done | bytes 8216
  29.2 0.0 copy-done.10
  29.2 4.4 %steps.1 = (f32[3,16,16,128]{3,2,1,0:T(8,128)}, f32[2,8,16,128]{3,2,1,0:T(8,128)}) custom-call(f32[16]{0:T(128)S(1)} %copy-done.10, f32[16,24,256]{2,1,0:T(8,128)S(1)} %get-tuple-element.17.us_in, f32[16,24,256]{2,1,0:T(8,128)S(1)} %get-tuple-element.18.vs_in, f32[16,24,256]{2,1,0:T(8,128)S(1)} %get-tuple-element.19.hs_in, ...), custom_call_target="tpu_custom_call" | custom-call | tf_op jit(solution)/shard_map/steps/pallas_call | solution.py:437
Async XLA Ops:
  2.7 4.2 %collective-permute-start.2 = (f32[16,256]{1,0:T(8,128)}, f32[16,256]{1,0:T(8,128)}, u32[]{:S(2)}, u32[]{:S(2)}) collective-permute-start(f32[16,256]{1,0:T(8,128)} %get-tuple-element.15), channel_id=1, source_target_pairs={{0,1},{1,2},{2,3},{3,0},{4,5},{5,6},{6,7},{7,4},{8,9},{9,10},{10,1... | collective-permute-start | bytes 49160 | tf_op jit(solution)/shard_map/ppermute | solution.py:402
  3.2 3.7 %collective-permute-start.3 = (f32[16,256]{1,0:T(8,128)}, f32[16,256]{1,0:T(8,128)}, u32[]{:S(2)}, u32[]{:S(2)}) collective-permute-start(f32[16,256]{1,0:T(8,128)} %get-tuple-element.16), channel_id=1, source_target_pairs={{0,3},{1,0},{2,1},{3,2},{4,7},{5,4},{6,5},{7,6},{8,11},{9,8},{10,9... | collective-permute-start | bytes 49160 | tf_op jit(solution)/shard_map/ppermute | solution.py:402
  9.3 7.9 %copy-start.11 = (f32[200,128]{1,0:T(8,128)S(1)}, f32[200,128]{1,0:T(8,128)}, u32[]{:S(2)}) copy-start(f32[200,128]{1,0:T(8,128)} %get-tuple-element.14) | copy-start | bytes 307204
  9.3 16.9 %copy-start = (f32[2,8,16,128]{3,2,1,0:T(8,128)S(1)}, f32[2,8,16,128]{3,2,1,0:T(8,128)}, u32[]{:S(2)}) copy-start(f32[2,8,16,128]{3,2,1,0:T(8,128)} %ocean.3) | copy-start | bytes 393220
  9.4 16.9 %copy-start.2 = (f32[16,128]{1,0:T(8,128)S(1)}, f32[16,128]{1,0:T(8,128)}, u32[]{:S(2)}) copy-start(f32[16,128]{1,0:T(8,128)} %depth.1) | copy-start | bytes 24580
  9.4 16.9 %copy-start.3 = (s32[16,128]{1,0:T(8,128)S(1)}, s32[16,128]{1,0:T(8,128)}, u32[]{:S(2)}) copy-start(s32[16,128]{1,0:T(8,128)} %wet.1) | copy-start | bytes 24580
  9.4 16.9 %copy-start.4 = (f32[16,128]{1,0:T(8,128)S(1)}, f32[16,128]{1,0:T(8,128)}, u32[]{:S(2)}) copy-start(f32[16,128]{1,0:T(8,128)} %kappa.1) | copy-start | bytes 24580
  9.4 19.1 %all-to-all-start = ((f32[4,64,128]{2,1,0:T(8,128)}), f32[4,64,128]{2,1,0:T(8,128)S(1)}, u32[]{:S(2)}, u32[]{:S(2)}) async-start(f32[4,64,128]{2,1,0:T(8,128)} %get-tuple-element.23), calls=%async_computation | async-start | bytes 262144 | tf_op jit(solution)/shard_map/all_to_all | solution.py:424
  15.2 9.7 %collective-permute-start = (f32[200,128]{1,0:T(8,128)}, f32[200,128]{1,0:T(8,128)S(1)}, u32[]{:S(2)}, u32[]{:S(2)}) collective-permute-start(f32[200,128]{1,0:T(8,128)} %get-tuple-element.13), channel_id=1, source_target_pairs={{0,4},{4,8},{8,12},{12,0},{1,5},{5,9},{9,13},{13,1},{2,6},{6,10},{... | collective-permute-start | bytes 307208 | tf_op jit(solution)/shard_map/ppermute | solution.py:402
  17.2 9.0 %collective-permute-start.1 = (f32[200,128]{1,0:T(8,128)S(1)}, f32[200,128]{1,0:T(8,128)S(1)}, u32[]{:S(2)}, u32[]{:S(2)}) collective-permute-start(f32[200,128]{1,0:T(8,128)S(1)} %copy-done.11), channel_id=1, source_target_pairs={{0,12},{4,0},{8,4},{12,8},{1,13},{5,1},{9,5},{13,9},{2,14},{6,2},{... | collective-permute-start | bytes 307208 | tf_op jit(solution)/shard_map/ppermute | solution.py:402
  26.3 1.0 %copy-start.1 = (f32[3,16,16,128]{3,2,1,0:T(8,128)S(1)}, f32[3,16,16,128]{3,2,1,0:T(8,128)}, u32[]{:S(2)}) copy-start(f32[3,16,16,128]{3,2,1,0:T(8,128)} %atm.1) | copy-start | bytes 1179652
  27.3 1.3 %copy-start.6 = (s32[1,1,2048,1]{2,3,1,0:T(1,128)S(1)}, s32[1,1,2048,1]{2,3,1,0:T(1,128)}, u32[]{:S(2)}) copy-start(s32[1,1,2048,1]{2,3,1,0:T(1,128)} %param.19) | copy-start | bytes 24580
  27.3 1.3 %copy-start.7 = (s32[1,1,2048]{2,1,0:T(1,128)S(1)}, s32[1,1,2048]{2,1,0:T(1,128)}, u32[]{:S(2)}) copy-start(s32[1,1,2048]{2,1,0:T(1,128)} %param.20) | copy-start | bytes 24580
  27.3 1.3 %copy-start.8 = (f32[1,1,2048]{2,1,0:T(1,128)S(1)}, f32[1,1,2048]{2,1,0:T(1,128)}, u32[]{:S(2)}) copy-start(f32[1,1,2048]{2,1,0:T(1,128)} %param.21) | copy-start | bytes 24580
  27.3 1.3 %copy-start.9 = (f32[1,2048]{1,0:T(1,128)S(1)}, f32[1,2048]{1,0:T(1,128)}, u32[]{:S(2)}) copy-start(f32[1,2048]{1,0:T(1,128)} %get-tuple-element.22.wair) | copy-start | bytes 24580
  28.5 0.7 %copy-start.5 = (s32[1,1,2048]{2,1,0:T(1,128)S(1)}, s32[1,1,2048]{2,1,0:T(1,128)}, u32[]{:S(2)}) copy-start(s32[1,1,2048]{2,1,0:T(1,128)} %param.18) | copy-start | bytes 24580
  28.5 0.7 %copy-start.10 = (f32[16]{0:T(128)S(1)}, f32[16]{0:T(128)}, u32[]{:S(2)}) copy-start(f32[16]{0:T(128)} %speed.1) | copy-start | bytes 196

commit v4 on v3

--- a/solution.py
+++ b/solution.py
@@ -187,50 +187,36 @@
     return jnp.where(low_half, a, b)
 
 
-def extend_kernel(atm, ocean, depth, wet, kappa, from_up, from_down, from_left, from_right, us, vs, hs, fs, ms):
-    levels = atm.shape[1]
-    rows, cols = atm.shape[2:]
-    tracers = ocean.shape[0] * ocean.shape[1]
-    each = ocean.shape[1]
+def row_slices(levels, tracers):
     per, obase, mbase, _ = row_slots(levels, tracers)
-    slots, _ = lane_slots(levels, tracers)
-    full = rows + 2 * AH
-
-    def side(ref):
-        return lambda i: ref[:, i * cols : (i + 1) * cols]
-
-    def extend(view, value, row_at, row_width, slot, width):
-        view[0:rows, 0:cols] = value
-        view[rows : rows + row_width, 0:cols] = from_down[row_at : row_at + row_width, :]
-        view[full - row_width : full, 0:cols] = from_up[row_at : row_at + row_width, :]
-        view[0:rows, cols : 2 * cols] = strips(cols, slot, width, side(from_left), side(from_right))
-
-    base = 3 * levels + tracers
-    extend(ms.at[0], depth[...], mbase, AH, slots[base], AH)
-    extend(ms.at[1], wet[...].astype(F32), mbase + AH, OH, slots[base + 1], AH)
-    extend(ms.at[2], kappa[...], mbase + AH + OH, OH, slots[base + 2], AH)
-    for i in range(tracers):
-        extend(fs.at[i], ocean[i // each, i % each], obase + OH * i, OH, slots[3 * levels + i], OH)
-    for level in range(levels):
-        at = per * level
-        extend(us.at[level], atm[0, level], at + AH, AH - 1, slots[level], AH)
-        extend(vs.at[level], atm[1, level], at, AH, slots[levels + level], AH)
-        extend(hs.at[level], atm[2, level], at + 2 * AH - 1, AH - 1, slots[2 * levels + level], AH)
+    out = [(per * level + AH, AH - 1) for level in range(levels)]
+    out += [(per * level, AH) for level in range(levels)]
+    out += [(per * level + 2 * AH - 1, AH - 1) for level in range(levels)]
+    out += [(obase + OH * i, OH) for i in range(tracers)]
+    return out + [(mbase, AH), (mbase + AH, OH), (mbase + AH + OH, OH)]
+
+
+def regroup_kernel(slices, from_up, from_down, tiles):
+    for i, (at, width) in enumerate(slices):
+        tiles[i, 0:width, :] = from_down[at : at + width, :]
+        tiles[i, 2 * AH - width : 2 * AH, :] = from_up[at : at + width, :]
 
 
 def final_kernel(
     speed,
-    us_in,
-    vs_in,
-    hs_in,
-    fs_in,
-    ms_in,
+    atm,
     ocean,
+    depth,
+    wet,
+    kappa,
     atm_cell,
     dest,
     sea_cell,
     weight,
     wair,
+    row_tiles,
+    from_left,
+    from_right,
     got,
     atm_out,
     ocean_out,
@@ -238,13 +224,14 @@
     vs,
     hs,
     fs,
+    ms,
     edge,
     atm_buf,
     ocean_buf,
     sems,
 ):
-    levels = us.shape[0]
-    rows, cols = ocean.shape[2:]
+    levels = atm.shape[1]
+    rows, cols = atm.shape[2:]
     tracers = fs.shape[0]
     each = ocean.shape[1]
     slots, lanes = lane_slots(levels, tracers)
@@ -277,10 +264,14 @@
         edge[i, AH : 2 * AH, :] = got[above, at : at + AH, :]
     half = lanes // cols
 
-    def load(ref, i, slot, width):
-        corner = strips(cols, slot, width, lambda t: edge[t], lambda t: edge[half + t])
-        outer = jnp.concatenate([ref[i, rows:full, 0:cols], corner], axis=1)
-        return jnp.concatenate([ref[i, 0:rows, :], outer], axis=0)
+    def extend(view, value, field, width):
+        slot = slots[field]
+        view[0:rows, 0:cols] = value
+        view[rows:full, 0:cols] = row_tiles[field]
+        view[0:rows, cols : 2 * cols] = strips(
+            cols, slot, width, lambda t: from_left[:, t * cols : (t + 1) * cols], lambda t: from_right[:, t * cols : (t + 1) * cols]
+        )
+        view[rows:full, cols : 2 * cols] = strips(cols, slot, width, lambda t: edge[t], lambda t: edge[half + t])
 
     def east(f):
         return pltpu.roll(f, 2 * cols - 1, 1)
@@ -295,12 +286,22 @@
         return pltpu.roll(f, 1, 0)
 
     base = 3 * levels + tracers
-    w = load(ms_in, 1, slots[base + 1], AH)
-    k = load(ms_in, 2, slots[base + 2], AH)
+    extend(ms.at[0], depth[...], base, AH)
+    extend(ms.at[1], wet[...].astype(F32), base + 1, AH)
+    extend(ms.at[2], kappa[...], base + 2, AH)
+    for i in range(tracers):
+        extend(fs.at[i], ocean[i // each, i % each], 3 * levels + i, OH)
+    for level in range(levels):
+        extend(us.at[level], atm[0, level], level, AH)
+        extend(vs.at[level], atm[1, level], levels + level, AH)
+        extend(hs.at[level], atm[2, level], 2 * levels + level, AH)
+
+    w = ms[1]
+    k = ms[2]
     we, ww, ws, wn = east(w), west(w), south(w), north(w)
     for step in range(OCEAN_STEPS):
         for i in range(tracers):
-            f = load(fs_in, i, slots[3 * levels + i], OH) if step == 0 else fs[i]
+            f = fs[i]
             total = we * (east(f) - f)
             total = total + ww * (west(f) - f)
             total = total + ws * (south(f) - f)
@@ -314,17 +315,11 @@
     copies = [pltpu.make_async_copy(ocean_buf, ocean_out, sems.at[0])]
     copies[0].start()
 
-    d = load(ms_in, 0, slots[base], AH)
+    d = ms[0]
     chunk = max(1, levels // 4)
     for step in range(ACOUSTIC):
         for level in range(levels):
-            if step == 0:
-                u = load(us_in, level, slots[level], AH)
-                v = load(vs_in, level, slots[levels + level], AH)
-                h = load(hs_in, level, slots[2 * levels + level], AH)
-                us[level], vs[level] = u, v
-            else:
-                u, v, h = us[level], vs[level], hs[level]
+            u, v, h = us[level], vs[level], hs[level]
             column_speed = speed[level] * d
             hs[level] = h - column_speed * ((east(u) - west(u)) * 0.5 + (south(v) - north(v)) * 0.5)
         for level in range(levels):
@@ -418,38 +413,53 @@
         + [pltpu.VMEM((rows, lanes), F32)] * 2
         + [pltpu.SemaphoreType.DMA((8,))],
         compiler_params=whole,
-        cost_estimate=pl.CostEstimate(flops=0, bytes_accessed=20_000_000, transcendentals=0),
+        cost_estimate=pl.CostEstimate(flops=0, bytes_accessed=200_000_000, transcendentals=0),
         name="exchange_send",
     )(air_temp, ocean_state, atm_cell, dest, sea_cell, weight, from_left, from_right)
     got = lax.all_to_all(message, "tile", split_axis=0, concat_axis=0, tiled=True)
 
-    extended = [shape(levels, full, 2 * cols)] * 3 + [shape(tracers, full, 2 * cols), shape(3, full, 2 * cols)]
-    us, vs, hs, fs, ms = pl.pallas_call(
-        extend_kernel,
-        out_shape=extended,
-        in_specs=[vmem] * 9,
-        out_specs=[vmem] * 5,
+    slices = row_slices(levels, tracers)
+    row_tiles = pl.pallas_call(
+        functools.partial(regroup_kernel, slices),
+        out_shape=shape(len(slices), 2 * AH, cols),
+        in_specs=[vmem] * 2,
+        out_specs=vmem,
         compiler_params=params,
-        cost_estimate=pl.CostEstimate(flops=0, bytes_accessed=8_000_000, transcendentals=0),
-        name="extend",
-    )(*fields, from_up, from_down, from_left, from_right)
-
-    results = pl.pallas_call(
-        final_kernel,
-        out_shape=[shape(*atm_state.shape), shape(*ocean_state.shape)],
-        in_specs=[smem] + [vmem] * 12,
-        out_specs=[hbm] * 2,
-        scratch_shapes=[pltpu.VMEM(x.shape, F32) for x in extended[:4]]
-        + [
-            pltpu.VMEM((2 * (lanes // cols), 2 * AH, cols), F32),
-            pltpu.VMEM(atm_state.shape, F32),
-            pltpu.VMEM(ocean_state.shape, F32),
-            pltpu.SemaphoreType.DMA((8,)),
-        ],
-        compiler_params=params,
-        name="steps",
-    )(wave_speed, us, vs, hs, fs, ms, ocean_state, atm_cell, dest, sea_cell, weight, wair, got)
-    return tuple(results)
+        cost_estimate=pl.CostEstimate(flops=0, bytes_accessed=200_000_000, transcendentals=0),
+        name="regroup",
+    )(from_up, from_down)
+
+    return tuple(
+        pl.pallas_call(
+            final_kernel,
+            out_shape=[shape(*atm_state.shape), shape(*ocean_state.shape)],
+            in_specs=[smem] + [vmem] * 14,
+            out_specs=[hbm] * 2,
+            scratch_shapes=[pltpu.VMEM((levels, full, 2 * cols), F32)] * 3
+            + [
+                pltpu.VMEM((tracers, full, 2 * cols), F32),
+                pltpu.VMEM((3, full, 2 * cols), F32),
+                pltpu.VMEM((2 * (lanes // cols), 2 * AH, cols), F32),
+                pltpu.VMEM(atm_state.shape, F32),
+                pltpu.VMEM(ocean_state.shape, F32),
+                pltpu.SemaphoreType.DMA((8,)),
+            ],
+            compiler_params=params,
+            name="steps",
+        )(
+            wave_speed,
+            *fields,
+            atm_cell,
+            dest,
+            sea_cell,
+            weight,
+            wair,
+            row_tiles,
+            from_left,
+            from_right,
+            got,
+        )
+    )
 
 
 def solution(mesh):

time: 34 us -> 31 us (0.912)
  Pallas kernels: 10.1 us -> 8.11 us
  local copies, waits for them, and re-layouts: 1.67 us -> 0.59 us
    pallas_call x1, Pallas kernels: 1.21 us -> 0.05 us  [on_device(): pl.pallas_call(functools.partial(regroup_kernel, slices), out_shape=shape...]
    unnamed x24 -> x22, local copies, waits for them, and re-layouts: 1.67 us -> 0.59 us
    pallas_call x1, Pallas kernels: 4.36 us -> 3.54 us  [on_device(): pl.pallas_call(final_kernel, out_shape=[shape(*atm_state.shape), shape(*o...]
  transfers between devices with their start and end apart: 5 -> 5, of which waited for: 3 -> 3; matrix products, arithmetic and copies ran while one was open for 0% -> 0% of each run, Pallas kernels for 4% -> 0%
where the time goes in v4:
time: 31 us; the launch traced here: 30.6 us
  starting transfers between devices  12.2 us (39%)
  waiting for transfers between devices  8.87 us (29%)
  Pallas kernels  8.11 us (26%)
  between operations  0.8 us (3%)
  local copies, waits for them, and re-layouts  0.59 us (2%)
    ppermute x4, waiting for transfers between devices, shift(): lax.ppermute(value, axes, [(i, (i + by) % count) for i in range(count)])  8.86 us
    ppermute x4, starting transfers between devices, shift(): lax.ppermute(value, axes, [(i, (i + by) % count) for i in range(count)])  6.4 us
    all_to_all x1, starting transfers between devices, on_device(): lax.all_to_all(message, 'tile', split_axis=0, concat_axis=0, tiled=True)  5.82 us
    pallas_call x1, Pallas kernels, on_device(): pl.pallas_call(final_kernel, out_shape=[shape(*atm_state.shape), shape(*o...  3.54 us
    pallas_call x1, Pallas kernels, on_device(): pl.pallas_call(send_kernel, out_shape=[shape(tile_count, 3 * rows + corne...  2.48 us
    pallas_call x1, Pallas kernels, on_device(): pl.pallas_call(pack_kernel, out_shape=[shape(message_rows, cols)] * 2 + [...  2.04 us
  transfers between devices with their start and end apart: 5, of which 3 were waited for; matrix products, arithmetic and copies ran while one was open for 0% of the time, Pallas kernels for 0%

profile of v4, /device:TPU:0, one launch (start us, length us, event | category | flops | bytes accessed | tf_op | source)
XLA Modules:
  0.0 30.6 jit_solution(2917847498192117132)
XLA Ops:
  0.6 2.0 %pack.1 = (f32[200,128]{1,0:T(8,128)}, f32[200,128]{1,0:T(8,128)}, f32[16,256]{1,0:T(8,128)}, f32[16,256]{1,0:T(8,128)}) custom-call(f32[3,16,16,128]{3,2,1,0:T(8,128)} %atm.1, f32[2,8,16,128]{3,2,1,0:T(8,128)} %ocean.1, f32[16,128]{1,0:T(8,128)} %depth.1, s32[16,128]{1,0:T(8,128)} %wet.1, f32[16,128]{1,0:T(8,128)} %kappa.1), custom_call_target="tpu_custom_call" | custom-call | tf_op jit(solution)/shard_map/pack/pallas_call | solution.py:379
  2.7 0.5 %collective-permute-start = (f32[16,256]{1,0:T(8,128)}, f32[16,256]{1,0:T(8,128)}, u32[]{:S(2)}, u32[]{:S(2)}) collective-permute-start(f32[16,256]{1,0:T(8,128)} %get-tuple-element.8), channel_id=1, source_target_pairs={{0,1},{1,2},{2,3},{3,0},{4,5},{5,6},{6,7},{7,4},{8,9},{9,10},{10,1... | collective-permute-start | bytes 49160 | tf_op jit(solution)/shard_map/ppermute | solution.py:397
  3.2 2.0 %collective-permute-start.1 = (f32[16,256]{1,0:T(8,128)}, f32[16,256]{1,0:T(8,128)}, u32[]{:S(2)}, u32[]{:S(2)}) collective-permute-start(f32[16,256]{1,0:T(8,128)} %get-tuple-element.9), channel_id=1, source_target_pairs={{0,3},{1,0},{2,1},{3,2},{4,7},{5,4},{6,5},{7,6},{8,11},{9,8},{10,9... | collective-permute-start | bytes 49160 | tf_op jit(solution)/shard_map/ppermute | solution.py:397
  5.2 1.7 %collective-permute-done.refs_6_.from_left = f32[16,256]{1,0:T(8,128)} collective-permute-done((f32[16,256]{1,0:T(8,128)}, f32[16,256]{1,0:T(8,128)}, u32[]{:S(2)}, u32[]{:S(2)}) %collective-permute-start) | collective-permute-done | bytes 16416 | tf_op jit(solution)/shard_map/ppermute | solution.py:397
  6.8 0.0 collective-permute-done.1.refs_7_.from_right
  6.8 2.5 %exchange_send.1 = (f32[4,64,128]{2,1,0:T(8,128)}, f32[1,2048]{1,0:T(1,128)}) custom-call(f32[16,128]{1,0:T(8,128)} %refs_0_.3, f32[2,8,16,128]{3,2,1,0:T(8,128)} %ocean.1, s32[1,2048]{1,0:T(1,128)} %bitcast.4, s32[1,2048]{1,0:T(1,128)} %bitcast.6, s32[1,2048]{1,0:T(1,128)} %bitcast.8, f32[1,2048]{1,0:T(1,128)} %bitcast.10, ...), custom_call_target="tpu_custom_call" | custom-call | bytes 200000000 | tf_op jit(solution)/shard_map/exchange_send/pallas_call | solution.py:405
  9.3 0.0 copy-start
  9.3 5.8 %all-to-all-start = ((f32[4,64,128]{2,1,0:T(8,128)}), f32[4,64,128]{2,1,0:T(8,128)S(1)}, u32[]{:S(2)}, u32[]{:S(2)}) async-start(f32[4,64,128]{2,1,0:T(8,128)} %get-tuple-element.13), calls=%async_computation | async-start | bytes 262144 | tf_op jit(solution)/shard_map/all_to_all | solution.py:419
  15.2 2.0 %collective-permute-start.2 = (f32[200,128]{1,0:T(8,128)}, f32[200,128]{1,0:T(8,128)S(1)}, u32[]{:S(2)}, u32[]{:S(2)}) collective-permute-start(f32[200,128]{1,0:T(8,128)} %get-tuple-element.11), channel_id=1, source_target_pairs={{0,4},{4,8},{8,12},{12,0},{1,5},{5,9},{9,13},{13,1},{2,6},{6,10},{... | collective-permute-start | bytes 307208 | tf_op jit(solution)/shard_map/ppermute | solution.py:397
  17.2 0.0 copy-start.1
  17.2 0.0 copy-start.2
  17.2 0.0 copy-start.3
  17.2 0.0 copy-start.4
  17.2 0.0 copy-start.5
  17.2 0.0 copy-start.6
  17.2 0.0 copy-start.7
  17.2 0.0 copy-start.8
  17.3 0.0 copy-start.9
  17.3 1.9 %collective-permute-start.3 = (f32[200,128]{1,0:T(8,128)}, f32[200,128]{1,0:T(8,128)S(1)}, u32[]{:S(2)}, u32[]{:S(2)}) collective-permute-start(f32[200,128]{1,0:T(8,128)} %get-tuple-element.12), channel_id=1, source_target_pairs={{0,12},{4,0},{8,4},{12,8},{1,13},{5,1},{9,5},{13,9},{2,14},{6,2},{... | collective-permute-start | bytes 307208 | tf_op jit(solution)/shard_map/ppermute | solution.py:397
  19.1 5.8 %collective-permute-done.2.from_up = f32[200,128]{1,0:T(8,128)S(1)} collective-permute-done((f32[200,128]{1,0:T(8,128)}, f32[200,128]{1,0:T(8,128)S(1)}, u32[]{:S(2)}, u32[]{:S(2)}) %collective-permute-start.2) | collective-permute-done | bytes 102432 | tf_op jit(solution)/shard_map/ppermute | solution.py:397
  24.9 1.4 %collective-permute-done.3.from_down = f32[200,128]{1,0:T(8,128)S(1)} collective-permute-done((f32[200,128]{1,0:T(8,128)}, f32[200,128]{1,0:T(8,128)S(1)}, u32[]{:S(2)}, u32[]{:S(2)}) %collective-permute-start.3) | collective-permute-done | bytes 102432 | tf_op jit(solution)/shard_map/ppermute | solution.py:397
  26.4 0.0 copy-start.10
  26.4 0.0 all-to-all-done.got
  26.4 0.0 copy-done
  26.4 0.0 copy-done.1
  26.4 0.0 copy-done.2
  26.4 0.0 copy-done.3
  26.4 0.0 copy-done.4
  26.5 0.0 copy-done.5
  26.5 0.0 copy-done.6
  26.5 0.0 copy-done.7
  26.5 0.0 copy-done.8
  26.5 0.0 copy-done.9
  26.5 0.5 %copy-done.10 = f32[16]{0:T(128)S(1)} copy-done((f32[16]{0:T(128)S(1)}, f32[16]{0:T(128)}, u32[]{:S(2)}) %copy-start.10) | copy-done | bytes 88
  27.0 3.5 %steps.1 = (f32[3,16,16,128]{3,2,1,0:T(8,128)}, f32[2,8,16,128]{3,2,1,0:T(8,128)}) custom-call(f32[16]{0:T(128)S(1)} %copy-done.10, f32[3,16,16,128]{3,2,1,0:T(8,128)S(1)} %copy-done, f32[2,8,16,128]{3,2,1,0:T(8,128)S(1)} %copy-done.1, f32[16,128]{1,0:T(8,128)S(1)} %copy-done.2, s32[16,128]{1,0:T(8,128)S(1)} %copy-done.3, f32[16,128]{1,0:T(8,128)S(1)} %copy-done.4, ...), custom_call_target="tpu_custom_call" | custom-call | tf_op jit(solution)/shard_map/steps/pallas_call | solution.py:433
  (1 shorter events, 0.0 us)
Async XLA Ops:
  2.7 4.2 %collective-permute-start = (f32[16,256]{1,0:T(8,128)}, f32[16,256]{1,0:T(8,128)}, u32[]{:S(2)}, u32[]{:S(2)}) collective-permute-start(f32[16,256]{1,0:T(8,128)} %get-tuple-element.8), channel_id=1, source_target_pairs={{0,1},{1,2},{2,3},{3,0},{4,5},{5,6},{6,7},{7,4},{8,9},{9,10},{10,1... | collective-permute-start | bytes 49160 | tf_op jit(solution)/shard_map/ppermute | solution.py:397
  3.2 3.7 %collective-permute-start.1 = (f32[16,256]{1,0:T(8,128)}, f32[16,256]{1,0:T(8,128)}, u32[]{:S(2)}, u32[]{:S(2)}) collective-permute-start(f32[16,256]{1,0:T(8,128)} %get-tuple-element.9), channel_id=1, source_target_pairs={{0,3},{1,0},{2,1},{3,2},{4,7},{5,4},{6,5},{7,6},{8,11},{9,8},{10,9... | collective-permute-start | bytes 49160 | tf_op jit(solution)/shard_map/ppermute | solution.py:397
  9.3 17.1 %copy-start = (f32[3,16,16,128]{3,2,1,0:T(8,128)S(1)}, f32[3,16,16,128]{3,2,1,0:T(8,128)}, u32[]{:S(2)}) copy-start(f32[3,16,16,128]{3,2,1,0:T(8,128)} %atm.1) | copy-start | bytes 1179652
  9.3 17.1 %all-to-all-start = ((f32[4,64,128]{2,1,0:T(8,128)}), f32[4,64,128]{2,1,0:T(8,128)S(1)}, u32[]{:S(2)}, u32[]{:S(2)}) async-start(f32[4,64,128]{2,1,0:T(8,128)} %get-tuple-element.13), calls=%async_computation | async-start | bytes 262144 | tf_op jit(solution)/shard_map/all_to_all | solution.py:419
  15.2 9.8 %collective-permute-start.2 = (f32[200,128]{1,0:T(8,128)}, f32[200,128]{1,0:T(8,128)S(1)}, u32[]{:S(2)}, u32[]{:S(2)}) collective-permute-start(f32[200,128]{1,0:T(8,128)} %get-tuple-element.11), channel_id=1, source_target_pairs={{0,4},{4,8},{8,12},{12,0},{1,5},{5,9},{9,13},{13,1},{2,6},{6,10},{... | collective-permute-start | bytes 307208 | tf_op jit(solution)/shard_map/ppermute | solution.py:397
  17.2 9.2 %copy-start.1 = (f32[2,8,16,128]{3,2,1,0:T(8,128)S(1)}, f32[2,8,16,128]{3,2,1,0:T(8,128)}, u32[]{:S(2)}) copy-start(f32[2,8,16,128]{3,2,1,0:T(8,128)} %ocean.1) | copy-start | bytes 393220
  17.2 9.2 %copy-start.2 = (f32[16,128]{1,0:T(8,128)S(1)}, f32[16,128]{1,0:T(8,128)}, u32[]{:S(2)}) copy-start(f32[16,128]{1,0:T(8,128)} %depth.1) | copy-start | bytes 24580
  17.2 9.2 %copy-start.3 = (s32[16,128]{1,0:T(8,128)S(1)}, s32[16,128]{1,0:T(8,128)}, u32[]{:S(2)}) copy-start(s32[16,128]{1,0:T(8,128)} %wet.1) | copy-start | bytes 24580
  17.2 9.3 %copy-start.4 = (f32[16,128]{1,0:T(8,128)S(1)}, f32[16,128]{1,0:T(8,128)}, u32[]{:S(2)}) copy-start(f32[16,128]{1,0:T(8,128)} %kappa.1) | copy-start | bytes 24580
  17.2 9.3 %copy-start.5 = (s32[1,1,2048]{2,1,0:T(1,128)S(1)}, s32[1,1,2048]{2,1,0:T(1,128)}, u32[]{:S(2)}) copy-start(s32[1,1,2048]{2,1,0:T(1,128)} %param.18) | copy-start | bytes 24580
  17.2 9.3 %copy-start.6 = (s32[1,1,2048,1]{2,3,1,0:T(1,128)S(1)}, s32[1,1,2048,1]{2,3,1,0:T(1,128)}, u32[]{:S(2)}) copy-start(s32[1,1,2048,1]{2,3,1,0:T(1,128)} %param.19) | copy-start | bytes 24580
  17.2 9.3 %copy-start.7 = (s32[1,1,2048]{2,1,0:T(1,128)S(1)}, s32[1,1,2048]{2,1,0:T(1,128)}, u32[]{:S(2)}) copy-start(s32[1,1,2048]{2,1,0:T(1,128)} %param.20) | copy-start | bytes 24580
  17.2 9.3 %copy-start.8 = (f32[1,1,2048]{2,1,0:T(1,128)S(1)}, f32[1,1,2048]{2,1,0:T(1,128)}, u32[]{:S(2)}) copy-start(f32[1,1,2048]{2,1,0:T(1,128)} %param.21) | copy-start | bytes 24580
  17.3 9.2 %copy-start.9 = (f32[1,2048]{1,0:T(1,128)S(1)}, f32[1,2048]{1,0:T(1,128)}, u32[]{:S(2)}) copy-start(f32[1,2048]{1,0:T(1,128)} %get-tuple-element.10.wair) | copy-start | bytes 24580
  17.3 9.1 %collective-permute-start.3 = (f32[200,128]{1,0:T(8,128)}, f32[200,128]{1,0:T(8,128)S(1)}, u32[]{:S(2)}, u32[]{:S(2)}) collective-permute-start(f32[200,128]{1,0:T(8,128)} %get-tuple-element.12), channel_id=1, source_target_pairs={{0,12},{4,0},{8,4},{12,8},{1,13},{5,1},{9,5},{13,9},{2,14},{6,2},{... | collective-permute-start | bytes 307208 | tf_op jit(solution)/shard_map/ppermute | solution.py:397
  26.4 0.7 %copy-start.10 = (f32[16]{0:T(128)S(1)}, f32[16]{0:T(128)}, u32[]{:S(2)}) copy-start(f32[16]{0:T(128)} %speed.1) | copy-start | bytes 196

commit v5 on v4

--- a/solution.py
+++ b/solution.py
@@ -135,8 +135,13 @@
     return out
 
 
-def send_kernel(*refs):
-    sources, (message, wair_out), held, sems = refs[:8], refs[8:10], refs[10:18], refs[18]
+def tile_at(shift, tiles):
+    return lax.rem(lax.axis_index("tile") + shift % tiles, tiles)
+
+
+def send_kernel(tiles, *refs):
+    sources, (*messages, wair_out) = refs[:8], refs[8:-9]
+    held, sems = refs[-9:-1], refs[-1]
     air, surface, atm_cell, dest, sea_cell, weight, from_left, from_right = held
     copies = [
         pltpu.make_async_copy(source.at[0, 0] if i == 1 else source, target, sems.at[i])
@@ -147,8 +152,6 @@
     for copy in copies:
         copy.wait()
     rows, cols = air.shape
-    tiles = message.shape[0]
-    tile_lanes = from_left.shape[1] // cols
     cell = atm_cell[...]
     hot_atm = jnp.where(one_hot(cell % cols, cols), 1.0, 0.0).astype(BF16)
     airx = gather_rows(air[...], one_hot(cell // cols, rows), hot_atm)
@@ -158,21 +161,21 @@
     cell = sea_cell[...]
     hot_sea = jnp.where(one_hot(cell % cols, cols), 1.0, 0.0).astype(BF16)
     row = dest[...] * rows + cell // cols
-    for tile in range(tiles):
-        s1, s2 = scatter_rows([wair, w], one_hot(row - tile * rows, rows), hot_sea)
-        message[tile, 0:rows, :] = s1
-        message[tile, rows : 2 * rows, :] = s2
-        message[tile, 2 * rows : 3 * rows, :] = surface[...]
-        message[tile, 3 * rows :, :] = jnp.zeros((message.shape[1] - 3 * rows, cols), F32)
-    me = lax.axis_index("tile")
-    above, below = lax.rem(me + tiles - 1, tiles), lax.rem(me + 1, tiles)
-    at = 3 * rows
-    for ref in (from_left, from_right):
-        for i in range(tile_lanes):
-            where = slice(i * cols, (i + 1) * cols)
-            message[above, at : at + AH, :] = ref[0:AH, where]
-            message[below, at : at + AH, :] = ref[rows - AH : rows, where]
-            at += AH
+    strip_tiles = from_left.shape[1] // cols
+    for shift in range(tiles):
+        target = tile_at(shift, tiles)
+        message = messages[shift] if len(messages) > 1 else messages[0].at[target]
+        s1, s2 = scatter_rows([wair, w], one_hot(row - target * rows, rows), hot_sea)
+        message[0:rows, :] = s1
+        message[rows : 2 * rows, :] = s2
+        message[2 * rows : 3 * rows, :] = surface[...]
+        if shift in (1, tiles - 1):
+            near = slice(rows - AH, rows) if shift == 1 else slice(0, AH)
+            at = 3 * rows
+            for ref in (from_left, from_right):
+                for i in range(strip_tiles):
+                    message[at : at + AH, :] = ref[near, i * cols : (i + 1) * cols]
+                    at += AH
 
 
 def strips(cols, slot, width, left_part, right_part):
@@ -202,67 +205,42 @@
         tiles[i, 2 * AH - width : 2 * AH, :] = from_up[at : at + width, :]
 
 
-def final_kernel(
-    speed,
-    atm,
-    ocean,
-    depth,
-    wet,
-    kappa,
-    atm_cell,
-    dest,
-    sea_cell,
-    weight,
-    wair,
-    row_tiles,
-    from_left,
-    from_right,
-    got,
-    atm_out,
-    ocean_out,
-    us,
-    vs,
-    hs,
-    fs,
-    ms,
-    edge,
-    atm_buf,
-    ocean_buf,
-    sems,
-):
+def final_kernel(tiles, *refs):
+    speed, atm, ocean, depth, wet, kappa, atm_cell, dest, sea_cell, weight, wair, row_tiles, from_left, from_right = refs[:14]
+    messages, (atm_out, ocean_out, us, vs, hs, fs, ms, edge, atm_buf, ocean_buf, sems) = refs[14:-11], refs[-11:]
     levels = atm.shape[1]
     rows, cols = atm.shape[2:]
     tracers = fs.shape[0]
     each = ocean.shape[1]
     slots, lanes = lane_slots(levels, tracers)
     full = rows + 2 * AH
-    tiles = got.shape[0]
-    me = lax.axis_index("tile")
-    above, below = lax.rem(me + tiles - 1, tiles), lax.rem(me + 1, tiles)
+
+    def message(shift):
+        return messages[shift] if len(messages) > 1 else messages[0].at[tile_at(-shift, tiles)]
 
     surface = ocean[0, 0]
-    s1, s2 = got[0, 0:rows, :], got[0, rows : 2 * rows, :]
-    for tile in range(1, tiles):
-        s1 = s1 + got[tile, 0:rows, :]
-        s2 = s2 + got[tile, rows : 2 * rows, :]
-    sea_flux = s1 - surface * s2
     cell = sea_cell[...]
     hot_sea = jnp.where(one_hot(cell % cols, cols), 1.0, 0.0).astype(BF16)
     row = dest[...] * rows + cell // cols
+    s1, s2 = message(0)[0:rows, :], message(0)[rows : 2 * rows, :]
     sstx = jnp.zeros(cell.shape, F32)
-    for tile in range(tiles):
-        table = got[tile, 2 * rows : 3 * rows, :]
-        sstx = sstx + gather_rows(table, one_hot(row - tile * rows, rows), hot_sea)
+    for shift in range(tiles):
+        if shift:
+            s1 = s1 + message(shift)[0:rows, :]
+            s2 = s2 + message(shift)[rows : 2 * rows, :]
+        table = message(shift)[2 * rows : 3 * rows, :]
+        sstx = sstx + gather_rows(table, one_hot(row - tile_at(-shift, tiles) * rows, rows), hot_sea)
+    sea_flux = s1 - surface * s2
     flux = wair[...] - weight[...] * sstx
     cell = atm_cell[...]
     hot_atm = jnp.where(one_hot(cell % cols, cols), 1.0, 0.0).astype(BF16)
     (atm_flux,) = scatter_rows([flux], one_hot(cell // cols, rows), hot_atm)
 
-    for i in range(2 * (lanes // cols)):
+    half = lanes // cols
+    for i in range(2 * half):
         at = 3 * rows + AH * i
-        edge[i, 0:AH, :] = got[below, at : at + AH, :]
-        edge[i, AH : 2 * AH, :] = got[above, at : at + AH, :]
-    half = lanes // cols
+        edge[i, 0:AH, :] = message(tiles - 1)[at : at + AH, :]
+        edge[i, AH : 2 * AH, :] = message(1)[at : at + AH, :]
 
     def extend(view, value, field, width):
         slot = slots[field]
@@ -402,11 +380,16 @@
     from_up = shift(down, "tile", tile_count, 1)
 
     corner_rows = 2 * AH * (lanes // cols)
-    message, wair = pl.pallas_call(
-        send_kernel,
-        out_shape=[shape(tile_count, 3 * rows + corner_rows, cols), shape(1, cells)],
+    by_shift = tile_count <= 4
+    if by_shift:
+        sums = [shape(3 * rows + (corner_rows if s in (1, tile_count - 1) else 0), cols) for s in range(tile_count)]
+    else:
+        sums = [shape(tile_count, 3 * rows + corner_rows, cols)]
+    *messages, wair = pl.pallas_call(
+        functools.partial(send_kernel, tile_count),
+        out_shape=sums + [shape(1, cells)],
         in_specs=[hbm] * 8,
-        out_specs=[vmem] * 2,
+        out_specs=[vmem] * (len(sums) + 1),
         scratch_shapes=[pltpu.VMEM((rows, cols), F32)] * 2
         + [pltpu.VMEM((1, cells), jnp.int32)] * 3
         + [pltpu.VMEM((1, cells), F32)]
@@ -416,7 +399,10 @@
         cost_estimate=pl.CostEstimate(flops=0, bytes_accessed=200_000_000, transcendentals=0),
         name="exchange_send",
     )(air_temp, ocean_state, atm_cell, dest, sea_cell, weight, from_left, from_right)
-    got = lax.all_to_all(message, "tile", split_axis=0, concat_axis=0, tiled=True)
+    if by_shift:
+        got = messages[:1] + [shift(messages[s], "tile", tile_count, s) for s in range(1, tile_count)]
+    else:
+        got = [lax.all_to_all(messages[0], "tile", split_axis=0, concat_axis=0, tiled=True)]
 
     slices = row_slices(levels, tracers)
     row_tiles = pl.pallas_call(
@@ -431,9 +417,9 @@
 
     return tuple(
         pl.pallas_call(
-            final_kernel,
+            functools.partial(final_kernel, tile_count),
             out_shape=[shape(*atm_state.shape), shape(*ocean_state.shape)],
-            in_specs=[smem] + [vmem] * 14,
+            in_specs=[smem] + [vmem] * (13 + len(got)),
             out_specs=[hbm] * 2,
             scratch_shapes=[pltpu.VMEM((levels, full, 2 * cols), F32)] * 3
             + [
@@ -457,7 +443,7 @@
             row_tiles,
             from_left,
             from_right,
-            got,
+            *got,
         )
     )
 

time: 31 us -> 28.2 us (0.910)
  waiting for transfers between devices: 8.87 us -> 5.57 us
  starting transfers between devices: 12.2 us -> 10.8 us
  Pallas kernels: 8.11 us -> 9.06 us
  local copies, waits for them, and re-layouts: 0.59 us -> 1.52 us
    all_to_all x1 -> x0, starting transfers between devices: 5.82 us -> none  [on_device(): lax.all_to_all(message, 'tile', split_axis=0, concat_axis=0, tiled=True)]
    ppermute x4 -> x7, starting transfers between devices: 6.4 us -> 10.8 us  [shift(): lax.ppermute(value, axes, [(i, (i + by) % count) for i in range(count)])]
    ppermute x4 -> x7, waiting for transfers between devices: 8.86 us -> 5.57 us  [shift(): lax.ppermute(value, axes, [(i, (i + by) % count) for i in range(count)])]
    pallas_call x1, Pallas kernels: 0.05 us -> 1.03 us  [on_device(): pl.pallas_call(functools.partial(regroup_kernel, slices), out_shape=shape...]
    unnamed x22 -> x24, local copies, waits for them, and re-layouts: 0.59 us -> 1.52 us
  transfers between devices with their start and end apart: 5 -> 7, of which waited for: 3 -> 2; matrix products, arithmetic and copies ran while one was open for 0% -> 0% of each run, Pallas kernels for 0% -> 13%
where the time goes in v5:
time: 28.2 us; the launch traced here: 27.8 us
  starting transfers between devices  10.8 us (38%)
  Pallas kernels  9.06 us (32%)
  waiting for transfers between devices  5.57 us (20%)
  local copies, waits for them, and re-layouts  1.52 us (5%)
  between operations  0.83 us (3%)
    ppermute x7, starting transfers between devices, shift(): lax.ppermute(value, axes, [(i, (i + by) % count) for i in range(count)])  10.8 us
    ppermute x7, waiting for transfers between devices, shift(): lax.ppermute(value, axes, [(i, (i + by) % count) for i in range(count)])  5.57 us
    pallas_call x1, Pallas kernels, on_device(): pl.pallas_call(functools.partial(final_kernel, tile_count), out_shape=[sh...  3.52 us
    pallas_call x1, Pallas kernels, on_device(): pl.pallas_call(functools.partial(send_kernel, tile_count), out_shape=sums...  2.47 us
    pallas_call x1, Pallas kernels, on_device(): pl.pallas_call(pack_kernel, out_shape=[shape(message_rows, cols)] * 2 + [...  2.04 us
    unnamed x24, local copies, waits for them, and re-layouts  1.52 us
    pallas_call x1, Pallas kernels, on_device(): pl.pallas_call(functools.partial(regroup_kernel, slices), out_shape=shape...  1.03 us
  transfers between devices with their start and end apart: 7, of which 2 were waited for; matrix products, arithmetic and copies ran while one was open for 0% of the time, Pallas kernels for 13%

profile of v5, /device:TPU:0, one launch (start us, length us, event | category | flops | bytes accessed | tf_op | source)
XLA Modules:
  0.0 27.8 jit_solution(11870326518019137757)
XLA Ops:
  0.6 2.0 %pack.1 = (f32[200,128]{1,0:T(8,128)}, f32[200,128]{1,0:T(8,128)}, f32[16,256]{1,0:T(8,128)}, f32[16,256]{1,0:T(8,128)}) custom-call(f32[3,16,16,128]{3,2,1,0:T(8,128)} %refs_1_.5, f32[2,8,16,128]{3,2,1,0:T(8,128)} %refs_2_.3, f32[16,128]{1,0:T(8,128)} %refs_3_.3, s32[16,128]{1,0:T(8,128)} %refs_4_.3, f32[16,128]{1,0:T(8,128)} %refs_5_.1), custom_call_target="tpu_custom_call" | custom-call | tf_op jit(solution)/shard_map/pack/pallas_call | solution.py:357
  2.7 3.1 %collective-permute-start.2 = (f32[200,128]{1,0:T(8,128)}, f32[200,128]{1,0:T(8,128)}, u32[]{:S(2)}, u32[]{:S(2)}) collective-permute-start(f32[200,128]{1,0:T(8,128)} %get-tuple-element.14), channel_id=1, source_target_pairs={{0,4},{4,8},{8,12},{12,0},{1,5},{5,9},{9,13},{13,1},{2,6},{6,10},{... | collective-permute-start | bytes 307208 | tf_op jit(solution)/shard_map/ppermute | solution.py:375
  5.8 2.1 %collective-permute-start.3 = (f32[200,128]{1,0:T(8,128)}, f32[200,128]{1,0:T(8,128)}, u32[]{:S(2)}, u32[]{:S(2)}) collective-permute-start(f32[200,128]{1,0:T(8,128)} %get-tuple-element.15), channel_id=1, source_target_pairs={{0,12},{4,0},{8,4},{12,8},{1,13},{5,1},{9,5},{13,9},{2,14},{6,2},{... | collective-permute-start | bytes 307208 | tf_op jit(solution)/shard_map/ppermute | solution.py:375
  7.8 0.0 collective-permute-start
  7.8 1.7 %collective-permute-start.1 = (f32[16,256]{1,0:T(8,128)}, f32[16,256]{1,0:T(8,128)}, u32[]{:S(2)}, u32[]{:S(2)}) collective-permute-start(f32[16,256]{1,0:T(8,128)} %get-tuple-element.12), channel_id=1, source_target_pairs={{0,3},{1,0},{2,1},{3,2},{4,7},{5,4},{6,5},{7,6},{8,11},{9,8},{10,9... | collective-permute-start | bytes 49160 | tf_op jit(solution)/shard_map/ppermute | solution.py:375
  9.6 1.7 %collective-permute-done.refs_6_.refs_12_ = f32[16,256]{1,0:T(8,128)} collective-permute-done((f32[16,256]{1,0:T(8,128)}, f32[16,256]{1,0:T(8,128)}, u32[]{:S(2)}, u32[]{:S(2)}) %collective-permute-start) | collective-permute-done | bytes 16416 | tf_op jit(solution)/shard_map/ppermute | solution.py:375
  11.3 0.0 collective-permute-done.1.refs_7_.refs_13_
  11.3 2.5 %exchange_send.1 = (f32[48,128]{1,0:T(8,128)}, f32[64,128]{1,0:T(8,128)}, f32[48,128]{1,0:T(8,128)}, f32[64,128]{1,0:T(8,128)}, f32[1,2048]{1,0:T(1,128)}) custom-call(f32[16,128]{1,0:T(8,128)} %refs_0_.4, f32[2,8,16,128]{3,2,1,0:T(8,128)} %refs_2_.3, s32[1,2048]{1,0:T(1,128)} %bitcast.4, s32[1,2048]{1,0:T(1,128)} %bitcast.6, s32[1,2048]{1,0:T(1,128)} %bitcast.8, ...), custom_call_target="tpu_custom_call" | custom-call | bytes 200000000 | tf_op jit(solution)/shard_map/exchange_send/pallas_call | solution.py:388
  13.8 0.0 copy-start
  13.8 0.1 collective-permute-start.4
  13.9 3.8 %collective-permute-start.6 = (f32[64,128]{1,0:T(8,128)}, f32[64,128]{1,0:T(8,128)S(1)}, u32[]{:S(2)}, u32[]{:S(2)}) collective-permute-start(f32[64,128]{1,0:T(8,128)} %get-tuple-element.19), channel_id=1, source_target_pairs={{0,12},{4,0},{8,4},{12,8},{1,13},{5,1},{9,5},{13,9},{2,14},{6,2},{... | collective-permute-start | bytes 98312 | tf_op jit(solution)/shard_map/ppermute | solution.py:375
  17.7 0.0 copy-start.9
  17.7 0.0 collective-permute-start.5
  17.7 0.0 collective-permute-done.2.from_up
  17.7 0.0 collective-permute-done.3.from_down
  17.7 0.0 copy-start.2
  17.7 0.0 copy-start.3
  17.7 0.0 copy-start.4
  17.8 0.0 copy-start.5
  17.8 0.0 copy-start.6
  17.8 0.0 copy-start.7
  17.8 0.0 copy-start.8
  17.8 0.0 copy-start.10
  17.8 1.0 %regroup.1.refs_11_ = f32[67,8,128]{2,1,0:T(8,128)S(1)} custom-call(f32[200,128]{1,0:T(8,128)} %collective-permute-done.2.from_up, f32[200,128]{1,0:T(8,128)} %collective-permute-done.3.from_down), custom_call_target="tpu_custom_call" | custom-call | bytes 200000000 | tf_op jit(solution)/shard_map/regroup/pallas_call | solution.py:408
  18.8 3.8 %collective-permute-done.5.refs_16_ = f32[48,128]{1,0:T(8,128)S(1)} collective-permute-done((f32[48,128]{1,0:T(8,128)}, f32[48,128]{1,0:T(8,128)S(1)}, u32[]{:S(2)}, u32[]{:S(2)}) %collective-permute-start.5) | collective-permute-done | bytes 24608 | tf_op jit(solution)/shard_map/ppermute | solution.py:375
  22.7 0.0 collective-permute-done.4.refs_15_
  22.7 0.0 collective-permute-done.6.refs_17_
  22.7 0.0 copy-start.11
  22.7 0.0 copy-done
  22.7 0.0 copy-done.9
  22.7 0.0 copy-done.2
  22.7 0.0 copy-done.3
  22.7 0.0 copy-done.4
  22.7 0.0 copy-done.5
  22.7 0.0 copy-done.6
  22.7 0.0 copy-done.7
  22.8 0.0 copy-done.8
  22.8 0.0 copy-done.10
  22.8 0.6 %copy-done.11 = f32[16]{0:T(128)S(1)} copy-done((f32[16]{0:T(128)S(1)}, f32[16]{0:T(128)}, u32[]{:S(2)}) %copy-start.11) | copy-done | bytes 88
  23.3 0.0 copy-start.1
  23.3 0.9 %copy-done.1 = f32[2,8,16,128]{3,2,1,0:T(8,128)S(1)} copy-done((f32[2,8,16,128]{3,2,1,0:T(8,128)S(1)}, f32[2,8,16,128]{3,2,1,0:T(8,128)}, u32[]{:S(2)}) %copy-start.1) | copy-done | bytes 131096
  24.2 3.5 %steps.1 = (f32[3,16,16,128]{3,2,1,0:T(8,128)}, f32[2,8,16,128]{3,2,1,0:T(8,128)}) custom-call(f32[16]{0:T(128)S(1)} %copy-done.11, f32[3,16,16,128]{3,2,1,0:T(8,128)S(1)} %copy-done, f32[2,8,16,128]{3,2,1,0:T(8,128)S(1)} %copy-done.1, f32[16,128]{1,0:T(8,128)S(1)} %copy-done.2, s32[16,128]{1,0:T(8,128)S(1)} %copy-done.3, f32[16,128]{1,0:T(8,128)S(1)} %copy-done.4, ...), custom_call_target="tpu_custom_call" | custom-call | tf_op jit(solution)/shard_map/steps/pallas_call | solution.py:419
Async XLA Ops:
  2.7 15.0 %collective-permute-start.2 = (f32[200,128]{1,0:T(8,128)}, f32[200,128]{1,0:T(8,128)}, u32[]{:S(2)}, u32[]{:S(2)}) collective-permute-start(f32[200,128]{1,0:T(8,128)} %get-tuple-element.14), channel_id=1, source_target_pairs={{0,4},{4,8},{8,12},{12,0},{1,5},{5,9},{9,13},{13,1},{2,6},{6,10},{... | collective-permute-start | bytes 307208 | tf_op jit(solution)/shard_map/ppermute | solution.py:375
  5.8 12.0 %collective-permute-start.3 = (f32[200,128]{1,0:T(8,128)}, f32[200,128]{1,0:T(8,128)}, u32[]{:S(2)}, u32[]{:S(2)}) collective-permute-start(f32[200,128]{1,0:T(8,128)} %get-tuple-element.15), channel_id=1, source_target_pairs={{0,12},{4,0},{8,4},{12,8},{1,13},{5,1},{9,5},{13,9},{2,14},{6,2},{... | collective-permute-start | bytes 307208 | tf_op jit(solution)/shard_map/ppermute | solution.py:375
  7.8 3.5 %collective-permute-start = (f32[16,256]{1,0:T(8,128)}, f32[16,256]{1,0:T(8,128)}, u32[]{:S(2)}, u32[]{:S(2)}) collective-permute-start(f32[16,256]{1,0:T(8,128)} %get-tuple-element.11), channel_id=1, source_target_pairs={{0,1},{1,2},{2,3},{3,0},{4,5},{5,6},{6,7},{7,4},{8,9},{9,10},{10,1... | collective-permute-start | bytes 49160 | tf_op jit(solution)/shard_map/ppermute | solution.py:375
  7.8 3.5 %collective-permute-start.1 = (f32[16,256]{1,0:T(8,128)}, f32[16,256]{1,0:T(8,128)}, u32[]{:S(2)}, u32[]{:S(2)}) collective-permute-start(f32[16,256]{1,0:T(8,128)} %get-tuple-element.12), channel_id=1, source_target_pairs={{0,3},{1,0},{2,1},{3,2},{4,7},{5,4},{6,5},{7,6},{8,11},{9,8},{10,9... | collective-permute-start | bytes 49160 | tf_op jit(solution)/shard_map/ppermute | solution.py:375
  13.8 8.9 %copy-start = (f32[3,16,16,128]{3,2,1,0:T(8,128)S(1)}, f32[3,16,16,128]{3,2,1,0:T(8,128)}, u32[]{:S(2)}) copy-start(f32[3,16,16,128]{3,2,1,0:T(8,128)} %refs_1_.5) | copy-start | bytes 1179652
  13.8 8.9 %collective-permute-start.4 = (f32[64,128]{1,0:T(8,128)}, f32[64,128]{1,0:T(8,128)S(1)}, u32[]{:S(2)}, u32[]{:S(2)}) collective-permute-start(f32[64,128]{1,0:T(8,128)} %get-tuple-element.17), channel_id=1, source_target_pairs={{0,4},{4,8},{8,12},{12,0},{1,5},{5,9},{9,13},{13,1},{2,6},{6,10},{... | collective-permute-start | bytes 98312 | tf_op jit(solution)/shard_map/ppermute | solution.py:375
  13.9 8.8 %collective-permute-start.6 = (f32[64,128]{1,0:T(8,128)}, f32[64,128]{1,0:T(8,128)S(1)}, u32[]{:S(2)}, u32[]{:S(2)}) collective-permute-start(f32[64,128]{1,0:T(8,128)} %get-tuple-element.19), channel_id=1, source_target_pairs={{0,12},{4,0},{8,4},{12,8},{1,13},{5,1},{9,5},{13,9},{2,14},{6,2},{... | collective-permute-start | bytes 98312 | tf_op jit(solution)/shard_map/ppermute | solution.py:375
  17.7 5.0 %copy-start.9 = (f32[48,128]{1,0:T(8,128)S(1)}, f32[48,128]{1,0:T(8,128)}, u32[]{:S(2)}) copy-start(f32[48,128]{1,0:T(8,128)} %get-tuple-element.16.refs_14_) | copy-start | bytes 73732
  17.7 5.0 %collective-permute-start.5 = (f32[48,128]{1,0:T(8,128)}, f32[48,128]{1,0:T(8,128)S(1)}, u32[]{:S(2)}, u32[]{:S(2)}) collective-permute-start(f32[48,128]{1,0:T(8,128)} %get-tuple-element.18), channel_id=1, source_target_pairs={{0,8},{4,12},{8,0},{12,4},{1,9},{5,13},{9,1},{13,5},{2,10},{6,14},... | collective-permute-start | bytes 73736 | tf_op jit(solution)/shard_map/ppermute | solution.py:375
  17.7 5.0 %copy-start.2 = (f32[16,128]{1,0:T(8,128)S(1)}, f32[16,128]{1,0:T(8,128)}, u32[]{:S(2)}) copy-start(f32[16,128]{1,0:T(8,128)} %refs_3_.3) | copy-start | bytes 24580
  17.7 5.0 %copy-start.3 = (s32[16,128]{1,0:T(8,128)S(1)}, s32[16,128]{1,0:T(8,128)}, u32[]{:S(2)}) copy-start(s32[16,128]{1,0:T(8,128)} %refs_4_.3) | copy-start | bytes 24580
  17.7 5.0 %copy-start.4 = (f32[16,128]{1,0:T(8,128)S(1)}, f32[16,128]{1,0:T(8,128)}, u32[]{:S(2)}) copy-start(f32[16,128]{1,0:T(8,128)} %refs_5_.1) | copy-start | bytes 24580
  17.8 5.0 %copy-start.5 = (s32[1,1,2048]{2,1,0:T(1,128)S(1)}, s32[1,1,2048]{2,1,0:T(1,128)}, u32[]{:S(2)}) copy-start(s32[1,1,2048]{2,1,0:T(1,128)} %param.18) | copy-start | bytes 24580
  17.8 5.0 %copy-start.6 = (s32[1,1,2048,1]{2,3,1,0:T(1,128)S(1)}, s32[1,1,2048,1]{2,3,1,0:T(1,128)}, u32[]{:S(2)}) copy-start(s32[1,1,2048,1]{2,3,1,0:T(1,128)} %param.19) | copy-start | bytes 24580
  17.8 5.0 %copy-start.7 = (s32[1,1,2048]{2,1,0:T(1,128)S(1)}, s32[1,1,2048]{2,1,0:T(1,128)}, u32[]{:S(2)}) copy-start(s32[1,1,2048]{2,1,0:T(1,128)} %param.20) | copy-start | bytes 24580
  17.8 5.0 %copy-start.8 = (f32[1,1,2048]{2,1,0:T(1,128)S(1)}, f32[1,1,2048]{2,1,0:T(1,128)}, u32[]{:S(2)}) copy-start(f32[1,1,2048]{2,1,0:T(1,128)} %param.21) | copy-start | bytes 24580
  17.8 5.0 %copy-start.10 = (f32[1,2048]{1,0:T(1,128)S(1)}, f32[1,2048]{1,0:T(1,128)}, u32[]{:S(2)}) copy-start(f32[1,2048]{1,0:T(1,128)} %get-tuple-element.13.refs_10_) | copy-start | bytes 24580
  22.7 0.7 %copy-start.11 = (f32[16]{0:T(128)S(1)}, f32[16]{0:T(128)}, u32[]{:S(2)}) copy-start(f32[16]{0:T(128)} %refs_0_.5) | copy-start | bytes 196
  23.3 0.9 %copy-start.1 = (f32[2,8,16,128]{3,2,1,0:T(8,128)S(1)}, f32[2,8,16,128]{3,2,1,0:T(8,128)}, u32[]{:S(2)}) copy-start(f32[2,8,16,128]{3,2,1,0:T(8,128)} %refs_2_.3) | copy-start | bytes 393220

commit v6 on v5

--- a/solution.py
+++ b/solution.py
@@ -140,9 +140,9 @@
 
 
 def send_kernel(tiles, *refs):
-    sources, (*messages, wair_out) = refs[:8], refs[8:-9]
-    held, sems = refs[-9:-1], refs[-1]
-    air, surface, atm_cell, dest, sea_cell, weight, from_left, from_right = held
+    sources, (*messages, wair_out) = refs[:6], refs[6:-7]
+    held, sems = refs[-7:-1], refs[-1]
+    air, surface, atm_cell, dest, sea_cell, weight = held
     copies = [
         pltpu.make_async_copy(source.at[0, 0] if i == 1 else source, target, sems.at[i])
         for i, (source, target) in enumerate(zip(sources, held))
@@ -161,7 +161,6 @@
     cell = sea_cell[...]
     hot_sea = jnp.where(one_hot(cell % cols, cols), 1.0, 0.0).astype(BF16)
     row = dest[...] * rows + cell // cols
-    strip_tiles = from_left.shape[1] // cols
     for shift in range(tiles):
         target = tile_at(shift, tiles)
         message = messages[shift] if len(messages) > 1 else messages[0].at[target]
@@ -169,13 +168,6 @@
         message[0:rows, :] = s1
         message[rows : 2 * rows, :] = s2
         message[2 * rows : 3 * rows, :] = surface[...]
-        if shift in (1, tiles - 1):
-            near = slice(rows - AH, rows) if shift == 1 else slice(0, AH)
-            at = 3 * rows
-            for ref in (from_left, from_right):
-                for i in range(strip_tiles):
-                    message[at : at + AH, :] = ref[near, i * cols : (i + 1) * cols]
-                    at += AH
 
 
 def strips(cols, slot, width, left_part, right_part):
@@ -199,26 +191,35 @@
     return out + [(mbase, AH), (mbase + AH, OH), (mbase + AH + OH, OH)]
 
 
-def regroup_kernel(slices, from_up, from_down, tiles):
-    for i, (at, width) in enumerate(slices):
-        tiles[i, 0:width, :] = from_down[at : at + width, :]
-        tiles[i, 2 * AH - width : 2 * AH, :] = from_up[at : at + width, :]
-
-
-def final_kernel(tiles, *refs):
-    speed, atm, ocean, depth, wet, kappa, atm_cell, dest, sea_cell, weight, wair, row_tiles, from_left, from_right = refs[:14]
-    messages, (atm_out, ocean_out, us, vs, hs, fs, ms, edge, atm_buf, ocean_buf, sems) = refs[14:-11], refs[-11:]
-    levels = atm.shape[1]
-    rows, cols = atm.shape[2:]
-    tracers = fs.shape[0]
-    each = ocean.shape[1]
+def final_kernel(tiles, parts, *refs):
+    speed_in, atm_in, ocean_in, depth_in, kappa_in = refs[:5]
+    sources, rest = refs[5 : 15 + parts], refs[15 + parts :]
+    atm_out, ocean_out, speed, us, vs, hs, fs, ms = rest[:8]
+    held, (edge, atm_buf, ocean_buf, sems) = rest[8 : 18 + parts], rest[18 + parts :]
+    wet, atm_cell, dest, sea_cell, weight, wair, from_up, from_down, from_left, from_right = held[:10]
+    messages = held[10:]
+    levels = us.shape[0]
+    each = ocean_out.shape[1]
+    tracers = ocean_out.shape[0] * each
+    rows, cols = atm_out.shape[2:]
     slots, lanes = lane_slots(levels, tracers)
+    slices = row_slices(levels, tracers)
     full = rows + 2 * AH
+    block = (slice(None), slice(0, rows), slice(0, cols))
+    pairs = list(zip(sources, held)) + [(speed_in, speed)]
+    pairs += [(atm_in.at[i], ref.at[block]) for i, ref in enumerate((us, vs, hs))]
+    pairs += [(ocean_in.at[i], fs.at[(i, *block)]) for i in range(ocean_out.shape[0])]
+    pairs += [(ref, ms.at[(i, *block[1:])]) for i, ref in ((0, depth_in), (2, kappa_in))]
+    copies = [pltpu.make_async_copy(source, target, sems.at[i]) for i, (source, target) in enumerate(pairs)]
+    for copy in copies:
+        copy.start()
+    for copy in copies:
+        copy.wait()
 
     def message(shift):
         return messages[shift] if len(messages) > 1 else messages[0].at[tile_at(-shift, tiles)]
 
-    surface = ocean[0, 0]
+    surface = fs[0, 0, 0:rows, 0:cols]
     cell = sea_cell[...]
     hot_sea = jnp.where(one_hot(cell % cols, cols), 1.0, 0.0).astype(BF16)
     row = dest[...] * rows + cell // cols
@@ -242,12 +243,17 @@
         edge[i, 0:AH, :] = message(tiles - 1)[at : at + AH, :]
         edge[i, AH : 2 * AH, :] = message(1)[at : at + AH, :]
 
-    def extend(view, value, field, width):
+    def extend(view, field, width):
+        at, high = slices[field]
         slot = slots[field]
-        view[0:rows, 0:cols] = value
-        view[rows:full, 0:cols] = row_tiles[field]
+        view[rows : rows + high, 0:cols] = from_down[at : at + high, :]
+        view[full - high : full, 0:cols] = from_up[at : at + high, :]
         view[0:rows, cols : 2 * cols] = strips(
-            cols, slot, width, lambda t: from_left[:, t * cols : (t + 1) * cols], lambda t: from_right[:, t * cols : (t + 1) * cols]
+            cols,
+            slot,
+            width,
+            lambda t: from_left[:, t * cols : (t + 1) * cols],
+            lambda t: from_right[:, t * cols : (t + 1) * cols],
         )
         view[rows:full, cols : 2 * cols] = strips(cols, slot, width, lambda t: edge[t], lambda t: edge[half + t])
 
@@ -264,33 +270,34 @@
         return pltpu.roll(f, 1, 0)
 
     base = 3 * levels + tracers
-    extend(ms.at[0], depth[...], base, AH)
-    extend(ms.at[1], wet[...].astype(F32), base + 1, AH)
-    extend(ms.at[2], kappa[...], base + 2, AH)
+    ms[1, 0:rows, 0:cols] = wet[...].astype(F32)
+    for i in range(3):
+        extend(ms.at[i], base + i, AH)
     for i in range(tracers):
-        extend(fs.at[i], ocean[i // each, i % each], 3 * levels + i, OH)
+        extend(fs.at[i // each, i % each], 3 * levels + i, OH)
     for level in range(levels):
-        extend(us.at[level], atm[0, level], level, AH)
-        extend(vs.at[level], atm[1, level], levels + level, AH)
-        extend(hs.at[level], atm[2, level], 2 * levels + level, AH)
+        extend(us.at[level], level, AH)
+        extend(vs.at[level], levels + level, AH)
+        extend(hs.at[level], 2 * levels + level, AH)
 
     w = ms[1]
     k = ms[2]
     we, ww, ws, wn = east(w), west(w), south(w), north(w)
     for step in range(OCEAN_STEPS):
         for i in range(tracers):
-            f = fs[i]
+            f = fs[i // each, i % each]
             total = we * (east(f) - f)
             total = total + ww * (west(f) - f)
             total = total + ws * (south(f) - f)
             total = total + wn * (north(f) - f)
             f = f + k * (w * total)
             if step < OCEAN_STEPS - 1:
-                fs[i] = f
+                fs[i // each, i % each] = f
             else:
                 f = f[0:rows, 0:cols]
                 ocean_buf[i // each, i % each] = f + SEA_GAIN * sea_flux if i == 0 else f
-    copies = [pltpu.make_async_copy(ocean_buf, ocean_out, sems.at[0])]
+    used = len(copies)
+    copies = [pltpu.make_async_copy(ocean_buf, ocean_out, sems.at[used])]
     copies[0].start()
 
     d = ms[0]
@@ -315,7 +322,7 @@
                     where = pl.ds(level + 1 - chunk, chunk)
                     copies.append(
                         pltpu.make_async_copy(
-                            atm_buf.at[:, where], atm_out.at[:, where], sems.at[len(copies)]
+                            atm_buf.at[:, where], atm_out.at[:, where], sems.at[used + len(copies)]
                         )
                     )
                     copies[-1].start()
@@ -345,8 +352,6 @@
     _, _, _, message_rows = row_slots(levels, tracers)
     vmem = pl.BlockSpec(memory_space=pltpu.VMEM)
     hbm = pl.BlockSpec(memory_space=pltpu.HBM)
-    smem = pl.BlockSpec(memory_space=pltpu.SMEM)
-    params = pltpu.CompilerParams(vmem_limit_bytes=16 * 1024 * 1024)
     whole = pltpu.CompilerParams(vmem_limit_bytes=64 * 1024 * 1024)
     full = rows + 2 * AH
 
@@ -379,72 +384,63 @@
     from_down = shift(up, "tile", tile_count, -1)
     from_up = shift(down, "tile", tile_count, 1)
 
-    corner_rows = 2 * AH * (lanes // cols)
     by_shift = tile_count <= 4
-    if by_shift:
-        sums = [shape(3 * rows + (corner_rows if s in (1, tile_count - 1) else 0), cols) for s in range(tile_count)]
-    else:
-        sums = [shape(tile_count, 3 * rows + corner_rows, cols)]
+    sums = [shape(3 * rows, cols)] * tile_count if by_shift else [shape(tile_count, 3 * rows, cols)]
     *messages, wair = pl.pallas_call(
         functools.partial(send_kernel, tile_count),
         out_shape=sums + [shape(1, cells)],
-        in_specs=[hbm] * 8,
+        in_specs=[hbm] * 6,
         out_specs=[vmem] * (len(sums) + 1),
         scratch_shapes=[pltpu.VMEM((rows, cols), F32)] * 2
         + [pltpu.VMEM((1, cells), jnp.int32)] * 3
-        + [pltpu.VMEM((1, cells), F32)]
-        + [pltpu.VMEM((rows, lanes), F32)] * 2
-        + [pltpu.SemaphoreType.DMA((8,))],
+        + [pltpu.VMEM((1, cells), F32), pltpu.SemaphoreType.DMA((6,))],
         compiler_params=whole,
         cost_estimate=pl.CostEstimate(flops=0, bytes_accessed=200_000_000, transcendentals=0),
         name="exchange_send",
-    )(air_temp, ocean_state, atm_cell, dest, sea_cell, weight, from_left, from_right)
+    )(air_temp, ocean_state, atm_cell, dest, sea_cell, weight)
+    near = {}
+    for s, low in ((1, rows - AH), (tile_count - 1, 0)):
+        near[s] = [
+            ref[low : low + AH, i * cols : (i + 1) * cols]
+            for ref in (from_left, from_right)
+            for i in range(lanes // cols)
+        ]
     if by_shift:
-        got = messages[:1] + [shift(messages[s], "tile", tile_count, s) for s in range(1, tile_count)]
+        got = messages[:1]
+        for s in range(1, tile_count):
+            joined = jnp.concatenate([messages[s]] + near[s]) if s in near else messages[s]
+            got.append(shift(joined, "tile", tile_count, s))
     else:
-        got = [lax.all_to_all(messages[0], "tile", split_axis=0, concat_axis=0, tiled=True)]
-
-    slices = row_slices(levels, tracers)
-    row_tiles = pl.pallas_call(
-        functools.partial(regroup_kernel, slices),
-        out_shape=shape(len(slices), 2 * AH, cols),
-        in_specs=[vmem] * 2,
-        out_specs=vmem,
-        compiler_params=params,
-        cost_estimate=pl.CostEstimate(flops=0, bytes_accessed=200_000_000, transcendentals=0),
-        name="regroup",
-    )(from_up, from_down)
-
+        corners = jnp.zeros((tile_count, 2 * AH * (lanes // cols), cols), F32)
+        for s in near:
+            corners = corners.at[(lax.axis_index("tile") + s) % tile_count].set(jnp.concatenate(near[s]))
+        joined = jnp.concatenate([messages[0], corners], axis=1)
+        got = [lax.all_to_all(joined, "tile", split_axis=0, concat_axis=0, tiled=True)]
+
+    operands = (wave_speed, atm_state, ocean_state, depth, diffusivity)
+    operands += (wet_mask, atm_cell, dest, sea_cell, weight, wair, from_up, from_down, from_left, from_right, *got)
     return tuple(
         pl.pallas_call(
-            functools.partial(final_kernel, tile_count),
+            functools.partial(final_kernel, tile_count, len(got)),
             out_shape=[shape(*atm_state.shape), shape(*ocean_state.shape)],
-            in_specs=[smem] + [vmem] * (13 + len(got)),
+            in_specs=[hbm] * len(operands),
             out_specs=[hbm] * 2,
-            scratch_shapes=[pltpu.VMEM((levels, full, 2 * cols), F32)] * 3
+            scratch_shapes=[pltpu.SMEM(wave_speed.shape, F32)]
+            + [pltpu.VMEM((levels, full, 2 * cols), F32)] * 3
             + [
-                pltpu.VMEM((tracers, full, 2 * cols), F32),
+                pltpu.VMEM((*ocean_state.shape[:2], full, 2 * cols), F32),
                 pltpu.VMEM((3, full, 2 * cols), F32),
+            ]
+            + [pltpu.VMEM(x.shape, x.dtype) for x in operands[5:]]
+            + [
                 pltpu.VMEM((2 * (lanes // cols), 2 * AH, cols), F32),
                 pltpu.VMEM(atm_state.shape, F32),
                 pltpu.VMEM(ocean_state.shape, F32),
-                pltpu.SemaphoreType.DMA((8,)),
+                pltpu.SemaphoreType.DMA((len(operands) + 10,)),
             ],
-            compiler_params=params,
+            compiler_params=whole,
             name="steps",
-        )(
-            wave_speed,
-            *fields,
-            atm_cell,
-            dest,
-            sea_cell,
-            weight,
-            wair,
-            row_tiles,
-            from_left,
-            from_right,
-            *got,
-        )
+        )(*operands)
     )
 
 

time: 28.2 us -> 27.3 us (0.968)
  local copies, waits for them, and re-layouts: 1.52 us -> 2.75 us
  waiting for transfers between devices: 5.57 us -> 4.74 us
  starting transfers between devices: 10.8 us -> 10.1 us
  Pallas kernels: 9.06 us -> 8.58 us
    slice x0 -> x2, local copies, waits for them, and re-layouts: none -> 1.4 us  [on_device(): ref[low:low + AH, i * cols:(i + 1) * cols]]
    ppermute x7, waiting for transfers between devices: 5.57 us -> 4.74 us  [shift(): lax.ppermute(value, axes, [(i, (i + by) % count) for i in range(count)])]
    ppermute x7, starting transfers between devices: 10.8 us -> 10.1 us  [shift(): lax.ppermute(value, axes, [(i, (i + by) % count) for i in range(count)])]
    pallas_call x2 -> x1, Pallas kernels: 4.55 us -> 4.16 us  [on_device(): pl.pallas_call(functools.partial(final_kernel, tile_count, len(got)), out...]
    unnamed x24 -> x8, local copies, waits for them, and re-layouts: 1.52 us -> 1.26 us
  transfers between devices with their start and end apart: 7 -> 7, of which waited for: 2 -> 1; matrix products, arithmetic and copies ran while one was open for 0% -> 6% of each run, Pallas kernels for 13% -> 9%
where the time goes in v6:
time: 27.3 us; the launch traced here: 26.8 us
  starting transfers between devices  10.1 us (37%)
  Pallas kernels  8.58 us (31%)
  waiting for transfers between devices  4.74 us (17%)
  local copies, waits for them, and re-layouts  2.75 us (10%)
  between operations  0.68 us (2%)
    ppermute x7, starting transfers between devices, shift(): lax.ppermute(value, axes, [(i, (i + by) % count) for i in range(count)])  10.1 us
    ppermute x7, waiting for transfers between devices, shift(): lax.ppermute(value, axes, [(i, (i + by) % count) for i in range(count)])  4.74 us
    pallas_call x1, Pallas kernels, on_device(): pl.pallas_call(functools.partial(final_kernel, tile_count, len(got)), out...  4.16 us
    pallas_call x1, Pallas kernels, on_device(): pl.pallas_call(functools.partial(send_kernel, tile_count), out_shape=sums...  2.38 us
    pallas_call x1, Pallas kernels, on_device(): pl.pallas_call(pack_kernel, out_shape=[shape(message_rows, cols)] * 2 + [...  2.04 us
    slice x2, local copies, waits for them, and re-layouts, on_device(): ref[low:low + AH, i * cols:(i + 1) * cols]  1.4 us
    unnamed x8, local copies, waits for them, and re-layouts  1.26 us
  transfers between devices with their start and end apart: 7, of which 1 were waited for; matrix products, arithmetic and copies ran while one was open for 6% of the time, Pallas kernels for 9%

profile of v6, /device:TPU:0, one launch (start us, length us, event | category | flops | bytes accessed | tf_op | source)
XLA Modules:
  0.0 26.8 jit_solution(14230984767180427341)
XLA Ops:
  0.6 2.0 %pack.1 = (f32[200,128]{1,0:T(8,128)}, f32[200,128]{1,0:T(8,128)}, f32[16,256]{1,0:T(8,128)}, f32[16,256]{1,0:T(8,128)}) custom-call(f32[3,16,16,128]{3,2,1,0:T(8,128)} %refs_1_.5, f32[2,8,16,128]{3,2,1,0:T(8,128)} %refs_2_.3, f32[16,128]{1,0:T(8,128)} %refs_3_.3, s32[16,128]{1,0:T(8,128)} %refs_5_.1, f32[16,128]{1,0:T(8,128)} %refs_4_.3), custom_call_target="tpu_custom_call" | custom-call | tf_op jit(solution)/shard_map/pack/pallas_call | solution.py:362
  2.7 0.5 %collective-permute-start.2 = (f32[16,256]{1,0:T(8,128)}, f32[16,256]{1,0:T(8,128)}, u32[]{:S(2)}, u32[]{:S(2)}) collective-permute-start(f32[16,256]{1,0:T(8,128)} %get-tuple-element.14), channel_id=1, source_target_pairs={{0,1},{1,2},{2,3},{3,0},{4,5},{5,6},{6,7},{7,4},{8,9},{9,10},{10,1... | collective-permute-start | bytes 49160 | tf_op jit(solution)/shard_map/ppermute | solution.py:380
  3.2 2.0 %collective-permute-start.3 = (f32[16,256]{1,0:T(8,128)}, f32[16,256]{1,0:T(8,128)}, u32[]{:S(2)}, u32[]{:S(2)}) collective-permute-start(f32[16,256]{1,0:T(8,128)} %get-tuple-element.15), channel_id=1, source_target_pairs={{0,3},{1,0},{2,1},{3,2},{4,7},{5,4},{6,5},{7,6},{8,11},{9,8},{10,9... | collective-permute-start | bytes 49160 | tf_op jit(solution)/shard_map/ppermute | solution.py:380
  5.2 2.3 %collective-permute-start = (f32[200,128]{1,0:T(8,128)}, f32[200,128]{1,0:T(8,128)}, u32[]{:S(2)}, u32[]{:S(2)}) collective-permute-start(f32[200,128]{1,0:T(8,128)} %get-tuple-element.12), channel_id=1, source_target_pairs={{0,4},{4,8},{8,12},{12,0},{1,5},{5,9},{9,13},{13,1},{2,6},{6,10},{... | collective-permute-start | bytes 307208 | tf_op jit(solution)/shard_map/ppermute | solution.py:380
  7.5 2.0 %collective-permute-start.1 = (f32[200,128]{1,0:T(8,128)}, f32[200,128]{1,0:T(8,128)}, u32[]{:S(2)}, u32[]{:S(2)}) collective-permute-start(f32[200,128]{1,0:T(8,128)} %get-tuple-element.13), channel_id=1, source_target_pairs={{0,12},{4,0},{8,4},{12,8},{1,13},{5,1},{9,5},{13,9},{2,14},{6,2},{... | collective-permute-start | bytes 307208 | tf_op jit(solution)/shard_map/ppermute | solution.py:380
  9.5 2.4 %exchange_send.1 = (f32[48,128]{1,0:T(8,128)}, f32[48,128]{1,0:T(8,128)}, f32[48,128]{1,0:T(8,128)}, f32[48,128]{1,0:T(8,128)}, f32[1,2048]{1,0:T(1,128)}) custom-call(f32[16,128]{1,0:T(8,128)} %refs_0_.3, f32[2,8,16,128]{3,2,1,0:T(8,128)} %refs_2_.3, s32[1,2048]{1,0:T(1,128)} %bitcast.4, s32[1,2048]{1,0:T(1,128)} %bitcast.6, s32[1,2048]{1,0:T(1,128)} %bitcast.8, ...), custom_call_target="tpu_custom_call" | custom-call | bytes 200000000 | tf_op jit(solution)/shard_map/exchange_send/pallas_call | solution.py:389
  11.9 0.0 copy-start.1
  11.9 0.0 collective-permute-done.2.refs_13_
  11.9 0.7 %fusion.1 = (f32[4,128]{1,0:T(4,128)S(1)}, f32[4,128]{1,0:T(4,128)S(1)}, f32[4,128]{1,0:T(4,128)S(1)}, f32[4,128]{1,0:T(4,128)S(1)}) fusion(f32[16,256]{1,0:T(8,128)} %collective-permute-done.2.refs_13_), kind=kLoop, calls=%fused_computation.1 | loop fusion | bytes 16384 | tf_op jit(solution)/shard_map/slice | solution.py:404
  12.6 0.0 collective-permute-done.3.refs_14_
  12.6 0.7 %fusion = (f32[4,128]{1,0:T(4,128)S(1)}, f32[4,128]{1,0:T(4,128)S(1)}, f32[4,128]{1,0:T(4,128)S(1)}, f32[4,128]{1,0:T(4,128)S(1)}) fusion(f32[16,256]{1,0:T(8,128)} %collective-permute-done.3.refs_14_), kind=kLoop, calls=%fused_computation | loop fusion | bytes 16384 | tf_op jit(solution)/shard_map/slice | solution.py:404
  13.3 0.0 copy-done.1
  13.3 0.0 copy-start
  13.4 0.0 collective-permute-start.4
  13.4 0.6 %copy-done = f32[48,128]{1,0:T(8,128)S(1)} copy-done((f32[48,128]{1,0:T(8,128)S(1)}, f32[48,128]{1,0:T(8,128)}, u32[]{:S(2)}) %copy-start) | copy-done | bytes 24600
  14.1 0.0 copy-start.3
  14.1 3.2 %collective-permute-start.6 = (f32[64,128]{1,0:T(8,128)S(1)}, f32[64,128]{1,0:T(8,128)}, u32[]{:S(2)}, u32[]{:S(2)}) collective-permute-start(f32[64,128]{1,0:T(8,128)S(1)} %concatenate.7), channel_id=1, source_target_pairs={{0,12},{4,0},{8,4},{12,8},{1,13},{5,1},{9,5},{13,9},{2,14},{6,2},{... | collective-permute-start | bytes 98312 | tf_op jit(solution)/shard_map/ppermute | solution.py:380
  17.3 0.0 copy-done.3
  17.3 0.0 collective-permute-start.5
  17.3 4.7 %collective-permute-done.5.refs_17_ = f32[48,128]{1,0:T(8,128)S(1)} collective-permute-done((f32[48,128]{1,0:T(8,128)S(1)}, f32[48,128]{1,0:T(8,128)S(1)}, u32[]{:S(2)}, u32[]{:S(2)}) %collective-permute-start.5) | collective-permute-done | bytes 24608 | tf_op jit(solution)/shard_map/ppermute | solution.py:380
  22.1 0.0 copy-start.2
  22.1 0.0 collective-permute-done.4.refs_16_
  22.1 0.0 collective-permute-done.6.refs_18_
  22.1 0.6 %copy-done.2 = f32[48,128]{1,0:T(8,128)} copy-done((f32[48,128]{1,0:T(8,128)}, f32[48,128]{1,0:T(8,128)S(1)}, u32[]{:S(2)}) %copy-start.2) | copy-done | bytes 24600
  22.7 0.0 collective-permute-done.refs_11_
  22.7 0.0 collective-permute-done.1.refs_12_
  22.7 4.2 %steps.1 = (f32[3,16,16,128]{3,2,1,0:T(8,128)}, f32[2,8,16,128]{3,2,1,0:T(8,128)}) custom-call(f32[16]{0:T(128)} %refs_0_.5, f32[3,16,16,128]{3,2,1,0:T(8,128)} %refs_1_.5, f32[2,8,16,128]{3,2,1,0:T(8,128)} %refs_2_.3, f32[16,128]{1,0:T(8,128)} %refs_3_.3, f32[16,128]{1,0:T(8,128)} %refs_4_.3, s32[16,128]{1,0:T(8,128)} %refs_5_.1, s32[1,2048]{1,0:T(1,128)} %bitcast.5, ...), custom_call_target="tpu_custom_call" | custom-call | tf_op jit(solution)/shard_map/steps/pallas_call | solution.py:423
  (2 shorter events, 0.1 us)
Async XLA Ops:
  2.7 9.3 %collective-permute-start.2 = (f32[16,256]{1,0:T(8,128)}, f32[16,256]{1,0:T(8,128)}, u32[]{:S(2)}, u32[]{:S(2)}) collective-permute-start(f32[16,256]{1,0:T(8,128)} %get-tuple-element.14), channel_id=1, source_target_pairs={{0,1},{1,2},{2,3},{3,0},{4,5},{5,6},{6,7},{7,4},{8,9},{9,10},{10,1... | collective-permute-start | bytes 49160 | tf_op jit(solution)/shard_map/ppermute | solution.py:380
  3.2 9.5 %collective-permute-start.3 = (f32[16,256]{1,0:T(8,128)}, f32[16,256]{1,0:T(8,128)}, u32[]{:S(2)}, u32[]{:S(2)}) collective-permute-start(f32[16,256]{1,0:T(8,128)} %get-tuple-element.15), channel_id=1, source_target_pairs={{0,3},{1,0},{2,1},{3,2},{4,7},{5,4},{6,5},{7,6},{8,11},{9,8},{10,9... | collective-permute-start | bytes 49160 | tf_op jit(solution)/shard_map/ppermute | solution.py:380
  5.2 17.5 %collective-permute-start = (f32[200,128]{1,0:T(8,128)}, f32[200,128]{1,0:T(8,128)}, u32[]{:S(2)}, u32[]{:S(2)}) collective-permute-start(f32[200,128]{1,0:T(8,128)} %get-tuple-element.12), channel_id=1, source_target_pairs={{0,4},{4,8},{8,12},{12,0},{1,5},{5,9},{9,13},{13,1},{2,6},{6,10},{... | collective-permute-start | bytes 307208 | tf_op jit(solution)/shard_map/ppermute | solution.py:380
  7.5 15.2 %collective-permute-start.1 = (f32[200,128]{1,0:T(8,128)}, f32[200,128]{1,0:T(8,128)}, u32[]{:S(2)}, u32[]{:S(2)}) collective-permute-start(f32[200,128]{1,0:T(8,128)} %get-tuple-element.13), channel_id=1, source_target_pairs={{0,12},{4,0},{8,4},{12,8},{1,13},{5,1},{9,5},{13,9},{2,14},{6,2},{... | collective-permute-start | bytes 307208 | tf_op jit(solution)/shard_map/ppermute | solution.py:380
  11.9 1.4 %copy-start.1 = (f32[48,128]{1,0:T(8,128)S(1)}, f32[48,128]{1,0:T(8,128)}, u32[]{:S(2)}) copy-start(f32[48,128]{1,0:T(8,128)} %get-tuple-element.17) | copy-start | bytes 73732
  13.3 0.7 %copy-start = (f32[48,128]{1,0:T(8,128)S(1)}, f32[48,128]{1,0:T(8,128)}, u32[]{:S(2)}) copy-start(f32[48,128]{1,0:T(8,128)} %get-tuple-element.19) | copy-start | bytes 73732
  13.4 8.7 %collective-permute-start.4 = (f32[64,128]{1,0:T(8,128)S(1)}, f32[64,128]{1,0:T(8,128)}, u32[]{:S(2)}, u32[]{:S(2)}) collective-permute-start(f32[64,128]{1,0:T(8,128)S(1)} %concatenate.6), channel_id=1, source_target_pairs={{0,4},{4,8},{8,12},{12,0},{1,5},{5,9},{9,13},{13,1},{2,6},{6,10},{... | collective-permute-start | bytes 98312 | tf_op jit(solution)/shard_map/ppermute | solution.py:380
  14.1 3.2 %copy-start.3 = (f32[48,128]{1,0:T(8,128)S(1)}, f32[48,128]{1,0:T(8,128)}, u32[]{:S(2)}) copy-start(f32[48,128]{1,0:T(8,128)} %get-tuple-element.18) | copy-start | bytes 73732
  14.1 7.9 %collective-permute-start.6 = (f32[64,128]{1,0:T(8,128)S(1)}, f32[64,128]{1,0:T(8,128)}, u32[]{:S(2)}, u32[]{:S(2)}) collective-permute-start(f32[64,128]{1,0:T(8,128)S(1)} %concatenate.7), channel_id=1, source_target_pairs={{0,12},{4,0},{8,4},{12,8},{1,13},{5,1},{9,5},{13,9},{2,14},{6,2},{... | collective-permute-start | bytes 98312 | tf_op jit(solution)/shard_map/ppermute | solution.py:380
  17.3 4.7 %collective-permute-start.5 = (f32[48,128]{1,0:T(8,128)S(1)}, f32[48,128]{1,0:T(8,128)S(1)}, u32[]{:S(2)}, u32[]{:S(2)}) collective-permute-start(f32[48,128]{1,0:T(8,128)S(1)} %copy-done.3), channel_id=1, source_target_pairs={{0,8},{4,12},{8,0},{12,4},{1,9},{5,13},{9,1},{13,5},{2,10},{6,14},... | collective-permute-start | bytes 73736 | tf_op jit(solution)/shard_map/ppermute | solution.py:380
  22.1 0.6 %copy-start.2 = (f32[48,128]{1,0:T(8,128)}, f32[48,128]{1,0:T(8,128)S(1)}, u32[]{:S(2)}) copy-start(f32[48,128]{1,0:T(8,128)S(1)} %collective-permute-done.5.refs_17_) | copy-start | bytes 73732

commit v7 on v6

--- a/solution.py
+++ b/solution.py
@@ -135,16 +135,11 @@
     return out
 
 
-def tile_at(shift, tiles):
-    return lax.rem(lax.axis_index("tile") + shift % tiles, tiles)
-
-
-def send_kernel(tiles, *refs):
-    sources, (*messages, wair_out) = refs[:6], refs[6:-7]
-    held, sems = refs[-7:-1], refs[-1]
-    air, surface, atm_cell, dest, sea_cell, weight = held
+def send_kernel(*refs):
+    sources, (sums, wair_out), held, sems = refs[:5], refs[5:7], refs[7:12], refs[12]
+    air, atm_cell, dest, sea_cell, weight = held
     copies = [
-        pltpu.make_async_copy(source.at[0, 0] if i == 1 else source, target, sems.at[i])
+        pltpu.make_async_copy(source, target, sems.at[i])
         for i, (source, target) in enumerate(zip(sources, held))
     ]
     for copy in copies:
@@ -161,13 +156,10 @@
     cell = sea_cell[...]
     hot_sea = jnp.where(one_hot(cell % cols, cols), 1.0, 0.0).astype(BF16)
     row = dest[...] * rows + cell // cols
-    for shift in range(tiles):
-        target = tile_at(shift, tiles)
-        message = messages[shift] if len(messages) > 1 else messages[0].at[target]
-        s1, s2 = scatter_rows([wair, w], one_hot(row - target * rows, rows), hot_sea)
-        message[0:rows, :] = s1
-        message[rows : 2 * rows, :] = s2
-        message[2 * rows : 3 * rows, :] = surface[...]
+    for tile in range(sums.shape[0]):
+        s1, s2 = scatter_rows([wair, w], one_hot(row - tile * rows, rows), hot_sea)
+        sums[tile, 0:rows, :] = s1
+        sums[tile, rows : 2 * rows, :] = s2
 
 
 def strips(cols, slot, width, left_part, right_part):
@@ -191,13 +183,15 @@
     return out + [(mbase, AH), (mbase + AH, OH), (mbase + AH + OH, OH)]
 
 
-def final_kernel(tiles, parts, *refs):
-    speed_in, atm_in, ocean_in, depth_in, kappa_in = refs[:5]
-    sources, rest = refs[5 : 15 + parts], refs[15 + parts :]
+def final_kernel(*refs):
+    speed_in, atm_in, ocean_in, depth_in, kappa_in, left_all, right_all = refs[:7]
+    sources, rest = refs[7:19], refs[19:]
     atm_out, ocean_out, speed, us, vs, hs, fs, ms = rest[:8]
-    held, (edge, atm_buf, ocean_buf, sems) = rest[8 : 18 + parts], rest[18 + parts :]
-    wet, atm_cell, dest, sea_cell, weight, wair, from_up, from_down, from_left, from_right = held[:10]
-    messages = held[10:]
+    held, (far, edge, atm_buf, ocean_buf, sems) = rest[8:20], rest[20:]
+    wet, atm_cell, dest, sea_cell, weight, wair, sst, sums, from_up, from_down, from_left, from_right = held
+    tiles = sst.shape[0]
+    me = lax.axis_index("tile")
+    above, below = lax.rem(me + tiles - 1, tiles), lax.rem(me + 1, tiles)
     levels = us.shape[0]
     each = ocean_out.shape[1]
     tracers = ocean_out.shape[0] * each
@@ -210,28 +204,23 @@
     pairs += [(atm_in.at[i], ref.at[block]) for i, ref in enumerate((us, vs, hs))]
     pairs += [(ocean_in.at[i], fs.at[(i, *block)]) for i in range(ocean_out.shape[0])]
     pairs += [(ref, ms.at[(i, *block[1:])]) for i, ref in ((0, depth_in), (2, kappa_in))]
+    part = far.shape[2]
+    for i, ref in enumerate((left_all, right_all)):
+        pairs += [(ref.at[below, 0:part], far.at[i, 0]), (ref.at[above, rows - part : rows], far.at[i, 1])]
     copies = [pltpu.make_async_copy(source, target, sems.at[i]) for i, (source, target) in enumerate(pairs)]
     for copy in copies:
         copy.start()
     for copy in copies:
         copy.wait()
-
-    def message(shift):
-        return messages[shift] if len(messages) > 1 else messages[0].at[tile_at(-shift, tiles)]
 
     surface = fs[0, 0, 0:rows, 0:cols]
     cell = sea_cell[...]
     hot_sea = jnp.where(one_hot(cell % cols, cols), 1.0, 0.0).astype(BF16)
     row = dest[...] * rows + cell // cols
-    s1, s2 = message(0)[0:rows, :], message(0)[rows : 2 * rows, :]
     sstx = jnp.zeros(cell.shape, F32)
-    for shift in range(tiles):
-        if shift:
-            s1 = s1 + message(shift)[0:rows, :]
-            s2 = s2 + message(shift)[rows : 2 * rows, :]
-        table = message(shift)[2 * rows : 3 * rows, :]
-        sstx = sstx + gather_rows(table, one_hot(row - tile_at(-shift, tiles) * rows, rows), hot_sea)
-    sea_flux = s1 - surface * s2
+    for tile in range(tiles):
+        sstx = sstx + gather_rows(sst[tile], one_hot(row - tile * rows, rows), hot_sea)
+    sea_flux = sums[0:rows, :] - surface * sums[rows : 2 * rows, :]
     flux = wair[...] - weight[...] * sstx
     cell = atm_cell[...]
     hot_atm = jnp.where(one_hot(cell % cols, cols), 1.0, 0.0).astype(BF16)
@@ -239,9 +228,9 @@
 
     half = lanes // cols
     for i in range(2 * half):
-        at = 3 * rows + AH * i
-        edge[i, 0:AH, :] = message(tiles - 1)[at : at + AH, :]
-        edge[i, AH : 2 * AH, :] = message(1)[at : at + AH, :]
+        where = slice(i % half * cols, (i % half + 1) * cols)
+        edge[i, 0:AH, :] = far[i // half, 0, 0:AH, where]
+        edge[i, AH : 2 * AH, :] = far[i // half, 1, part - AH : part, where]
 
     def extend(view, field, width):
         at, high = slices[field]
@@ -384,46 +373,30 @@
     from_down = shift(up, "tile", tile_count, -1)
     from_up = shift(down, "tile", tile_count, 1)
 
-    by_shift = tile_count <= 4
-    sums = [shape(3 * rows, cols)] * tile_count if by_shift else [shape(tile_count, 3 * rows, cols)]
-    *messages, wair = pl.pallas_call(
-        functools.partial(send_kernel, tile_count),
-        out_shape=sums + [shape(1, cells)],
-        in_specs=[hbm] * 6,
-        out_specs=[vmem] * (len(sums) + 1),
-        scratch_shapes=[pltpu.VMEM((rows, cols), F32)] * 2
+    sums, wair = pl.pallas_call(
+        send_kernel,
+        out_shape=[shape(tile_count, 2 * rows, cols), shape(1, cells)],
+        in_specs=[hbm] * 5,
+        out_specs=[vmem] * 2,
+        scratch_shapes=[pltpu.VMEM((rows, cols), F32)]
         + [pltpu.VMEM((1, cells), jnp.int32)] * 3
-        + [pltpu.VMEM((1, cells), F32), pltpu.SemaphoreType.DMA((6,))],
+        + [pltpu.VMEM((1, cells), F32), pltpu.SemaphoreType.DMA((5,))],
         compiler_params=whole,
-        cost_estimate=pl.CostEstimate(flops=0, bytes_accessed=200_000_000, transcendentals=0),
+        cost_estimate=pl.CostEstimate(flops=0, bytes_accessed=20_000_000, transcendentals=0),
         name="exchange_send",
-    )(air_temp, ocean_state, atm_cell, dest, sea_cell, weight)
-    near = {}
-    for s, low in ((1, rows - AH), (tile_count - 1, 0)):
-        near[s] = [
-            ref[low : low + AH, i * cols : (i + 1) * cols]
-            for ref in (from_left, from_right)
-            for i in range(lanes // cols)
-        ]
-    if by_shift:
-        got = messages[:1]
-        for s in range(1, tile_count):
-            joined = jnp.concatenate([messages[s]] + near[s]) if s in near else messages[s]
-            got.append(shift(joined, "tile", tile_count, s))
-    else:
-        corners = jnp.zeros((tile_count, 2 * AH * (lanes // cols), cols), F32)
-        for s in near:
-            corners = corners.at[(lax.axis_index("tile") + s) % tile_count].set(jnp.concatenate(near[s]))
-        joined = jnp.concatenate([messages[0], corners], axis=1)
-        got = [lax.all_to_all(joined, "tile", split_axis=0, concat_axis=0, tiled=True)]
-
-    operands = (wave_speed, atm_state, ocean_state, depth, diffusivity)
-    operands += (wet_mask, atm_cell, dest, sea_cell, weight, wair, from_up, from_down, from_left, from_right, *got)
+    )(air_temp, atm_cell, dest, sea_cell, weight)
+    sums = lax.psum_scatter(sums, "tile", scatter_dimension=0)
+    sst = lax.all_gather(ocean_state[0, 0], "tile")
+    left_all = lax.all_gather(from_left, "tile")
+    right_all = lax.all_gather(from_right, "tile")
+
+    moved = (wave_speed, atm_state, ocean_state, depth, diffusivity, left_all, right_all)
+    kept = (wet_mask, atm_cell, dest, sea_cell, weight, wair, sst, sums, from_up, from_down, from_left, from_right)
     return tuple(
         pl.pallas_call(
-            functools.partial(final_kernel, tile_count, len(got)),
+            final_kernel,
             out_shape=[shape(*atm_state.shape), shape(*ocean_state.shape)],
-            in_specs=[hbm] * len(operands),
+            in_specs=[hbm] * (len(moved) + len(kept)),
             out_specs=[hbm] * 2,
             scratch_shapes=[pltpu.SMEM(wave_speed.shape, F32)]
             + [pltpu.VMEM((levels, full, 2 * cols), F32)] * 3
@@ -431,16 +404,17 @@
                 pltpu.VMEM((*ocean_state.shape[:2], full, 2 * cols), F32),
                 pltpu.VMEM((3, full, 2 * cols), F32),
             ]
-            + [pltpu.VMEM(x.shape, x.dtype) for x in operands[5:]]
+            + [pltpu.VMEM(x.shape, x.dtype) for x in kept]
             + [
+                pltpu.VMEM((2, 2, 8, lanes), F32),
                 pltpu.VMEM((2 * (lanes // cols), 2 * AH, cols), F32),
                 pltpu.VMEM(atm_state.shape, F32),
                 pltpu.VMEM(ocean_state.shape, F32),
-                pltpu.SemaphoreType.DMA((len(operands) + 10,)),
+                pltpu.SemaphoreType.DMA((len(moved) + len(kept) + 20,)),
             ],
             compiler_params=whole,
             name="steps",
-        )(*operands)
+        )(*moved, *kept)
     )
 
 

time: 27.3 us -> 71.4 us (2.62)
  blocking collectives: 0 us -> 41.6 us
  between operations: 0.68 us -> 14.1 us
  waiting for transfers between devices: 4.74 us -> 0.05 us
  starting transfers between devices: 10.1 us -> 5.86 us
  local copies, waits for them, and re-layouts: 2.75 us -> 0.71 us
    all_gather x0 -> x3, blocking collectives: none -> 41.6 us  [the longest x1 13.9 us: on_device(): left_all = lax.all_gather(from_left, 'tile')]
    ppermute x7 -> x4, waiting for transfers between devices: 4.74 us -> 0.01 us  [shift(): lax.ppermute(value, axes, [(i, (i + by) % count) for i in range(count)])]
    ppermute x7 -> x4, starting transfers between devices: 10.1 us -> 5.83 us  [shift(): lax.ppermute(value, axes, [(i, (i + by) % count) for i in range(count)])]
    unnamed x8 -> x4, local copies, waits for them, and re-layouts: 1.26 us -> 0.01 us
  transfers between devices with their start and end apart: 7 -> 5, of which waited for: 1 -> 0; matrix products, arithmetic and copies ran while one was open for 6% -> 1% of each run, Pallas kernels for 9% -> 3%
where the time goes in v7:
time: 71.4 us; the launch traced here: 71 us
  blocking collectives  41.6 us (58%)
  between operations  14.1 us (20%)
  Pallas kernels  8.68 us (12%)
  starting transfers between devices  5.86 us (8%)
    all_gather x1, blocking collectives, on_device(): left_all = lax.all_gather(from_left, 'tile')  13.9 us
    all_gather x1, blocking collectives, on_device(): right_all = lax.all_gather(from_right, 'tile')  13.9 us
    all_gather x1, blocking collectives, on_device(): sst = lax.all_gather(ocean_state[0, 0], 'tile')  13.8 us
    ppermute x4, starting transfers between devices, shift(): lax.ppermute(value, axes, [(i, (i + by) % count) for i in range(count)])  5.83 us
    pallas_call x1, Pallas kernels, on_device(): pl.pallas_call(final_kernel, out_shape=[shape(*atm_state.shape), shape(*o...  4.29 us
    pallas_call x1, Pallas kernels, on_device(): pl.pallas_call(send_kernel, out_shape=[shape(tile_count, 2 * rows, cols),...  2.35 us
    pallas_call x1, Pallas kernels, on_device(): pl.pallas_call(pack_kernel, out_shape=[shape(message_rows, cols)] * 2 + [...  2.04 us
  transfers between devices with their start and end apart: 5, of which 0 were waited for; matrix products, arithmetic and copies ran while one was open for 1% of the time, Pallas kernels for 3%

profile of v7, /device:TPU:0, one launch (start us, length us, event | category | flops | bytes accessed | tf_op | source)
XLA Modules:
  0.0 71.0 jit_solution(9651489973960369829)
XLA Ops:
  7.2 0.0 reduce-scatter.2.cloned.1.call-start
  7.2 2.4 %exchange_send.1 = (f32[4,32,128]{2,1,0:T(8,128)}, f32[1,2048]{1,0:T(1,128)}) custom-call(f32[16,128]{1,0:T(8,128)} %refs_0_.4, s32[1,2048]{1,0:T(1,128)} %bitcast.11, s32[1,2048]{1,0:T(1,128)} %bitcast.13, s32[1,2048]{1,0:T(1,128)} %bitcast.15, f32[1,2048]{1,0:T(1,128)} %bitcast.17), custom_call_target="tpu_custom_call" | custom-call | bytes 20000000 | tf_op jit(solution)/shard_map/exchange_send/pallas_call | solution.py:376
  9.6 0.0 reduce-scatter.2.cloned.1.call-update
  9.6 2.0 %pack.1 = (f32[200,128]{1,0:T(8,128)}, f32[200,128]{1,0:T(8,128)}, f32[16,256]{1,0:T(8,128)}, f32[16,256]{1,0:T(8,128)}) custom-call(f32[3,16,16,128]{3,2,1,0:T(8,128)} %refs_1_.3, f32[2,8,16,128]{3,2,1,0:T(8,128)} %refs_2_.3, f32[16,128]{1,0:T(8,128)} %refs_3_.3, s32[16,128]{1,0:T(8,128)} %refs_7_.1, f32[16,128]{1,0:T(8,128)} %refs_4_.3), custom_call_target="tpu_custom_call" | custom-call | tf_op jit(solution)/shard_map/pack/pallas_call | solution.py:351
  11.6 3.1 %collective-permute-start.2 = (f32[200,128]{1,0:T(8,128)}, f32[200,128]{1,0:T(8,128)}, u32[]{:S(2)}, u32[]{:S(2)}) collective-permute-start(f32[200,128]{1,0:T(8,128)} %get-tuple-element.12), channel_id=1, source_target_pairs={{0,4},{4,8},{8,12},{12,0},{1,5},{5,9},{9,13},{13,1},{2,6},{6,10},{... | collective-permute-start | bytes 307208 | tf_op jit(solution)/shard_map/ppermute | solution.py:369
  14.7 2.1 %collective-permute-start.3 = (f32[200,128]{1,0:T(8,128)}, f32[200,128]{1,0:T(8,128)}, u32[]{:S(2)}, u32[]{:S(2)}) collective-permute-start(f32[200,128]{1,0:T(8,128)} %get-tuple-element.13), channel_id=1, source_target_pairs={{0,12},{4,0},{8,4},{12,8},{1,13},{5,1},{9,5},{13,9},{2,14},{6,2},{... | collective-permute-start | bytes 307208 | tf_op jit(solution)/shard_map/ppermute | solution.py:369
  16.8 0.7 collective-permute-start.1
  17.5 0.0 collective-permute-start
  17.5 0.7 slice.3
  18.2 13.8 %all-gather.2 = f32[4,1,16,128]{3,2,1,0:T(8,128)} all-gather(f32[1,1,16,128]{3,2,1,0:T(8,128)S(1)} %slice.3), channel_id=4, replica_groups=mesh['member'=2,'tile'=4,'sub'=2,'comp'=2] {'tile'}, dimensions={0}, use_global_device_ids=true | all-gather | bytes 40960 | tf_op jit(solution)/shard_map/all_gather | solution.py:389
  32.0 0.0 collective-permute-done.1.refs_18_
  32.0 0.0 copy-start
  32.0 13.9 %all-gather.1 = f32[64,256]{1,0:T(8,128)} all-gather(f32[16,256]{1,0:T(8,128)S(1)} %collective-permute-done.1.refs_18_), channel_id=3, replica_groups=mesh['member'=2,'tile'=4,'sub'=2,'comp'=2] {'tile'}, dimensions={0}, use_global_device_ids=true | all-gather | bytes 81920 | tf_op jit(solution)/shard_map/all_gather | solution.py:391
  45.9 0.0 copy-done
  45.9 0.0 collective-permute-done.refs_17_
  45.9 0.0 copy-start.1
  45.9 13.9 %all-gather = f32[64,256]{1,0:T(8,128)} all-gather(f32[16,256]{1,0:T(8,128)S(1)} %collective-permute-done.refs_17_), channel_id=2, replica_groups=mesh['member'=2,'tile'=4,'sub'=2,'comp'=2] {'tile'}, dimensions={0}, use_global_device_ids=true | all-gather | bytes 81920 | tf_op jit(solution)/shard_map/all_gather | solution.py:390
  59.8 0.0 copy-done.1
  59.8 0.0 collective-permute-done.2.refs_15_
  59.8 0.0 collective-permute-done.3.refs_16_
  59.8 0.0 reduce-scatter.2.cloned.1.call-done
  59.8 4.3 %steps.1 = (f32[3,16,16,128]{3,2,1,0:T(8,128)}, f32[2,8,16,128]{3,2,1,0:T(8,128)}) custom-call(f32[16]{0:T(128)} %refs_0_.5, f32[3,16,16,128]{3,2,1,0:T(8,128)} %refs_1_.3, f32[2,8,16,128]{3,2,1,0:T(8,128)} %refs_2_.3, f32[16,128]{1,0:T(8,128)} %refs_3_.3, f32[16,128]{1,0:T(8,128)} %refs_4_.3, f32[4,16,256]{2,1,0:T(8,128)} %bitcast.9, ...), custom_call_target="tpu_custom_call" | custom-call | tf_op jit(solution)/shard_map/steps/pallas_call | solution.py:396
Async XLA Ops:
  7.2 52.6 %reduce-scatter.2.cloned.1.call-start = ((), (), s32[]{:S(2)}) async-start(), calls=%async_computation.1 | async-start | bytes 81920 | tf_op jit(solution)/shard_map/reduce_scatter | solution.py:388
  11.6 48.1 %collective-permute-start.2 = (f32[200,128]{1,0:T(8,128)}, f32[200,128]{1,0:T(8,128)}, u32[]{:S(2)}, u32[]{:S(2)}) collective-permute-start(f32[200,128]{1,0:T(8,128)} %get-tuple-element.12), channel_id=1, source_target_pairs={{0,4},{4,8},{8,12},{12,0},{1,5},{5,9},{9,13},{13,1},{2,6},{6,10},{... | collective-permute-start | bytes 307208 | tf_op jit(solution)/shard_map/ppermute | solution.py:369
  14.7 45.1 %collective-permute-start.3 = (f32[200,128]{1,0:T(8,128)}, f32[200,128]{1,0:T(8,128)}, u32[]{:S(2)}, u32[]{:S(2)}) collective-permute-start(f32[200,128]{1,0:T(8,128)} %get-tuple-element.13), channel_id=1, source_target_pairs={{0,12},{4,0},{8,4},{12,8},{1,13},{5,1},{9,5},{13,9},{2,14},{6,2},{... | collective-permute-start | bytes 307208 | tf_op jit(solution)/shard_map/ppermute | solution.py:369
  16.8 15.2 %collective-permute-start.1 = (f32[16,256]{1,0:T(8,128)}, f32[16,256]{1,0:T(8,128)S(1)}, u32[]{:S(2)}, u32[]{:S(2)}) collective-permute-start(f32[16,256]{1,0:T(8,128)} %get-tuple-element.9), channel_id=1, source_target_pairs={{0,3},{1,0},{2,1},{3,2},{4,7},{5,4},{6,5},{7,6},{8,11},{9,8},{10,9... | collective-permute-start | bytes 49160 | tf_op jit(solution)/shard_map/ppermute | solution.py:369
  17.5 28.4 %collective-permute-start = (f32[16,256]{1,0:T(8,128)}, f32[16,256]{1,0:T(8,128)S(1)}, u32[]{:S(2)}, u32[]{:S(2)}) collective-permute-start(f32[16,256]{1,0:T(8,128)} %get-tuple-element.8), channel_id=1, source_target_pairs={{0,1},{1,2},{2,3},{3,0},{4,5},{5,6},{6,7},{7,4},{8,9},{9,10},{10,1... | collective-permute-start | bytes 49160 | tf_op jit(solution)/shard_map/ppermute | solution.py:369
  32.0 13.9 %copy-start = (f32[16,256]{1,0:T(8,128)}, f32[16,256]{1,0:T(8,128)S(1)}, u32[]{:S(2)}) copy-start(f32[16,256]{1,0:T(8,128)S(1)} %collective-permute-done.1.refs_18_) | copy-start | bytes 49156
  45.9 13.9 %copy-start.1 = (f32[16,256]{1,0:T(8,128)}, f32[16,256]{1,0:T(8,128)S(1)}, u32[]{:S(2)}) copy-start(f32[16,256]{1,0:T(8,128)S(1)} %collective-permute-done.refs_17_) | copy-start | bytes 49156
Sparse Core Ops, SparseCore 0:
  10.2 21.6 reduce-scatter.1

commit v8 on v6

--- a/solution.py
+++ b/solution.py
@@ -36,23 +36,71 @@
     return per, base, misc, misc + AH + 2 * OH
 
 
-def pack_kernel(*refs):
-    sources, (up, down, left, right), held, sems = refs[:5], refs[5:9], refs[9:14], refs[14]
-    atm, ocean, depth, wet, kappa = held
-    copies = [
-        pltpu.make_async_copy(source, target, sems.at[i])
-        for i, (source, target) in enumerate(zip(sources, held))
-    ]
-    for copy in copies:
-        copy.start()
+def split3(value):
+    hi = value.astype(BF16)
+    rest = value - hi.astype(F32)
+    mid = rest.astype(BF16)
+    low = (rest - mid.astype(F32)).astype(BF16)
+    return hi, mid, low
+
+
+def one_hot(index, size):
+    shape = (size, index.shape[-1])
+    return lax.broadcasted_iota(jnp.int32, shape, 0) == index
+
+
+def gather_rows(table, hot_rows, hot_cols):
+    r = table.shape[0]
+    parts = jnp.concatenate(split3(table), axis=0)
+    g = jnp.dot(parts, hot_cols, preferred_element_type=F32)
+    g = g[0:r] + g[r : 2 * r] + g[2 * r : 3 * r]
+    return jnp.sum(jnp.where(hot_rows, g, 0.0), axis=0, keepdims=True)
+
+
+def scatter_rows(values, hot_rows, hot_cols):
+    r = hot_rows.shape[0]
+    parts = []
+    for value in values:
+        for part in split3(value):
+            parts.append(jnp.where(hot_rows, part.astype(F32), 0.0).astype(BF16))
+    s = lax.dot_general(
+        jnp.concatenate(parts, axis=0),
+        hot_cols,
+        (((1,), (1,)), ((), ())),
+        preferred_element_type=F32,
+    )
+    out = []
+    for i in range(len(values)):
+        base = 3 * r * i
+        out.append(s[base : base + r] + s[base + r : base + 2 * r] + s[base + 2 * r : base + 3 * r])
+    return out
+
+
+def tile_at(shift, tiles):
+    return lax.rem(lax.axis_index("tile") + shift % tiles, tiles)
+
+
+def first_kernel(tiles, *refs):
+    sources, (left_out, right_out, up_out, down_out, wair_out, *sums_out) = refs[:10], refs[10:-17]
+    held, (up, down, left, right, wair_buf, sums, sems) = refs[-17:-7], refs[-7:]
+    atm, ocean, depth, wet, kappa, air, atm_cell, dest, sea_cell, weight = held
+    used = []
+
+    def copy(source, target):
+        used.append(pltpu.make_async_copy(source, target, sems.at[len(used)]))
+        used[-1].start()
+
+    for source, target in zip(sources, held):
+        copy(source, target)
     levels = atm.shape[1]
     rows, cols = atm.shape[2:]
     tracers = ocean.shape[0] * ocean.shape[1]
     each = ocean.shape[1]
     per, obase, mbase, _ = row_slots(levels, tracers)
     slots, _ = lane_slots(levels, tracers)
-    for copy in copies:
-        copy.wait()
+    for one in used:
+        one.wait()
+    arrived = len(used)
     wetness = wet[...].astype(F32)
 
     lane = lax.broadcasted_iota(jnp.int32, (rows, cols), 1)
@@ -77,6 +125,9 @@
         left[:, where] = a
         right[:, where] = b
 
+    copy(left, left_out)
+    copy(right, right_out)
+
     for level in range(levels):
         base = per * level
         for at, which, width in ((0, 1, AH), (AH, 0, AH - 1), (2 * AH - 1, 2, AH - 1)):
@@ -93,81 +144,36 @@
     ):
         up[at : at + width, :] = value[0:width]
         down[at : at + width, :] = value[rows - width : rows]
-
-
-def split3(value):
-    hi = value.astype(BF16)
-    rest = value - hi.astype(F32)
-    mid = rest.astype(BF16)
-    low = (rest - mid.astype(F32)).astype(BF16)
-    return hi, mid, low
-
-
-def one_hot(index, size):
-    shape = (size, index.shape[-1])
-    return lax.broadcasted_iota(jnp.int32, shape, 0) == index
-
-
-def gather_rows(table, hot_rows, hot_cols):
-    r = table.shape[0]
-    parts = jnp.concatenate(split3(table), axis=0)
-    g = jnp.dot(parts, hot_cols, preferred_element_type=F32)
-    g = g[0:r] + g[r : 2 * r] + g[2 * r : 3 * r]
-    return jnp.sum(jnp.where(hot_rows, g, 0.0), axis=0, keepdims=True)
-
-
-def scatter_rows(values, hot_rows, hot_cols):
-    r = hot_rows.shape[0]
-    parts = []
-    for value in values:
-        for part in split3(value):
-            parts.append(jnp.where(hot_rows, part.astype(F32), 0.0).astype(BF16))
-    s = lax.dot_general(
-        jnp.concatenate(parts, axis=0),
-        hot_cols,
-        (((1,), (1,)), ((), ())),
-        preferred_element_type=F32,
-    )
-    out = []
-    for i in range(len(values)):
-        base = 3 * r * i
-        out.append(s[base : base + r] + s[base + r : base + 2 * r] + s[base + 2 * r : base + 3 * r])
-    return out
-
-
-def tile_at(shift, tiles):
-    return lax.rem(lax.axis_index("tile") + shift % tiles, tiles)
-
-
-def send_kernel(tiles, *refs):
-    sources, (*messages, wair_out) = refs[:6], refs[6:-7]
-    held, sems = refs[-7:-1], refs[-1]
-    air, surface, atm_cell, dest, sea_cell, weight = held
-    copies = [
-        pltpu.make_async_copy(source.at[0, 0] if i == 1 else source, target, sems.at[i])
-        for i, (source, target) in enumerate(zip(sources, held))
-    ]
-    for copy in copies:
-        copy.start()
-    for copy in copies:
-        copy.wait()
-    rows, cols = air.shape
+    halo = up.shape[0]
+    copy(up, up_out.at[0:halo])
+    copy(down, down_out.at[0:halo])
+
     cell = atm_cell[...]
     hot_atm = jnp.where(one_hot(cell % cols, cols), 1.0, 0.0).astype(BF16)
     airx = gather_rows(air[...], one_hot(cell // cols, rows), hot_atm)
     w = weight[...]
     wair = w * airx
-    wair_out[...] = wair
+    wair_buf[...] = wair
+    copy(wair_buf, wair_out)
     cell = sea_cell[...]
     hot_sea = jnp.where(one_hot(cell % cols, cols), 1.0, 0.0).astype(BF16)
     row = dest[...] * rows + cell // cols
     for shift in range(tiles):
         target = tile_at(shift, tiles)
-        message = messages[shift] if len(messages) > 1 else messages[0].at[target]
         s1, s2 = scatter_rows([wair, w], one_hot(row - target * rows, rows), hot_sea)
-        message[0:rows, :] = s1
-        message[rows : 2 * rows, :] = s2
-        message[2 * rows : 3 * rows, :] = surface[...]
+        sums[shift, 0:rows, :] = s1
+        sums[shift, rows : 2 * rows, :] = s2
+        sums[shift, 2 * rows : 3 * rows, :] = ocean[0, 0]
+        if len(sums_out) == 1:
+            copy(sums.at[shift], sums_out[0].at[target])
+        elif shift == 1:
+            copy(sums.at[shift], down_out.at[halo : halo + 3 * rows])
+        elif shift == tiles - 1:
+            copy(sums.at[shift], up_out.at[halo : halo + 3 * rows])
+        else:
+            copy(sums.at[shift], sums_out[max(shift - 1, 0)])
+    for one in used[arrived:]:
+        one.wait()
 
 
 def strips(cols, slot, width, left_part, right_part):
@@ -191,13 +197,14 @@
     return out + [(mbase, AH), (mbase + AH, OH), (mbase + AH + OH, OH)]
 
 
-def final_kernel(tiles, parts, *refs):
+def final_kernel(tiles, *refs):
     speed_in, atm_in, ocean_in, depth_in, kappa_in = refs[:5]
-    sources, rest = refs[5 : 15 + parts], refs[15 + parts :]
+    kept = (len(refs) - 5 - 8 - 4) // 2
+    sources, rest = refs[5 : 5 + kept], refs[5 + kept :]
     atm_out, ocean_out, speed, us, vs, hs, fs, ms = rest[:8]
-    held, (edge, atm_buf, ocean_buf, sems) = rest[8 : 18 + parts], rest[18 + parts :]
-    wet, atm_cell, dest, sea_cell, weight, wair, from_up, from_down, from_left, from_right = held[:10]
-    messages = held[10:]
+    held, (edge, atm_buf, ocean_buf, sems) = rest[8 : 8 + kept], rest[8 + kept :]
+    wet, atm_cell, dest, sea_cell, weight, wair, from_up, from_down, from_left, from_right, from_below, from_above = held[:12]
+    messages = held[12:]
     levels = us.shape[0]
     each = ocean_out.shape[1]
     tracers = ocean_out.shape[0] * each
@@ -216,21 +223,27 @@
     for copy in copies:
         copy.wait()
 
-    def message(shift):
-        return messages[shift] if len(messages) > 1 else messages[0].at[tile_at(-shift, tiles)]
+    halo = row_slots(levels, tracers)[3]
+
+    def message(shift, part):
+        where = slice(part * rows, (part + 1) * rows)
+        if len(messages) == 1:
+            return messages[0][tile_at(-shift, tiles), where, :]
+        if shift in (1, tiles - 1):
+            return (from_up if shift == 1 else from_down)[halo + part * rows : halo + (part + 1) * rows, :]
+        return messages[max(shift - 1, 0)][where, :]
 
     surface = fs[0, 0, 0:rows, 0:cols]
     cell = sea_cell[...]
     hot_sea = jnp.where(one_hot(cell % cols, cols), 1.0, 0.0).astype(BF16)
     row = dest[...] * rows + cell // cols
-    s1, s2 = message(0)[0:rows, :], message(0)[rows : 2 * rows, :]
+    s1, s2 = message(0, 0), message(0, 1)
     sstx = jnp.zeros(cell.shape, F32)
     for shift in range(tiles):
         if shift:
-            s1 = s1 + message(shift)[0:rows, :]
-            s2 = s2 + message(shift)[rows : 2 * rows, :]
-        table = message(shift)[2 * rows : 3 * rows, :]
-        sstx = sstx + gather_rows(table, one_hot(row - tile_at(-shift, tiles) * rows, rows), hot_sea)
+            s1 = s1 + message(shift, 0)
+            s2 = s2 + message(shift, 1)
+        sstx = sstx + gather_rows(message(shift, 2), one_hot(row - tile_at(-shift, tiles) * rows, rows), hot_sea)
     sea_flux = s1 - surface * s2
     flux = wair[...] - weight[...] * sstx
     cell = atm_cell[...]
@@ -239,9 +252,9 @@
 
     half = lanes // cols
     for i in range(2 * half):
-        at = 3 * rows + AH * i
-        edge[i, 0:AH, :] = message(tiles - 1)[at : at + AH, :]
-        edge[i, AH : 2 * AH, :] = message(1)[at : at + AH, :]
+        at, where = i // half * AH, slice(i % half * cols, (i % half + 1) * cols)
+        edge[i, 0:AH, :] = from_below[at : at + AH, where]
+        edge[i, AH : 2 * AH, :] = from_above[at : at + AH, where]
 
     def extend(view, field, width):
         at, high = slices[field]
@@ -349,7 +362,8 @@
     tracers = ocean_state.shape[0] * ocean_state.shape[1]
     cells = xg_weight.shape[-1]
     _, lanes = lane_slots(levels, tracers)
-    _, _, _, message_rows = row_slots(levels, tracers)
+    _, _, _, halo = row_slots(levels, tracers)
+    message_rows = halo
     vmem = pl.BlockSpec(memory_space=pltpu.VMEM)
     hbm = pl.BlockSpec(memory_space=pltpu.HBM)
     whole = pltpu.CompilerParams(vmem_limit_bytes=64 * 1024 * 1024)
@@ -358,20 +372,33 @@
     def shape(*dims):
         return jax.ShapeDtypeStruct(dims, F32)
 
-    fields = (atm_state, ocean_state, depth, wet_mask, diffusivity)
-    up, down, left, right = pl.pallas_call(
-        pack_kernel,
-        out_shape=[shape(message_rows, cols)] * 2 + [shape(rows, lanes)] * 2,
-        in_specs=[hbm] * 5,
-        out_specs=[vmem] * 4,
-        scratch_shapes=[pltpu.VMEM(x.shape, x.dtype) for x in fields] + [pltpu.SemaphoreType.DMA((5,))],
-        compiler_params=whole,
-        name="pack",
-    )(*fields)
+    by_shift = tile_count <= 4
+    if by_shift:
+        message_rows += 3 * rows
+        sums = [shape(3 * rows, cols)] * (tile_count - 2)
+    else:
+        sums = [shape(tile_count, 3 * rows, cols)]
     atm_cell = xg_atm_cell.reshape(1, cells)
     dest = xg_dest.reshape(1, cells)
     sea_cell = xg_ocean_cell.reshape(1, cells)
     weight = xg_weight.reshape(1, cells)
+    operands = (atm_state, ocean_state, depth, wet_mask, diffusivity, air_temp, atm_cell, dest, sea_cell, weight)
+    left, right, up, down, wair, *messages = pl.pallas_call(
+        functools.partial(first_kernel, tile_count),
+        out_shape=[shape(rows, lanes)] * 2 + [shape(message_rows, cols)] * 2 + [shape(1, cells)] + sums,
+        in_specs=[hbm] * 10,
+        out_specs=[hbm] * (5 + len(sums)),
+        scratch_shapes=[pltpu.VMEM(x.shape, x.dtype) for x in operands]
+        + [pltpu.VMEM((halo, cols), F32)] * 2
+        + [pltpu.VMEM((rows, lanes), F32)] * 2
+        + [
+            pltpu.VMEM((1, cells), F32),
+            pltpu.VMEM((tile_count, 3 * rows, cols), F32),
+            pltpu.SemaphoreType.DMA((15 + tile_count,)),
+        ],
+        compiler_params=whole,
+        name="first",
+    )(*operands)
 
     column_axes = ("sub", "comp")
     column_count = lax.axis_size("sub") * lax.axis_size("comp")
@@ -384,44 +411,19 @@
     from_down = shift(up, "tile", tile_count, -1)
     from_up = shift(down, "tile", tile_count, 1)
 
-    by_shift = tile_count <= 4
-    sums = [shape(3 * rows, cols)] * tile_count if by_shift else [shape(tile_count, 3 * rows, cols)]
-    *messages, wair = pl.pallas_call(
-        functools.partial(send_kernel, tile_count),
-        out_shape=sums + [shape(1, cells)],
-        in_specs=[hbm] * 6,
-        out_specs=[vmem] * (len(sums) + 1),
-        scratch_shapes=[pltpu.VMEM((rows, cols), F32)] * 2
-        + [pltpu.VMEM((1, cells), jnp.int32)] * 3
-        + [pltpu.VMEM((1, cells), F32), pltpu.SemaphoreType.DMA((6,))],
-        compiler_params=whole,
-        cost_estimate=pl.CostEstimate(flops=0, bytes_accessed=200_000_000, transcendentals=0),
-        name="exchange_send",
-    )(air_temp, ocean_state, atm_cell, dest, sea_cell, weight)
-    near = {}
-    for s, low in ((1, rows - AH), (tile_count - 1, 0)):
-        near[s] = [
-            ref[low : low + AH, i * cols : (i + 1) * cols]
-            for ref in (from_left, from_right)
-            for i in range(lanes // cols)
-        ]
+    from_below = shift(jnp.concatenate([from_left[0:AH], from_right[0:AH]]), "tile", tile_count, -1)
+    from_above = shift(jnp.concatenate([from_left[rows - AH :], from_right[rows - AH :]]), "tile", tile_count, 1)
     if by_shift:
-        got = messages[:1]
-        for s in range(1, tile_count):
-            joined = jnp.concatenate([messages[s]] + near[s]) if s in near else messages[s]
-            got.append(shift(joined, "tile", tile_count, s))
+        got = messages[:1] + [shift(messages[s - 1], "tile", tile_count, s) for s in range(2, tile_count - 1)]
     else:
-        corners = jnp.zeros((tile_count, 2 * AH * (lanes // cols), cols), F32)
-        for s in near:
-            corners = corners.at[(lax.axis_index("tile") + s) % tile_count].set(jnp.concatenate(near[s]))
-        joined = jnp.concatenate([messages[0], corners], axis=1)
-        got = [lax.all_to_all(joined, "tile", split_axis=0, concat_axis=0, tiled=True)]
+        got = [lax.all_to_all(messages[0], "tile", split_axis=0, concat_axis=0, tiled=True)]
 
     operands = (wave_speed, atm_state, ocean_state, depth, diffusivity)
-    operands += (wet_mask, atm_cell, dest, sea_cell, weight, wair, from_up, from_down, from_left, from_right, *got)
+    operands += (wet_mask, atm_cell, dest, sea_cell, weight, wair, from_up, from_down, from_left, from_right)
+    operands += (from_below, from_above, *got)
     return tuple(
         pl.pallas_call(
-            functools.partial(final_kernel, tile_count, len(got)),
+            functools.partial(final_kernel, tile_count),
             out_shape=[shape(*atm_state.shape), shape(*ocean_state.shape)],
             in_specs=[hbm] * len(operands),
             out_specs=[hbm] * 2,

time: 27.3 us -> 23.8 us (0.87)
  local copies, waits for them, and re-layouts: 2.75 us -> 0.58 us
  Pallas kernels: 8.58 us -> 6.93 us
  starting transfers between devices: 10.1 us -> 11.7 us
  waiting for transfers between devices: 4.74 us -> 3.61 us
    pallas_call x3 -> x2, Pallas kernels: 8.58 us -> 6.93 us  [the longest x1 4.18 us: on_device(): pl.pallas_call(functools.partial(final_kernel, tile_count), out_shape=[sh...]
    ppermute x7, starting transfers between devices: 10.1 us -> 11.7 us  [shift(): lax.ppermute(value, axes, [(i, (i + by) % count) for i in range(count)])]
    slice x2, local copies, waits for them, and re-layouts: 1.4 us -> 0.01 us  [the longest x1 0.01 us: on_device(): from_right[rows - AH:]]
    ppermute x7, waiting for transfers between devices: 4.74 us -> 3.61 us  [shift(): lax.ppermute(value, axes, [(i, (i + by) % count) for i in range(count)])]
    unnamed x8 -> x4, local copies, waits for them, and re-layouts: 1.26 us -> 0.57 us
  transfers between devices with their start and end apart: 7 -> 7, of which waited for: 1 -> 2; matrix products, arithmetic and copies ran while one was open for 6% -> 0% of each run, Pallas kernels for 9% -> 0%
where the time goes in v8:
time: 23.8 us; the launch traced here: 23.6 us
  starting transfers between devices  11.7 us (49%)
  Pallas kernels  6.93 us (29%)
  waiting for transfers between devices  3.61 us (15%)
  between operations  0.69 us (3%)
  local copies, waits for them, and re-layouts  0.58 us (2%)
    ppermute x7, starting transfers between devices, shift(): lax.ppermute(value, axes, [(i, (i + by) % count) for i in range(count)])  11.7 us
    pallas_call x1, Pallas kernels, on_device(): pl.pallas_call(functools.partial(final_kernel, tile_count), out_shape=[sh...  4.18 us
    ppermute x7, waiting for transfers between devices, shift(): lax.ppermute(value, axes, [(i, (i + by) % count) for i in range(count)])  3.61 us
    pallas_call x1, Pallas kernels, on_device(): pl.pallas_call(functools.partial(first_kernel, tile_count), out_shape=[sh...  2.75 us
    unnamed x4, local copies, waits for them, and re-layouts  0.57 us
  transfers between devices with their start and end apart: 7, of which 2 were waited for; matrix products, arithmetic and copies ran while one was open for 0% of the time, Pallas kernels for 0%

profile of v8, /device:TPU:0, one launch (start us, length us, event | category | flops | bytes accessed | tf_op | source)
XLA Modules:
  0.0 23.6 jit_solution(8474918394241307670)
XLA Ops:
  0.6 2.8 %first.1 = (f32[16,256]{1,0:T(8,128)}, f32[16,256]{1,0:T(8,128)}, f32[248,128]{1,0:T(8,128)}, f32[248,128]{1,0:T(8,128)}, f32[1,2048]{1,0:T(1,128)}, /*index=5*/f32[48,128]{1,0:T(8,128)}, f32[48,128]{1,0:T(8,128)}) custom-call(f32[3,16,16,128]{3,2,1,0:T(8,128)} %refs_1_.3, f32[2,8,16,128]{3,2,1,0:T(8,128)} %refs_2_.3, f32[16,128]{1,0:T(8,128)} %refs_3_.3, ...), custom_call_target="tpu_custom_call" | custom-call | tf_op jit(solution)/shard_map/first/pallas_call | solution.py:386
  3.4 0.5 %collective-permute-start.2 = (f32[16,256]{1,0:T(8,128)}, f32[16,256]{1,0:T(8,128)S(1)}, u32[]{:S(2)}, u32[]{:S(2)}) collective-permute-start(f32[16,256]{1,0:T(8,128)} %get-tuple-element.12), channel_id=1, source_target_pairs={{0,1},{1,2},{2,3},{3,0},{4,5},{5,6},{6,7},{7,4},{8,9},{9,10},{10,1... | collective-permute-start | bytes 49160 | tf_op jit(solution)/shard_map/ppermute | solution.py:407
  3.9 2.0 %collective-permute-start.3 = (f32[16,256]{1,0:T(8,128)}, f32[16,256]{1,0:T(8,128)S(1)}, u32[]{:S(2)}, u32[]{:S(2)}) collective-permute-start(f32[16,256]{1,0:T(8,128)} %get-tuple-element.13), channel_id=1, source_target_pairs={{0,3},{1,0},{2,1},{3,2},{4,7},{5,4},{6,5},{7,6},{8,11},{9,8},{10,9... | collective-permute-start | bytes 49160 | tf_op jit(solution)/shard_map/ppermute | solution.py:407
  5.9 3.3 %collective-permute-start.6 = (f32[48,128]{1,0:T(8,128)}, f32[48,128]{1,0:T(8,128)}, u32[]{:S(2)}, u32[]{:S(2)}) collective-permute-start(f32[48,128]{1,0:T(8,128)} %get-tuple-element.15), channel_id=1, source_target_pairs={{0,8},{4,12},{8,0},{12,4},{1,9},{5,13},{9,1},{13,5},{2,10},{6,14},... | collective-permute-start | bytes 73736 | tf_op jit(solution)/shard_map/ppermute | solution.py:407
  9.2 1.6 %collective-permute-start = (f32[248,128]{1,0:T(8,128)}, f32[248,128]{1,0:T(8,128)}, u32[]{:S(2)}, u32[]{:S(2)}) collective-permute-start(f32[248,128]{1,0:T(8,128)} %get-tuple-element.10), channel_id=1, source_target_pairs={{0,4},{4,8},{8,12},{12,0},{1,5},{5,9},{9,13},{13,1},{2,6},{6,10},{... | collective-permute-start | bytes 380936 | tf_op jit(solution)/shard_map/ppermute | solution.py:407
  10.8 2.2 %collective-permute-start.1 = (f32[248,128]{1,0:T(8,128)}, f32[248,128]{1,0:T(8,128)}, u32[]{:S(2)}, u32[]{:S(2)}) collective-permute-start(f32[248,128]{1,0:T(8,128)} %get-tuple-element.11), channel_id=1, source_target_pairs={{0,12},{4,0},{8,4},{12,8},{1,13},{5,1},{9,5},{13,9},{2,14},{6,2},{... | collective-permute-start | bytes 380936 | tf_op jit(solution)/shard_map/ppermute | solution.py:407
  13.0 0.0 collective-permute-done.2.refs_13_
  13.1 0.0 copy-start
  13.1 0.0 collective-permute-done.3.refs_14_
  13.1 0.0 copy-start.1
  13.1 0.6 %copy-done = f32[16,256]{1,0:T(8,128)} copy-done((f32[16,256]{1,0:T(8,128)}, f32[16,256]{1,0:T(8,128)S(1)}, u32[]{:S(2)}) %copy-start) | copy-done | bytes 16408
  13.7 0.0 copy-done.1
  13.7 0.1 collective-permute-start.4
  13.8 2.0 %collective-permute-start.5 = (f32[8,256]{1,0:T(8,128)S(1)}, f32[8,256]{1,0:T(8,128)}, u32[]{:S(2)}, u32[]{:S(2)}) collective-permute-start(f32[8,256]{1,0:T(8,128)S(1)} %pad_maximum_fusion.1), channel_id=1, source_target_pairs={{0,4},{4,8},{8,12},{12,0},{1,5},{5,9},{9,13},{13,1},{2,6},{6,10},{... | collective-permute-start | bytes 24584 | tf_op jit(solution)/shard_map/ppermute | solution.py:407
  15.8 3.0 %collective-permute-done.4.refs_15_ = f32[8,256]{1,0:T(8,128)} collective-permute-done((f32[8,256]{1,0:T(8,128)S(1)}, f32[8,256]{1,0:T(8,128)}, u32[]{:S(2)}, u32[]{:S(2)}) %collective-permute-start.4) | collective-permute-done | bytes 8224 | tf_op jit(solution)/shard_map/ppermute | solution.py:407
  18.7 0.6 %collective-permute-done.5.refs_16_ = f32[8,256]{1,0:T(8,128)} collective-permute-done((f32[8,256]{1,0:T(8,128)S(1)}, f32[8,256]{1,0:T(8,128)}, u32[]{:S(2)}, u32[]{:S(2)}) %collective-permute-start.5) | collective-permute-done | bytes 8224 | tf_op jit(solution)/shard_map/ppermute | solution.py:407
  19.4 0.0 collective-permute-done.6.refs_18_
  19.4 0.0 collective-permute-done.refs_11_
  19.4 0.0 collective-permute-done.1.refs_12_
  19.4 4.2 %steps.1 = (f32[3,16,16,128]{3,2,1,0:T(8,128)}, f32[2,8,16,128]{3,2,1,0:T(8,128)}) custom-call(f32[16]{0:T(128)} %refs_0_.3, f32[3,16,16,128]{3,2,1,0:T(8,128)} %refs_1_.3, f32[2,8,16,128]{3,2,1,0:T(8,128)} %refs_2_.3, f32[16,128]{1,0:T(8,128)} %refs_3_.3, f32[16,128]{1,0:T(8,128)} %refs_4_.3, s32[16,128]{1,0:T(8,128)} %refs_5_.3, s32[1,2048]{1,0:T(1,128)} %bitcast.5, ...), custom_call_target="tpu_custom_call" | custom-call | tf_op jit(solution)/shard_map/steps/pallas_call | solution.py:425
  (4 shorter events, 0.0 us)
Async XLA Ops:
  3.4 9.7 %collective-permute-start.2 = (f32[16,256]{1,0:T(8,128)}, f32[16,256]{1,0:T(8,128)S(1)}, u32[]{:S(2)}, u32[]{:S(2)}) collective-permute-start(f32[16,256]{1,0:T(8,128)} %get-tuple-element.12), channel_id=1, source_target_pairs={{0,1},{1,2},{2,3},{3,0},{4,5},{5,6},{6,7},{7,4},{8,9},{9,10},{10,1... | collective-permute-start | bytes 49160 | tf_op jit(solution)/shard_map/ppermute | solution.py:407
  3.9 9.2 %collective-permute-start.3 = (f32[16,256]{1,0:T(8,128)}, f32[16,256]{1,0:T(8,128)S(1)}, u32[]{:S(2)}, u32[]{:S(2)}) collective-permute-start(f32[16,256]{1,0:T(8,128)} %get-tuple-element.13), channel_id=1, source_target_pairs={{0,3},{1,0},{2,1},{3,2},{4,7},{5,4},{6,5},{7,6},{8,11},{9,8},{10,9... | collective-permute-start | bytes 49160 | tf_op jit(solution)/shard_map/ppermute | solution.py:407
  5.9 13.5 %collective-permute-start.6 = (f32[48,128]{1,0:T(8,128)}, f32[48,128]{1,0:T(8,128)}, u32[]{:S(2)}, u32[]{:S(2)}) collective-permute-start(f32[48,128]{1,0:T(8,128)} %get-tuple-element.15), channel_id=1, source_target_pairs={{0,8},{4,12},{8,0},{12,4},{1,9},{5,13},{9,1},{13,5},{2,10},{6,14},... | collective-permute-start | bytes 73736 | tf_op jit(solution)/shard_map/ppermute | solution.py:407
  9.2 10.1 %collective-permute-start = (f32[248,128]{1,0:T(8,128)}, f32[248,128]{1,0:T(8,128)}, u32[]{:S(2)}, u32[]{:S(2)}) collective-permute-start(f32[248,128]{1,0:T(8,128)} %get-tuple-element.10), channel_id=1, source_target_pairs={{0,4},{4,8},{8,12},{12,0},{1,5},{5,9},{9,13},{13,1},{2,6},{6,10},{... | collective-permute-start | bytes 380936 | tf_op jit(solution)/shard_map/ppermute | solution.py:407
  10.8 8.6 %collective-permute-start.1 = (f32[248,128]{1,0:T(8,128)}, f32[248,128]{1,0:T(8,128)}, u32[]{:S(2)}, u32[]{:S(2)}) collective-permute-start(f32[248,128]{1,0:T(8,128)} %get-tuple-element.11), channel_id=1, source_target_pairs={{0,12},{4,0},{8,4},{12,8},{1,13},{5,1},{9,5},{13,9},{2,14},{6,2},{... | collective-permute-start | bytes 380936 | tf_op jit(solution)/shard_map/ppermute | solution.py:407
  13.1 0.6 %copy-start = (f32[16,256]{1,0:T(8,128)}, f32[16,256]{1,0:T(8,128)S(1)}, u32[]{:S(2)}) copy-start(f32[16,256]{1,0:T(8,128)S(1)} %collective-permute-done.2.refs_13_) | copy-start | bytes 49156
  13.1 0.6 %copy-start.1 = (f32[16,256]{1,0:T(8,128)}, f32[16,256]{1,0:T(8,128)S(1)}, u32[]{:S(2)}) copy-start(f32[16,256]{1,0:T(8,128)S(1)} %collective-permute-done.3.refs_14_) | copy-start | bytes 49156
  13.7 5.0 %collective-permute-start.4 = (f32[8,256]{1,0:T(8,128)S(1)}, f32[8,256]{1,0:T(8,128)}, u32[]{:S(2)}, u32[]{:S(2)}) collective-permute-start(f32[8,256]{1,0:T(8,128)S(1)} %pad_maximum_fusion), channel_id=1, source_target_pairs={{0,12},{4,0},{8,4},{12,8},{1,13},{5,1},{9,5},{13,9},{2,14},{6,2},{... | collective-permute-start | bytes 24584 | tf_op jit(solution)/shard_map/ppermute | solution.py:407
  13.8 5.6 %collective-permute-start.5 = (f32[8,256]{1,0:T(8,128)S(1)}, f32[8,256]{1,0:T(8,128)}, u32[]{:S(2)}, u32[]{:S(2)}) collective-permute-start(f32[8,256]{1,0:T(8,128)S(1)} %pad_maximum_fusion.1), channel_id=1, source_target_pairs={{0,4},{4,8},{8,12},{12,0},{1,5},{5,9},{9,13},{13,1},{2,6},{6,10},{... | collective-permute-start | bytes 24584 | tf_op jit(solution)/shard_map/ppermute | solution.py:407

commit v9 on v8

--- a/solution.py
+++ b/solution.py
@@ -414,6 +414,7 @@
     from_below = shift(jnp.concatenate([from_left[0:AH], from_right[0:AH]]), "tile", tile_count, -1)
     from_above = shift(jnp.concatenate([from_left[rows - AH :], from_right[rows - AH :]]), "tile", tile_count, 1)
     if by_shift:
+        *messages, from_left = lax.optimization_barrier((*messages, from_left))
         got = messages[:1] + [shift(messages[s - 1], "tile", tile_count, s) for s in range(2, tile_count - 1)]
     else:
         got = [lax.all_to_all(messages[0], "tile", split_axis=0, concat_axis=0, tiled=True)]

time: 23.8 us -> 23 us (0.966)
  starting transfers between devices: 11.7 us -> 9.93 us
  waiting for transfers between devices: 3.61 us -> 4.61 us
    ppermute x7, starting transfers between devices: 11.7 us -> 9.93 us  [shift(): lax.ppermute(value, axes, [(i, (i + by) % count) for i in range(count)])]
    ppermute x7, waiting for transfers between devices: 3.61 us -> 4.61 us  [shift(): lax.ppermute(value, axes, [(i, (i + by) % count) for i in range(count)])]
    unnamed x4 -> x6, local copies, waits for them, and re-layouts: 0.57 us -> 0.58 us
where the time goes in v9:
time: 23 us; the launch traced here: 22.8 us
  starting transfers between devices  9.93 us (43%)
  Pallas kernels  6.93 us (30%)
  waiting for transfers between devices  4.61 us (20%)
  between operations  0.68 us (3%)
  local copies, waits for them, and re-layouts  0.59 us (3%)
    ppermute x7, starting transfers between devices, shift(): lax.ppermute(value, axes, [(i, (i + by) % count) for i in range(count)])  9.93 us
    ppermute x7, waiting for transfers between devices, shift(): lax.ppermute(value, axes, [(i, (i + by) % count) for i in range(count)])  4.61 us
    pallas_call x1, Pallas kernels, on_device(): pl.pallas_call(functools.partial(final_kernel, tile_count), out_shape=[sh...  4.18 us
    pallas_call x1, Pallas kernels, on_device(): pl.pallas_call(functools.partial(first_kernel, tile_count), out_shape=[sh...  2.75 us
    unnamed x6, local copies, waits for them, and re-layouts  0.58 us
  transfers between devices with their start and end apart: 7, of which 2 were waited for; matrix products, arithmetic and copies ran while one was open for 0% of the time, Pallas kernels for 0%

profile of v9, /device:TPU:0, one launch (start us, length us, event | category | flops | bytes accessed | tf_op | source)
XLA Modules:
  0.0 22.8 jit_solution(7914548874599454509)
XLA Ops:
  0.6 2.8 %first.1 = (f32[16,256]{1,0:T(8,128)}, f32[16,256]{1,0:T(8,128)}, f32[248,128]{1,0:T(8,128)}, f32[248,128]{1,0:T(8,128)}, f32[1,2048]{1,0:T(1,128)}, /*index=5*/f32[48,128]{1,0:T(8,128)}, f32[48,128]{1,0:T(8,128)}) custom-call(f32[3,16,16,128]{3,2,1,0:T(8,128)} %refs_1_.3, f32[2,8,16,128]{3,2,1,0:T(8,128)} %refs_2_.3, f32[16,128]{1,0:T(8,128)} %refs_3_.3, ...), custom_call_target="tpu_custom_call" | custom-call | tf_op jit(solution)/shard_map/first/pallas_call | solution.py:386
  3.4 0.5 %collective-permute-start.2 = (f32[16,256]{1,0:T(8,128)}, f32[16,256]{1,0:T(8,128)S(1)}, u32[]{:S(2)}, u32[]{:S(2)}) collective-permute-start(f32[16,256]{1,0:T(8,128)} %get-tuple-element.17), channel_id=1, source_target_pairs={{0,1},{1,2},{2,3},{3,0},{4,5},{5,6},{6,7},{7,4},{8,9},{9,10},{10,1... | collective-permute-start | bytes 49160 | tf_op jit(solution)/shard_map/ppermute | solution.py:407
  3.9 2.0 %collective-permute-start.3 = (f32[16,256]{1,0:T(8,128)}, f32[16,256]{1,0:T(8,128)S(1)}, u32[]{:S(2)}, u32[]{:S(2)}) collective-permute-start(f32[16,256]{1,0:T(8,128)} %get-tuple-element.19), channel_id=1, source_target_pairs={{0,3},{1,0},{2,1},{3,2},{4,7},{5,4},{6,5},{7,6},{8,11},{9,8},{10,9... | collective-permute-start | bytes 49160 | tf_op jit(solution)/shard_map/ppermute | solution.py:407
  5.9 2.3 %collective-permute-start = (f32[248,128]{1,0:T(8,128)}, f32[248,128]{1,0:T(8,128)}, u32[]{:S(2)}, u32[]{:S(2)}) collective-permute-start(f32[248,128]{1,0:T(8,128)} %get-tuple-element.13), channel_id=1, source_target_pairs={{0,4},{4,8},{8,12},{12,0},{1,5},{5,9},{9,13},{13,1},{2,6},{6,10},{... | collective-permute-start | bytes 380936 | tf_op jit(solution)/shard_map/ppermute | solution.py:407
  8.2 0.0 copy-start.2
  8.2 2.0 %collective-permute-start.1 = (f32[248,128]{1,0:T(8,128)}, f32[248,128]{1,0:T(8,128)}, u32[]{:S(2)}, u32[]{:S(2)}) collective-permute-start(f32[248,128]{1,0:T(8,128)} %get-tuple-element.14), channel_id=1, source_target_pairs={{0,12},{4,0},{8,4},{12,8},{1,13},{5,1},{9,5},{13,9},{2,14},{6,2},{... | collective-permute-start | bytes 380936 | tf_op jit(solution)/shard_map/ppermute | solution.py:407
  10.2 0.0 collective-permute-done.2.refs_13_
  10.2 0.0 copy-start
  10.3 0.0 collective-permute-done.3.refs_14_
  10.3 0.0 copy-start.1
  10.3 0.6 %copy-done = f32[16,256]{1,0:T(8,128)} copy-done((f32[16,256]{1,0:T(8,128)}, f32[16,256]{1,0:T(8,128)S(1)}, u32[]{:S(2)}) %copy-start) | copy-done | bytes 16408
  10.9 0.0 copy-done.1
  10.9 2.1 %collective-permute-start.4 = (f32[8,256]{1,0:T(8,128)S(1)}, f32[8,256]{1,0:T(8,128)}, u32[]{:S(2)}, u32[]{:S(2)}) collective-permute-start(f32[8,256]{1,0:T(8,128)S(1)} %pad_maximum_fusion), channel_id=1, source_target_pairs={{0,12},{4,0},{8,4},{12,8},{1,13},{5,1},{9,5},{13,9},{2,14},{6,2},{... | collective-permute-start | bytes 24584 | tf_op jit(solution)/shard_map/ppermute | solution.py:407
  12.9 0.0 copy-done.2
  12.9 0.0 collective-permute-start.6
  13.0 1.0 %collective-permute-start.5 = (f32[8,256]{1,0:T(8,128)S(1)}, f32[8,256]{1,0:T(8,128)}, u32[]{:S(2)}, u32[]{:S(2)}) collective-permute-start(f32[8,256]{1,0:T(8,128)S(1)} %pad_maximum_fusion.1), channel_id=1, source_target_pairs={{0,4},{4,8},{8,12},{12,0},{1,5},{5,9},{9,13},{13,1},{2,6},{6,10},{... | collective-permute-start | bytes 24584 | tf_op jit(solution)/shard_map/ppermute | solution.py:407
  14.0 2.4 %collective-permute-done.4.refs_15_ = f32[8,256]{1,0:T(8,128)} collective-permute-done((f32[8,256]{1,0:T(8,128)S(1)}, f32[8,256]{1,0:T(8,128)}, u32[]{:S(2)}, u32[]{:S(2)}) %collective-permute-start.4) | collective-permute-done | bytes 8224 | tf_op jit(solution)/shard_map/ppermute | solution.py:407
  16.3 2.2 %collective-permute-done.5.refs_16_ = f32[8,256]{1,0:T(8,128)} collective-permute-done((f32[8,256]{1,0:T(8,128)S(1)}, f32[8,256]{1,0:T(8,128)}, u32[]{:S(2)}, u32[]{:S(2)}) %collective-permute-start.5) | collective-permute-done | bytes 8224 | tf_op jit(solution)/shard_map/ppermute | solution.py:407
  18.6 0.0 collective-permute-done.6.refs_18_
  18.6 0.0 collective-permute-done.refs_11_
  18.6 0.0 collective-permute-done.1.refs_12_
  18.6 4.2 %steps.1 = (f32[3,16,16,128]{3,2,1,0:T(8,128)}, f32[2,8,16,128]{3,2,1,0:T(8,128)}) custom-call(f32[16]{0:T(128)} %refs_0_.3, f32[3,16,16,128]{3,2,1,0:T(8,128)} %refs_1_.3, f32[2,8,16,128]{3,2,1,0:T(8,128)} %refs_2_.3, f32[16,128]{1,0:T(8,128)} %refs_3_.3, f32[16,128]{1,0:T(8,128)} %refs_4_.3, s32[16,128]{1,0:T(8,128)} %refs_5_.3, s32[1,2048]{1,0:T(1,128)} %bitcast.5, ...), custom_call_target="tpu_custom_call" | custom-call | tf_op jit(solution)/shard_map/steps/pallas_call | solution.py:426
  (4 shorter events, 0.0 us)
Async XLA Ops:
  3.4 6.9 %collective-permute-start.2 = (f32[16,256]{1,0:T(8,128)}, f32[16,256]{1,0:T(8,128)S(1)}, u32[]{:S(2)}, u32[]{:S(2)}) collective-permute-start(f32[16,256]{1,0:T(8,128)} %get-tuple-element.17), channel_id=1, source_target_pairs={{0,1},{1,2},{2,3},{3,0},{4,5},{5,6},{6,7},{7,4},{8,9},{9,10},{10,1... | collective-permute-start | bytes 49160 | tf_op jit(solution)/shard_map/ppermute | solution.py:407
  3.9 6.4 %collective-permute-start.3 = (f32[16,256]{1,0:T(8,128)}, f32[16,256]{1,0:T(8,128)S(1)}, u32[]{:S(2)}, u32[]{:S(2)}) collective-permute-start(f32[16,256]{1,0:T(8,128)} %get-tuple-element.19), channel_id=1, source_target_pairs={{0,3},{1,0},{2,1},{3,2},{4,7},{5,4},{6,5},{7,6},{8,11},{9,8},{10,9... | collective-permute-start | bytes 49160 | tf_op jit(solution)/shard_map/ppermute | solution.py:407
  5.9 12.7 %collective-permute-start = (f32[248,128]{1,0:T(8,128)}, f32[248,128]{1,0:T(8,128)}, u32[]{:S(2)}, u32[]{:S(2)}) collective-permute-start(f32[248,128]{1,0:T(8,128)} %get-tuple-element.13), channel_id=1, source_target_pairs={{0,4},{4,8},{8,12},{12,0},{1,5},{5,9},{9,13},{13,1},{2,6},{6,10},{... | collective-permute-start | bytes 380936 | tf_op jit(solution)/shard_map/ppermute | solution.py:407
  8.2 4.7 %copy-start.2 = (f32[48,128]{1,0:T(8,128)S(1)}, f32[48,128]{1,0:T(8,128)}, u32[]{:S(2)}) copy-start(f32[48,128]{1,0:T(8,128)} %get-tuple-element.21) | copy-start | bytes 73732
  8.2 10.4 %collective-permute-start.1 = (f32[248,128]{1,0:T(8,128)}, f32[248,128]{1,0:T(8,128)}, u32[]{:S(2)}, u32[]{:S(2)}) collective-permute-start(f32[248,128]{1,0:T(8,128)} %get-tuple-element.14), channel_id=1, source_target_pairs={{0,12},{4,0},{8,4},{12,8},{1,13},{5,1},{9,5},{13,9},{2,14},{6,2},{... | collective-permute-start | bytes 380936 | tf_op jit(solution)/shard_map/ppermute | solution.py:407
  10.2 0.6 %copy-start = (f32[16,256]{1,0:T(8,128)}, f32[16,256]{1,0:T(8,128)S(1)}, u32[]{:S(2)}) copy-start(f32[16,256]{1,0:T(8,128)S(1)} %collective-permute-done.2.refs_13_) | copy-start | bytes 49156
  10.3 0.6 %copy-start.1 = (f32[16,256]{1,0:T(8,128)}, f32[16,256]{1,0:T(8,128)S(1)}, u32[]{:S(2)}) copy-start(f32[16,256]{1,0:T(8,128)S(1)} %collective-permute-done.3.refs_14_) | copy-start | bytes 49156
  10.9 5.4 %collective-permute-start.4 = (f32[8,256]{1,0:T(8,128)S(1)}, f32[8,256]{1,0:T(8,128)}, u32[]{:S(2)}, u32[]{:S(2)}) collective-permute-start(f32[8,256]{1,0:T(8,128)S(1)} %pad_maximum_fusion), channel_id=1, source_target_pairs={{0,12},{4,0},{8,4},{12,8},{1,13},{5,1},{9,5},{13,9},{2,14},{6,2},{... | collective-permute-start | bytes 24584 | tf_op jit(solution)/shard_map/ppermute | solution.py:407
  12.9 5.6 %collective-permute-start.6 = (f32[48,128]{1,0:T(8,128)S(1)}, f32[48,128]{1,0:T(8,128)}, u32[]{:S(2)}, u32[]{:S(2)}) collective-permute-start(f32[48,128]{1,0:T(8,128)S(1)} %copy-done.2), channel_id=1, source_target_pairs={{0,8},{4,12},{8,0},{12,4},{1,9},{5,13},{9,1},{13,5},{2,10},{6,14},... | collective-permute-start | bytes 73736 | tf_op jit(solution)/shard_map/ppermute | solution.py:407
  13.0 5.6 %collective-permute-start.5 = (f32[8,256]{1,0:T(8,128)S(1)}, f32[8,256]{1,0:T(8,128)}, u32[]{:S(2)}, u32[]{:S(2)}) collective-permute-start(f32[8,256]{1,0:T(8,128)S(1)} %pad_maximum_fusion.1), channel_id=1, source_target_pairs={{0,4},{4,8},{8,12},{12,0},{1,5},{5,9},{9,13},{13,1},{2,6},{6,10},{... | collective-permute-start | bytes 24584 | tf_op jit(solution)/shard_map/ppermute | solution.py:407

commit v10 on v9

--- a/solution.py
+++ b/solution.py
@@ -30,10 +30,30 @@
 
 
 def row_slots(levels, tracers):
-    per = 3 * AH - 2
-    base = per * levels
-    misc = base + OH * tracers
-    return per, base, misc, misc + AH + 2 * OH
+    tracer = 5 * levels
+    misc = tracer + OH * tracers
+    own = misc + AH + 2 * OH
+    _, lanes = lane_slots(levels, tracers)
+    return tracer, misc, own, own + 2 * AH * (lanes // 128)
+
+
+def near_rows(u, v, h, speed, rows, cols):
+    east_west = (pltpu.roll(u, cols - 1, 1) - pltpu.roll(u, 1, 1)) * 0.5
+    south_north = (pltpu.roll(v, rows - 1, 0) - pltpu.roll(v, 1, 0)) * 0.5
+    h1 = h - speed * (east_west + south_north)
+    out = []
+    for near, turn in ((0, 1), (rows - 1, -1)):
+        at = [slice(near + turn * i, near + turn * i + 1) for i in range(3)]
+        out.append(
+            (
+                u[at[0]],
+                v[at[0]],
+                h[at[0]] - (0.5 * turn) * speed[at[0]] * v[at[1]],
+                h1[at[1]],
+                h1[at[2]] - (2.0 * turn) * v[at[1]],
+            )
+        )
+    return out
 
 
 def split3(value):
@@ -81,9 +101,9 @@
 
 
 def first_kernel(tiles, *refs):
-    sources, (left_out, right_out, up_out, down_out, wair_out, *sums_out) = refs[:10], refs[10:-17]
-    held, (up, down, left, right, wair_buf, sums, sems) = refs[-17:-7], refs[-7:]
-    atm, ocean, depth, wet, kappa, air, atm_cell, dest, sea_cell, weight = held
+    sources, (left_out, right_out, up_out, down_out, wair_out, *sums_out) = refs[:11], refs[11:-18]
+    held, (up, down, left, right, wair_buf, sums, sems) = refs[-18:-7], refs[-7:]
+    atm, ocean, depth, wet, kappa, air, atm_cell, dest, sea_cell, weight, wave_speed = held
     used = []
 
     def copy(source, target):
@@ -96,7 +116,7 @@
     rows, cols = atm.shape[2:]
     tracers = ocean.shape[0] * ocean.shape[1]
     each = ocean.shape[1]
-    per, obase, mbase, _ = row_slots(levels, tracers)
+    obase, mbase, own, halo = row_slots(levels, tracers)
     slots, _ = lane_slots(levels, tracers)
     for one in used:
         one.wait()
@@ -129,10 +149,19 @@
     copy(right, right_out)
 
     for level in range(levels):
-        base = per * level
-        for at, which, width in ((0, 1, AH), (AH, 0, AH - 1), (2 * AH - 1, 2, AH - 1)):
-            up[base + at : base + at + width, :] = atm[which, level, 0:width, :]
-            down[base + at : base + at + width, :] = atm[which, level, rows - width : rows, :]
+        speed = wave_speed[level] * depth[...]
+        both = near_rows(atm[0, level], atm[1, level], atm[2, level], speed, rows, cols)
+        for ref, values in zip((up, down), both):
+            for i, value in enumerate(values):
+                at = i * levels + level
+                ref[at : at + 1, :] = value
+    at = own
+    for strip in (left, right):
+        for i in range(strip.shape[1] // cols):
+            where = slice(i * cols, (i + 1) * cols)
+            up[at : at + AH, :] = strip[0:AH, where]
+            down[at : at + AH, :] = strip[rows - AH : rows, where]
+            at += AH
     for i in range(tracers):
         at = obase + OH * i
         up[at : at + OH, :] = ocean[i // each, i % each, 0:OH, :]
@@ -144,7 +173,6 @@
     ):
         up[at : at + width, :] = value[0:width]
         down[at : at + width, :] = value[rows - width : rows]
-    halo = up.shape[0]
     copy(up, up_out.at[0:halo])
     copy(down, down_out.at[0:halo])
 
@@ -188,15 +216,6 @@
     return jnp.where(low_half, a, b)
 
 
-def row_slices(levels, tracers):
-    per, obase, mbase, _ = row_slots(levels, tracers)
-    out = [(per * level + AH, AH - 1) for level in range(levels)]
-    out += [(per * level, AH) for level in range(levels)]
-    out += [(per * level + 2 * AH - 1, AH - 1) for level in range(levels)]
-    out += [(obase + OH * i, OH) for i in range(tracers)]
-    return out + [(mbase, AH), (mbase + AH, OH), (mbase + AH + OH, OH)]
-
-
 def final_kernel(tiles, *refs):
     speed_in, atm_in, ocean_in, depth_in, kappa_in = refs[:5]
     kept = (len(refs) - 5 - 8 - 4) // 2
@@ -210,7 +229,7 @@
     tracers = ocean_out.shape[0] * each
     rows, cols = atm_out.shape[2:]
     slots, lanes = lane_slots(levels, tracers)
-    slices = row_slices(levels, tracers)
+    obase, mbase, own, halo = row_slots(levels, tracers)
     full = rows + 2 * AH
     block = (slice(None), slice(0, rows), slice(0, cols))
     pairs = list(zip(sources, held)) + [(speed_in, speed)]
@@ -222,8 +241,6 @@
         copy.start()
     for copy in copies:
         copy.wait()
-
-    halo = row_slots(levels, tracers)[3]
 
     def message(shift, part):
         where = slice(part * rows, (part + 1) * rows)
@@ -255,12 +272,12 @@
         at, where = i // half * AH, slice(i % half * cols, (i % half + 1) * cols)
         edge[i, 0:AH, :] = from_below[at : at + AH, where]
         edge[i, AH : 2 * AH, :] = from_above[at : at + AH, where]
+        at = own + AH * i
+        edge[2 * half + i, 0:AH, :] = from_down[at : at + AH, :]
+        edge[2 * half + i, AH : 2 * AH, :] = from_up[at : at + AH, :]
 
     def extend(view, field, width):
-        at, high = slices[field]
         slot = slots[field]
-        view[rows : rows + high, 0:cols] = from_down[at : at + high, :]
-        view[full - high : full, 0:cols] = from_up[at : at + high, :]
         view[0:rows, cols : 2 * cols] = strips(
             cols,
             slot,
@@ -270,6 +287,33 @@
         )
         view[rows:full, cols : 2 * cols] = strips(cols, slot, width, lambda t: edge[t], lambda t: edge[half + t])
 
+    def extend_rows(view, at, high):
+        view[rows : rows + high, 0:cols] = from_down[at : at + high, :]
+        view[full - high : full, 0:cols] = from_up[at : at + high, :]
+
+    lane = lax.broadcasted_iota(jnp.int32, (2 * AH, cols), 1)
+    line = lax.broadcasted_iota(jnp.int32, (2 * AH, cols), 0)
+    whole_strip = (lane < AH) | (lane >= cols - AH)
+    outer = (lane < AH - 1) | (lane > cols - AH)
+
+    def near(which, level):
+        at = which * levels + level
+        return from_down[at : at + 1, :], from_up[at : at + 1, :]
+
+    def extend_level(view, which, level):
+        strip = strips(cols, slots[which * levels + level], AH, lambda t: edge[3 * half + t], lambda t: edge[2 * half + t])
+        below, above = near(which, level)
+        inner = jnp.where(line == 0, below, jnp.where(line == 2 * AH - 1, above, 0.0))
+        view[rows:full, 0:cols] = jnp.where(whole_strip if which == 0 else outer, strip, inner)
+
+    def new_height_rows(tile, level):
+        below, above = near(3, level), near(4, level)
+        sent = jnp.where(
+            line == 1, below[0], jnp.where(line == 2, above[0], jnp.where(line == 2 * AH - 3, above[1], below[1]))
+        )
+        here = (line == 1) | (line == 2) | (line == 2 * AH - 3) | (line == 2 * AH - 2)
+        return jnp.where(here & jnp.logical_not(outer), sent, tile)
+
     def east(f):
         return pltpu.roll(f, 2 * cols - 1, 1)
 
@@ -284,14 +328,16 @@
 
     base = 3 * levels + tracers
     ms[1, 0:rows, 0:cols] = wet[...].astype(F32)
-    for i in range(3):
+    for i, (at, high) in enumerate(((mbase, AH), (mbase + AH, OH), (mbase + AH + OH, OH))):
         extend(ms.at[i], base + i, AH)
+        extend_rows(ms.at[i], at, high)
     for i in range(tracers):
         extend(fs.at[i // each, i % each], 3 * levels + i, OH)
+        extend_rows(fs.at[i // each, i % each], obase + OH * i, OH)
     for level in range(levels):
-        extend(us.at[level], level, AH)
-        extend(vs.at[level], levels + level, AH)
-        extend(hs.at[level], 2 * levels + level, AH)
+        for which, ref in enumerate((us, vs, hs)):
+            extend(ref.at[level], which * levels + level, AH)
+            extend_level(ref.at[level], which, level)
 
     w = ms[1]
     k = ms[2]
@@ -320,6 +366,8 @@
             u, v, h = us[level], vs[level], hs[level]
             column_speed = speed[level] * d
             hs[level] = h - column_speed * ((east(u) - west(u)) * 0.5 + (south(v) - north(v)) * 0.5)
+            if step == 0:
+                hs[level, rows:full, 0:cols] = new_height_rows(hs[level, rows:full, 0:cols], level)
         for level in range(levels):
             u, v, h = us[level], vs[level], hs[level]
             u = u - (east(h) - west(h)) * 0.5
@@ -383,18 +431,20 @@
     sea_cell = xg_ocean_cell.reshape(1, cells)
     weight = xg_weight.reshape(1, cells)
     operands = (atm_state, ocean_state, depth, wet_mask, diffusivity, air_temp, atm_cell, dest, sea_cell, weight)
+    operands += (wave_speed,)
     left, right, up, down, wair, *messages = pl.pallas_call(
         functools.partial(first_kernel, tile_count),
         out_shape=[shape(rows, lanes)] * 2 + [shape(message_rows, cols)] * 2 + [shape(1, cells)] + sums,
-        in_specs=[hbm] * 10,
+        in_specs=[hbm] * 11,
         out_specs=[hbm] * (5 + len(sums)),
-        scratch_shapes=[pltpu.VMEM(x.shape, x.dtype) for x in operands]
+        scratch_shapes=[pltpu.VMEM(x.shape, x.dtype) for x in operands[:-1]]
+        + [pltpu.SMEM(wave_speed.shape, F32)]
         + [pltpu.VMEM((halo, cols), F32)] * 2
         + [pltpu.VMEM((rows, lanes), F32)] * 2
         + [
             pltpu.VMEM((1, cells), F32),
             pltpu.VMEM((tile_count, 3 * rows, cols), F32),
-            pltpu.SemaphoreType.DMA((15 + tile_count,)),
+            pltpu.SemaphoreType.DMA((16 + tile_count,)),
         ],
         compiler_params=whole,
         name="first",
@@ -436,7 +486,7 @@
             ]
             + [pltpu.VMEM(x.shape, x.dtype) for x in operands[5:]]
             + [
-                pltpu.VMEM((2 * (lanes // cols), 2 * AH, cols), F32),
+                pltpu.VMEM((4 * (lanes // cols), 2 * AH, cols), F32),
                 pltpu.VMEM(atm_state.shape, F32),
                 pltpu.VMEM(ocean_state.shape, F32),
                 pltpu.SemaphoreType.DMA((len(operands) + 10,)),

time: 23 us -> 23.1 us (level)
  no operation moved by 1% of the time
where the time goes in v10:
time: 23.1 us; the launch traced here: 22.9 us
  starting transfers between devices  9.94 us (43%)
  Pallas kernels  7.03 us (30%)
  waiting for transfers between devices  4.61 us (20%)
  between operations  0.68 us (3%)
  local copies, waits for them, and re-layouts  0.58 us (3%)
    ppermute x7, starting transfers between devices, shift(): lax.ppermute(value, axes, [(i, (i + by) % count) for i in range(count)])  9.94 us
    ppermute x7, waiting for transfers between devices, shift(): lax.ppermute(value, axes, [(i, (i + by) % count) for i in range(count)])  4.61 us
    pallas_call x1, Pallas kernels, on_device(): pl.pallas_call(functools.partial(final_kernel, tile_count), out_shape=[sh...  4.22 us
    pallas_call x1, Pallas kernels, on_device(): pl.pallas_call(functools.partial(first_kernel, tile_count), out_shape=[sh...  2.81 us
    unnamed x6, local copies, waits for them, and re-layouts  0.57 us
  transfers between devices with their start and end apart: 7, of which 2 were waited for; matrix products, arithmetic and copies ran while one was open for 0% of the time, Pallas kernels for 0%

profile of v10, /device:TPU:0, one launch (start us, length us, event | category | flops | bytes accessed | tf_op | source)
XLA Modules:
  0.0 22.9 jit_solution(16676276692476546103)
XLA Ops:
  0.6 2.8 %first.1 = (f32[16,256]{1,0:T(8,128)}, f32[16,256]{1,0:T(8,128)}, f32[184,128]{1,0:T(8,128)}, f32[184,128]{1,0:T(8,128)}, f32[1,2048]{1,0:T(1,128)}, /*index=5*/f32[48,128]{1,0:T(8,128)}, f32[48,128]{1,0:T(8,128)}) custom-call(f32[3,16,16,128]{3,2,1,0:T(8,128)} %refs_1_.3, f32[2,8,16,128]{3,2,1,0:T(8,128)} %refs_2_.3, f32[16,128]{1,0:T(8,128)} %refs_3_.3, ...), custom_call_target="tpu_custom_call" | custom-call | tf_op jit(solution)/shard_map/first/pallas_call | solution.py:435
  3.5 0.5 %collective-permute-start.2 = (f32[16,256]{1,0:T(8,128)}, f32[16,256]{1,0:T(8,128)S(1)}, u32[]{:S(2)}, u32[]{:S(2)}) collective-permute-start(f32[16,256]{1,0:T(8,128)} %get-tuple-element.17), channel_id=1, source_target_pairs={{0,1},{1,2},{2,3},{3,0},{4,5},{5,6},{6,7},{7,4},{8,9},{9,10},{10,1... | collective-permute-start | bytes 49160 | tf_op jit(solution)/shard_map/ppermute | solution.py:457
  4.0 2.0 %collective-permute-start.3 = (f32[16,256]{1,0:T(8,128)}, f32[16,256]{1,0:T(8,128)S(1)}, u32[]{:S(2)}, u32[]{:S(2)}) collective-permute-start(f32[16,256]{1,0:T(8,128)} %get-tuple-element.19), channel_id=1, source_target_pairs={{0,3},{1,0},{2,1},{3,2},{4,7},{5,4},{6,5},{7,6},{8,11},{9,8},{10,9... | collective-permute-start | bytes 49160 | tf_op jit(solution)/shard_map/ppermute | solution.py:457
  5.9 2.3 %collective-permute-start = (f32[184,128]{1,0:T(8,128)}, f32[184,128]{1,0:T(8,128)}, u32[]{:S(2)}, u32[]{:S(2)}) collective-permute-start(f32[184,128]{1,0:T(8,128)} %get-tuple-element.13), channel_id=1, source_target_pairs={{0,4},{4,8},{8,12},{12,0},{1,5},{5,9},{9,13},{13,1},{2,6},{6,10},{... | collective-permute-start | bytes 282632 | tf_op jit(solution)/shard_map/ppermute | solution.py:457
  8.3 0.0 copy-start.2
  8.3 2.0 %collective-permute-start.1 = (f32[184,128]{1,0:T(8,128)}, f32[184,128]{1,0:T(8,128)}, u32[]{:S(2)}, u32[]{:S(2)}) collective-permute-start(f32[184,128]{1,0:T(8,128)} %get-tuple-element.14), channel_id=1, source_target_pairs={{0,12},{4,0},{8,4},{12,8},{1,13},{5,1},{9,5},{13,9},{2,14},{6,2},{... | collective-permute-start | bytes 282632 | tf_op jit(solution)/shard_map/ppermute | solution.py:457
  10.3 0.0 collective-permute-done.2.refs_13_
  10.3 0.0 copy-start
  10.3 0.0 collective-permute-done.3.refs_14_
  10.3 0.0 copy-start.1
  10.4 0.6 %copy-done = f32[16,256]{1,0:T(8,128)} copy-done((f32[16,256]{1,0:T(8,128)}, f32[16,256]{1,0:T(8,128)S(1)}, u32[]{:S(2)}) %copy-start) | copy-done | bytes 16408
  10.9 0.0 copy-done.1
  10.9 2.1 %collective-permute-start.4 = (f32[8,256]{1,0:T(8,128)S(1)}, f32[8,256]{1,0:T(8,128)}, u32[]{:S(2)}, u32[]{:S(2)}) collective-permute-start(f32[8,256]{1,0:T(8,128)S(1)} %pad_maximum_fusion), channel_id=1, source_target_pairs={{0,12},{4,0},{8,4},{12,8},{1,13},{5,1},{9,5},{13,9},{2,14},{6,2},{... | collective-permute-start | bytes 24584 | tf_op jit(solution)/shard_map/ppermute | solution.py:457
  13.0 0.0 copy-done.2
  13.0 0.0 collective-permute-start.6
  13.0 1.0 %collective-permute-start.5 = (f32[8,256]{1,0:T(8,128)S(1)}, f32[8,256]{1,0:T(8,128)}, u32[]{:S(2)}, u32[]{:S(2)}) collective-permute-start(f32[8,256]{1,0:T(8,128)S(1)} %pad_maximum_fusion.1), channel_id=1, source_target_pairs={{0,4},{4,8},{8,12},{12,0},{1,5},{5,9},{9,13},{13,1},{2,6},{6,10},{... | collective-permute-start | bytes 24584 | tf_op jit(solution)/shard_map/ppermute | solution.py:457
  14.0 1.0 %collective-permute-done.4.refs_15_ = f32[8,256]{1,0:T(8,128)} collective-permute-done((f32[8,256]{1,0:T(8,128)S(1)}, f32[8,256]{1,0:T(8,128)}, u32[]{:S(2)}, u32[]{:S(2)}) %collective-permute-start.4) | collective-permute-done | bytes 8224 | tf_op jit(solution)/shard_map/ppermute | solution.py:457
  15.0 3.6 %collective-permute-done.5.refs_16_ = f32[8,256]{1,0:T(8,128)} collective-permute-done((f32[8,256]{1,0:T(8,128)S(1)}, f32[8,256]{1,0:T(8,128)}, u32[]{:S(2)}, u32[]{:S(2)}) %collective-permute-start.5) | collective-permute-done | bytes 8224 | tf_op jit(solution)/shard_map/ppermute | solution.py:457
  18.6 0.0 collective-permute-done.6.refs_18_
  18.6 0.0 collective-permute-done.refs_11_
  18.6 0.0 collective-permute-done.1.refs_12_
  18.6 4.2 %steps.1 = (f32[3,16,16,128]{3,2,1,0:T(8,128)}, f32[2,8,16,128]{3,2,1,0:T(8,128)}) custom-call(f32[16]{0:T(128)} %refs_0_.3, f32[3,16,16,128]{3,2,1,0:T(8,128)} %refs_1_.3, f32[2,8,16,128]{3,2,1,0:T(8,128)} %refs_2_.3, f32[16,128]{1,0:T(8,128)} %refs_3_.3, f32[16,128]{1,0:T(8,128)} %refs_4_.3, s32[16,128]{1,0:T(8,128)} %refs_5_.3, s32[1,2048]{1,0:T(1,128)} %bitcast.5, ...), custom_call_target="tpu_custom_call" | custom-call | tf_op jit(solution)/shard_map/steps/pallas_call | solution.py:476
  (4 shorter events, 0.0 us)
Async XLA Ops:
  3.5 6.9 %collective-permute-start.2 = (f32[16,256]{1,0:T(8,128)}, f32[16,256]{1,0:T(8,128)S(1)}, u32[]{:S(2)}, u32[]{:S(2)}) collective-permute-start(f32[16,256]{1,0:T(8,128)} %get-tuple-element.17), channel_id=1, source_target_pairs={{0,1},{1,2},{2,3},{3,0},{4,5},{5,6},{6,7},{7,4},{8,9},{9,10},{10,1... | collective-permute-start | bytes 49160 | tf_op jit(solution)/shard_map/ppermute | solution.py:457
  4.0 6.4 %collective-permute-start.3 = (f32[16,256]{1,0:T(8,128)}, f32[16,256]{1,0:T(8,128)S(1)}, u32[]{:S(2)}, u32[]{:S(2)}) collective-permute-start(f32[16,256]{1,0:T(8,128)} %get-tuple-element.19), channel_id=1, source_target_pairs={{0,3},{1,0},{2,1},{3,2},{4,7},{5,4},{6,5},{7,6},{8,11},{9,8},{10,9... | collective-permute-start | bytes 49160 | tf_op jit(solution)/shard_map/ppermute | solution.py:457
  5.9 12.7 %collective-permute-start = (f32[184,128]{1,0:T(8,128)}, f32[184,128]{1,0:T(8,128)}, u32[]{:S(2)}, u32[]{:S(2)}) collective-permute-start(f32[184,128]{1,0:T(8,128)} %get-tuple-element.13), channel_id=1, source_target_pairs={{0,4},{4,8},{8,12},{12,0},{1,5},{5,9},{9,13},{13,1},{2,6},{6,10},{... | collective-permute-start | bytes 282632 | tf_op jit(solution)/shard_map/ppermute | solution.py:457
  8.3 4.7 %copy-start.2 = (f32[48,128]{1,0:T(8,128)S(1)}, f32[48,128]{1,0:T(8,128)}, u32[]{:S(2)}) copy-start(f32[48,128]{1,0:T(8,128)} %get-tuple-element.21) | copy-start | bytes 73732
  8.3 10.4 %collective-permute-start.1 = (f32[184,128]{1,0:T(8,128)}, f32[184,128]{1,0:T(8,128)}, u32[]{:S(2)}, u32[]{:S(2)}) collective-permute-start(f32[184,128]{1,0:T(8,128)} %get-tuple-element.14), channel_id=1, source_target_pairs={{0,12},{4,0},{8,4},{12,8},{1,13},{5,1},{9,5},{13,9},{2,14},{6,2},{... | collective-permute-start | bytes 282632 | tf_op jit(solution)/shard_map/ppermute | solution.py:457
  10.3 0.6 %copy-start = (f32[16,256]{1,0:T(8,128)}, f32[16,256]{1,0:T(8,128)S(1)}, u32[]{:S(2)}) copy-start(f32[16,256]{1,0:T(8,128)S(1)} %collective-permute-done.2.refs_13_) | copy-start | bytes 49156
  10.3 0.6 %copy-start.1 = (f32[16,256]{1,0:T(8,128)}, f32[16,256]{1,0:T(8,128)S(1)}, u32[]{:S(2)}) copy-start(f32[16,256]{1,0:T(8,128)S(1)} %collective-permute-done.3.refs_14_) | copy-start | bytes 49156
  10.9 4.1 %collective-permute-start.4 = (f32[8,256]{1,0:T(8,128)S(1)}, f32[8,256]{1,0:T(8,128)}, u32[]{:S(2)}, u32[]{:S(2)}) collective-permute-start(f32[8,256]{1,0:T(8,128)S(1)} %pad_maximum_fusion), channel_id=1, source_target_pairs={{0,12},{4,0},{8,4},{12,8},{1,13},{5,1},{9,5},{13,9},{2,14},{6,2},{... | collective-permute-start | bytes 24584 | tf_op jit(solution)/shard_map/ppermute | solution.py:457
  13.0 5.6 %collective-permute-start.6 = (f32[48,128]{1,0:T(8,128)S(1)}, f32[48,128]{1,0:T(8,128)}, u32[]{:S(2)}, u32[]{:S(2)}) collective-permute-start(f32[48,128]{1,0:T(8,128)S(1)} %copy-done.2), channel_id=1, source_target_pairs={{0,8},{4,12},{8,0},{12,4},{1,9},{5,13},{9,1},{13,5},{2,10},{6,14},... | collective-permute-start | bytes 73736 | tf_op jit(solution)/shard_map/ppermute | solution.py:457
  13.0 5.6 %collective-permute-start.5 = (f32[8,256]{1,0:T(8,128)S(1)}, f32[8,256]{1,0:T(8,128)}, u32[]{:S(2)}, u32[]{:S(2)}) collective-permute-start(f32[8,256]{1,0:T(8,128)S(1)} %pad_maximum_fusion.1), channel_id=1, source_target_pairs={{0,4},{4,8},{8,12},{12,0},{1,5},{5,9},{9,13},{13,1},{2,6},{6,10},{... | collective-permute-start | bytes 24584 | tf_op jit(solution)/shard_map/ppermute | solution.py:457

commit v11 on v10

--- a/solution.py
+++ b/solution.py
@@ -100,8 +100,16 @@
     return lax.rem(lax.axis_index("tile") + shift % tiles, tiles)
 
 
+def tile_parity():
+    return lax.rem(lax.axis_index("tile"), 2)
+
+
+def column_parity():
+    return lax.rem(lax.axis_index(("sub", "comp")), 2)
+
+
 def first_kernel(tiles, *refs):
-    sources, (left_out, right_out, up_out, down_out, wair_out, *sums_out) = refs[:11], refs[11:-18]
+    sources, (cols_a, cols_b, rows_a, rows_b, wair_out, *sums_out) = refs[:11], refs[11:-18]
     held, (up, down, left, right, wair_buf, sums, sems) = refs[-18:-7], refs[-7:]
     atm, ocean, depth, wet, kappa, air, atm_cell, dest, sea_cell, weight, wave_speed = held
     used = []
@@ -110,6 +118,13 @@
         used.append(pltpu.make_async_copy(source, target, sems.at[len(used)]))
         used[-1].start()
 
+    def copy_either(parity, source, even, odd):
+        choices = [pltpu.make_async_copy(source, target, sems.at[len(used)]) for target in (even, odd)]
+        pl.when(parity == 0)(choices[0].start)
+        pl.when(parity != 0)(choices[1].start)
+        used.append(choices[0])
+
+    column, line = column_parity(), tile_parity()
     for source, target in zip(sources, held):
         copy(source, target)
     levels = atm.shape[1]
@@ -145,8 +160,8 @@
         left[:, where] = a
         right[:, where] = b
 
-    copy(left, left_out)
-    copy(right, right_out)
+    copy_either(column, right, cols_a, cols_b)
+    copy_either(column, left, cols_b, cols_a)
 
     for level in range(levels):
         speed = wave_speed[level] * depth[...]
@@ -173,8 +188,8 @@
     ):
         up[at : at + width, :] = value[0:width]
         down[at : at + width, :] = value[rows - width : rows]
-    copy(up, up_out.at[0:halo])
-    copy(down, down_out.at[0:halo])
+    copy_either(line, down, rows_a.at[0:halo], rows_b.at[0:halo])
+    copy_either(line, up, rows_b.at[0:halo], rows_a.at[0:halo])
 
     cell = atm_cell[...]
     hot_atm = jnp.where(one_hot(cell % cols, cols), 1.0, 0.0).astype(BF16)
@@ -186,6 +201,7 @@
     cell = sea_cell[...]
     hot_sea = jnp.where(one_hot(cell % cols, cols), 1.0, 0.0).astype(BF16)
     row = dest[...] * rows + cell // cols
+    tail = slice(halo, halo + 3 * rows)
     for shift in range(tiles):
         target = tile_at(shift, tiles)
         s1, s2 = scatter_rows([wair, w], one_hot(row - target * rows, rows), hot_sea)
@@ -195,9 +211,9 @@
         if len(sums_out) == 1:
             copy(sums.at[shift], sums_out[0].at[target])
         elif shift == 1:
-            copy(sums.at[shift], down_out.at[halo : halo + 3 * rows])
+            copy_either(line, sums.at[shift], rows_a.at[tail], rows_b.at[tail])
         elif shift == tiles - 1:
-            copy(sums.at[shift], up_out.at[halo : halo + 3 * rows])
+            copy_either(line, sums.at[shift], rows_b.at[tail], rows_a.at[tail])
         else:
             copy(sums.at[shift], sums_out[max(shift - 1, 0)])
     for one in used[arrived:]:
@@ -232,15 +248,25 @@
     obase, mbase, own, halo = row_slots(levels, tracers)
     full = rows + 2 * AH
     block = (slice(None), slice(0, rows), slice(0, cols))
-    pairs = list(zip(sources, held)) + [(speed_in, speed)]
+    rows_a, rows_b, cols_a, cols_b = sources[6:10]
+    either = [(tile_parity(), rows_b, rows_a, from_up), (tile_parity(), rows_a, rows_b, from_down)]
+    either += [(column_parity(), cols_b, cols_a, from_left), (column_parity(), cols_a, cols_b, from_right)]
+    pairs = [pair for i, pair in enumerate(zip(sources, held)) if not 6 <= i < 10] + [(speed_in, speed)]
     pairs += [(atm_in.at[i], ref.at[block]) for i, ref in enumerate((us, vs, hs))]
     pairs += [(ocean_in.at[i], fs.at[(i, *block)]) for i in range(ocean_out.shape[0])]
     pairs += [(ref, ms.at[(i, *block[1:])]) for i, ref in ((0, depth_in), (2, kappa_in))]
     copies = [pltpu.make_async_copy(source, target, sems.at[i]) for i, (source, target) in enumerate(pairs)]
     for copy in copies:
         copy.start()
+    for parity, even, odd, target in either:
+        choices = [pltpu.make_async_copy(source, target, sems.at[len(copies)]) for source in (even, odd)]
+        pl.when(parity == 0)(choices[0].start)
+        pl.when(parity != 0)(choices[1].start)
+        copies.append(choices[0])
     for copy in copies:
         copy.wait()
+    corner_a, corner_b = from_below, from_above
+    even_line, even_column = tile_parity() == 0, column_parity() == 0
 
     def message(shift, part):
         where = slice(part * rows, (part + 1) * rows)
@@ -269,9 +295,12 @@
 
     half = lanes // cols
     for i in range(2 * half):
-        at, where = i // half * AH, slice(i % half * cols, (i % half + 1) * cols)
-        edge[i, 0:AH, :] = from_below[at : at + AH, where]
-        edge[i, AH : 2 * AH, :] = from_above[at : at + AH, where]
+        where = slice(i % half * cols, (i % half + 1) * cols)
+        first, second = (slice(AH, 2 * AH), slice(0, AH)) if i < half else (slice(0, AH), slice(AH, 2 * AH))
+        a = jnp.where(even_column, corner_a[first, where], corner_a[second, where])
+        b = jnp.where(even_column, corner_b[first, where], corner_b[second, where])
+        edge[i, 0:AH, :] = jnp.where(even_line, a, b)
+        edge[i, AH : 2 * AH, :] = jnp.where(even_line, b, a)
         at = own + AH * i
         edge[2 * half + i, 0:AH, :] = from_down[at : at + AH, :]
         edge[2 * half + i, AH : 2 * AH, :] = from_up[at : at + AH, :]
@@ -432,7 +461,7 @@
     weight = xg_weight.reshape(1, cells)
     operands = (atm_state, ocean_state, depth, wet_mask, diffusivity, air_temp, atm_cell, dest, sea_cell, weight)
     operands += (wave_speed,)
-    left, right, up, down, wair, *messages = pl.pallas_call(
+    cols_a, cols_b, rows_a, rows_b, wair, *messages = pl.pallas_call(
         functools.partial(first_kernel, tile_count),
         out_shape=[shape(rows, lanes)] * 2 + [shape(message_rows, cols)] * 2 + [shape(1, cells)] + sums,
         in_specs=[hbm] * 11,
@@ -456,22 +485,29 @@
     def shift(value, axes, count, by):
         return lax.ppermute(value, axes, [(i, (i + by) % count) for i in range(count)])
 
-    from_right = shift(left, column_axes, column_count, -1)
-    from_left = shift(right, column_axes, column_count, 1)
-    from_down = shift(up, "tile", tile_count, -1)
-    from_up = shift(down, "tile", tile_count, 1)
-
-    from_below = shift(jnp.concatenate([from_left[0:AH], from_right[0:AH]]), "tile", tile_count, -1)
-    from_above = shift(jnp.concatenate([from_left[rows - AH :], from_right[rows - AH :]]), "tile", tile_count, 1)
+    def swap(value, axes, count, odd):
+        return lax.ppermute(value, axes, [(i, (i + (1 if (i + odd) % 2 == 0 else -1)) % count) for i in range(count)])
+
+    got_a = swap(cols_a, column_axes, column_count, 0)
+    got_b = swap(cols_b, column_axes, column_count, 1)
+    near_a = swap(rows_a, "tile", tile_count, 0)
+    near_b = swap(rows_b, "tile", tile_count, 1)
+
+    low = jnp.where(tile_parity() == 0, rows - AH, 0)
+    corner_a, corner_b = [
+        jnp.concatenate([lax.dynamic_slice_in_dim(x, at, AH) for x in (got_a, got_b)]) for at in (low, rows - AH - low)
+    ]
+    corner_a = swap(corner_a, "tile", tile_count, 0)
+    corner_b = swap(corner_b, "tile", tile_count, 1)
     if by_shift:
-        *messages, from_left = lax.optimization_barrier((*messages, from_left))
+        *messages, got_b = lax.optimization_barrier((*messages, got_b))
         got = messages[:1] + [shift(messages[s - 1], "tile", tile_count, s) for s in range(2, tile_count - 1)]
     else:
         got = [lax.all_to_all(messages[0], "tile", split_axis=0, concat_axis=0, tiled=True)]
 
     operands = (wave_speed, atm_state, ocean_state, depth, diffusivity)
-    operands += (wet_mask, atm_cell, dest, sea_cell, weight, wair, from_up, from_down, from_left, from_right)
-    operands += (from_below, from_above, *got)
+    operands += (wet_mask, atm_cell, dest, sea_cell, weight, wair, near_a, near_b, got_a, got_b)
+    operands += (corner_a, corner_b, *got)
     return tuple(
         pl.pallas_call(
             functools.partial(final_kernel, tile_count),

time: 23.1 us -> 23.4 us (1.013)
  starting transfers between devices: 9.94 us -> 11.6 us
  waiting for transfers between devices: 4.61 us -> 3.18 us
    ppermute x0 -> x6, starting transfers between devices: none -> 10.3 us  [swap(): lax.ppermute(value, axes, [(i, (i + (1 if (i + odd) % 2 == 0 else -1)) %...]
    ppermute x7 -> x1, starting transfers between devices: 9.94 us -> 1.32 us  [shift(): lax.ppermute(value, axes, [(i, (i + by) % count) for i in range(count)])]
    ppermute x7 -> x1, waiting for transfers between devices: 4.61 us -> 0.01 us  [shift(): lax.ppermute(value, axes, [(i, (i + by) % count) for i in range(count)])]
    ppermute x0 -> x6, waiting for transfers between devices: none -> 3.17 us  [swap(): lax.ppermute(value, axes, [(i, (i + (1 if (i + odd) % 2 == 0 else -1)) %...]
  transfers between devices with their start and end apart: 7 -> 7, of which waited for: 2 -> 1; matrix products, arithmetic and copies ran while one was open for 0% -> 0% of each run, Pallas kernels for 0% -> 0%
where the time goes in v11:
time: 23.4 us; the launch traced here: 23.2 us
  starting transfers between devices  11.6 us (50%)
  Pallas kernels  7.09 us (30%)
  waiting for transfers between devices  3.18 us (14%)
  between operations  0.69 us (3%)
  local copies, waits for them, and re-layouts  0.58 us (2%)
    ppermute x6, starting transfers between devices, swap(): lax.ppermute(value, axes, [(i, (i + (1 if (i + odd) % 2 == 0 else -1)) %...  10.3 us
    pallas_call x1, Pallas kernels, on_device(): pl.pallas_call(functools.partial(final_kernel, tile_count), out_shape=[sh...  4.28 us
    ppermute x6, waiting for transfers between devices, swap(): lax.ppermute(value, axes, [(i, (i + (1 if (i + odd) % 2 == 0 else -1)) %...  3.17 us
    pallas_call x1, Pallas kernels, on_device(): pl.pallas_call(functools.partial(first_kernel, tile_count), out_shape=[sh...  2.81 us
    ppermute x1, starting transfers between devices, shift(): lax.ppermute(value, axes, [(i, (i + by) % count) for i in range(count)])  1.32 us
    unnamed x6, local copies, waits for them, and re-layouts  0.56 us
  transfers between devices with their start and end apart: 7, of which 1 were waited for; matrix products, arithmetic and copies ran while one was open for 0% of the time, Pallas kernels for 0%

profile of v11, /device:TPU:0, one launch (start us, length us, event | category | flops | bytes accessed | tf_op | source)
XLA Modules:
  0.0 23.2 jit_solution(4328118188021101383)
XLA Ops:
  0.6 2.8 %first.1 = (f32[16,256]{1,0:T(8,128)}, f32[16,256]{1,0:T(8,128)}, f32[184,128]{1,0:T(8,128)}, f32[184,128]{1,0:T(8,128)}, f32[1,2048]{1,0:T(1,128)}, /*index=5*/f32[48,128]{1,0:T(8,128)}, f32[48,128]{1,0:T(8,128)}) custom-call(f32[3,16,16,128]{3,2,1,0:T(8,128)} %refs_1_.3, f32[2,8,16,128]{3,2,1,0:T(8,128)} %refs_2_.3, f32[16,128]{1,0:T(8,128)} %refs_3_.3, ...), custom_call_target="tpu_custom_call" | custom-call | tf_op jit(solution)/shard_map/first/pallas_call | solution.py:464
  3.4 2.4 %collective-permute-start.3 = (f32[16,256]{1,0:T(8,128)}, f32[16,256]{1,0:T(8,128)S(1)}, u32[]{:S(2)}, u32[]{:S(2)}) collective-permute-start(f32[16,256]{1,0:T(8,128)} %get-tuple-element.18), channel_id=1, source_target_pairs={{0,3},{1,2},{2,1},{3,0},{4,7},{5,6},{6,5},{7,4},{8,11},{9,10},{10,... | collective-permute-start | bytes 49160 | tf_op jit(solution)/shard_map/ppermute | solution.py:489
  5.9 0.7 %collective-permute-start.2 = (f32[16,256]{1,0:T(8,128)}, f32[16,256]{1,0:T(8,128)S(1)}, u32[]{:S(2)}, u32[]{:S(2)}) collective-permute-start(f32[16,256]{1,0:T(8,128)} %get-tuple-element.15), channel_id=1, source_target_pairs={{0,1},{1,0},{2,3},{3,2},{4,5},{5,4},{6,7},{7,6},{8,9},{9,8},{10,11... | collective-permute-start | bytes 49160 | tf_op jit(solution)/shard_map/ppermute | solution.py:489
  6.6 1.6 %collective-permute-start = (f32[184,128]{1,0:T(8,128)}, f32[184,128]{1,0:T(8,128)}, u32[]{:S(2)}, u32[]{:S(2)}) collective-permute-start(f32[184,128]{1,0:T(8,128)} %get-tuple-element.13), channel_id=1, source_target_pairs={{0,4},{4,0},{8,12},{12,8},{1,5},{5,1},{9,13},{13,9},{2,6},{6,2},{1... | collective-permute-start | bytes 282632 | tf_op jit(solution)/shard_map/ppermute | solution.py:489
  8.1 2.5 %collective-permute-start.1 = (f32[184,128]{1,0:T(8,128)}, f32[184,128]{1,0:T(8,128)}, u32[]{:S(2)}, u32[]{:S(2)}) collective-permute-start(f32[184,128]{1,0:T(8,128)} %get-tuple-element.14), channel_id=1, source_target_pairs={{0,12},{4,8},{8,4},{12,0},{1,13},{5,9},{9,5},{13,1},{2,14},{6,10},... | collective-permute-start | bytes 282632 | tf_op jit(solution)/shard_map/ppermute | solution.py:489
  10.6 0.0 collective-permute-done.3.refs_14_
  10.6 0.0 copy-start
  10.6 0.0 copy-start.2
  10.6 0.0 collective-permute-done.2.refs_13_
  10.7 0.0 copy-start.1
  10.7 0.5 %copy-done = f32[16,256]{1,0:T(8,128)} copy-done((f32[16,256]{1,0:T(8,128)}, f32[16,256]{1,0:T(8,128)S(1)}, u32[]{:S(2)}) %copy-start) | copy-done | bytes 16408
  11.2 0.0 copy-done.1
  11.3 0.7 %collective-permute-start.4 = (f32[8,256]{1,0:T(8,128)S(1)}, f32[8,256]{1,0:T(8,128)}, u32[]{:S(2)}, u32[]{:S(2)}) collective-permute-start(f32[8,256]{1,0:T(8,128)S(1)} %pad_maximum_fusion), channel_id=1, source_target_pairs={{0,4},{4,0},{8,12},{12,8},{1,5},{5,1},{9,13},{13,9},{2,6},{6,2},{1... | collective-permute-start | bytes 24584 | tf_op jit(solution)/shard_map/ppermute | solution.py:489
  12.0 0.0 copy-done.2
  12.0 1.3 %collective-permute-start.6 = (f32[48,128]{1,0:T(8,128)S(1)}, f32[48,128]{1,0:T(8,128)}, u32[]{:S(2)}, u32[]{:S(2)}) collective-permute-start(f32[48,128]{1,0:T(8,128)S(1)} %copy-done.2), channel_id=1, source_target_pairs={{0,8},{4,12},{8,0},{12,4},{1,9},{5,13},{9,1},{13,5},{2,10},{6,14},... | collective-permute-start | bytes 73736 | tf_op jit(solution)/shard_map/ppermute | solution.py:486
  13.3 2.4 %collective-permute-start.5 = (f32[8,256]{1,0:T(8,128)S(1)}, f32[8,256]{1,0:T(8,128)}, u32[]{:S(2)}, u32[]{:S(2)}) collective-permute-start(f32[8,256]{1,0:T(8,128)S(1)} %pad_maximum_fusion.1), channel_id=1, source_target_pairs={{0,12},{4,8},{8,4},{12,0},{1,13},{5,9},{9,5},{13,1},{2,14},{6,10},... | collective-permute-start | bytes 24584 | tf_op jit(solution)/shard_map/ppermute | solution.py:489
  15.7 0.0 collective-permute-done.4.refs_15_
  15.7 3.1 %collective-permute-done.5.refs_16_ = f32[8,256]{1,0:T(8,128)} collective-permute-done((f32[8,256]{1,0:T(8,128)S(1)}, f32[8,256]{1,0:T(8,128)}, u32[]{:S(2)}, u32[]{:S(2)}) %collective-permute-start.5) | collective-permute-done | bytes 8224 | tf_op jit(solution)/shard_map/ppermute | solution.py:489
  18.9 0.0 collective-permute-done.6.refs_18_
  18.9 0.0 collective-permute-done.refs_11_
  18.9 0.0 collective-permute-done.1.refs_12_
  18.9 4.3 %steps.1 = (f32[3,16,16,128]{3,2,1,0:T(8,128)}, f32[2,8,16,128]{3,2,1,0:T(8,128)}) custom-call(f32[16]{0:T(128)} %refs_0_.3, f32[3,16,16,128]{3,2,1,0:T(8,128)} %refs_1_.3, f32[2,8,16,128]{3,2,1,0:T(8,128)} %refs_2_.3, f32[16,128]{1,0:T(8,128)} %refs_3_.3, f32[16,128]{1,0:T(8,128)} %refs_4_.3, s32[16,128]{1,0:T(8,128)} %refs_5_.3, s32[1,2048]{1,0:T(1,128)} %bitcast.5, ...), custom_call_target="tpu_custom_call" | custom-call | tf_op jit(solution)/shard_map/steps/pallas_call | solution.py:512
  (4 shorter events, 0.0 us)
Async XLA Ops:
  3.4 7.2 %collective-permute-start.3 = (f32[16,256]{1,0:T(8,128)}, f32[16,256]{1,0:T(8,128)S(1)}, u32[]{:S(2)}, u32[]{:S(2)}) collective-permute-start(f32[16,256]{1,0:T(8,128)} %get-tuple-element.18), channel_id=1, source_target_pairs={{0,3},{1,2},{2,1},{3,0},{4,7},{5,6},{6,5},{7,4},{8,11},{9,10},{10,... | collective-permute-start | bytes 49160 | tf_op jit(solution)/shard_map/ppermute | solution.py:489
  5.9 4.8 %collective-permute-start.2 = (f32[16,256]{1,0:T(8,128)}, f32[16,256]{1,0:T(8,128)S(1)}, u32[]{:S(2)}, u32[]{:S(2)}) collective-permute-start(f32[16,256]{1,0:T(8,128)} %get-tuple-element.15), channel_id=1, source_target_pairs={{0,1},{1,0},{2,3},{3,2},{4,5},{5,4},{6,7},{7,6},{8,9},{9,8},{10,11... | collective-permute-start | bytes 49160 | tf_op jit(solution)/shard_map/ppermute | solution.py:489
  6.6 12.3 %collective-permute-start = (f32[184,128]{1,0:T(8,128)}, f32[184,128]{1,0:T(8,128)}, u32[]{:S(2)}, u32[]{:S(2)}) collective-permute-start(f32[184,128]{1,0:T(8,128)} %get-tuple-element.13), channel_id=1, source_target_pairs={{0,4},{4,0},{8,12},{12,8},{1,5},{5,1},{9,13},{13,9},{2,6},{6,2},{1... | collective-permute-start | bytes 282632 | tf_op jit(solution)/shard_map/ppermute | solution.py:489
  8.1 10.7 %collective-permute-start.1 = (f32[184,128]{1,0:T(8,128)}, f32[184,128]{1,0:T(8,128)}, u32[]{:S(2)}, u32[]{:S(2)}) collective-permute-start(f32[184,128]{1,0:T(8,128)} %get-tuple-element.14), channel_id=1, source_target_pairs={{0,12},{4,8},{8,4},{12,0},{1,13},{5,9},{9,5},{13,1},{2,14},{6,10},... | collective-permute-start | bytes 282632 | tf_op jit(solution)/shard_map/ppermute | solution.py:489
  10.6 0.6 %copy-start = (f32[16,256]{1,0:T(8,128)}, f32[16,256]{1,0:T(8,128)S(1)}, u32[]{:S(2)}) copy-start(f32[16,256]{1,0:T(8,128)S(1)} %collective-permute-done.3.refs_14_) | copy-start | bytes 49156
  10.6 1.3 %copy-start.2 = (f32[48,128]{1,0:T(8,128)S(1)}, f32[48,128]{1,0:T(8,128)}, u32[]{:S(2)}) copy-start(f32[48,128]{1,0:T(8,128)} %get-tuple-element.21) | copy-start | bytes 73732
  10.7 0.6 %copy-start.1 = (f32[16,256]{1,0:T(8,128)}, f32[16,256]{1,0:T(8,128)S(1)}, u32[]{:S(2)}) copy-start(f32[16,256]{1,0:T(8,128)S(1)} %collective-permute-done.2.refs_13_) | copy-start | bytes 49156
  11.3 4.5 %collective-permute-start.4 = (f32[8,256]{1,0:T(8,128)S(1)}, f32[8,256]{1,0:T(8,128)}, u32[]{:S(2)}, u32[]{:S(2)}) collective-permute-start(f32[8,256]{1,0:T(8,128)S(1)} %pad_maximum_fusion), channel_id=1, source_target_pairs={{0,4},{4,0},{8,12},{12,8},{1,5},{5,1},{9,13},{13,9},{2,6},{6,2},{1... | collective-permute-start | bytes 24584 | tf_op jit(solution)/shard_map/ppermute | solution.py:489
  12.0 6.9 %collective-permute-start.6 = (f32[48,128]{1,0:T(8,128)S(1)}, f32[48,128]{1,0:T(8,128)}, u32[]{:S(2)}, u32[]{:S(2)}) collective-permute-start(f32[48,128]{1,0:T(8,128)S(1)} %copy-done.2), channel_id=1, source_target_pairs={{0,8},{4,12},{8,0},{12,4},{1,9},{5,13},{9,1},{13,5},{2,10},{6,14},... | collective-permute-start | bytes 73736 | tf_op jit(solution)/shard_map/ppermute | solution.py:486
  13.3 5.6 %collective-permute-start.5 = (f32[8,256]{1,0:T(8,128)S(1)}, f32[8,256]{1,0:T(8,128)}, u32[]{:S(2)}, u32[]{:S(2)}) collective-permute-start(f32[8,256]{1,0:T(8,128)S(1)} %pad_maximum_fusion.1), channel_id=1, source_target_pairs={{0,12},{4,8},{8,4},{12,0},{1,13},{5,9},{9,5},{13,1},{2,14},{6,10},... | collective-permute-start | bytes 24584 | tf_op jit(solution)/shard_map/ppermute | solution.py:489

commit v12 on v11

--- a/solution.py
+++ b/solution.py
@@ -101,7 +101,7 @@
 
 
 def tile_parity():
-    return lax.rem(lax.axis_index("tile"), 2)
+    return lax.rem(lax.axis_index("tile") + 1, 2)
 
 
 def column_parity():
@@ -490,15 +490,15 @@
 
     got_a = swap(cols_a, column_axes, column_count, 0)
     got_b = swap(cols_b, column_axes, column_count, 1)
-    near_a = swap(rows_a, "tile", tile_count, 0)
-    near_b = swap(rows_b, "tile", tile_count, 1)
+    near_a = swap(rows_a, "tile", tile_count, 1)
+    near_b = swap(rows_b, "tile", tile_count, 0)
 
     low = jnp.where(tile_parity() == 0, rows - AH, 0)
     corner_a, corner_b = [
         jnp.concatenate([lax.dynamic_slice_in_dim(x, at, AH) for x in (got_a, got_b)]) for at in (low, rows - AH - low)
     ]
-    corner_a = swap(corner_a, "tile", tile_count, 0)
-    corner_b = swap(corner_b, "tile", tile_count, 1)
+    corner_a = swap(corner_a, "tile", tile_count, 1)
+    corner_b = swap(corner_b, "tile", tile_count, 0)
     if by_shift:
         *messages, got_b = lax.optimization_barrier((*messages, got_b))
         got = messages[:1] + [shift(messages[s - 1], "tile", tile_count, s) for s in range(2, tile_count - 1)]

time: 23.4 us -> 22.6 us (0.966)
  starting transfers between devices: 11.6 us -> 11.1 us
  waiting for transfers between devices: 3.18 us -> 2.87 us
    ppermute x6, starting transfers between devices: 10.3 us -> 9.54 us  [swap(): lax.ppermute(value, axes, [(i, (i + (1 if (i + odd) % 2 == 0 else -1)) %...]
    ppermute x6, waiting for transfers between devices: 3.17 us -> 2.86 us  [swap(): lax.ppermute(value, axes, [(i, (i + (1 if (i + odd) % 2 == 0 else -1)) %...]
    ppermute x1, starting transfers between devices: 1.32 us -> 1.61 us  [shift(): lax.ppermute(value, axes, [(i, (i + by) % count) for i in range(count)])]
  transfers between devices with their start and end apart: 7 -> 7, of which waited for: 1 -> 2; matrix products, arithmetic and copies ran while one was open for 0% -> 0% of each run, Pallas kernels for 0% -> 0%
where the time goes in v12:
time: 22.6 us; the launch traced here: 22.4 us
  starting transfers between devices  11.1 us (49%)
  Pallas kernels  7.09 us (31%)
  waiting for transfers between devices  2.87 us (13%)
  between operations  0.69 us (3%)
  local copies, waits for them, and re-layouts  0.59 us (3%)
    ppermute x6, starting transfers between devices, swap(): lax.ppermute(value, axes, [(i, (i + (1 if (i + odd) % 2 == 0 else -1)) %...  9.54 us
    pallas_call x1, Pallas kernels, on_device(): pl.pallas_call(functools.partial(final_kernel, tile_count), out_shape=[sh...  4.28 us
    ppermute x6, waiting for transfers between devices, swap(): lax.ppermute(value, axes, [(i, (i + (1 if (i + odd) % 2 == 0 else -1)) %...  2.86 us
    pallas_call x1, Pallas kernels, on_device(): pl.pallas_call(functools.partial(first_kernel, tile_count), out_shape=[sh...  2.81 us
    ppermute x1, starting transfers between devices, shift(): lax.ppermute(value, axes, [(i, (i + by) % count) for i in range(count)])  1.61 us
    unnamed x6, local copies, waits for them, and re-layouts  0.56 us
  transfers between devices with their start and end apart: 7, of which 2 were waited for; matrix products, arithmetic and copies ran while one was open for 0% of the time, Pallas kernels for 0%

profile of v12, /device:TPU:0, one launch (start us, length us, event | category | flops | bytes accessed | tf_op | source)
XLA Modules:
  0.0 22.4 jit_solution(5664795289517135224)
XLA Ops:
  0.6 2.8 %first.1 = (f32[16,256]{1,0:T(8,128)}, f32[16,256]{1,0:T(8,128)}, f32[184,128]{1,0:T(8,128)}, f32[184,128]{1,0:T(8,128)}, f32[1,2048]{1,0:T(1,128)}, /*index=5*/f32[48,128]{1,0:T(8,128)}, f32[48,128]{1,0:T(8,128)}) custom-call(f32[3,16,16,128]{3,2,1,0:T(8,128)} %refs_1_.3, f32[2,8,16,128]{3,2,1,0:T(8,128)} %refs_2_.3, f32[16,128]{1,0:T(8,128)} %refs_3_.3, ...), custom_call_target="tpu_custom_call" | custom-call | tf_op jit(solution)/shard_map/first/pallas_call | solution.py:464
  3.4 2.4 %collective-permute-start.3 = (f32[16,256]{1,0:T(8,128)}, f32[16,256]{1,0:T(8,128)S(1)}, u32[]{:S(2)}, u32[]{:S(2)}) collective-permute-start(f32[16,256]{1,0:T(8,128)} %get-tuple-element.18), channel_id=1, source_target_pairs={{0,3},{1,2},{2,1},{3,0},{4,7},{5,6},{6,5},{7,4},{8,11},{9,10},{10,... | collective-permute-start | bytes 49160 | tf_op jit(solution)/shard_map/ppermute | solution.py:489
  5.9 0.7 %collective-permute-start.2 = (f32[16,256]{1,0:T(8,128)}, f32[16,256]{1,0:T(8,128)S(1)}, u32[]{:S(2)}, u32[]{:S(2)}) collective-permute-start(f32[16,256]{1,0:T(8,128)} %get-tuple-element.15), channel_id=1, source_target_pairs={{0,1},{1,0},{2,3},{3,2},{4,5},{5,4},{6,7},{7,6},{8,9},{9,8},{10,11... | collective-permute-start | bytes 49160 | tf_op jit(solution)/shard_map/ppermute | solution.py:489
  6.6 3.6 %collective-permute-start = (f32[184,128]{1,0:T(8,128)}, f32[184,128]{1,0:T(8,128)}, u32[]{:S(2)}, u32[]{:S(2)}) collective-permute-start(f32[184,128]{1,0:T(8,128)} %get-tuple-element.13), channel_id=1, source_target_pairs={{0,12},{4,8},{8,4},{12,0},{1,13},{5,9},{9,5},{13,1},{2,14},{6,10},... | collective-permute-start | bytes 282632 | tf_op jit(solution)/shard_map/ppermute | solution.py:489
  10.2 0.0 collective-permute-start.1
  10.2 0.0 collective-permute-done.3.refs_14_
  10.2 0.0 copy-start
  10.2 0.0 copy-start.2
  10.2 0.0 collective-permute-done.2.refs_13_
  10.2 0.0 copy-start.1
  10.3 0.5 %copy-done = f32[16,256]{1,0:T(8,128)} copy-done((f32[16,256]{1,0:T(8,128)}, f32[16,256]{1,0:T(8,128)S(1)}, u32[]{:S(2)}) %copy-start) | copy-done | bytes 16408
  10.8 0.0 copy-done.1
  10.8 1.9 %collective-permute-start.4 = (f32[8,256]{1,0:T(8,128)S(1)}, f32[8,256]{1,0:T(8,128)}, u32[]{:S(2)}, u32[]{:S(2)}) collective-permute-start(f32[8,256]{1,0:T(8,128)S(1)} %pad_maximum_fusion), channel_id=1, source_target_pairs={{0,12},{4,8},{8,4},{12,0},{1,13},{5,9},{9,5},{13,1},{2,14},{6,10},... | collective-permute-start | bytes 24584 | tf_op jit(solution)/shard_map/ppermute | solution.py:489
  12.7 0.0 copy-done.2
  12.7 1.6 %collective-permute-start.6 = (f32[48,128]{1,0:T(8,128)S(1)}, f32[48,128]{1,0:T(8,128)}, u32[]{:S(2)}, u32[]{:S(2)}) collective-permute-start(f32[48,128]{1,0:T(8,128)S(1)} %copy-done.2), channel_id=1, source_target_pairs={{0,8},{4,12},{8,0},{12,4},{1,9},{5,13},{9,1},{13,5},{2,10},{6,14},... | collective-permute-start | bytes 73736 | tf_op jit(solution)/shard_map/ppermute | solution.py:486
  14.4 0.9 %collective-permute-start.5 = (f32[8,256]{1,0:T(8,128)S(1)}, f32[8,256]{1,0:T(8,128)}, u32[]{:S(2)}, u32[]{:S(2)}) collective-permute-start(f32[8,256]{1,0:T(8,128)S(1)} %pad_maximum_fusion.1), channel_id=1, source_target_pairs={{0,4},{4,0},{8,12},{12,8},{1,5},{5,1},{9,13},{13,9},{2,6},{6,2},{1... | collective-permute-start | bytes 24584 | tf_op jit(solution)/shard_map/ppermute | solution.py:489
  15.3 1.3 %collective-permute-done.4.refs_15_ = f32[8,256]{1,0:T(8,128)} collective-permute-done((f32[8,256]{1,0:T(8,128)S(1)}, f32[8,256]{1,0:T(8,128)}, u32[]{:S(2)}, u32[]{:S(2)}) %collective-permute-start.4) | collective-permute-done | bytes 8224 | tf_op jit(solution)/shard_map/ppermute | solution.py:489
  16.5 1.6 %collective-permute-done.5.refs_16_ = f32[8,256]{1,0:T(8,128)} collective-permute-done((f32[8,256]{1,0:T(8,128)S(1)}, f32[8,256]{1,0:T(8,128)}, u32[]{:S(2)}, u32[]{:S(2)}) %collective-permute-start.5) | collective-permute-done | bytes 8224 | tf_op jit(solution)/shard_map/ppermute | solution.py:489
  18.1 0.0 collective-permute-done.6.refs_18_
  18.1 0.0 collective-permute-done.refs_11_
  18.1 0.0 collective-permute-done.1.refs_12_
  18.1 4.3 %steps.1 = (f32[3,16,16,128]{3,2,1,0:T(8,128)}, f32[2,8,16,128]{3,2,1,0:T(8,128)}) custom-call(f32[16]{0:T(128)} %refs_0_.3, f32[3,16,16,128]{3,2,1,0:T(8,128)} %refs_1_.3, f32[2,8,16,128]{3,2,1,0:T(8,128)} %refs_2_.3, f32[16,128]{1,0:T(8,128)} %refs_3_.3, f32[16,128]{1,0:T(8,128)} %refs_4_.3, s32[16,128]{1,0:T(8,128)} %refs_5_.3, s32[1,2048]{1,0:T(1,128)} %bitcast.5, ...), custom_call_target="tpu_custom_call" | custom-call | tf_op jit(solution)/shard_map/steps/pallas_call | solution.py:512
  (4 shorter events, 0.0 us)
Async XLA Ops:
  3.4 6.7 %collective-permute-start.3 = (f32[16,256]{1,0:T(8,128)}, f32[16,256]{1,0:T(8,128)S(1)}, u32[]{:S(2)}, u32[]{:S(2)}) collective-permute-start(f32[16,256]{1,0:T(8,128)} %get-tuple-element.18), channel_id=1, source_target_pairs={{0,3},{1,2},{2,1},{3,0},{4,7},{5,6},{6,5},{7,4},{8,11},{9,10},{10,... | collective-permute-start | bytes 49160 | tf_op jit(solution)/shard_map/ppermute | solution.py:489
  5.9 4.3 %collective-permute-start.2 = (f32[16,256]{1,0:T(8,128)}, f32[16,256]{1,0:T(8,128)S(1)}, u32[]{:S(2)}, u32[]{:S(2)}) collective-permute-start(f32[16,256]{1,0:T(8,128)} %get-tuple-element.15), channel_id=1, source_target_pairs={{0,1},{1,0},{2,3},{3,2},{4,5},{5,4},{6,7},{7,6},{8,9},{9,8},{10,11... | collective-permute-start | bytes 49160 | tf_op jit(solution)/shard_map/ppermute | solution.py:489
  6.6 11.5 %collective-permute-start = (f32[184,128]{1,0:T(8,128)}, f32[184,128]{1,0:T(8,128)}, u32[]{:S(2)}, u32[]{:S(2)}) collective-permute-start(f32[184,128]{1,0:T(8,128)} %get-tuple-element.13), channel_id=1, source_target_pairs={{0,12},{4,8},{8,4},{12,0},{1,13},{5,9},{9,5},{13,1},{2,14},{6,10},... | collective-permute-start | bytes 282632 | tf_op jit(solution)/shard_map/ppermute | solution.py:489
  10.2 7.9 %collective-permute-start.1 = (f32[184,128]{1,0:T(8,128)}, f32[184,128]{1,0:T(8,128)}, u32[]{:S(2)}, u32[]{:S(2)}) collective-permute-start(f32[184,128]{1,0:T(8,128)} %get-tuple-element.14), channel_id=1, source_target_pairs={{0,4},{4,0},{8,12},{12,8},{1,5},{5,1},{9,13},{13,9},{2,6},{6,2},{1... | collective-permute-start | bytes 282632 | tf_op jit(solution)/shard_map/ppermute | solution.py:489
  10.2 0.6 %copy-start = (f32[16,256]{1,0:T(8,128)}, f32[16,256]{1,0:T(8,128)S(1)}, u32[]{:S(2)}) copy-start(f32[16,256]{1,0:T(8,128)S(1)} %collective-permute-done.3.refs_14_) | copy-start | bytes 49156
  10.2 2.5 %copy-start.2 = (f32[48,128]{1,0:T(8,128)S(1)}, f32[48,128]{1,0:T(8,128)}, u32[]{:S(2)}) copy-start(f32[48,128]{1,0:T(8,128)} %get-tuple-element.21) | copy-start | bytes 73732
  10.2 0.6 %copy-start.1 = (f32[16,256]{1,0:T(8,128)}, f32[16,256]{1,0:T(8,128)S(1)}, u32[]{:S(2)}) copy-start(f32[16,256]{1,0:T(8,128)S(1)} %collective-permute-done.2.refs_13_) | copy-start | bytes 49156
  10.8 5.7 %collective-permute-start.4 = (f32[8,256]{1,0:T(8,128)S(1)}, f32[8,256]{1,0:T(8,128)}, u32[]{:S(2)}, u32[]{:S(2)}) collective-permute-start(f32[8,256]{1,0:T(8,128)S(1)} %pad_maximum_fusion), channel_id=1, source_target_pairs={{0,12},{4,8},{8,4},{12,0},{1,13},{5,9},{9,5},{13,1},{2,14},{6,10},... | collective-permute-start | bytes 24584 | tf_op jit(solution)/shard_map/ppermute | solution.py:489
  12.7 5.4 %collective-permute-start.6 = (f32[48,128]{1,0:T(8,128)S(1)}, f32[48,128]{1,0:T(8,128)}, u32[]{:S(2)}, u32[]{:S(2)}) collective-permute-start(f32[48,128]{1,0:T(8,128)S(1)} %copy-done.2), channel_id=1, source_target_pairs={{0,8},{4,12},{8,0},{12,4},{1,9},{5,13},{9,1},{13,5},{2,10},{6,14},... | collective-permute-start | bytes 73736 | tf_op jit(solution)/shard_map/ppermute | solution.py:486
  14.4 3.8 %collective-permute-start.5 = (f32[8,256]{1,0:T(8,128)S(1)}, f32[8,256]{1,0:T(8,128)}, u32[]{:S(2)}, u32[]{:S(2)}) collective-permute-start(f32[8,256]{1,0:T(8,128)S(1)} %pad_maximum_fusion.1), channel_id=1, source_target_pairs={{0,4},{4,0},{8,12},{12,8},{1,5},{5,1},{9,13},{13,9},{2,6},{6,2},{1... | collective-permute-start | bytes 24584 | tf_op jit(solution)/shard_map/ppermute | solution.py:489

commit v13 on v12

--- a/solution.py
+++ b/solution.py
@@ -79,10 +79,8 @@
 
 def scatter_rows(values, hot_rows, hot_cols):
     r = hot_rows.shape[0]
-    parts = []
-    for value in values:
-        for part in split3(value):
-            parts.append(jnp.where(hot_rows, part.astype(F32), 0.0).astype(BF16))
+    hot = jnp.where(hot_rows, 1.0, 0.0).astype(BF16)
+    parts = [hot * part for value in values for part in split3(value)]
     s = lax.dot_general(
         jnp.concatenate(parts, axis=0),
         hot_cols,
@@ -370,15 +368,13 @@
 
     w = ms[1]
     k = ms[2]
-    we, ww, ws, wn = east(w), west(w), south(w), north(w)
+    kw = k * w
+    ce, cw, cs, cn = kw * east(w), kw * west(w), kw * south(w), kw * north(w)
+    center = 1.0 - (ce + cw + cs + cn)
     for step in range(OCEAN_STEPS):
         for i in range(tracers):
             f = fs[i // each, i % each]
-            total = we * (east(f) - f)
-            total = total + ww * (west(f) - f)
-            total = total + ws * (south(f) - f)
-            total = total + wn * (north(f) - f)
-            f = f + k * (w * total)
+            f = center * f + ce * east(f) + cw * west(f) + cs * south(f) + cn * north(f)
             if step < OCEAN_STEPS - 1:
                 fs[i // each, i % each] = f
             else:
@@ -388,13 +384,12 @@
     copies = [pltpu.make_async_copy(ocean_buf, ocean_out, sems.at[used])]
     copies[0].start()
 
-    d = ms[0]
+    d = 0.5 * ms[0]
     chunk = max(1, levels // 4)
     for step in range(ACOUSTIC):
         for level in range(levels):
             u, v, h = us[level], vs[level], hs[level]
-            column_speed = speed[level] * d
-            hs[level] = h - column_speed * ((east(u) - west(u)) * 0.5 + (south(v) - north(v)) * 0.5)
+            hs[level] = h - (speed[level] * d) * ((east(u) - west(u)) + (south(v) - north(v)))
             if step == 0:
                 hs[level, rows:full, 0:cols] = new_height_rows(hs[level, rows:full, 0:cols], level)
         for level in range(levels):
@@ -500,7 +495,6 @@
     corner_a = swap(corner_a, "tile", tile_count, 1)
     corner_b = swap(corner_b, "tile", tile_count, 0)
     if by_shift:
-        *messages, got_b = lax.optimization_barrier((*messages, got_b))
         got = messages[:1] + [shift(messages[s - 1], "tile", tile_count, s) for s in range(2, tile_count - 1)]
     else:
         got = [lax.all_to_all(messages[0], "tile", split_axis=0, concat_axis=0, tiled=True)]

time: 22.6 us -> 22.6 us (level)
  waiting for transfers between devices: 2.87 us -> 3.32 us
  starting transfers between devices: 11.1 us -> 10.7 us
    ppermute x6, starting transfers between devices: 9.54 us -> 8.13 us  [swap(): lax.ppermute(value, axes, [(i, (i + (1 if (i + odd) % 2 == 0 else -1)) %...]
    ppermute x1, starting transfers between devices: 1.61 us -> 2.59 us  [shift(): lax.ppermute(value, axes, [(i, (i + by) % count) for i in range(count)])]
    ppermute x6, waiting for transfers between devices: 2.86 us -> 3.32 us  [swap(): lax.ppermute(value, axes, [(i, (i + (1 if (i + odd) % 2 == 0 else -1)) %...]
    unnamed x6 -> x4, local copies, waits for them, and re-layouts: 0.56 us -> 0.56 us
where the time goes in v13:
time: 22.6 us; the launch traced here: 22.4 us
  starting transfers between devices  10.7 us (47%)
  Pallas kernels  7.03 us (31%)
  waiting for transfers between devices  3.32 us (15%)
  between operations  0.68 us (3%)
  local copies, waits for them, and re-layouts  0.58 us (3%)
    ppermute x6, starting transfers between devices, swap(): lax.ppermute(value, axes, [(i, (i + (1 if (i + odd) % 2 == 0 else -1)) %...  8.13 us
    pallas_call x1, Pallas kernels, on_device(): pl.pallas_call(functools.partial(final_kernel, tile_count), out_shape=[sh...  4.22 us
    ppermute x6, waiting for transfers between devices, swap(): lax.ppermute(value, axes, [(i, (i + (1 if (i + odd) % 2 == 0 else -1)) %...  3.32 us
    pallas_call x1, Pallas kernels, on_device(): pl.pallas_call(functools.partial(first_kernel, tile_count), out_shape=[sh...  2.81 us
    ppermute x1, starting transfers between devices, shift(): lax.ppermute(value, axes, [(i, (i + by) % count) for i in range(count)])  2.59 us
    unnamed x4, local copies, waits for them, and re-layouts  0.56 us
  transfers between devices with their start and end apart: 7, of which 2 were waited for; matrix products, arithmetic and copies ran while one was open for 0% of the time, Pallas kernels for 0%

profile of v13, /device:TPU:0, one launch (start us, length us, event | category | flops | bytes accessed | tf_op | source)
XLA Modules:
  0.0 22.4 jit_solution(17955818381799108902)
XLA Ops:
  0.6 2.8 %first.1 = (f32[16,256]{1,0:T(8,128)}, f32[16,256]{1,0:T(8,128)}, f32[184,128]{1,0:T(8,128)}, f32[184,128]{1,0:T(8,128)}, f32[1,2048]{1,0:T(1,128)}, /*index=5*/f32[48,128]{1,0:T(8,128)}, f32[48,128]{1,0:T(8,128)}) custom-call(f32[3,16,16,128]{3,2,1,0:T(8,128)} %refs_1_.3, f32[2,8,16,128]{3,2,1,0:T(8,128)} %refs_2_.3, f32[16,128]{1,0:T(8,128)} %refs_3_.3, ...), custom_call_target="tpu_custom_call" | custom-call | tf_op jit(solution)/shard_map/first/pallas_call | solution.py:459
  3.4 0.5 %collective-permute-start.2 = (f32[16,256]{1,0:T(8,128)}, f32[16,256]{1,0:T(8,128)S(1)}, u32[]{:S(2)}, u32[]{:S(2)}) collective-permute-start(f32[16,256]{1,0:T(8,128)} %get-tuple-element.12), channel_id=1, source_target_pairs={{0,1},{1,0},{2,3},{3,2},{4,5},{5,4},{6,7},{7,6},{8,9},{9,8},{10,11... | collective-permute-start | bytes 49160 | tf_op jit(solution)/shard_map/ppermute | solution.py:484
  4.0 2.6 %collective-permute-start.3 = (f32[16,256]{1,0:T(8,128)}, f32[16,256]{1,0:T(8,128)S(1)}, u32[]{:S(2)}, u32[]{:S(2)}) collective-permute-start(f32[16,256]{1,0:T(8,128)} %get-tuple-element.13), channel_id=1, source_target_pairs={{0,3},{1,2},{2,1},{3,0},{4,7},{5,6},{6,5},{7,4},{8,11},{9,10},{10,... | collective-permute-start | bytes 49160 | tf_op jit(solution)/shard_map/ppermute | solution.py:484
  6.6 2.6 %collective-permute-start.6 = (f32[48,128]{1,0:T(8,128)}, f32[48,128]{1,0:T(8,128)}, u32[]{:S(2)}, u32[]{:S(2)}) collective-permute-start(f32[48,128]{1,0:T(8,128)} %get-tuple-element.15), channel_id=1, source_target_pairs={{0,8},{4,12},{8,0},{12,4},{1,9},{5,13},{9,1},{13,5},{2,10},{6,14},... | collective-permute-start | bytes 73736 | tf_op jit(solution)/shard_map/ppermute | solution.py:481
  9.2 1.3 %collective-permute-start = (f32[184,128]{1,0:T(8,128)}, f32[184,128]{1,0:T(8,128)}, u32[]{:S(2)}, u32[]{:S(2)}) collective-permute-start(f32[184,128]{1,0:T(8,128)} %get-tuple-element.10), channel_id=1, source_target_pairs={{0,12},{4,8},{8,4},{12,0},{1,13},{5,9},{9,5},{13,1},{2,14},{6,10},... | collective-permute-start | bytes 282632 | tf_op jit(solution)/shard_map/ppermute | solution.py:484
  10.5 0.2 %collective-permute-start.1 = (f32[184,128]{1,0:T(8,128)}, f32[184,128]{1,0:T(8,128)}, u32[]{:S(2)}, u32[]{:S(2)}) collective-permute-start(f32[184,128]{1,0:T(8,128)} %get-tuple-element.11), channel_id=1, source_target_pairs={{0,4},{4,0},{8,12},{12,8},{1,5},{5,1},{9,13},{13,9},{2,6},{6,2},{1... | collective-permute-start | bytes 282632 | tf_op jit(solution)/shard_map/ppermute | solution.py:484
  10.8 0.0 collective-permute-done.2.refs_13_
  10.8 0.0 copy-start
  10.8 0.0 collective-permute-done.3.refs_14_
  10.8 0.0 copy-start.1
  10.8 0.5 %copy-done = f32[16,256]{1,0:T(8,128)} copy-done((f32[16,256]{1,0:T(8,128)}, f32[16,256]{1,0:T(8,128)S(1)}, u32[]{:S(2)}) %copy-start) | copy-done | bytes 16408
  11.4 0.0 copy-done.1
  11.4 3.0 %collective-permute-start.4 = (f32[8,256]{1,0:T(8,128)S(1)}, f32[8,256]{1,0:T(8,128)}, u32[]{:S(2)}, u32[]{:S(2)}) collective-permute-start(f32[8,256]{1,0:T(8,128)S(1)} %pad_maximum_fusion), channel_id=1, source_target_pairs={{0,12},{4,8},{8,4},{12,0},{1,13},{5,9},{9,5},{13,1},{2,14},{6,10},... | collective-permute-start | bytes 24584 | tf_op jit(solution)/shard_map/ppermute | solution.py:484
  14.4 0.4 %collective-permute-start.5 = (f32[8,256]{1,0:T(8,128)S(1)}, f32[8,256]{1,0:T(8,128)}, u32[]{:S(2)}, u32[]{:S(2)}) collective-permute-start(f32[8,256]{1,0:T(8,128)S(1)} %pad_maximum_fusion.1), channel_id=1, source_target_pairs={{0,4},{4,0},{8,12},{12,8},{1,5},{5,1},{9,13},{13,9},{2,6},{6,2},{1... | collective-permute-start | bytes 24584 | tf_op jit(solution)/shard_map/ppermute | solution.py:484
  14.8 3.2 %collective-permute-done.4.refs_15_ = f32[8,256]{1,0:T(8,128)} collective-permute-done((f32[8,256]{1,0:T(8,128)S(1)}, f32[8,256]{1,0:T(8,128)}, u32[]{:S(2)}, u32[]{:S(2)}) %collective-permute-start.4) | collective-permute-done | bytes 8224 | tf_op jit(solution)/shard_map/ppermute | solution.py:484
  18.0 0.1 collective-permute-done.5.refs_16_
  18.1 0.0 collective-permute-done.6.refs_18_
  18.1 0.0 collective-permute-done.refs_11_
  18.1 0.0 collective-permute-done.1.refs_12_
  18.1 4.2 %steps.1 = (f32[3,16,16,128]{3,2,1,0:T(8,128)}, f32[2,8,16,128]{3,2,1,0:T(8,128)}) custom-call(f32[16]{0:T(128)} %refs_0_.3, f32[3,16,16,128]{3,2,1,0:T(8,128)} %refs_1_.3, f32[2,8,16,128]{3,2,1,0:T(8,128)} %refs_2_.3, f32[16,128]{1,0:T(8,128)} %refs_3_.3, f32[16,128]{1,0:T(8,128)} %refs_4_.3, s32[16,128]{1,0:T(8,128)} %refs_5_.3, s32[1,2048]{1,0:T(1,128)} %bitcast.5, ...), custom_call_target="tpu_custom_call" | custom-call | tf_op jit(solution)/shard_map/steps/pallas_call | solution.py:506
  (4 shorter events, 0.0 us)
Async XLA Ops:
  3.4 7.3 %collective-permute-start.2 = (f32[16,256]{1,0:T(8,128)}, f32[16,256]{1,0:T(8,128)S(1)}, u32[]{:S(2)}, u32[]{:S(2)}) collective-permute-start(f32[16,256]{1,0:T(8,128)} %get-tuple-element.12), channel_id=1, source_target_pairs={{0,1},{1,0},{2,3},{3,2},{4,5},{5,4},{6,7},{7,6},{8,9},{9,8},{10,11... | collective-permute-start | bytes 49160 | tf_op jit(solution)/shard_map/ppermute | solution.py:484
  4.0 6.8 %collective-permute-start.3 = (f32[16,256]{1,0:T(8,128)}, f32[16,256]{1,0:T(8,128)S(1)}, u32[]{:S(2)}, u32[]{:S(2)}) collective-permute-start(f32[16,256]{1,0:T(8,128)} %get-tuple-element.13), channel_id=1, source_target_pairs={{0,3},{1,2},{2,1},{3,0},{4,7},{5,6},{6,5},{7,4},{8,11},{9,10},{10,... | collective-permute-start | bytes 49160 | tf_op jit(solution)/shard_map/ppermute | solution.py:484
  6.6 11.5 %collective-permute-start.6 = (f32[48,128]{1,0:T(8,128)}, f32[48,128]{1,0:T(8,128)}, u32[]{:S(2)}, u32[]{:S(2)}) collective-permute-start(f32[48,128]{1,0:T(8,128)} %get-tuple-element.15), channel_id=1, source_target_pairs={{0,8},{4,12},{8,0},{12,4},{1,9},{5,13},{9,1},{13,5},{2,10},{6,14},... | collective-permute-start | bytes 73736 | tf_op jit(solution)/shard_map/ppermute | solution.py:481
  9.2 9.0 %collective-permute-start = (f32[184,128]{1,0:T(8,128)}, f32[184,128]{1,0:T(8,128)}, u32[]{:S(2)}, u32[]{:S(2)}) collective-permute-start(f32[184,128]{1,0:T(8,128)} %get-tuple-element.10), channel_id=1, source_target_pairs={{0,12},{4,8},{8,4},{12,0},{1,13},{5,9},{9,5},{13,1},{2,14},{6,10},... | collective-permute-start | bytes 282632 | tf_op jit(solution)/shard_map/ppermute | solution.py:484
  10.5 7.6 %collective-permute-start.1 = (f32[184,128]{1,0:T(8,128)}, f32[184,128]{1,0:T(8,128)}, u32[]{:S(2)}, u32[]{:S(2)}) collective-permute-start(f32[184,128]{1,0:T(8,128)} %get-tuple-element.11), channel_id=1, source_target_pairs={{0,4},{4,0},{8,12},{12,8},{1,5},{5,1},{9,13},{13,9},{2,6},{6,2},{1... | collective-permute-start | bytes 282632 | tf_op jit(solution)/shard_map/ppermute | solution.py:484
  10.8 0.6 %copy-start = (f32[16,256]{1,0:T(8,128)}, f32[16,256]{1,0:T(8,128)S(1)}, u32[]{:S(2)}) copy-start(f32[16,256]{1,0:T(8,128)S(1)} %collective-permute-done.2.refs_13_) | copy-start | bytes 49156
  10.8 0.6 %copy-start.1 = (f32[16,256]{1,0:T(8,128)}, f32[16,256]{1,0:T(8,128)S(1)}, u32[]{:S(2)}) copy-start(f32[16,256]{1,0:T(8,128)S(1)} %collective-permute-done.3.refs_14_) | copy-start | bytes 49156
  11.4 6.6 %collective-permute-start.4 = (f32[8,256]{1,0:T(8,128)S(1)}, f32[8,256]{1,0:T(8,128)}, u32[]{:S(2)}, u32[]{:S(2)}) collective-permute-start(f32[8,256]{1,0:T(8,128)S(1)} %pad_maximum_fusion), channel_id=1, source_target_pairs={{0,12},{4,8},{8,4},{12,0},{1,13},{5,9},{9,5},{13,1},{2,14},{6,10},... | collective-permute-start | bytes 24584 | tf_op jit(solution)/shard_map/ppermute | solution.py:484
  14.4 3.8 %collective-permute-start.5 = (f32[8,256]{1,0:T(8,128)S(1)}, f32[8,256]{1,0:T(8,128)}, u32[]{:S(2)}, u32[]{:S(2)}) collective-permute-start(f32[8,256]{1,0:T(8,128)S(1)} %pad_maximum_fusion.1), channel_id=1, source_target_pairs={{0,4},{4,0},{8,12},{12,8},{1,5},{5,1},{9,13},{13,9},{2,6},{6,2},{1... | collective-permute-start | bytes 24584 | tf_op jit(solution)/shard_map/ppermute | solution.py:484

commit v14 on v13

--- a/solution.py
+++ b/solution.py
@@ -216,6 +216,15 @@
             copy(sums.at[shift], sums_out[max(shift - 1, 0)])
     for one in used[arrived:]:
         one.wait()
+
+
+def corner_kernel(got_a, got_b, corner_a, corner_b):
+    rows = got_a.shape[0]
+    first = tile_parity() == 0
+    for i, ref in enumerate((got_a, got_b)):
+        low, high = ref[0:AH, :], ref[rows - AH : rows, :]
+        corner_a[i * AH : (i + 1) * AH, :] = jnp.where(first, high, low)
+        corner_b[i * AH : (i + 1) * AH, :] = jnp.where(first, low, high)
 
 
 def strips(cols, slot, width, left_part, right_part):
@@ -488,10 +497,15 @@
     near_a = swap(rows_a, "tile", tile_count, 1)
     near_b = swap(rows_b, "tile", tile_count, 0)
 
-    low = jnp.where(tile_parity() == 0, rows - AH, 0)
-    corner_a, corner_b = [
-        jnp.concatenate([lax.dynamic_slice_in_dim(x, at, AH) for x in (got_a, got_b)]) for at in (low, rows - AH - low)
-    ]
+    corner_a, corner_b = pl.pallas_call(
+        corner_kernel,
+        out_shape=[shape(2 * AH, lanes)] * 2,
+        in_specs=[vmem] * 2,
+        out_specs=[vmem] * 2,
+        compiler_params=pltpu.CompilerParams(vmem_limit_bytes=4 * 1024 * 1024),
+        cost_estimate=pl.CostEstimate(flops=0, bytes_accessed=100000, transcendentals=0),
+        name="corners",
+    )(got_a, got_b)
     corner_a = swap(corner_a, "tile", tile_count, 1)
     corner_b = swap(corner_b, "tile", tile_count, 0)
     if by_shift:

time: 22.6 us -> 23.8 us (1.053)
  waiting for transfers between devices: 3.32 us -> 4.64 us
  starting transfers between devices: 10.7 us -> 10.1 us
  local copies, waits for them, and re-layouts: 0.58 us -> 1.17 us
    ppermute x1, starting transfers between devices: 2.59 us -> 0.78 us  [shift(): lax.ppermute(value, axes, [(i, (i + by) % count) for i in range(count)])]
    ppermute x6, waiting for transfers between devices: 3.32 us -> 4.64 us  [swap(): lax.ppermute(value, axes, [(i, (i + (1 if (i + odd) % 2 == 0 else -1)) %...]
    ppermute x6, starting transfers between devices: 8.13 us -> 9.36 us  [swap(): lax.ppermute(value, axes, [(i, (i + (1 if (i + odd) % 2 == 0 else -1)) %...]
    unnamed x4 -> x8, local copies, waits for them, and re-layouts: 0.56 us -> 1.17 us
  transfers between devices with their start and end apart: 7 -> 7, of which waited for: 2 -> 3; matrix products, arithmetic and copies ran while one was open for 0% -> 0% of each run, Pallas kernels for 0% -> 0%
where the time goes in v14:
time: 23.8 us; the launch traced here: 23.6 us
  starting transfers between devices  10.1 us (42%)
  Pallas kernels  7.03 us (30%)
  waiting for transfers between devices  4.64 us (19%)
  local copies, waits for them, and re-layouts  1.17 us (5%)
  between operations  0.66 us (3%)
    ppermute x6, starting transfers between devices, swap(): lax.ppermute(value, axes, [(i, (i + (1 if (i + odd) % 2 == 0 else -1)) %...  9.36 us
    ppermute x6, waiting for transfers between devices, swap(): lax.ppermute(value, axes, [(i, (i + (1 if (i + odd) % 2 == 0 else -1)) %...  4.64 us
    pallas_call x1, Pallas kernels, on_device(): pl.pallas_call(functools.partial(final_kernel, tile_count), out_shape=[sh...  4.21 us
    pallas_call x1, Pallas kernels, on_device(): pl.pallas_call(functools.partial(first_kernel, tile_count), out_shape=[sh...  2.81 us
    unnamed x8, local copies, waits for them, and re-layouts  1.17 us
    ppermute x1, starting transfers between devices, shift(): lax.ppermute(value, axes, [(i, (i + by) % count) for i in range(count)])  0.78 us
  transfers between devices with their start and end apart: 7, of which 3 were waited for; matrix products, arithmetic and copies ran while one was open for 0% of the time, Pallas kernels for 0%

profile of v14, /device:TPU:0, one launch (start us, length us, event | category | flops | bytes accessed | tf_op | source)
XLA Modules:
  0.0 23.6 jit_solution(1406107532178894816)
XLA Ops:
  0.6 2.8 %first.1 = (f32[16,256]{1,0:T(8,128)}, f32[16,256]{1,0:T(8,128)}, f32[184,128]{1,0:T(8,128)}, f32[184,128]{1,0:T(8,128)}, f32[1,2048]{1,0:T(1,128)}, /*index=5*/f32[48,128]{1,0:T(8,128)}, f32[48,128]{1,0:T(8,128)}) custom-call(f32[3,16,16,128]{3,2,1,0:T(8,128)} %refs_1_.3, f32[2,8,16,128]{3,2,1,0:T(8,128)} %refs_2_.3, f32[16,128]{1,0:T(8,128)} %refs_3_.3, ...), custom_call_target="tpu_custom_call" | custom-call | tf_op jit(solution)/shard_map/first/pallas_call | solution.py:468
  3.4 5.1 %collective-permute-start = (f32[184,128]{1,0:T(8,128)}, f32[184,128]{1,0:T(8,128)}, u32[]{:S(2)}, u32[]{:S(2)}) collective-permute-start(f32[184,128]{1,0:T(8,128)} %get-tuple-element.12), channel_id=1, source_target_pairs={{0,12},{4,8},{8,4},{12,0},{1,13},{5,9},{9,5},{13,1},{2,14},{6,10},... | collective-permute-start | bytes 282632 | tf_op jit(solution)/shard_map/ppermute | solution.py:493
  8.6 0.0 collective-permute-start.1
  8.6 0.0 collective-permute-start.2
  8.6 1.6 %collective-permute-start.3 = (f32[16,256]{1,0:T(8,128)}, f32[16,256]{1,0:T(8,128)S(1)}, u32[]{:S(2)}, u32[]{:S(2)}) collective-permute-start(f32[16,256]{1,0:T(8,128)} %get-tuple-element.15), channel_id=1, source_target_pairs={{0,3},{1,2},{2,1},{3,0},{4,7},{5,6},{6,5},{7,4},{8,11},{9,10},{10,... | collective-permute-start | bytes 49160 | tf_op jit(solution)/shard_map/ppermute | solution.py:493
  10.2 0.8 %collective-permute-start.6 = (f32[48,128]{1,0:T(8,128)}, f32[48,128]{1,0:T(8,128)}, u32[]{:S(2)}, u32[]{:S(2)}) collective-permute-start(f32[48,128]{1,0:T(8,128)} %get-tuple-element.19), channel_id=1, source_target_pairs={{0,8},{4,12},{8,0},{12,4},{1,9},{5,13},{9,1},{13,5},{2,10},{6,14},... | collective-permute-start | bytes 73736 | tf_op jit(solution)/shard_map/ppermute | solution.py:490
  11.0 0.0 collective-permute-done.2.got_a.refs_13_
  11.0 0.0 copy-start
  11.0 1.0 %collective-permute-done.3.got_b.refs_14_ = f32[16,256]{1,0:T(8,128)S(1)} collective-permute-done((f32[16,256]{1,0:T(8,128)}, f32[16,256]{1,0:T(8,128)S(1)}, u32[]{:S(2)}, u32[]{:S(2)}) %collective-permute-start.3) | collective-permute-done | bytes 16416 | tf_op jit(solution)/shard_map/ppermute | solution.py:493
  11.9 0.0 copy-start.1
  12.0 0.0 copy-done
  12.0 0.6 %copy-done.1 = f32[16,256]{1,0:T(8,128)} copy-done((f32[16,256]{1,0:T(8,128)}, f32[16,256]{1,0:T(8,128)S(1)}, u32[]{:S(2)}) %copy-start.1) | copy-done | bytes 16408
  12.5 2.6 %collective-permute-start.4 = (f32[8,256]{1,0:T(8,128)S(1)}, f32[8,256]{1,0:T(8,128)S(1)}, u32[]{:S(2)}, u32[]{:S(2)}) collective-permute-start(f32[8,256]{1,0:T(8,128)S(1)} %get-tuple-element.16), channel_id=1, source_target_pairs={{0,12},{4,8},{8,4},{12,0},{1,13},{5,9},{9,5},{13,1},{2,14},{6,10},... | collective-permute-start | bytes 24584 | tf_op jit(solution)/shard_map/ppermute | solution.py:493
  15.2 0.0 collective-permute-start.5
  15.2 2.8 %collective-permute-done.4.refs_15_ = f32[8,256]{1,0:T(8,128)S(1)} collective-permute-done((f32[8,256]{1,0:T(8,128)S(1)}, f32[8,256]{1,0:T(8,128)S(1)}, u32[]{:S(2)}, u32[]{:S(2)}) %collective-permute-start.4) | collective-permute-done | bytes 8224 | tf_op jit(solution)/shard_map/ppermute | solution.py:493
  18.0 0.0 copy-start.2
  18.0 0.8 %collective-permute-done.5.refs_16_ = f32[8,256]{1,0:T(8,128)S(1)} collective-permute-done((f32[8,256]{1,0:T(8,128)S(1)}, f32[8,256]{1,0:T(8,128)S(1)}, u32[]{:S(2)}, u32[]{:S(2)}) %collective-permute-start.5) | collective-permute-done | bytes 8224 | tf_op jit(solution)/shard_map/ppermute | solution.py:493
  18.8 0.0 copy-done.2
  18.8 0.0 copy-start.3
  18.8 0.0 collective-permute-done.6.refs_18_
  18.8 0.6 %copy-done.3 = f32[8,256]{1,0:T(8,128)} copy-done((f32[8,256]{1,0:T(8,128)}, f32[8,256]{1,0:T(8,128)S(1)}, u32[]{:S(2)}) %copy-start.3) | copy-done | bytes 8216
  19.4 0.0 collective-permute-done.refs_11_
  19.4 0.0 collective-permute-done.1.refs_12_
  19.4 4.2 %steps.1 = (f32[3,16,16,128]{3,2,1,0:T(8,128)}, f32[2,8,16,128]{3,2,1,0:T(8,128)}) custom-call(f32[16]{0:T(128)} %refs_0_.3, f32[3,16,16,128]{3,2,1,0:T(8,128)} %refs_1_.3, f32[2,8,16,128]{3,2,1,0:T(8,128)} %refs_2_.3, f32[16,128]{1,0:T(8,128)} %refs_3_.3, f32[16,128]{1,0:T(8,128)} %refs_4_.3, s32[16,128]{1,0:T(8,128)} %refs_5_.3, s32[1,2048]{1,0:T(1,128)} %bitcast.5, ...), custom_call_target="tpu_custom_call" | custom-call | tf_op jit(solution)/shard_map/steps/pallas_call | solution.py:520
  (1 shorter events, 0.0 us)
Async XLA Ops:
  3.4 16.0 %collective-permute-start = (f32[184,128]{1,0:T(8,128)}, f32[184,128]{1,0:T(8,128)}, u32[]{:S(2)}, u32[]{:S(2)}) collective-permute-start(f32[184,128]{1,0:T(8,128)} %get-tuple-element.12), channel_id=1, source_target_pairs={{0,12},{4,8},{8,4},{12,0},{1,13},{5,9},{9,5},{13,1},{2,14},{6,10},... | collective-permute-start | bytes 282632 | tf_op jit(solution)/shard_map/ppermute | solution.py:493
  8.6 10.9 %collective-permute-start.1 = (f32[184,128]{1,0:T(8,128)}, f32[184,128]{1,0:T(8,128)}, u32[]{:S(2)}, u32[]{:S(2)}) collective-permute-start(f32[184,128]{1,0:T(8,128)} %get-tuple-element.13), channel_id=1, source_target_pairs={{0,4},{4,0},{8,12},{12,8},{1,5},{5,1},{9,13},{13,9},{2,6},{6,2},{1... | collective-permute-start | bytes 282632 | tf_op jit(solution)/shard_map/ppermute | solution.py:493
  8.6 2.4 %collective-permute-start.2 = (f32[16,256]{1,0:T(8,128)}, f32[16,256]{1,0:T(8,128)S(1)}, u32[]{:S(2)}, u32[]{:S(2)}) collective-permute-start(f32[16,256]{1,0:T(8,128)} %get-tuple-element.14), channel_id=1, source_target_pairs={{0,1},{1,0},{2,3},{3,2},{4,5},{5,4},{6,7},{7,6},{8,9},{9,8},{10,11... | collective-permute-start | bytes 49160 | tf_op jit(solution)/shard_map/ppermute | solution.py:493
  8.6 3.4 %collective-permute-start.3 = (f32[16,256]{1,0:T(8,128)}, f32[16,256]{1,0:T(8,128)S(1)}, u32[]{:S(2)}, u32[]{:S(2)}) collective-permute-start(f32[16,256]{1,0:T(8,128)} %get-tuple-element.15), channel_id=1, source_target_pairs={{0,3},{1,2},{2,1},{3,0},{4,7},{5,6},{6,5},{7,4},{8,11},{9,10},{10,... | collective-permute-start | bytes 49160 | tf_op jit(solution)/shard_map/ppermute | solution.py:493
  10.2 8.7 %collective-permute-start.6 = (f32[48,128]{1,0:T(8,128)}, f32[48,128]{1,0:T(8,128)}, u32[]{:S(2)}, u32[]{:S(2)}) collective-permute-start(f32[48,128]{1,0:T(8,128)} %get-tuple-element.19), channel_id=1, source_target_pairs={{0,8},{4,12},{8,0},{12,4},{1,9},{5,13},{9,1},{13,5},{2,10},{6,14},... | collective-permute-start | bytes 73736 | tf_op jit(solution)/shard_map/ppermute | solution.py:490
  11.0 1.0 %copy-start = (f32[16,256]{1,0:T(8,128)}, f32[16,256]{1,0:T(8,128)S(1)}, u32[]{:S(2)}) copy-start(f32[16,256]{1,0:T(8,128)S(1)} %collective-permute-done.2.got_a.refs_13_) | copy-start | bytes 49156
  11.9 0.6 %copy-start.1 = (f32[16,256]{1,0:T(8,128)}, f32[16,256]{1,0:T(8,128)S(1)}, u32[]{:S(2)}) copy-start(f32[16,256]{1,0:T(8,128)S(1)} %collective-permute-done.3.got_b.refs_14_) | copy-start | bytes 49156
  12.5 5.5 %collective-permute-start.4 = (f32[8,256]{1,0:T(8,128)S(1)}, f32[8,256]{1,0:T(8,128)S(1)}, u32[]{:S(2)}, u32[]{:S(2)}) collective-permute-start(f32[8,256]{1,0:T(8,128)S(1)} %get-tuple-element.16), channel_id=1, source_target_pairs={{0,12},{4,8},{8,4},{12,0},{1,13},{5,9},{9,5},{13,1},{2,14},{6,10},... | collective-permute-start | bytes 24584 | tf_op jit(solution)/shard_map/ppermute | solution.py:493
  15.2 3.7 %collective-permute-start.5 = (f32[8,256]{1,0:T(8,128)S(1)}, f32[8,256]{1,0:T(8,128)S(1)}, u32[]{:S(2)}, u32[]{:S(2)}) collective-permute-start(f32[8,256]{1,0:T(8,128)S(1)} %get-tuple-element.17), channel_id=1, source_target_pairs={{0,4},{4,0},{8,12},{12,8},{1,5},{5,1},{9,13},{13,9},{2,6},{6,2},{1... | collective-permute-start | bytes 24584 | tf_op jit(solution)/shard_map/ppermute | solution.py:493
  18.0 0.8 %copy-start.2 = (f32[8,256]{1,0:T(8,128)}, f32[8,256]{1,0:T(8,128)S(1)}, u32[]{:S(2)}) copy-start(f32[8,256]{1,0:T(8,128)S(1)} %collective-permute-done.4.refs_15_) | copy-start | bytes 24580
  18.8 0.6 %copy-start.3 = (f32[8,256]{1,0:T(8,128)}, f32[8,256]{1,0:T(8,128)S(1)}, u32[]{:S(2)}) copy-start(f32[8,256]{1,0:T(8,128)S(1)} %collective-permute-done.5.refs_16_) | copy-start | bytes 24580

commit v15 on v13

--- a/solution.py
+++ b/solution.py
@@ -244,8 +244,8 @@
     rows, cols = atm_out.shape[2:]
     slots, lanes = lane_slots(levels, tracers)
     obase, mbase, own, halo = row_slots(levels, tracers)
-    full = rows + 2 * AH
-    block = (slice(None), slice(0, rows), slice(0, cols))
+    top, end = 2 * AH, 2 * AH + rows
+    block = (slice(None), slice(top, end), slice(0, cols))
     rows_a, rows_b, cols_a, cols_b = sources[6:10]
     either = [(tile_parity(), rows_b, rows_a, from_up), (tile_parity(), rows_a, rows_b, from_down)]
     either += [(column_parity(), cols_b, cols_a, from_left), (column_parity(), cols_a, cols_b, from_right)]
@@ -274,7 +274,7 @@
             return (from_up if shift == 1 else from_down)[halo + part * rows : halo + (part + 1) * rows, :]
         return messages[max(shift - 1, 0)][where, :]
 
-    surface = fs[0, 0, 0:rows, 0:cols]
+    surface = fs[0, 0, top:end, 0:cols]
     cell = sea_cell[...]
     hot_sea = jnp.where(one_hot(cell % cols, cols), 1.0, 0.0).astype(BF16)
     row = dest[...] * rows + cell // cols
@@ -305,18 +305,20 @@
 
     def extend(view, field, width):
         slot = slots[field]
-        view[0:rows, cols : 2 * cols] = strips(
+        view[top:end, cols : 2 * cols] = strips(
             cols,
             slot,
             width,
             lambda t: from_left[:, t * cols : (t + 1) * cols],
             lambda t: from_right[:, t * cols : (t + 1) * cols],
         )
-        view[rows:full, cols : 2 * cols] = strips(cols, slot, width, lambda t: edge[t], lambda t: edge[half + t])
+        both = strips(cols, slot, width, lambda t: edge[t], lambda t: edge[half + t])
+        view[end : end + AH, cols : 2 * cols] = both[0:AH]
+        view[top - AH : top, cols : 2 * cols] = both[AH : 2 * AH]
 
     def extend_rows(view, at, high):
-        view[rows : rows + high, 0:cols] = from_down[at : at + high, :]
-        view[full - high : full, 0:cols] = from_up[at : at + high, :]
+        view[end : end + high, 0:cols] = from_down[at : at + high, :]
+        view[top - high : top, 0:cols] = from_up[at : at + high, :]
 
     lane = lax.broadcasted_iota(jnp.int32, (2 * AH, cols), 1)
     line = lax.broadcasted_iota(jnp.int32, (2 * AH, cols), 0)
@@ -331,15 +333,16 @@
         strip = strips(cols, slots[which * levels + level], AH, lambda t: edge[3 * half + t], lambda t: edge[2 * half + t])
         below, above = near(which, level)
         inner = jnp.where(line == 0, below, jnp.where(line == 2 * AH - 1, above, 0.0))
-        view[rows:full, 0:cols] = jnp.where(whole_strip if which == 0 else outer, strip, inner)
-
-    def new_height_rows(tile, level):
+        both = jnp.where(whole_strip if which == 0 else outer, strip, inner)
+        view[end : end + AH, 0:cols] = both[0:AH]
+        view[top - AH : top, 0:cols] = both[AH : 2 * AH]
+
+    def new_height_rows(view, level):
         below, above = near(3, level), near(4, level)
-        sent = jnp.where(
-            line == 1, below[0], jnp.where(line == 2, above[0], jnp.where(line == 2 * AH - 3, above[1], below[1]))
-        )
-        here = (line == 1) | (line == 2) | (line == 2 * AH - 3) | (line == 2 * AH - 2)
-        return jnp.where(here & jnp.logical_not(outer), sent, tile)
+        here = ((line[0:AH] == 1) | (line[0:AH] == 2)) & jnp.logical_not(outer[0:AH])
+        for at, one, two in ((end, below[0], above[0]), (top - AH, above[1], below[1])):
+            sent = jnp.where(line[0:AH] == 1, one, two)
+            view[at : at + AH, 0:cols] = jnp.where(here, sent, view[at : at + AH, 0:cols])
 
     def east(f):
         return pltpu.roll(f, 2 * cols - 1, 1)
@@ -347,14 +350,13 @@
     def west(f):
         return pltpu.roll(f, 1, 1)
 
-    def south(f):
-        return pltpu.roll(f, full - 1, 0)
-
-    def north(f):
-        return pltpu.roll(f, 1, 0)
+    wide, inner = (top - AH, rows + 2 * AH), (top, rows)
+
+    def rows_of(window, shift=0):
+        return slice(window[0] + shift, window[0] + shift + window[1])
 
     base = 3 * levels + tracers
-    ms[1, 0:rows, 0:cols] = wet[...].astype(F32)
+    ms[1, top:end, 0:cols] = wet[...].astype(F32)
     for i, (at, high) in enumerate(((mbase, AH), (mbase + AH, OH), (mbase + AH + OH, OH))):
         extend(ms.at[i], base + i, AH)
         extend_rows(ms.at[i], at, high)
@@ -366,42 +368,52 @@
             extend(ref.at[level], which * levels + level, AH)
             extend_level(ref.at[level], which, level)
 
-    w = ms[1]
-    k = ms[2]
-    kw = k * w
-    ce, cw, cs, cn = kw * east(w), kw * west(w), kw * south(w), kw * north(w)
-    center = 1.0 - (ce + cw + cs + cn)
+    here, lower, upper = rows_of(wide), rows_of(wide, 1), rows_of(wide, -1)
+    w = ms[1, here]
+    kw = ms[2, here] * w
+    weights = (kw * east(w), kw * west(w), kw * ms[1, lower], kw * ms[1, upper])
+    for i, weight_of in enumerate(weights):
+        ms[3 + i, here] = weight_of
+    ms[7, here] = 1.0 - (weights[0] + weights[1] + weights[2] + weights[3])
     for step in range(OCEAN_STEPS):
+        window = wide if step < OCEAN_STEPS - 1 else inner
+        here, lower, upper = rows_of(window), rows_of(window, 1), rows_of(window, -1)
+        ce, cw, cs, cn, center = [ms[3 + i, here] for i in range(5)]
         for i in range(tracers):
-            f = fs[i // each, i % each]
-            f = center * f + ce * east(f) + cw * west(f) + cs * south(f) + cn * north(f)
+            view = fs.at[i // each, i % each]
+            f = view[here]
+            f = center * f + ce * east(f) + cw * west(f) + cs * view[lower] + cn * view[upper]
             if step < OCEAN_STEPS - 1:
-                fs[i // each, i % each] = f
+                view[here] = f
             else:
-                f = f[0:rows, 0:cols]
+                f = f[:, 0:cols]
                 ocean_buf[i // each, i % each] = f + SEA_GAIN * sea_flux if i == 0 else f
     used = len(copies)
     copies = [pltpu.make_async_copy(ocean_buf, ocean_out, sems.at[used])]
     copies[0].start()
 
-    d = 0.5 * ms[0]
+    d = 0.5 * ms[0, rows_of(wide)]
     chunk = max(1, levels // 4)
     for step in range(ACOUSTIC):
+        here, lower, upper = rows_of(wide), rows_of(wide, 1), rows_of(wide, -1)
         for level in range(levels):
-            u, v, h = us[level], vs[level], hs[level]
-            hs[level] = h - (speed[level] * d) * ((east(u) - west(u)) + (south(v) - north(v)))
+            u = us[level, here]
+            turning = (east(u) - west(u)) + (vs[level, lower] - vs[level, upper])
+            hs[level, here] = hs[level, here] - (speed[level] * d) * turning
             if step == 0:
-                hs[level, rows:full, 0:cols] = new_height_rows(hs[level, rows:full, 0:cols], level)
+                new_height_rows(hs.at[level], level)
+        window = wide if step < ACOUSTIC - 1 else inner
+        here, lower, upper = rows_of(window), rows_of(window, 1), rows_of(window, -1)
         for level in range(levels):
-            u, v, h = us[level], vs[level], hs[level]
-            u = u - (east(h) - west(h)) * 0.5
-            v = v - (south(h) - north(h)) * 0.5
+            h = hs[level, here]
+            u = us[level, here] - (east(h) - west(h)) * 0.5
+            v = vs[level, here] - (hs[level, lower] - hs[level, upper]) * 0.5
             if step < ACOUSTIC - 1:
-                us[level], vs[level] = u, v
+                us[level, here], vs[level, here] = u, v
             else:
-                h = h[0:rows, 0:cols]
-                atm_buf[0, level] = u[0:rows, 0:cols]
-                atm_buf[1, level] = v[0:rows, 0:cols]
+                h = h[:, 0:cols]
+                atm_buf[0, level] = u[:, 0:cols]
+                atm_buf[1, level] = v[:, 0:cols]
                 atm_buf[2, level] = h - ATM_GAIN * atm_flux if level == levels - 1 else h
                 if (level + 1) % chunk == 0:
                     where = pl.ds(level + 1 - chunk, chunk)
@@ -439,7 +451,7 @@
     vmem = pl.BlockSpec(memory_space=pltpu.VMEM)
     hbm = pl.BlockSpec(memory_space=pltpu.HBM)
     whole = pltpu.CompilerParams(vmem_limit_bytes=64 * 1024 * 1024)
-    full = rows + 2 * AH
+    full = rows + 4 * AH
 
     def shape(*dims):
         return jax.ShapeDtypeStruct(dims, F32)
@@ -512,7 +524,7 @@
             + [pltpu.VMEM((levels, full, 2 * cols), F32)] * 3
             + [
                 pltpu.VMEM((*ocean_state.shape[:2], full, 2 * cols), F32),
-                pltpu.VMEM((3, full, 2 * cols), F32),
+                pltpu.VMEM((8, full, 2 * cols), F32),
             ]
             + [pltpu.VMEM(x.shape, x.dtype) for x in operands[5:]]
             + [

time: 22.6 us -> 23 us (1.018)
  Pallas kernels: 7.03 us -> 7.48 us
    pallas_call x1, Pallas kernels: 4.22 us -> 4.67 us  [on_device(): pl.pallas_call(functools.partial(final_kernel, tile_count), out_shape=[sh...]
where the time goes in v15:
time: 23 us; the launch traced here: 22.8 us
  starting transfers between devices  10.7 us (47%)
  Pallas kernels  7.48 us (33%)
  waiting for transfers between devices  3.32 us (14%)
  between operations  0.68 us (3%)
  local copies, waits for them, and re-layouts  0.58 us (3%)
    ppermute x6, starting transfers between devices, swap(): lax.ppermute(value, axes, [(i, (i + (1 if (i + odd) % 2 == 0 else -1)) %...  8.13 us
    pallas_call x1, Pallas kernels, on_device(): pl.pallas_call(functools.partial(final_kernel, tile_count), out_shape=[sh...  4.67 us
    ppermute x6, waiting for transfers between devices, swap(): lax.ppermute(value, axes, [(i, (i + (1 if (i + odd) % 2 == 0 else -1)) %...  3.32 us
    pallas_call x1, Pallas kernels, on_device(): pl.pallas_call(functools.partial(first_kernel, tile_count), out_shape=[sh...  2.81 us
    ppermute x1, starting transfers between devices, shift(): lax.ppermute(value, axes, [(i, (i + by) % count) for i in range(count)])  2.59 us
    unnamed x4, local copies, waits for them, and re-layouts  0.56 us
  transfers between devices with their start and end apart: 7, of which 2 were waited for; matrix products, arithmetic and copies ran while one was open for 0% of the time, Pallas kernels for 0%

profile of v15, /device:TPU:0, one launch (start us, length us, event | category | flops | bytes accessed | tf_op | source)
XLA Modules:
  0.0 22.8 jit_solution(17123307270308213810)
XLA Ops:
  0.6 2.8 %first.1 = (f32[16,256]{1,0:T(8,128)}, f32[16,256]{1,0:T(8,128)}, f32[184,128]{1,0:T(8,128)}, f32[184,128]{1,0:T(8,128)}, f32[1,2048]{1,0:T(1,128)}, /*index=5*/f32[48,128]{1,0:T(8,128)}, f32[48,128]{1,0:T(8,128)}) custom-call(f32[3,16,16,128]{3,2,1,0:T(8,128)} %refs_1_.3, f32[2,8,16,128]{3,2,1,0:T(8,128)} %refs_2_.3, f32[16,128]{1,0:T(8,128)} %refs_3_.3, ...), custom_call_target="tpu_custom_call" | custom-call | tf_op jit(solution)/shard_map/first/pallas_call | solution.py:471
  3.4 0.5 %collective-permute-start.2 = (f32[16,256]{1,0:T(8,128)}, f32[16,256]{1,0:T(8,128)S(1)}, u32[]{:S(2)}, u32[]{:S(2)}) collective-permute-start(f32[16,256]{1,0:T(8,128)} %get-tuple-element.12), channel_id=1, source_target_pairs={{0,1},{1,0},{2,3},{3,2},{4,5},{5,4},{6,7},{7,6},{8,9},{9,8},{10,11... | collective-permute-start | bytes 49160 | tf_op jit(solution)/shard_map/ppermute | solution.py:496
  4.0 2.6 %collective-permute-start.3 = (f32[16,256]{1,0:T(8,128)}, f32[16,256]{1,0:T(8,128)S(1)}, u32[]{:S(2)}, u32[]{:S(2)}) collective-permute-start(f32[16,256]{1,0:T(8,128)} %get-tuple-element.13), channel_id=1, source_target_pairs={{0,3},{1,2},{2,1},{3,0},{4,7},{5,6},{6,5},{7,4},{8,11},{9,10},{10,... | collective-permute-start | bytes 49160 | tf_op jit(solution)/shard_map/ppermute | solution.py:496
  6.6 2.6 %collective-permute-start.6 = (f32[48,128]{1,0:T(8,128)}, f32[48,128]{1,0:T(8,128)}, u32[]{:S(2)}, u32[]{:S(2)}) collective-permute-start(f32[48,128]{1,0:T(8,128)} %get-tuple-element.15), channel_id=1, source_target_pairs={{0,8},{4,12},{8,0},{12,4},{1,9},{5,13},{9,1},{13,5},{2,10},{6,14},... | collective-permute-start | bytes 73736 | tf_op jit(solution)/shard_map/ppermute | solution.py:493
  9.2 1.3 %collective-permute-start = (f32[184,128]{1,0:T(8,128)}, f32[184,128]{1,0:T(8,128)}, u32[]{:S(2)}, u32[]{:S(2)}) collective-permute-start(f32[184,128]{1,0:T(8,128)} %get-tuple-element.10), channel_id=1, source_target_pairs={{0,12},{4,8},{8,4},{12,0},{1,13},{5,9},{9,5},{13,1},{2,14},{6,10},... | collective-permute-start | bytes 282632 | tf_op jit(solution)/shard_map/ppermute | solution.py:496
  10.5 0.2 %collective-permute-start.1 = (f32[184,128]{1,0:T(8,128)}, f32[184,128]{1,0:T(8,128)}, u32[]{:S(2)}, u32[]{:S(2)}) collective-permute-start(f32[184,128]{1,0:T(8,128)} %get-tuple-element.11), channel_id=1, source_target_pairs={{0,4},{4,0},{8,12},{12,8},{1,5},{5,1},{9,13},{13,9},{2,6},{6,2},{1... | collective-permute-start | bytes 282632 | tf_op jit(solution)/shard_map/ppermute | solution.py:496
  10.8 0.0 collective-permute-done.2.refs_13_
  10.8 0.0 copy-start
  10.8 0.0 collective-permute-done.3.refs_14_
  10.8 0.0 copy-start.1
  10.8 0.5 %copy-done = f32[16,256]{1,0:T(8,128)} copy-done((f32[16,256]{1,0:T(8,128)}, f32[16,256]{1,0:T(8,128)S(1)}, u32[]{:S(2)}) %copy-start) | copy-done | bytes 16408
  11.4 0.0 copy-done.1
  11.4 3.0 %collective-permute-start.4 = (f32[8,256]{1,0:T(8,128)S(1)}, f32[8,256]{1,0:T(8,128)}, u32[]{:S(2)}, u32[]{:S(2)}) collective-permute-start(f32[8,256]{1,0:T(8,128)S(1)} %pad_maximum_fusion), channel_id=1, source_target_pairs={{0,12},{4,8},{8,4},{12,0},{1,13},{5,9},{9,5},{13,1},{2,14},{6,10},... | collective-permute-start | bytes 24584 | tf_op jit(solution)/shard_map/ppermute | solution.py:496
  14.4 0.4 %collective-permute-start.5 = (f32[8,256]{1,0:T(8,128)S(1)}, f32[8,256]{1,0:T(8,128)}, u32[]{:S(2)}, u32[]{:S(2)}) collective-permute-start(f32[8,256]{1,0:T(8,128)S(1)} %pad_maximum_fusion.1), channel_id=1, source_target_pairs={{0,4},{4,0},{8,12},{12,8},{1,5},{5,1},{9,13},{13,9},{2,6},{6,2},{1... | collective-permute-start | bytes 24584 | tf_op jit(solution)/shard_map/ppermute | solution.py:496
  14.8 3.2 %collective-permute-done.4.refs_15_ = f32[8,256]{1,0:T(8,128)} collective-permute-done((f32[8,256]{1,0:T(8,128)S(1)}, f32[8,256]{1,0:T(8,128)}, u32[]{:S(2)}, u32[]{:S(2)}) %collective-permute-start.4) | collective-permute-done | bytes 8224 | tf_op jit(solution)/shard_map/ppermute | solution.py:496
  18.0 0.1 collective-permute-done.5.refs_16_
  18.1 0.0 collective-permute-done.6.refs_18_
  18.1 0.0 collective-permute-done.refs_11_
  18.1 0.0 collective-permute-done.1.refs_12_
  18.1 4.7 %steps.1 = (f32[3,16,16,128]{3,2,1,0:T(8,128)}, f32[2,8,16,128]{3,2,1,0:T(8,128)}) custom-call(f32[16]{0:T(128)} %refs_0_.3, f32[3,16,16,128]{3,2,1,0:T(8,128)} %refs_1_.3, f32[2,8,16,128]{3,2,1,0:T(8,128)} %refs_2_.3, f32[16,128]{1,0:T(8,128)} %refs_3_.3, f32[16,128]{1,0:T(8,128)} %refs_4_.3, s32[16,128]{1,0:T(8,128)} %refs_5_.3, s32[1,2048]{1,0:T(1,128)} %bitcast.5, ...), custom_call_target="tpu_custom_call" | custom-call | tf_op jit(solution)/shard_map/steps/pallas_call | solution.py:518
  (4 shorter events, 0.0 us)
Async XLA Ops:
  3.4 7.3 %collective-permute-start.2 = (f32[16,256]{1,0:T(8,128)}, f32[16,256]{1,0:T(8,128)S(1)}, u32[]{:S(2)}, u32[]{:S(2)}) collective-permute-start(f32[16,256]{1,0:T(8,128)} %get-tuple-element.12), channel_id=1, source_target_pairs={{0,1},{1,0},{2,3},{3,2},{4,5},{5,4},{6,7},{7,6},{8,9},{9,8},{10,11... | collective-permute-start | bytes 49160 | tf_op jit(solution)/shard_map/ppermute | solution.py:496
  4.0 6.8 %collective-permute-start.3 = (f32[16,256]{1,0:T(8,128)}, f32[16,256]{1,0:T(8,128)S(1)}, u32[]{:S(2)}, u32[]{:S(2)}) collective-permute-start(f32[16,256]{1,0:T(8,128)} %get-tuple-element.13), channel_id=1, source_target_pairs={{0,3},{1,2},{2,1},{3,0},{4,7},{5,6},{6,5},{7,4},{8,11},{9,10},{10,... | collective-permute-start | bytes 49160 | tf_op jit(solution)/shard_map/ppermute | solution.py:496
  6.6 11.5 %collective-permute-start.6 = (f32[48,128]{1,0:T(8,128)}, f32[48,128]{1,0:T(8,128)}, u32[]{:S(2)}, u32[]{:S(2)}) collective-permute-start(f32[48,128]{1,0:T(8,128)} %get-tuple-element.15), channel_id=1, source_target_pairs={{0,8},{4,12},{8,0},{12,4},{1,9},{5,13},{9,1},{13,5},{2,10},{6,14},... | collective-permute-start | bytes 73736 | tf_op jit(solution)/shard_map/ppermute | solution.py:493
  9.2 9.0 %collective-permute-start = (f32[184,128]{1,0:T(8,128)}, f32[184,128]{1,0:T(8,128)}, u32[]{:S(2)}, u32[]{:S(2)}) collective-permute-start(f32[184,128]{1,0:T(8,128)} %get-tuple-element.10), channel_id=1, source_target_pairs={{0,12},{4,8},{8,4},{12,0},{1,13},{5,9},{9,5},{13,1},{2,14},{6,10},... | collective-permute-start | bytes 282632 | tf_op jit(solution)/shard_map/ppermute | solution.py:496
  10.5 7.6 %collective-permute-start.1 = (f32[184,128]{1,0:T(8,128)}, f32[184,128]{1,0:T(8,128)}, u32[]{:S(2)}, u32[]{:S(2)}) collective-permute-start(f32[184,128]{1,0:T(8,128)} %get-tuple-element.11), channel_id=1, source_target_pairs={{0,4},{4,0},{8,12},{12,8},{1,5},{5,1},{9,13},{13,9},{2,6},{6,2},{1... | collective-permute-start | bytes 282632 | tf_op jit(solution)/shard_map/ppermute | solution.py:496
  10.8 0.6 %copy-start = (f32[16,256]{1,0:T(8,128)}, f32[16,256]{1,0:T(8,128)S(1)}, u32[]{:S(2)}) copy-start(f32[16,256]{1,0:T(8,128)S(1)} %collective-permute-done.2.refs_13_) | copy-start | bytes 49156
  10.8 0.6 %copy-start.1 = (f32[16,256]{1,0:T(8,128)}, f32[16,256]{1,0:T(8,128)S(1)}, u32[]{:S(2)}) copy-start(f32[16,256]{1,0:T(8,128)S(1)} %collective-permute-done.3.refs_14_) | copy-start | bytes 49156
  11.4 6.6 %collective-permute-start.4 = (f32[8,256]{1,0:T(8,128)S(1)}, f32[8,256]{1,0:T(8,128)}, u32[]{:S(2)}, u32[]{:S(2)}) collective-permute-start(f32[8,256]{1,0:T(8,128)S(1)} %pad_maximum_fusion), channel_id=1, source_target_pairs={{0,12},{4,8},{8,4},{12,0},{1,13},{5,9},{9,5},{13,1},{2,14},{6,10},... | collective-permute-start | bytes 24584 | tf_op jit(solution)/shard_map/ppermute | solution.py:496
  14.4 3.8 %collective-permute-start.5 = (f32[8,256]{1,0:T(8,128)S(1)}, f32[8,256]{1,0:T(8,128)}, u32[]{:S(2)}, u32[]{:S(2)}) collective-permute-start(f32[8,256]{1,0:T(8,128)S(1)} %pad_maximum_fusion.1), channel_id=1, source_target_pairs={{0,4},{4,0},{8,12},{12,8},{1,5},{5,1},{9,13},{13,9},{2,6},{6,2},{1... | collective-permute-start | bytes 24584 | tf_op jit(solution)/shard_map/ppermute | solution.py:496

commit v16 on v13

--- a/solution.py
+++ b/solution.py
@@ -134,6 +134,14 @@
     for one in used:
         one.wait()
     arrived = len(used)
+    cell = atm_cell[...]
+    hot_atm = jnp.where(one_hot(cell % cols, cols), 1.0, 0.0).astype(BF16)
+    airx = gather_rows(air[...], one_hot(cell // cols, rows), hot_atm)
+    w = weight[...]
+    wair = w * airx
+    wair_buf[...] = wair
+    copy(wair_buf, wair_out)
+
     wetness = wet[...].astype(F32)
 
     lane = lax.broadcasted_iota(jnp.int32, (rows, cols), 1)
@@ -189,13 +197,6 @@
     copy_either(line, down, rows_a.at[0:halo], rows_b.at[0:halo])
     copy_either(line, up, rows_b.at[0:halo], rows_a.at[0:halo])
 
-    cell = atm_cell[...]
-    hot_atm = jnp.where(one_hot(cell % cols, cols), 1.0, 0.0).astype(BF16)
-    airx = gather_rows(air[...], one_hot(cell // cols, rows), hot_atm)
-    w = weight[...]
-    wair = w * airx
-    wair_buf[...] = wair
-    copy(wair_buf, wair_out)
     cell = sea_cell[...]
     hot_sea = jnp.where(one_hot(cell % cols, cols), 1.0, 0.0).astype(BF16)
     row = dest[...] * rows + cell // cols
@@ -279,17 +280,10 @@
     hot_sea = jnp.where(one_hot(cell % cols, cols), 1.0, 0.0).astype(BF16)
     row = dest[...] * rows + cell // cols
     s1, s2 = message(0, 0), message(0, 1)
-    sstx = jnp.zeros(cell.shape, F32)
-    for shift in range(tiles):
-        if shift:
-            s1 = s1 + message(shift, 0)
-            s2 = s2 + message(shift, 1)
-        sstx = sstx + gather_rows(message(shift, 2), one_hot(row - tile_at(-shift, tiles) * rows, rows), hot_sea)
+    for shift in range(1, tiles):
+        s1 = s1 + message(shift, 0)
+        s2 = s2 + message(shift, 1)
     sea_flux = s1 - surface * s2
-    flux = wair[...] - weight[...] * sstx
-    cell = atm_cell[...]
-    hot_atm = jnp.where(one_hot(cell % cols, cols), 1.0, 0.0).astype(BF16)
-    (atm_flux,) = scatter_rows([flux], one_hot(cell // cols, rows), hot_atm)
 
     half = lanes // cols
     for i in range(2 * half):
@@ -358,13 +352,19 @@
     for i, (at, high) in enumerate(((mbase, AH), (mbase + AH, OH), (mbase + AH + OH, OH))):
         extend(ms.at[i], base + i, AH)
         extend_rows(ms.at[i], at, high)
-    for i in range(tracers):
-        extend(fs.at[i // each, i % each], 3 * levels + i, OH)
-        extend_rows(fs.at[i // each, i % each], obase + OH * i, OH)
-    for level in range(levels):
-        for which, ref in enumerate((us, vs, hs)):
-            extend(ref.at[level], which * levels + level, AH)
-            extend_level(ref.at[level], which, level)
+    sstx = jnp.zeros(cell.shape, F32)
+    for shift in range(tiles):
+        sstx = sstx + gather_rows(message(shift, 2), one_hot(row - tile_at(-shift, tiles) * rows, rows), hot_sea)
+        for i in range(tracers * shift // tiles, tracers * (shift + 1) // tiles):
+            extend(fs.at[i // each, i % each], 3 * levels + i, OH)
+            extend_rows(fs.at[i // each, i % each], obase + OH * i, OH)
+        for level in range(levels * shift // tiles, levels * (shift + 1) // tiles):
+            for which, ref in enumerate((us, vs, hs)):
+                extend(ref.at[level], which * levels + level, AH)
+                extend_level(ref.at[level], which, level)
+    flux = wair[...] - weight[...] * sstx
+    cell = atm_cell[...]
+    hot_atm = jnp.where(one_hot(cell % cols, cols), 1.0, 0.0).astype(BF16)
 
     w = ms[1]
     k = ms[2]
@@ -372,6 +372,8 @@
     ce, cw, cs, cn = kw * east(w), kw * west(w), kw * south(w), kw * north(w)
     center = 1.0 - (ce + cw + cs + cn)
     for step in range(OCEAN_STEPS):
+        if step == OCEAN_STEPS - 1:
+            (atm_flux,) = scatter_rows([flux], one_hot(cell // cols, rows), hot_atm)
         for i in range(tracers):
             f = fs[i // each, i % each]
             f = center * f + ce * east(f) + cw * west(f) + cs * south(f) + cn * north(f)

time: 22.6 us -> 22.6 us (level)
  no operation moved by 1% of the time
where the time goes in v16:
time: 22.6 us; the launch traced here: 22.4 us
  starting transfers between devices  10.7 us (47%)
  Pallas kernels  7.04 us (31%)
  waiting for transfers between devices  3.32 us (15%)
  between operations  0.68 us (3%)
  local copies, waits for them, and re-layouts  0.58 us (3%)
    ppermute x6, starting transfers between devices, swap(): lax.ppermute(value, axes, [(i, (i + (1 if (i + odd) % 2 == 0 else -1)) %...  8.14 us
    pallas_call x1, Pallas kernels, on_device(): pl.pallas_call(functools.partial(final_kernel, tile_count), out_shape=[sh...  4.22 us
    ppermute x6, waiting for transfers between devices, swap(): lax.ppermute(value, axes, [(i, (i + (1 if (i + odd) % 2 == 0 else -1)) %...  3.32 us
    pallas_call x1, Pallas kernels, on_device(): pl.pallas_call(functools.partial(first_kernel, tile_count), out_shape=[sh...  2.82 us
    ppermute x1, starting transfers between devices, shift(): lax.ppermute(value, axes, [(i, (i + by) % count) for i in range(count)])  2.59 us
    unnamed x4, local copies, waits for them, and re-layouts  0.56 us
  transfers between devices with their start and end apart: 7, of which 2 were waited for; matrix products, arithmetic and copies ran while one was open for 0% of the time, Pallas kernels for 0%

profile of v16, /device:TPU:0, one launch (start us, length us, event | category | flops | bytes accessed | tf_op | source)
XLA Modules:
  0.0 22.4 jit_solution(2734156007733547402)
XLA Ops:
  0.6 2.8 %first.1 = (f32[16,256]{1,0:T(8,128)}, f32[16,256]{1,0:T(8,128)}, f32[184,128]{1,0:T(8,128)}, f32[184,128]{1,0:T(8,128)}, f32[1,2048]{1,0:T(1,128)}, /*index=5*/f32[48,128]{1,0:T(8,128)}, f32[48,128]{1,0:T(8,128)}) custom-call(f32[3,16,16,128]{3,2,1,0:T(8,128)} %refs_1_.3, f32[2,8,16,128]{3,2,1,0:T(8,128)} %refs_2_.3, f32[16,128]{1,0:T(8,128)} %refs_3_.3, ...), custom_call_target="tpu_custom_call" | custom-call | tf_op jit(solution)/shard_map/first/pallas_call | solution.py:461
  3.5 0.5 %collective-permute-start.2 = (f32[16,256]{1,0:T(8,128)}, f32[16,256]{1,0:T(8,128)S(1)}, u32[]{:S(2)}, u32[]{:S(2)}) collective-permute-start(f32[16,256]{1,0:T(8,128)} %get-tuple-element.12), channel_id=1, source_target_pairs={{0,1},{1,0},{2,3},{3,2},{4,5},{5,4},{6,7},{7,6},{8,9},{9,8},{10,11... | collective-permute-start | bytes 49160 | tf_op jit(solution)/shard_map/ppermute | solution.py:486
  4.0 2.6 %collective-permute-start.3 = (f32[16,256]{1,0:T(8,128)}, f32[16,256]{1,0:T(8,128)S(1)}, u32[]{:S(2)}, u32[]{:S(2)}) collective-permute-start(f32[16,256]{1,0:T(8,128)} %get-tuple-element.13), channel_id=1, source_target_pairs={{0,3},{1,2},{2,1},{3,0},{4,7},{5,6},{6,5},{7,4},{8,11},{9,10},{10,... | collective-permute-start | bytes 49160 | tf_op jit(solution)/shard_map/ppermute | solution.py:486
  6.6 2.6 %collective-permute-start.6 = (f32[48,128]{1,0:T(8,128)}, f32[48,128]{1,0:T(8,128)}, u32[]{:S(2)}, u32[]{:S(2)}) collective-permute-start(f32[48,128]{1,0:T(8,128)} %get-tuple-element.15), channel_id=1, source_target_pairs={{0,8},{4,12},{8,0},{12,4},{1,9},{5,13},{9,1},{13,5},{2,10},{6,14},... | collective-permute-start | bytes 73736 | tf_op jit(solution)/shard_map/ppermute | solution.py:483
  9.2 1.3 %collective-permute-start = (f32[184,128]{1,0:T(8,128)}, f32[184,128]{1,0:T(8,128)}, u32[]{:S(2)}, u32[]{:S(2)}) collective-permute-start(f32[184,128]{1,0:T(8,128)} %get-tuple-element.10), channel_id=1, source_target_pairs={{0,12},{4,8},{8,4},{12,0},{1,13},{5,9},{9,5},{13,1},{2,14},{6,10},... | collective-permute-start | bytes 282632 | tf_op jit(solution)/shard_map/ppermute | solution.py:486
  10.5 0.2 %collective-permute-start.1 = (f32[184,128]{1,0:T(8,128)}, f32[184,128]{1,0:T(8,128)}, u32[]{:S(2)}, u32[]{:S(2)}) collective-permute-start(f32[184,128]{1,0:T(8,128)} %get-tuple-element.11), channel_id=1, source_target_pairs={{0,4},{4,0},{8,12},{12,8},{1,5},{5,1},{9,13},{13,9},{2,6},{6,2},{1... | collective-permute-start | bytes 282632 | tf_op jit(solution)/shard_map/ppermute | solution.py:486
  10.8 0.0 collective-permute-done.2.refs_13_
  10.8 0.0 copy-start
  10.8 0.0 collective-permute-done.3.refs_14_
  10.8 0.0 copy-start.1
  10.8 0.5 %copy-done = f32[16,256]{1,0:T(8,128)} copy-done((f32[16,256]{1,0:T(8,128)}, f32[16,256]{1,0:T(8,128)S(1)}, u32[]{:S(2)}) %copy-start) | copy-done | bytes 16408
  11.4 0.0 copy-done.1
  11.4 3.0 %collective-permute-start.4 = (f32[8,256]{1,0:T(8,128)S(1)}, f32[8,256]{1,0:T(8,128)}, u32[]{:S(2)}, u32[]{:S(2)}) collective-permute-start(f32[8,256]{1,0:T(8,128)S(1)} %pad_maximum_fusion), channel_id=1, source_target_pairs={{0,12},{4,8},{8,4},{12,0},{1,13},{5,9},{9,5},{13,1},{2,14},{6,10},... | collective-permute-start | bytes 24584 | tf_op jit(solution)/shard_map/ppermute | solution.py:486
  14.4 0.4 %collective-permute-start.5 = (f32[8,256]{1,0:T(8,128)S(1)}, f32[8,256]{1,0:T(8,128)}, u32[]{:S(2)}, u32[]{:S(2)}) collective-permute-start(f32[8,256]{1,0:T(8,128)S(1)} %pad_maximum_fusion.1), channel_id=1, source_target_pairs={{0,4},{4,0},{8,12},{12,8},{1,5},{5,1},{9,13},{13,9},{2,6},{6,2},{1... | collective-permute-start | bytes 24584 | tf_op jit(solution)/shard_map/ppermute | solution.py:486
  14.8 3.2 %collective-permute-done.4.refs_15_ = f32[8,256]{1,0:T(8,128)} collective-permute-done((f32[8,256]{1,0:T(8,128)S(1)}, f32[8,256]{1,0:T(8,128)}, u32[]{:S(2)}, u32[]{:S(2)}) %collective-permute-start.4) | collective-permute-done | bytes 8224 | tf_op jit(solution)/shard_map/ppermute | solution.py:486
  18.0 0.1 collective-permute-done.5.refs_16_
  18.1 0.0 collective-permute-done.6.refs_18_
  18.1 0.0 collective-permute-done.refs_11_
  18.1 0.0 collective-permute-done.1.refs_12_
  18.1 4.2 %steps.1 = (f32[3,16,16,128]{3,2,1,0:T(8,128)}, f32[2,8,16,128]{3,2,1,0:T(8,128)}) custom-call(f32[16]{0:T(128)} %refs_0_.3, f32[3,16,16,128]{3,2,1,0:T(8,128)} %refs_1_.3, f32[2,8,16,128]{3,2,1,0:T(8,128)} %refs_2_.3, f32[16,128]{1,0:T(8,128)} %refs_3_.3, f32[16,128]{1,0:T(8,128)} %refs_4_.3, s32[16,128]{1,0:T(8,128)} %refs_5_.3, s32[1,2048]{1,0:T(1,128)} %bitcast.5, ...), custom_call_target="tpu_custom_call" | custom-call | tf_op jit(solution)/shard_map/steps/pallas_call | solution.py:508
  (4 shorter events, 0.0 us)
Async XLA Ops:
  3.5 7.3 %collective-permute-start.2 = (f32[16,256]{1,0:T(8,128)}, f32[16,256]{1,0:T(8,128)S(1)}, u32[]{:S(2)}, u32[]{:S(2)}) collective-permute-start(f32[16,256]{1,0:T(8,128)} %get-tuple-element.12), channel_id=1, source_target_pairs={{0,1},{1,0},{2,3},{3,2},{4,5},{5,4},{6,7},{7,6},{8,9},{9,8},{10,11... | collective-permute-start | bytes 49160 | tf_op jit(solution)/shard_map/ppermute | solution.py:486
  4.0 6.8 %collective-permute-start.3 = (f32[16,256]{1,0:T(8,128)}, f32[16,256]{1,0:T(8,128)S(1)}, u32[]{:S(2)}, u32[]{:S(2)}) collective-permute-start(f32[16,256]{1,0:T(8,128)} %get-tuple-element.13), channel_id=1, source_target_pairs={{0,3},{1,2},{2,1},{3,0},{4,7},{5,6},{6,5},{7,4},{8,11},{9,10},{10,... | collective-permute-start | bytes 49160 | tf_op jit(solution)/shard_map/ppermute | solution.py:486
  6.6 11.5 %collective-permute-start.6 = (f32[48,128]{1,0:T(8,128)}, f32[48,128]{1,0:T(8,128)}, u32[]{:S(2)}, u32[]{:S(2)}) collective-permute-start(f32[48,128]{1,0:T(8,128)} %get-tuple-element.15), channel_id=1, source_target_pairs={{0,8},{4,12},{8,0},{12,4},{1,9},{5,13},{9,1},{13,5},{2,10},{6,14},... | collective-permute-start | bytes 73736 | tf_op jit(solution)/shard_map/ppermute | solution.py:483
  9.2 9.0 %collective-permute-start = (f32[184,128]{1,0:T(8,128)}, f32[184,128]{1,0:T(8,128)}, u32[]{:S(2)}, u32[]{:S(2)}) collective-permute-start(f32[184,128]{1,0:T(8,128)} %get-tuple-element.10), channel_id=1, source_target_pairs={{0,12},{4,8},{8,4},{12,0},{1,13},{5,9},{9,5},{13,1},{2,14},{6,10},... | collective-permute-start | bytes 282632 | tf_op jit(solution)/shard_map/ppermute | solution.py:486
  10.5 7.6 %collective-permute-start.1 = (f32[184,128]{1,0:T(8,128)}, f32[184,128]{1,0:T(8,128)}, u32[]{:S(2)}, u32[]{:S(2)}) collective-permute-start(f32[184,128]{1,0:T(8,128)} %get-tuple-element.11), channel_id=1, source_target_pairs={{0,4},{4,0},{8,12},{12,8},{1,5},{5,1},{9,13},{13,9},{2,6},{6,2},{1... | collective-permute-start | bytes 282632 | tf_op jit(solution)/shard_map/ppermute | solution.py:486
  10.8 0.6 %copy-start = (f32[16,256]{1,0:T(8,128)}, f32[16,256]{1,0:T(8,128)S(1)}, u32[]{:S(2)}) copy-start(f32[16,256]{1,0:T(8,128)S(1)} %collective-permute-done.2.refs_13_) | copy-start | bytes 49156
  10.8 0.6 %copy-start.1 = (f32[16,256]{1,0:T(8,128)}, f32[16,256]{1,0:T(8,128)S(1)}, u32[]{:S(2)}) copy-start(f32[16,256]{1,0:T(8,128)S(1)} %collective-permute-done.3.refs_14_) | copy-start | bytes 49156
  11.4 6.6 %collective-permute-start.4 = (f32[8,256]{1,0:T(8,128)S(1)}, f32[8,256]{1,0:T(8,128)}, u32[]{:S(2)}, u32[]{:S(2)}) collective-permute-start(f32[8,256]{1,0:T(8,128)S(1)} %pad_maximum_fusion), channel_id=1, source_target_pairs={{0,12},{4,8},{8,4},{12,0},{1,13},{5,9},{9,5},{13,1},{2,14},{6,10},... | collective-permute-start | bytes 24584 | tf_op jit(solution)/shard_map/ppermute | solution.py:486
  14.4 3.8 %collective-permute-start.5 = (f32[8,256]{1,0:T(8,128)S(1)}, f32[8,256]{1,0:T(8,128)}, u32[]{:S(2)}, u32[]{:S(2)}) collective-permute-start(f32[8,256]{1,0:T(8,128)S(1)} %pad_maximum_fusion.1), channel_id=1, source_target_pairs={{0,4},{4,0},{8,12},{12,8},{1,5},{5,1},{9,13},{13,9},{2,6},{6,2},{1... | collective-permute-start | bytes 24584 | tf_op jit(solution)/shard_map/ppermute | solution.py:486

commit v17 on v16

--- a/solution.py
+++ b/solution.py
@@ -494,6 +494,8 @@
     corner_a, corner_b = [
         jnp.concatenate([lax.dynamic_slice_in_dim(x, at, AH) for x in (got_a, got_b)]) for at in (low, rows - AH - low)
     ]
+    if by_shift:
+        *messages, corner_a, corner_b = lax.optimization_barrier((*messages, corner_a, corner_b))
     corner_a = swap(corner_a, "tile", tile_count, 1)
     corner_b = swap(corner_b, "tile", tile_count, 0)
     if by_shift:

time: 22.6 us -> 24.1 us (1.066)
  local copies, waits for them, and re-layouts: 0.58 us -> 1.28 us
  waiting for transfers between devices: 3.32 us -> 3.77 us
  starting transfers between devices: 10.7 us -> 11.1 us
    ppermute x6, starting transfers between devices: 8.14 us -> 10.3 us  [swap(): lax.ppermute(value, axes, [(i, (i + (1 if (i + odd) % 2 == 0 else -1)) %...]
    ppermute x1, starting transfers between devices: 2.59 us -> 0.78 us  [shift(): lax.ppermute(value, axes, [(i, (i + by) % count) for i in range(count)])]
    unnamed x4 -> x6, local copies, waits for them, and re-layouts: 0.56 us -> 1.26 us
    ppermute x6, waiting for transfers between devices: 3.32 us -> 3.76 us  [swap(): lax.ppermute(value, axes, [(i, (i + (1 if (i + odd) % 2 == 0 else -1)) %...]
where the time goes in v17:
time: 24.1 us; the launch traced here: 23.9 us
  starting transfers between devices  11.1 us (46%)
  Pallas kernels  7.04 us (29%)
  waiting for transfers between devices  3.77 us (16%)
  local copies, waits for them, and re-layouts  1.28 us (5%)
  between operations  0.69 us (3%)
    ppermute x6, starting transfers between devices, swap(): lax.ppermute(value, axes, [(i, (i + (1 if (i + odd) % 2 == 0 else -1)) %...  10.3 us
    pallas_call x1, Pallas kernels, on_device(): pl.pallas_call(functools.partial(final_kernel, tile_count), out_shape=[sh...  4.22 us
    ppermute x6, waiting for transfers between devices, swap(): lax.ppermute(value, axes, [(i, (i + (1 if (i + odd) % 2 == 0 else -1)) %...  3.76 us
    pallas_call x1, Pallas kernels, on_device(): pl.pallas_call(functools.partial(first_kernel, tile_count), out_shape=[sh...  2.82 us
    unnamed x6, local copies, waits for them, and re-layouts  1.26 us
    ppermute x1, starting transfers between devices, shift(): lax.ppermute(value, axes, [(i, (i + by) % count) for i in range(count)])  0.78 us
  transfers between devices with their start and end apart: 7, of which 2 were waited for; matrix products, arithmetic and copies ran while one was open for 0% of the time, Pallas kernels for 0%

profile of v17, /device:TPU:0, one launch (start us, length us, event | category | flops | bytes accessed | tf_op | source)
XLA Modules:
  0.0 23.9 jit_solution(5982322524531284141)
XLA Ops:
  0.6 2.8 %first.1 = (f32[16,256]{1,0:T(8,128)}, f32[16,256]{1,0:T(8,128)}, f32[184,128]{1,0:T(8,128)}, f32[184,128]{1,0:T(8,128)}, f32[1,2048]{1,0:T(1,128)}, /*index=5*/f32[48,128]{1,0:T(8,128)}, f32[48,128]{1,0:T(8,128)}) custom-call(f32[3,16,16,128]{3,2,1,0:T(8,128)} %refs_1_.3, f32[2,8,16,128]{3,2,1,0:T(8,128)} %refs_2_.3, f32[16,128]{1,0:T(8,128)} %refs_3_.3, ...), custom_call_target="tpu_custom_call" | custom-call | tf_op jit(solution)/shard_map/first/pallas_call | solution.py:461
  3.5 0.5 %collective-permute-start.2 = (f32[16,256]{1,0:T(8,128)}, f32[16,256]{1,0:T(8,128)S(1)}, u32[]{:S(2)}, u32[]{:S(2)}) collective-permute-start(f32[16,256]{1,0:T(8,128)} %get-tuple-element.16), channel_id=1, source_target_pairs={{0,1},{1,0},{2,3},{3,2},{4,5},{5,4},{6,7},{7,6},{8,9},{9,8},{10,11... | collective-permute-start | bytes 49160 | tf_op jit(solution)/shard_map/ppermute | solution.py:486
  4.0 2.6 %collective-permute-start.3 = (f32[16,256]{1,0:T(8,128)}, f32[16,256]{1,0:T(8,128)S(1)}, u32[]{:S(2)}, u32[]{:S(2)}) collective-permute-start(f32[16,256]{1,0:T(8,128)} %get-tuple-element.17), channel_id=1, source_target_pairs={{0,3},{1,2},{2,1},{3,0},{4,7},{5,6},{6,5},{7,4},{8,11},{9,10},{10,... | collective-permute-start | bytes 49160 | tf_op jit(solution)/shard_map/ppermute | solution.py:486
  6.6 3.6 %collective-permute-start = (f32[184,128]{1,0:T(8,128)}, f32[184,128]{1,0:T(8,128)}, u32[]{:S(2)}, u32[]{:S(2)}) collective-permute-start(f32[184,128]{1,0:T(8,128)} %get-tuple-element.14), channel_id=1, source_target_pairs={{0,12},{4,8},{8,4},{12,0},{1,13},{5,9},{9,5},{13,1},{2,14},{6,10},... | collective-permute-start | bytes 282632 | tf_op jit(solution)/shard_map/ppermute | solution.py:486
  10.2 0.0 collective-permute-start.1
  10.2 0.0 collective-permute-done.2.refs_13_
  10.2 0.0 copy-start
  10.2 0.0 collective-permute-done.3.refs_14_
  10.2 0.0 copy-start.1
  10.3 0.5 %copy-done = f32[16,256]{1,0:T(8,128)} copy-done((f32[16,256]{1,0:T(8,128)}, f32[16,256]{1,0:T(8,128)S(1)}, u32[]{:S(2)}) %copy-start) | copy-done | bytes 16408
  10.8 0.0 copy-start.2
  10.8 0.0 copy-done.1
  10.8 0.7 %copy-done.2 = f32[48,128]{1,0:T(8,128)S(1)} copy-done((f32[48,128]{1,0:T(8,128)S(1)}, f32[48,128]{1,0:T(8,128)}, u32[]{:S(2)}) %copy-start.2) | copy-done | bytes 24600
  11.5 0.8 %collective-permute-start.6 = (f32[48,128]{1,0:T(8,128)S(1)}, f32[48,128]{1,0:T(8,128)}, u32[]{:S(2)}, u32[]{:S(2)}) collective-permute-start(f32[48,128]{1,0:T(8,128)S(1)} %copy-done.2), channel_id=1, source_target_pairs={{0,8},{4,12},{8,0},{12,4},{1,9},{5,13},{9,1},{13,5},{2,10},{6,14},... | collective-permute-start | bytes 73736 | tf_op jit(solution)/shard_map/ppermute | solution.py:483
  12.3 3.6 %collective-permute-start.4 = (f32[8,256]{1,0:T(8,128)S(1)}, f32[8,256]{1,0:T(8,128)}, u32[]{:S(2)}, u32[]{:S(2)}) collective-permute-start(f32[8,256]{1,0:T(8,128)S(1)} %get-tuple-element.20), channel_id=1, source_target_pairs={{0,12},{4,8},{8,4},{12,0},{1,13},{5,9},{9,5},{13,1},{2,14},{6,10},... | collective-permute-start | bytes 24584 | tf_op jit(solution)/shard_map/ppermute | solution.py:486
  15.9 0.0 collective-permute-start.5
  15.9 2.0 %collective-permute-done.4.refs_15_ = f32[8,256]{1,0:T(8,128)} collective-permute-done((f32[8,256]{1,0:T(8,128)S(1)}, f32[8,256]{1,0:T(8,128)}, u32[]{:S(2)}, u32[]{:S(2)}) %collective-permute-start.4) | collective-permute-done | bytes 8224 | tf_op jit(solution)/shard_map/ppermute | solution.py:486
  17.9 1.8 %collective-permute-done.5.refs_16_ = f32[8,256]{1,0:T(8,128)} collective-permute-done((f32[8,256]{1,0:T(8,128)S(1)}, f32[8,256]{1,0:T(8,128)}, u32[]{:S(2)}, u32[]{:S(2)}) %collective-permute-start.5) | collective-permute-done | bytes 8224 | tf_op jit(solution)/shard_map/ppermute | solution.py:486
  19.7 0.0 collective-permute-done.6.refs_18_
  19.7 0.0 collective-permute-done.refs_11_
  19.7 0.0 collective-permute-done.1.refs_12_
  19.7 4.2 %steps.1 = (f32[3,16,16,128]{3,2,1,0:T(8,128)}, f32[2,8,16,128]{3,2,1,0:T(8,128)}) custom-call(f32[16]{0:T(128)} %refs_0_.3, f32[3,16,16,128]{3,2,1,0:T(8,128)} %refs_1_.3, f32[2,8,16,128]{3,2,1,0:T(8,128)} %refs_2_.3, f32[16,128]{1,0:T(8,128)} %refs_3_.3, f32[16,128]{1,0:T(8,128)} %refs_4_.3, s32[16,128]{1,0:T(8,128)} %refs_5_.3, s32[1,2048]{1,0:T(1,128)} %bitcast.5, ...), custom_call_target="tpu_custom_call" | custom-call | tf_op jit(solution)/shard_map/steps/pallas_call | solution.py:510
  (3 shorter events, 0.0 us)
Async XLA Ops:
  3.5 6.7 %collective-permute-start.2 = (f32[16,256]{1,0:T(8,128)}, f32[16,256]{1,0:T(8,128)S(1)}, u32[]{:S(2)}, u32[]{:S(2)}) collective-permute-start(f32[16,256]{1,0:T(8,128)} %get-tuple-element.16), channel_id=1, source_target_pairs={{0,1},{1,0},{2,3},{3,2},{4,5},{5,4},{6,7},{7,6},{8,9},{9,8},{10,11... | collective-permute-start | bytes 49160 | tf_op jit(solution)/shard_map/ppermute | solution.py:486
  4.0 6.3 %collective-permute-start.3 = (f32[16,256]{1,0:T(8,128)}, f32[16,256]{1,0:T(8,128)S(1)}, u32[]{:S(2)}, u32[]{:S(2)}) collective-permute-start(f32[16,256]{1,0:T(8,128)} %get-tuple-element.17), channel_id=1, source_target_pairs={{0,3},{1,2},{2,1},{3,0},{4,7},{5,6},{6,5},{7,4},{8,11},{9,10},{10,... | collective-permute-start | bytes 49160 | tf_op jit(solution)/shard_map/ppermute | solution.py:486
  6.6 13.1 %collective-permute-start = (f32[184,128]{1,0:T(8,128)}, f32[184,128]{1,0:T(8,128)}, u32[]{:S(2)}, u32[]{:S(2)}) collective-permute-start(f32[184,128]{1,0:T(8,128)} %get-tuple-element.14), channel_id=1, source_target_pairs={{0,12},{4,8},{8,4},{12,0},{1,13},{5,9},{9,5},{13,1},{2,14},{6,10},... | collective-permute-start | bytes 282632 | tf_op jit(solution)/shard_map/ppermute | solution.py:486
  10.2 9.5 %collective-permute-start.1 = (f32[184,128]{1,0:T(8,128)}, f32[184,128]{1,0:T(8,128)}, u32[]{:S(2)}, u32[]{:S(2)}) collective-permute-start(f32[184,128]{1,0:T(8,128)} %get-tuple-element.15), channel_id=1, source_target_pairs={{0,4},{4,0},{8,12},{12,8},{1,5},{5,1},{9,13},{13,9},{2,6},{6,2},{1... | collective-permute-start | bytes 282632 | tf_op jit(solution)/shard_map/ppermute | solution.py:486
  10.2 0.6 %copy-start = (f32[16,256]{1,0:T(8,128)}, f32[16,256]{1,0:T(8,128)S(1)}, u32[]{:S(2)}) copy-start(f32[16,256]{1,0:T(8,128)S(1)} %collective-permute-done.2.refs_13_) | copy-start | bytes 49156
  10.2 0.6 %copy-start.1 = (f32[16,256]{1,0:T(8,128)}, f32[16,256]{1,0:T(8,128)S(1)}, u32[]{:S(2)}) copy-start(f32[16,256]{1,0:T(8,128)S(1)} %collective-permute-done.3.refs_14_) | copy-start | bytes 49156
  10.8 0.7 %copy-start.2 = (f32[48,128]{1,0:T(8,128)S(1)}, f32[48,128]{1,0:T(8,128)}, u32[]{:S(2)}) copy-start(f32[48,128]{1,0:T(8,128)} %get-tuple-element.23) | copy-start | bytes 73732
  11.5 8.1 %collective-permute-start.6 = (f32[48,128]{1,0:T(8,128)S(1)}, f32[48,128]{1,0:T(8,128)}, u32[]{:S(2)}, u32[]{:S(2)}) collective-permute-start(f32[48,128]{1,0:T(8,128)S(1)} %copy-done.2), channel_id=1, source_target_pairs={{0,8},{4,12},{8,0},{12,4},{1,9},{5,13},{9,1},{13,5},{2,10},{6,14},... | collective-permute-start | bytes 73736 | tf_op jit(solution)/shard_map/ppermute | solution.py:483
  12.3 5.6 %collective-permute-start.4 = (f32[8,256]{1,0:T(8,128)S(1)}, f32[8,256]{1,0:T(8,128)}, u32[]{:S(2)}, u32[]{:S(2)}) collective-permute-start(f32[8,256]{1,0:T(8,128)S(1)} %get-tuple-element.20), channel_id=1, source_target_pairs={{0,12},{4,8},{8,4},{12,0},{1,13},{5,9},{9,5},{13,1},{2,14},{6,10},... | collective-permute-start | bytes 24584 | tf_op jit(solution)/shard_map/ppermute | solution.py:486
  15.9 3.8 %collective-permute-start.5 = (f32[8,256]{1,0:T(8,128)S(1)}, f32[8,256]{1,0:T(8,128)}, u32[]{:S(2)}, u32[]{:S(2)}) collective-permute-start(f32[8,256]{1,0:T(8,128)S(1)} %get-tuple-element.21), channel_id=1, source_target_pairs={{0,4},{4,0},{8,12},{12,8},{1,5},{5,1},{9,13},{13,9},{2,6},{6,2},{1... | collective-permute-start | bytes 24584 | tf_op jit(solution)/shard_map/ppermute | solution.py:486

commit v18 on v16

--- a/solution.py
+++ b/solution.py
@@ -497,6 +497,7 @@
     corner_a = swap(corner_a, "tile", tile_count, 1)
     corner_b = swap(corner_b, "tile", tile_count, 0)
     if by_shift:
+        *messages, got_b = lax.optimization_barrier((*messages, got_b))
         got = messages[:1] + [shift(messages[s - 1], "tile", tile_count, s) for s in range(2, tile_count - 1)]
     else:
         got = [lax.all_to_all(messages[0], "tile", split_axis=0, concat_axis=0, tiled=True)]

time: 22.6 us -> 22.6 us (level)
  waiting for transfers between devices: 3.32 us -> 2.87 us
  starting transfers between devices: 10.7 us -> 11.1 us
    ppermute x6, starting transfers between devices: 8.14 us -> 9.54 us  [swap(): lax.ppermute(value, axes, [(i, (i + (1 if (i + odd) % 2 == 0 else -1)) %...]
    ppermute x1, starting transfers between devices: 2.59 us -> 1.6 us  [shift(): lax.ppermute(value, axes, [(i, (i + by) % count) for i in range(count)])]
    ppermute x6, waiting for transfers between devices: 3.32 us -> 2.86 us  [swap(): lax.ppermute(value, axes, [(i, (i + (1 if (i + odd) % 2 == 0 else -1)) %...]
    unnamed x4 -> x6, local copies, waits for them, and re-layouts: 0.56 us -> 0.56 us
where the time goes in v18:
time: 22.6 us; the launch traced here: 22.4 us
  starting transfers between devices  11.1 us (49%)
  Pallas kernels  7.04 us (31%)
  waiting for transfers between devices  2.87 us (13%)
  between operations  0.69 us (3%)
  local copies, waits for them, and re-layouts  0.59 us (3%)
    ppermute x6, starting transfers between devices, swap(): lax.ppermute(value, axes, [(i, (i + (1 if (i + odd) % 2 == 0 else -1)) %...  9.54 us
    pallas_call x1, Pallas kernels, on_device(): pl.pallas_call(functools.partial(final_kernel, tile_count), out_shape=[sh...  4.22 us
    ppermute x6, waiting for transfers between devices, swap(): lax.ppermute(value, axes, [(i, (i + (1 if (i + odd) % 2 == 0 else -1)) %...  2.86 us
    pallas_call x1, Pallas kernels, on_device(): pl.pallas_call(functools.partial(first_kernel, tile_count), out_shape=[sh...  2.82 us
    ppermute x1, starting transfers between devices, shift(): lax.ppermute(value, axes, [(i, (i + by) % count) for i in range(count)])  1.6 us
    unnamed x6, local copies, waits for them, and re-layouts  0.56 us
  transfers between devices with their start and end apart: 7, of which 2 were waited for; matrix products, arithmetic and copies ran while one was open for 0% of the time, Pallas kernels for 0%

profile of v18, /device:TPU:0, one launch (start us, length us, event | category | flops | bytes accessed | tf_op | source)
XLA Modules:
  0.0 22.4 jit_solution(5875957619636590126)
XLA Ops:
  0.6 2.8 %first.1 = (f32[16,256]{1,0:T(8,128)}, f32[16,256]{1,0:T(8,128)}, f32[184,128]{1,0:T(8,128)}, f32[184,128]{1,0:T(8,128)}, f32[1,2048]{1,0:T(1,128)}, /*index=5*/f32[48,128]{1,0:T(8,128)}, f32[48,128]{1,0:T(8,128)}) custom-call(f32[3,16,16,128]{3,2,1,0:T(8,128)} %refs_1_.3, f32[2,8,16,128]{3,2,1,0:T(8,128)} %refs_2_.3, f32[16,128]{1,0:T(8,128)} %refs_3_.3, ...), custom_call_target="tpu_custom_call" | custom-call | tf_op jit(solution)/shard_map/first/pallas_call | solution.py:461
  3.5 2.4 %collective-permute-start.3 = (f32[16,256]{1,0:T(8,128)}, f32[16,256]{1,0:T(8,128)S(1)}, u32[]{:S(2)}, u32[]{:S(2)}) collective-permute-start(f32[16,256]{1,0:T(8,128)} %get-tuple-element.18), channel_id=1, source_target_pairs={{0,3},{1,2},{2,1},{3,0},{4,7},{5,6},{6,5},{7,4},{8,11},{9,10},{10,... | collective-permute-start | bytes 49160 | tf_op jit(solution)/shard_map/ppermute | solution.py:486
  5.9 0.7 %collective-permute-start.2 = (f32[16,256]{1,0:T(8,128)}, f32[16,256]{1,0:T(8,128)S(1)}, u32[]{:S(2)}, u32[]{:S(2)}) collective-permute-start(f32[16,256]{1,0:T(8,128)} %get-tuple-element.15), channel_id=1, source_target_pairs={{0,1},{1,0},{2,3},{3,2},{4,5},{5,4},{6,7},{7,6},{8,9},{9,8},{10,11... | collective-permute-start | bytes 49160 | tf_op jit(solution)/shard_map/ppermute | solution.py:486
  6.6 3.6 %collective-permute-start = (f32[184,128]{1,0:T(8,128)}, f32[184,128]{1,0:T(8,128)}, u32[]{:S(2)}, u32[]{:S(2)}) collective-permute-start(f32[184,128]{1,0:T(8,128)} %get-tuple-element.13), channel_id=1, source_target_pairs={{0,12},{4,8},{8,4},{12,0},{1,13},{5,9},{9,5},{13,1},{2,14},{6,10},... | collective-permute-start | bytes 282632 | tf_op jit(solution)/shard_map/ppermute | solution.py:486
  10.2 0.0 collective-permute-start.1
  10.2 0.0 collective-permute-done.3.refs_14_
  10.2 0.0 copy-start
  10.2 0.0 copy-start.2
  10.2 0.0 collective-permute-done.2.refs_13_
  10.2 0.0 copy-start.1
  10.3 0.5 %copy-done = f32[16,256]{1,0:T(8,128)} copy-done((f32[16,256]{1,0:T(8,128)}, f32[16,256]{1,0:T(8,128)S(1)}, u32[]{:S(2)}) %copy-start) | copy-done | bytes 16408
  10.8 0.0 copy-done.1
  10.8 1.9 %collective-permute-start.4 = (f32[8,256]{1,0:T(8,128)S(1)}, f32[8,256]{1,0:T(8,128)}, u32[]{:S(2)}, u32[]{:S(2)}) collective-permute-start(f32[8,256]{1,0:T(8,128)S(1)} %pad_maximum_fusion), channel_id=1, source_target_pairs={{0,12},{4,8},{8,4},{12,0},{1,13},{5,9},{9,5},{13,1},{2,14},{6,10},... | collective-permute-start | bytes 24584 | tf_op jit(solution)/shard_map/ppermute | solution.py:486
  12.7 0.0 copy-done.2
  12.7 1.6 %collective-permute-start.6 = (f32[48,128]{1,0:T(8,128)S(1)}, f32[48,128]{1,0:T(8,128)}, u32[]{:S(2)}, u32[]{:S(2)}) collective-permute-start(f32[48,128]{1,0:T(8,128)S(1)} %copy-done.2), channel_id=1, source_target_pairs={{0,8},{4,12},{8,0},{12,4},{1,9},{5,13},{9,1},{13,5},{2,10},{6,14},... | collective-permute-start | bytes 73736 | tf_op jit(solution)/shard_map/ppermute | solution.py:483
  14.4 0.9 %collective-permute-start.5 = (f32[8,256]{1,0:T(8,128)S(1)}, f32[8,256]{1,0:T(8,128)}, u32[]{:S(2)}, u32[]{:S(2)}) collective-permute-start(f32[8,256]{1,0:T(8,128)S(1)} %pad_maximum_fusion.1), channel_id=1, source_target_pairs={{0,4},{4,0},{8,12},{12,8},{1,5},{5,1},{9,13},{13,9},{2,6},{6,2},{1... | collective-permute-start | bytes 24584 | tf_op jit(solution)/shard_map/ppermute | solution.py:486
  15.3 1.3 %collective-permute-done.4.refs_15_ = f32[8,256]{1,0:T(8,128)} collective-permute-done((f32[8,256]{1,0:T(8,128)S(1)}, f32[8,256]{1,0:T(8,128)}, u32[]{:S(2)}, u32[]{:S(2)}) %collective-permute-start.4) | collective-permute-done | bytes 8224 | tf_op jit(solution)/shard_map/ppermute | solution.py:486
  16.5 1.6 %collective-permute-done.5.refs_16_ = f32[8,256]{1,0:T(8,128)} collective-permute-done((f32[8,256]{1,0:T(8,128)S(1)}, f32[8,256]{1,0:T(8,128)}, u32[]{:S(2)}, u32[]{:S(2)}) %collective-permute-start.5) | collective-permute-done | bytes 8224 | tf_op jit(solution)/shard_map/ppermute | solution.py:486
  18.1 0.0 collective-permute-done.6.refs_18_
  18.1 0.0 collective-permute-done.refs_11_
  18.1 0.0 collective-permute-done.1.refs_12_
  18.1 4.2 %steps.1 = (f32[3,16,16,128]{3,2,1,0:T(8,128)}, f32[2,8,16,128]{3,2,1,0:T(8,128)}) custom-call(f32[16]{0:T(128)} %refs_0_.3, f32[3,16,16,128]{3,2,1,0:T(8,128)} %refs_1_.3, f32[2,8,16,128]{3,2,1,0:T(8,128)} %refs_2_.3, f32[16,128]{1,0:T(8,128)} %refs_3_.3, f32[16,128]{1,0:T(8,128)} %refs_4_.3, s32[16,128]{1,0:T(8,128)} %refs_5_.3, s32[1,2048]{1,0:T(1,128)} %bitcast.5, ...), custom_call_target="tpu_custom_call" | custom-call | tf_op jit(solution)/shard_map/steps/pallas_call | solution.py:509
  (4 shorter events, 0.0 us)
Async XLA Ops:
  3.5 6.7 %collective-permute-start.3 = (f32[16,256]{1,0:T(8,128)}, f32[16,256]{1,0:T(8,128)S(1)}, u32[]{:S(2)}, u32[]{:S(2)}) collective-permute-start(f32[16,256]{1,0:T(8,128)} %get-tuple-element.18), channel_id=1, source_target_pairs={{0,3},{1,2},{2,1},{3,0},{4,7},{5,6},{6,5},{7,4},{8,11},{9,10},{10,... | collective-permute-start | bytes 49160 | tf_op jit(solution)/shard_map/ppermute | solution.py:486
  5.9 4.3 %collective-permute-start.2 = (f32[16,256]{1,0:T(8,128)}, f32[16,256]{1,0:T(8,128)S(1)}, u32[]{:S(2)}, u32[]{:S(2)}) collective-permute-start(f32[16,256]{1,0:T(8,128)} %get-tuple-element.15), channel_id=1, source_target_pairs={{0,1},{1,0},{2,3},{3,2},{4,5},{5,4},{6,7},{7,6},{8,9},{9,8},{10,11... | collective-permute-start | bytes 49160 | tf_op jit(solution)/shard_map/ppermute | solution.py:486
  6.6 11.5 %collective-permute-start = (f32[184,128]{1,0:T(8,128)}, f32[184,128]{1,0:T(8,128)}, u32[]{:S(2)}, u32[]{:S(2)}) collective-permute-start(f32[184,128]{1,0:T(8,128)} %get-tuple-element.13), channel_id=1, source_target_pairs={{0,12},{4,8},{8,4},{12,0},{1,13},{5,9},{9,5},{13,1},{2,14},{6,10},... | collective-permute-start | bytes 282632 | tf_op jit(solution)/shard_map/ppermute | solution.py:486
  10.2 7.9 %collective-permute-start.1 = (f32[184,128]{1,0:T(8,128)}, f32[184,128]{1,0:T(8,128)}, u32[]{:S(2)}, u32[]{:S(2)}) collective-permute-start(f32[184,128]{1,0:T(8,128)} %get-tuple-element.14), channel_id=1, source_target_pairs={{0,4},{4,0},{8,12},{12,8},{1,5},{5,1},{9,13},{13,9},{2,6},{6,2},{1... | collective-permute-start | bytes 282632 | tf_op jit(solution)/shard_map/ppermute | solution.py:486
  10.2 0.6 %copy-start = (f32[16,256]{1,0:T(8,128)}, f32[16,256]{1,0:T(8,128)S(1)}, u32[]{:S(2)}) copy-start(f32[16,256]{1,0:T(8,128)S(1)} %collective-permute-done.3.refs_14_) | copy-start | bytes 49156
  10.2 2.5 %copy-start.2 = (f32[48,128]{1,0:T(8,128)S(1)}, f32[48,128]{1,0:T(8,128)}, u32[]{:S(2)}) copy-start(f32[48,128]{1,0:T(8,128)} %get-tuple-element.21) | copy-start | bytes 73732
  10.2 0.6 %copy-start.1 = (f32[16,256]{1,0:T(8,128)}, f32[16,256]{1,0:T(8,128)S(1)}, u32[]{:S(2)}) copy-start(f32[16,256]{1,0:T(8,128)S(1)} %collective-permute-done.2.refs_13_) | copy-start | bytes 49156
  10.8 5.7 %collective-permute-start.4 = (f32[8,256]{1,0:T(8,128)S(1)}, f32[8,256]{1,0:T(8,128)}, u32[]{:S(2)}, u32[]{:S(2)}) collective-permute-start(f32[8,256]{1,0:T(8,128)S(1)} %pad_maximum_fusion), channel_id=1, source_target_pairs={{0,12},{4,8},{8,4},{12,0},{1,13},{5,9},{9,5},{13,1},{2,14},{6,10},... | collective-permute-start | bytes 24584 | tf_op jit(solution)/shard_map/ppermute | solution.py:486
  12.7 5.4 %collective-permute-start.6 = (f32[48,128]{1,0:T(8,128)S(1)}, f32[48,128]{1,0:T(8,128)}, u32[]{:S(2)}, u32[]{:S(2)}) collective-permute-start(f32[48,128]{1,0:T(8,128)S(1)} %copy-done.2), channel_id=1, source_target_pairs={{0,8},{4,12},{8,0},{12,4},{1,9},{5,13},{9,1},{13,5},{2,10},{6,14},... | collective-permute-start | bytes 73736 | tf_op jit(solution)/shard_map/ppermute | solution.py:483
  14.4 3.8 %collective-permute-start.5 = (f32[8,256]{1,0:T(8,128)S(1)}, f32[8,256]{1,0:T(8,128)}, u32[]{:S(2)}, u32[]{:S(2)}) collective-permute-start(f32[8,256]{1,0:T(8,128)S(1)} %pad_maximum_fusion.1), channel_id=1, source_target_pairs={{0,4},{4,0},{8,12},{12,8},{1,5},{5,1},{9,13},{13,9},{2,6},{6,2},{1... | collective-permute-start | bytes 24584 | tf_op jit(solution)/shard_map/ppermute | solution.py:486
